TPU v7x, 256 devices: a whole 4x4x8 slice. The times are simulated.
256 devices in a mesh: ctx: 128 (over x, y, z), tp: 2 (over core).
Axes of the slice: x: 4, y: 4, z: 8, core: 2. Of those that a mesh axis runs over, the one named last changes fastest.
Arguments:
- x_in: bfloat16 [16384, 32, 128], P('ctx', 'tp'), may hold values from -60 to 60
- z_in: bfloat16 [16384, 32, 128], P('ctx', 'tp'), may hold values from -6 to 6
- b_in: bfloat16 [16384, 128], P('ctx'), may hold values from -0.29882812 to 0.29882812
- c_in: bfloat16 [16384, 128], P('ctx'), may hold values from -0.5 to 0.5
- log_decay: float32 [32, 16384], P('tp', 'ctx'), may hold values from -1 to 0
- d_skip: float32 [32], P('tp'), may hold values from 0.5 to 1.5
- norm_gain: float32 [32, 128], P('tp'), may hold values from 0.1 to 1.9
- w_out: bfloat16 [4096, 2048], P('tp'), may hold values from -0.09375 to 0.09375
Outputs:
- mixed: bfloat16 [16384, 2048], P(('ctx', 'tp'))
All inputs are finite; a program needn't handle non-finite values.
Results may differ from a plain program's by a relative error of at most 0.005.
Values sent between devices are 32-bit elements; how exact they have to be, the bound alone decides.
No kernel may reach another device: no remote copies, remote signals or barrier semaphores. Data moves between devices by JAX's collectives and lax.ppermute only.
A program may use at most 320 MiB of HBM per device.

v0:
```python
import jax
import jax.numpy as jnp
from jax import lax
from jax.sharding import PartitionSpec as P


def prefix(value, axis, join, neutral):
    count, mine = (lax.axis_size(axis), lax.axis_index(axis))
    pieces = jax.tree.map(lambda part: lax.all_gather(part, axis), value)
    so_far = jax.tree.map(
        lambda part, zero: jnp.full_like(part, 0) + jnp.asarray(zero, part.dtype), value, neutral
    )

    def hop(position, so_far):
        longer = join(so_far, jax.tree.map(lambda part: part[position], pieces))
        return jax.tree.map(lambda new, old: jnp.where(position < mine, new, old), longer, so_far)

    return lax.fori_loop(0, count - 1, hop, so_far)


def join_states(earlier, later):
    return (earlier[0] * later[0], later[0][:, None, None] * earlier[1] + later[1])


def per_device(x_in, z_in, b_in, c_in, log_decay, d_skip, norm_gain, w_out):
    length = x_in.shape[0]
    heads = x_in.shape[1]
    width = x_in.shape[2]
    states = b_in.shape[1]
    highest = lax.Precision.HIGHEST
    block = min(128, length)
    count = length // block
    positions = jnp.arange(block)
    lower = positions[:, None] >= positions[None, :]
    x_blocks = x_in.reshape(count, block, heads, width)
    b_blocks = b_in.reshape(count, block, states)
    c_blocks = c_in.reshape(count, block, states)
    decay_blocks = log_decay.reshape(heads, count, block).transpose(1, 0, 2)

    def advance(state, pieces):
        x_blk, b_blk, c_blk, decay_blk = pieces
        cum = jnp.cumsum(decay_blk, axis=1)
        differ = cum[:, :, None] - cum[:, None, :]
        within = jnp.where(lower[None], jnp.exp(jnp.where(lower[None], differ, 0.0)), 0.0)
        scores = jnp.dot(c_blk, b_blk.T, preferred_element_type=jnp.float32)
        block_weights = (within * scores[None]).astype(jnp.bfloat16)
        inner = jnp.einsum("hts,shp->thp", block_weights, x_blk, preferred_element_type=jnp.float32)
        x_wide = x_blk.astype(jnp.float32)
        b_wide = b_blk.astype(jnp.float32)
        c_wide = c_blk.astype(jnp.float32)
        carried = jnp.einsum("tn,hnp->thp", c_wide, state, precision=highest)
        carried = jnp.exp(cum).T[:, :, None] * carried
        last = cum[:, -1]
        weights = jnp.exp(last[:, None] - cum)
        fresh = jnp.einsum("sn,shp->hnp", b_wide, x_wide * weights.T[:, :, None], precision=highest)
        new_state = jnp.exp(last)[:, None, None] * state + fresh
        return (new_state, inner + carried)

    start = jnp.zeros((heads, states, width), jnp.float32)
    local_state, partial_value = lax.scan(
        advance, start, (x_blocks, b_blocks, c_blocks, decay_blocks)
    )
    partial_value = partial_value.reshape(length, heads, width)
    cum_all = jnp.cumsum(log_decay, axis=1)
    total = jnp.exp(jnp.sum(log_decay, axis=1))
    identity = (jnp.ones_like(total), jnp.zeros_like(local_state))
    _, state_in = prefix((total, local_state), "ctx", join_states, identity)
    c_wide = c_in.astype(jnp.float32)
    entering = jnp.einsum("tn,hnp->thp", c_wide, state_in, precision=highest)
    entering = jnp.exp(cum_all).T[:, :, None] * entering
    ssm_out = partial_value + entering + d_skip[None, :, None] * x_in.astype(jnp.float32)
    gated = ssm_out * jax.nn.silu(z_in.astype(jnp.float32))
    meansq = jnp.mean(gated * gated, axis=-1, keepdims=True)
    normed = (gated * lax.rsqrt(meansq + 1e-05) * norm_gain[None]).astype(jnp.bfloat16)
    normed = normed.reshape(length, heads * width)
    summed = lax.psum_scatter(
        jnp.dot(normed, w_out, preferred_element_type=jnp.float32),
        "tp",
        scatter_dimension=0,
        tiled=True,
    )
    return summed.astype(jnp.bfloat16)


def solution(mesh):
    return jax.shard_map(
        per_device,
        mesh=mesh,
        in_specs=(
            P("ctx", "tp", None),
            P("ctx", "tp", None),
            P("ctx", None),
            P("ctx", None),
            P("tp", "ctx"),
            P("tp"),
            P("tp", None),
            P("tp", None),
        ),
        out_specs=P(("ctx", "tp"), None),
        check_vma=False,
    )
```

profile of v0, /device:TPU:1, one launch (start us, length us, event | category | flops | bytes accessed | tf_op | source)
XLA Modules:
  0.0 848.0 jit_solution(14917046088485742616)
XLA Ops:
  7.8 1.5 copy.23
  15.0 310.3 %all-reduce = f32[2048]{0:T(1024)S(1)} all-reduce(f32[2048]{0:T(1024)S(1)} %exponential_dynamic-update-slice_fusion), channel_id=2, replica_groups=mesh['ctx'=128,'tp'=2] {'ctx'}, use_global_device_ids=true, to_apply=%add | all-reduce | flops 2048 | bytes 16384
  325.3 1.5 copy.27
  328.3 301.4 %all-gather.4.cloned.1.call-done = f32[2048,128,128]{2,1,0:T(8,128)} async-done(((f32[16,128,128]{2,1,0:T(8,128)}), f32[2048,128,128]{2,1,0:T(8,128)}) %all-gather.4.cloned.1.call-update) | async-done | bytes 134217744 | tf_op jit(solution)/shard_map/all_gather | solution.py:9
  629.7 190.3 %while.9 = (s32[]{:T(128)}, f32[16,128,128]{2,1,0:T(8,128)S(1)}, s32[]{:T(128)}, f32[128,16]{1,0:T(8,128)S(1)}, f32[128,16,128,128]{3,2,1,0:T(8,128)}, /*index=5*/s32[]{:T(128)}, s32[]{:T(128)}) while((s32[]{:T(128)}, f32[16,128,128]{2,1,0:T(8,128)S(1)}, s32[]{:T(128)}, f32[128,16]{1,0:T(8,128)S(1)}, ...), condition=%wide.region_3.4_spmd.clone, body=%wide.region_2.3_spmd.clone.sunk | while | flops 1048580 | bytes 3146025 | solution.py:18
  629.7 1.5 fusion.32
  631.2 1.5 fusion.32
  634.2 1.5 fusion.32
  635.7 1.5 fusion.32
  637.2 1.5 fusion.32
  638.7 1.5 fusion.32
  641.7 1.5 fusion.32
  643.2 1.5 fusion.32
  646.2 1.5 fusion.32
  647.7 1.5 fusion.32
  649.2 1.5 fusion.32
  650.7 1.5 fusion.32
  653.7 1.5 fusion.32
  655.2 1.5 fusion.32
  658.2 1.5 fusion.32
  659.7 1.5 fusion.32
  662.7 1.5 fusion.32
  664.2 1.5 fusion.32
  665.7 1.5 fusion.32
  667.2 1.5 fusion.32
  670.2 1.5 fusion.32
  671.7 1.5 fusion.32
  674.7 1.5 fusion.32
  676.2 1.5 fusion.32
  677.7 1.5 fusion.32
  679.2 1.5 fusion.32
  682.2 1.5 fusion.32
  683.7 1.5 fusion.32
  686.7 1.5 fusion.32
  688.2 1.5 fusion.32
  691.2 1.5 fusion.32
  692.7 1.5 fusion.32
  694.2 1.5 fusion.32
  695.7 1.5 fusion.32
  698.7 1.5 fusion.32
  700.2 1.5 fusion.32
  703.2 1.5 fusion.32
  704.7 1.5 fusion.32
  706.2 1.5 fusion.32
  707.7 1.5 fusion.32
  710.7 1.5 fusion.32
  712.2 1.5 fusion.32
  715.2 1.5 fusion.32
  716.7 1.5 fusion.32
  719.7 1.5 fusion.32
  721.2 1.5 fusion.32
  722.7 1.5 fusion.32
  724.2 1.5 fusion.32
  727.2 1.5 fusion.32
  728.7 1.5 fusion.32
  731.7 1.5 fusion.32
  733.2 1.5 fusion.32
  734.7 1.5 fusion.32
  736.2 1.5 fusion.32
  739.1 1.5 fusion.32
  740.6 1.5 fusion.32
  822.4 5.7 fusion.24
  828.1 11.2 %reduce-scatter.2.cloned.1.call-done = f32[64,2048]{1,0:T(8,128)} async-done(((f32[128,2048]{1,0:T(8,128)}), f32[64,2048]{1,0:T(8,128)}) %reduce-scatter.2.cloned.1.call-update) | async-done | bytes 524304 | tf_op jit(solution)/shard_map/reduce_scatter | solution.py:76
  839.3 1.8 convert_element_type.27
  (227 shorter events, 114.9 us)
Async XLA Ops:
  6.5 320.3 %copy-start = (bf16[128,128]{1,0:T(8,128)(2,1)S(1)}, bf16[128,128]{1,0:T(8,128)(2,1)}, u32[]{:S(2)}) copy-start(bf16[128,128]{1,0:T(8,128)(2,1)} %param.13) | copy-start | bytes 98308
  6.5 623.2 %all-gather.4.cloned.1.call-start = ((), (), s32[]{:S(2)}) async-start(), calls=%async_computation.2 | async-start | bytes 135266304 | tf_op jit(solution)/shard_map/all_gather | solution.py:9
  12.0 827.3 %reduce-scatter.2.cloned.1.call-start = ((), (), s32[]{:S(2)}) async-start(), calls=%async_computation.1 | async-start | bytes 1572864 | tf_op jit(solution)/shard_map/reduce_scatter | solution.py:76
  629.7 191.4 %copy-start.2 = (f32[16]{0:T(128)S(1)}, f32[16]{0:T(128)}, u32[]{:S(2)}) copy-start(f32[16]{0:T(128)} %param.15) | copy-start | bytes 196
  820.1 2.0 copy-start.1
Sparse Core Ops, SparseCore 0:
  12.2 617.5 all-gather.3
  828.2 11.0 reduce-scatter.1
where the time goes:
time: 853 us; the launch traced here: 848 us
  waiting for transfers between devices  313 us (37%)
  blocking collectives  310 us (36%)
  other arithmetic  189 us (22%)
  between operations  14.2 us (2%)
  matrix products  10.5 us (1%)
    unnamed x1, blocking collectives  310 us
    all_gather x1, waiting for transfers between devices, prefix(): pieces = jax.tree.map(lambda part: lax.all_gather(part, axis), value)  301 us
    select_n x127, other arithmetic, hop(): jnp.where(position < mine, new, old)  185 us
  transfers between devices with their start and end apart: 2, of which 2 were waited for; matrix products, arithmetic and copies ran while one was open for 1% of the time, Pallas kernels for 0%

commit v1 on v0

v1 whole, which is shorter than its diff:
```python
import functools

import jax
import jax.numpy as jnp
from jax import lax
from jax.experimental import pallas as pl
from jax.experimental.pallas import tpu as pltpu
from jax.sharding import PartitionSpec as P

F32 = jnp.float32
BF16 = jnp.bfloat16
HIGHEST = lax.Precision.HIGHEST
NX, NY, NZ = 4, 4, 8
HEADS = 16
W = 128
CHUNKS = 2
PER_CHUNK = HEADS // CHUNKS
OWN = PER_CHUNK // NZ
ROWS = OWN * W
MSG = ROWS + 8
VMEM = pl.BlockSpec(memory_space=pltpu.VMEM)
SMEM = pl.BlockSpec(memory_space=pltpu.SMEM)


def z_shift(k):
    return [(i, i // NZ * NZ + (i + k) % NZ) for i in range(NX * NY * NZ)]


def y_shift(k):
    span = NY * NZ
    return [(i, i // span * span + (i + k * NZ) % span) for i in range(NX * NY * NZ)]


def x_shift(k):
    total = NX * NY * NZ
    return [(i, (i + k * NY * NZ) % total) for i in range(total)]


def split(value):
    high = value.astype(BF16)
    return high, (value - high.astype(F32)).astype(BF16)


def lower_mask():
    rows = lax.broadcasted_iota(jnp.int32, (W, W), 0)
    columns = lax.broadcasted_iota(jnp.int32, (W, W), 1)
    return rows >= columns


def running_sum(log_decay):
    upper = jnp.where(lower_mask(), 1.0, 0.0).T
    return jnp.dot(log_decay, upper, precision=HIGHEST, preferred_element_type=F32)


def decay_tile(rows):
    place = lax.broadcasted_iota(jnp.int32, (8, W), 0)
    tile = jnp.zeros((8, W), F32)
    for i, row in enumerate(rows):
        tile = jnp.where(place == i, jnp.broadcast_to(row, (8, W)), tile)
    return tile


def local_state_kernel(chunk, pos, x, b, log_decay, *refs):
    outs, cum_ref = refs[:NZ], refs[NZ]
    cum_ref[...] = running_sum(log_decay[...])
    b_t = b[...].astype(F32).T
    for k in range(NZ):
        owner = (pos[0] + k) & (NZ - 1)
        lasts = []
        for i in range(OWN):
            head = chunk * PER_CHUNK + owner * OWN + i
            cum = cum_ref[pl.ds(head, 1), :]
            last = jnp.broadcast_to(cum[:, W - 1 :], (1, W))
            high, low = split(b_t * jnp.exp(last - cum))
            x_head = x[:, pl.ds(pl.multiple_of(head * W, W), W)]
            state = jnp.dot(high, x_head, preferred_element_type=F32)
            state += jnp.dot(low, x_head, preferred_element_type=F32)
            outs[k][i * W : (i + 1) * W, :] = state
            lasts.append(last)
        outs[k][ROWS:, :] = decay_tile(lasts)


def row_total_kernel(pos, *refs):
    parts, out = refs[:NZ], refs[NZ]
    places = [(pos[0] - k) & (NZ - 1) for k in range(NZ)]
    totals = []
    for i in range(OWN):
        logs = [part[ROWS + i : ROWS + i + 1, :] for part in parts]
        total = jnp.zeros((W, W), F32)
        for k in range(NZ):
            after = jnp.zeros((1, W), F32)
            for j in range(NZ):
                if j != k:
                    after += jnp.where(places[j] > places[k], logs[j], 0.0)
            total += jnp.exp(after) * parts[k][i * W : (i + 1) * W, :]
        out[i * W : (i + 1) * W, :] = total
        totals.append(sum(logs))
    out[ROWS:, :] = decay_tile(totals)


def plane_kernel(pos, *refs):
    parts, plane, before = refs[:NY], refs[NY], refs[NY + 1]
    places = [(pos[1] - k) & (NY - 1) for k in range(NY)]
    plane_logs, before_logs = [], []
    for i in range(OWN):
        logs = [part[ROWS + i : ROWS + i + 1, :] for part in parts]
        total = jnp.zeros((W, W), F32)
        earlier = jnp.zeros((W, W), F32)
        to_row = jnp.zeros((1, W), F32)
        for k in range(NY):
            after = jnp.zeros((1, W), F32)
            between = jnp.zeros((1, W), F32)
            for j in range(NY):
                if j != k:
                    later = jnp.where(places[j] > places[k], logs[j], 0.0)
                    after += later
                    between += jnp.where(places[j] < pos[1], later, 0.0)
            piece = parts[k][i * W : (i + 1) * W, :]
            total += jnp.exp(after) * piece
            if k > 0:
                mine = places[k] < pos[1]
                earlier += jnp.where(mine, jnp.exp(between), 0.0) * piece
                to_row += jnp.where(mine, logs[k], 0.0)
        plane[i * W : (i + 1) * W, :] = total
        before[i * W : (i + 1) * W, :] = earlier
        plane_logs.append(sum(logs))
        before_logs.append(to_row)
    plane[ROWS:, :] = decay_tile(plane_logs)
    before[ROWS:, :] = decay_tile(before_logs)


def entering_kernel(pos, *refs):
    planes, before = refs[: NX - 1], refs[NX - 1]
    parts = refs[NX : NX + NZ]
    outs = refs[NX + NZ : NX + 2 * NZ]
    ordered, entering = refs[NX + 2 * NZ :]
    for k in range(NZ):
        ordered[(pos[0] - k) & (NZ - 1)] = parts[k][...]
    for i in range(OWN):
        carry = jnp.zeros((W, W), F32)
        between = jnp.zeros((1, W), F32)
        for k in range(1, NX):
            earlier = k <= pos[2]
            piece = planes[k - 1][i * W : (i + 1) * W, :]
            carry += jnp.where(earlier, jnp.exp(between), 0.0) * piece
            between += jnp.where(earlier, planes[k - 1][ROWS + i : ROWS + i + 1, :], 0.0)
        carry = jnp.exp(before[ROWS + i : ROWS + i + 1, :]) * carry
        carry += before[i * W : (i + 1) * W, :]
        for place in range(NZ):
            entering[place, i * W : (i + 1) * W, :] = carry
            if place < NZ - 1:
                decay = jnp.exp(ordered[place, ROWS + i : ROWS + i + 1, :])
                carry = decay * carry + ordered[place, i * W : (i + 1) * W, :]
    for k in range(NZ):
        outs[k][...] = entering[(pos[0] + k) & (NZ - 1)]


def inside_kernel(skip, x, z, b, c, log_decay, fixed, slope):
    lower = lower_mask()
    logs = log_decay[...]
    cum = running_sum(logs)
    cum_t = lax.dot_general(
        jnp.where(lower, 1.0, 0.0), logs, (((1,), (1,)), ((), ())),
        precision=HIGHEST, preferred_element_type=F32,
    )
    scores = lax.dot_general(c[...], b[...], (((1,), (1,)), ((), ())), preferred_element_type=F32)
    for head in range(HEADS):
        at = slice(head * W, (head + 1) * W)
        column = cum_t[:, head : head + 1]
        differ = column - cum[head : head + 1, :]
        within = jnp.where(lower, jnp.exp(jnp.where(lower, differ, 0.0)), 0.0)
        x_head = x[:, at]
        inner = jnp.dot((within * scores).astype(BF16), x_head, preferred_element_type=F32)
        gate = z[:, at].astype(F32)
        gate = gate / (1.0 + jnp.exp(-gate))
        fixed[:, at] = (inner + skip[head] * x_head.astype(F32)) * gate
        slope[:, at] = jnp.exp(column) * gate


def head_norm_kernel(chunk, pos, *refs):
    states = refs[:NZ]
    c, fixed, slope, gain, normed = refs[NZ:]
    read = c[...]
    for k in range(NZ):
        owner = (pos[0] - k) & (NZ - 1)
        for i in range(OWN):
            local = owner * OWN + i
            head = chunk * PER_CHUNK + local
            high, low = split(states[k][i * W : (i + 1) * W, :])
            carried = jnp.dot(read, high, preferred_element_type=F32)
            carried += jnp.dot(read, low, preferred_element_type=F32)
            at = pl.ds(pl.multiple_of(head * W, W), W)
            gated = fixed[:, at] + slope[:, at] * carried
            meansq = jnp.mean(gated * gated, axis=-1, keepdims=True)
            value = gated * lax.rsqrt(meansq + 1e-05) * gain[pl.ds(head, 1), :]
            normed[:, pl.ds(pl.multiple_of(local * W, W), W)] = value.astype(BF16)


def call(kernel, outs, specs, scratch=(), flops=0, moved=0, name=None):
    return pl.pallas_call(
        kernel,
        out_shape=outs,
        in_specs=specs,
        out_specs=jax.tree.map(lambda _: VMEM, outs),
        scratch_shapes=scratch,
        compiler_params=pltpu.CompilerParams(vmem_limit_bytes=24 * 1024 * 1024),
        cost_estimate=pl.CostEstimate(flops=flops, bytes_accessed=moved, transcendentals=0),
        name=name,
    )


def shaped(*shape, dtype=F32):
    return jax.ShapeDtypeStruct(shape, dtype)


def per_device(x_in, z_in, b_in, c_in, log_decay, d_skip, norm_gain, w_out):
    index = lax.axis_index("ctx")
    pos = jnp.stack([index % NZ, index // NZ % NY, index // (NZ * NY)]).astype(jnp.int32)
    x = x_in.reshape(W, HEADS * W)
    message = [shaped(MSG, W)] * NZ
    kept, normed_parts = {}, []
    for chunk in range(CHUNKS):
        kept[chunk] = call(
            functools.partial(local_state_kernel, chunk), message, [SMEM, VMEM, VMEM, VMEM],
            [pltpu.VMEM((HEADS, W), F32)], moved=1 << 20, name=f"local_state_{chunk}",
        )(pos, x, b_in, log_decay)
    z = z_in.reshape(W, HEADS * W)
    fixed, slope = call(
        inside_kernel, [shaped(W, HEADS * W)] * 2, [SMEM] + [VMEM] * 5, moved=8 << 20, name="inside",
    )(d_skip, x, z, b_in, c_in, log_decay)
    for chunk in range(CHUNKS):
        out = kept[chunk]
        parts = [out[0]] + [lax.ppermute(out[k], "ctx", z_shift(k)) for k in range(1, NZ)]
        total = call(row_total_kernel, shaped(MSG, W), [SMEM] + [VMEM] * NZ, name=f"row_total_{chunk}")(pos, *parts)
        rows = [total] + [lax.ppermute(total, "ctx", y_shift(k)) for k in range(1, NY)]
        plane, before = call(
            plane_kernel, [shaped(MSG, W)] * 2, [SMEM] + [VMEM] * NY, name=f"plane_{chunk}"
        )(pos, *rows)
        planes = [lax.ppermute(plane, "ctx", x_shift(k)) for k in range(1, NX)]
        back = call(
            entering_kernel, [shaped(ROWS, W)] * NZ, [SMEM] + [VMEM] * (NX + NZ),
            [pltpu.VMEM((NZ, MSG, W), F32), pltpu.VMEM((NZ, ROWS, W), F32)], name=f"entering_{chunk}",
        )(pos, *planes, before, *parts)
        states = [back[0]] + [lax.ppermute(back[k], "ctx", z_shift(k)) for k in range(1, NZ)]
        normed_parts.append(call(
            functools.partial(head_norm_kernel, chunk), shaped(W, PER_CHUNK * W, dtype=BF16),
            [SMEM] + [VMEM] * (NZ + 4), name=f"head_norm_{chunk}",
        )(pos, *states, c_in, fixed, slope, norm_gain))
    mixed = sum(
        jnp.dot(
            normed, w_out[chunk * PER_CHUNK * W : (chunk + 1) * PER_CHUNK * W],
            preferred_element_type=F32,
        )
        for chunk, normed in enumerate(normed_parts)
    )
    core = lax.axis_index("tp")
    half = W // 2
    mine = lax.dynamic_slice_in_dim(mixed, core * half, half, 0)
    other = lax.dynamic_slice_in_dim(mixed, (1 - core) * half, half, 0)
    return (mine + lax.ppermute(other, "tp", [(0, 1), (1, 0)])).astype(BF16)


def solution(mesh):
    return jax.shard_map(
        per_device,
        mesh=mesh,
        in_specs=(
            P("ctx", "tp", None),
            P("ctx", "tp", None),
            P("ctx", None),
            P("ctx", None),
            P("tp", "ctx"),
            P("tp"),
            P("tp", None),
            P("tp", None),
        ),
        out_specs=P(("ctx", "tp"), None),
        check_vma=False,
    )
```

time: 853 us -> 109 us (0.13)
  blocking collectives: 310 us -> 0 us
  waiting for transfers between devices: 313 us -> 3.01 us
  other arithmetic: 189 us -> 0.83 us
  starting transfers between devices: 0.04 us -> 83.5 us
  between operations: 14.2 us -> 0.21 us
  Pallas kernels: 0 us -> 10.1 us
    unnamed x1 -> x0, blocking collectives: 310 us -> none
    all_gather x1 -> x0, waiting for transfers between devices: 301 us -> none  [prefix(): pieces = jax.tree.map(lambda part: lax.all_gather(part, axis), value)]
    select_n x127 -> x0, other arithmetic: 185 us -> none  [hop(): jnp.where(position < mine, new, old)]
    ppermute x0 -> x41, starting transfers between devices: none -> 83.5 us  [the longest x14 31.1 us: per_device(): lax.ppermute(out[k], 'ctx', z_shift(k))]
    reduce_scatter x1 -> x0, waiting for transfers between devices: 11.2 us -> none  [per_device(): lax.psum_scatter(jnp.dot(normed, w_out, preferred_element_type=jnp.float3...]
    pallas_call x0 -> x11, Pallas kernels: none -> 10.1 us  [the longest x2 2.68 us: per_device(): call(functools.partial(local_state_kernel, chunk), message, [SMEM, VMEM,...]
  transfers between devices with their start and end apart: 2 -> 41, of which waited for: 2 -> 5; matrix products, arithmetic and copies ran while one was open for 1% -> 3% of each run, Pallas kernels for 0% -> 7%
where the time goes in v1:
time: 109 us; the launch traced here: 108 us
  starting transfers between devices  83.5 us (77%)
  Pallas kernels  10.1 us (9%)
  local copies, waits for them, and re-layouts  7.26 us (7%)
  matrix products  3.65 us (3%)
  waiting for transfers between devices  3.01 us (3%)
    ppermute x14, starting transfers between devices, per_device(): lax.ppermute(out[k], 'ctx', z_shift(k))  31.1 us
    ppermute x14, starting transfers between devices, per_device(): lax.ppermute(back[k], 'ctx', z_shift(k))  26.8 us
    ppermute x6, starting transfers between devices, per_device(): lax.ppermute(total, 'ctx', y_shift(k))  10.3 us
    ppermute x6, starting transfers between devices, per_device(): planes = [lax.ppermute(plane, 'ctx', x_shift(k)) for k in range(1, NX)]  7.83 us
    ppermute x1, starting transfers between devices, per_device(): return (mine + lax.ppermute(other, 'tp', [(0, 1), (1, 0)])).astype(BF16)  7.41 us
    unnamed x18, local copies, waits for them, and re-layouts  5.78 us
    dot_general x2, matrix products, per_device(): jnp.dot(normed, w_out[chunk * PER_CHUNK * W:(chunk + 1) * PER_CHUNK * W],...  3.65 us
    pallas_call x2, Pallas kernels, per_device(): call(functools.partial(local_state_kernel, chunk), message, [SMEM, VMEM,...  2.68 us
  transfers between devices with their start and end apart: 41, of which 5 were waited for; matrix products, arithmetic and copies ran while one was open for 3% of the time, Pallas kernels for 7%

profile of v1, /device:TPU:1, one launch (start us, length us, event | category | flops | bytes accessed | tf_op | source)
XLA Modules:
  0.0 108.5 jit_solution(8505645532230934171)
XLA Ops:
  0.0 1.4 %copy_bitcast_fusion = (bf16[128,2048]{1,0:T(8,128)(2,1)S(1)}, bf16[128,2048]{1,0:T(8,128)(2,1)S(1)}) fusion(bf16[16,8,16,128]{3,2,1,0:T(8,128)(2,1)} %bitcast.11, bf16[16,8,16,128]{3,2,1,0:T(8,128)(2,1)} %bitcast.12), kind=kLoop, calls=%fused_computation.5 | loop fusion | bytes 2097152 | tf_op jit(solution)/shard_map/reshape | solution.py:227
  1.5 0.8 copy-done.2
  2.3 0.7 copy-done.4
  3.0 1.3 %local_state_0.1 = (f32[136,128]{1,0:T(8,128)S(1)}, f32[136,128]{1,0:T(8,128)S(1)}, f32[136,128]{1,0:T(8,128)S(1)}, f32[136,128]{1,0:T(8,128)S(1)}, f32[136,128]...) custom-call(s32[3]{0:T(128)S(1)} %pad_add_fusion.pos, ...), custom_call_target="tpu_custom_call" | custom-call | bytes 1048576 | tf_op jit(solution)/shard_map/local_state_0/pallas_call | solution.py:223
  4.3 2.5 %collective-permute-start = (f32[136,128]{1,0:T(8,128)S(1)}, f32[136,128]{1,0:T(8,128)S(1)}, u32[]{:S(2)}, u32[]{:S(2)}) collective-permute-start(f32[136,128]{1,0:T(8,128)S(1)} %get-tuple-element.44), channel_id=1, source_target_pairs={{0,2},{2,4},{4,6},{6,8},{8,10},{10,12},{12,14},{14,0},{16,18},{18,... | collective-permute-start | bytes 208904 | tf_op jit(solution)/shard_map/ppermute | solution.py:233
  6.9 3.0 %collective-permute-start.1 = (f32[136,128]{1,0:T(8,128)S(1)}, f32[136,128]{1,0:T(8,128)S(1)}, u32[]{:S(2)}, u32[]{:S(2)}) collective-permute-start(f32[136,128]{1,0:T(8,128)S(1)} %get-tuple-element.45), channel_id=1, source_target_pairs={{0,4},{2,6},{4,8},{6,10},{8,12},{10,14},{12,0},{14,2},{16,20},{18,... | collective-permute-start | bytes 208904 | tf_op jit(solution)/shard_map/ppermute | solution.py:233
  9.9 1.3 %local_state_1.1 = (f32[136,128]{1,0:T(8,128)S(1)}, f32[136,128]{1,0:T(8,128)S(1)}, f32[136,128]{1,0:T(8,128)S(1)}, f32[136,128]{1,0:T(8,128)S(1)}, f32[136,128]...) custom-call(s32[3]{0:T(128)S(1)} %pad_add_fusion.pos, ...), custom_call_target="tpu_custom_call" | custom-call | bytes 1048576 | tf_op jit(solution)/shard_map/local_state_1/pallas_call | solution.py:223
  11.2 2.9 %collective-permute-start.20 = (f32[136,128]{1,0:T(8,128)S(1)}, f32[136,128]{1,0:T(8,128)S(1)}, u32[]{:S(2)}, u32[]{:S(2)}) collective-permute-start(f32[136,128]{1,0:T(8,128)S(1)} %get-tuple-element.64), channel_id=1, source_target_pairs={{0,2},{2,4},{4,6},{6,8},{8,10},{10,12},{12,14},{14,0},{16,18},{18,... | collective-permute-start | bytes 208904 | tf_op jit(solution)/shard_map/ppermute | solution.py:233
  14.1 1.2 %collective-permute-start.21 = (f32[136,128]{1,0:T(8,128)S(1)}, f32[136,128]{1,0:T(8,128)S(1)}, u32[]{:S(2)}, u32[]{:S(2)}) collective-permute-start(f32[136,128]{1,0:T(8,128)S(1)} %get-tuple-element.65), channel_id=1, source_target_pairs={{0,4},{2,6},{4,8},{6,10},{8,12},{10,14},{12,0},{14,2},{16,20},{18,... | collective-permute-start | bytes 208904 | tf_op jit(solution)/shard_map/ppermute | solution.py:233
  15.3 0.5 collective-permute-start.22
  15.8 4.5 %collective-permute-start.23 = (f32[136,128]{1,0:T(8,128)S(1)}, f32[136,128]{1,0:T(8,128)S(1)}, u32[]{:S(2)}, u32[]{:S(2)}) collective-permute-start(f32[136,128]{1,0:T(8,128)S(1)} %get-tuple-element.67), channel_id=1, source_target_pairs={{0,8},{2,10},{4,12},{6,14},{8,0},{10,2},{12,4},{14,6},{16,24},{18,... | collective-permute-start | bytes 208904 | tf_op jit(solution)/shard_map/ppermute | solution.py:233
  20.3 3.4 %collective-permute-start.25 = (f32[136,128]{1,0:T(8,128)S(1)}, f32[136,128]{1,0:T(8,128)S(1)}, u32[]{:S(2)}, u32[]{:S(2)}) collective-permute-start(f32[136,128]{1,0:T(8,128)S(1)} %get-tuple-element.69), channel_id=1, source_target_pairs={{0,12},{2,14},{4,0},{6,2},{8,4},{10,6},{12,8},{14,10},{16,28},{18,... | collective-permute-start | bytes 208904 | tf_op jit(solution)/shard_map/ppermute | solution.py:233
  23.6 1.4 %collective-permute-start.26 = (f32[136,128]{1,0:T(8,128)S(1)}, f32[136,128]{1,0:T(8,128)S(1)}, u32[]{:S(2)}, u32[]{:S(2)}) collective-permute-start(f32[136,128]{1,0:T(8,128)S(1)} %get-tuple-element.70), channel_id=1, source_target_pairs={{0,14},{2,0},{4,2},{6,4},{8,6},{10,8},{12,10},{14,12},{16,30},{18,... | collective-permute-start | bytes 208904 | tf_op jit(solution)/shard_map/ppermute | solution.py:233
  25.0 0.4 collective-permute-done.22.refs_3_.refs_7_
  25.8 4.6 %collective-permute-start.3 = (f32[136,128]{1,0:T(8,128)S(1)}, f32[136,128]{1,0:T(8,128)S(1)}, u32[]{:S(2)}, u32[]{:S(2)}) collective-permute-start(f32[136,128]{1,0:T(8,128)S(1)} %get-tuple-element.47), channel_id=1, source_target_pairs={{0,8},{2,10},{4,12},{6,14},{8,0},{10,2},{12,4},{14,6},{16,24},{18,... | collective-permute-start | bytes 208904 | tf_op jit(solution)/shard_map/ppermute | solution.py:233
  30.4 1.8 %collective-permute-start.4 = (f32[136,128]{1,0:T(8,128)S(1)}, f32[136,128]{1,0:T(8,128)S(1)}, u32[]{:S(2)}, u32[]{:S(2)}) collective-permute-start(f32[136,128]{1,0:T(8,128)S(1)} %get-tuple-element.48), channel_id=1, source_target_pairs={{0,10},{2,12},{4,14},{6,0},{8,2},{10,4},{12,6},{14,8},{16,26},{18,... | collective-permute-start | bytes 208904 | tf_op jit(solution)/shard_map/ppermute | solution.py:233
  32.1 3.2 %collective-permute-start.5 = (f32[136,128]{1,0:T(8,128)S(1)}, f32[136,128]{1,0:T(8,128)S(1)}, u32[]{:S(2)}, u32[]{:S(2)}) collective-permute-start(f32[136,128]{1,0:T(8,128)S(1)} %get-tuple-element.49), channel_id=1, source_target_pairs={{0,12},{2,14},{4,0},{6,2},{8,4},{10,6},{12,8},{14,10},{16,28},{18,... | collective-permute-start | bytes 208904 | tf_op jit(solution)/shard_map/ppermute | solution.py:233
  35.4 2.0 %collective-permute-start.6 = (f32[136,128]{1,0:T(8,128)S(1)}, f32[136,128]{1,0:T(8,128)S(1)}, u32[]{:S(2)}, u32[]{:S(2)}) collective-permute-start(f32[136,128]{1,0:T(8,128)S(1)} %get-tuple-element.50), channel_id=1, source_target_pairs={{0,14},{2,0},{4,2},{6,4},{8,6},{10,8},{12,10},{14,12},{16,30},{18,... | collective-permute-start | bytes 208904 | tf_op jit(solution)/shard_map/ppermute | solution.py:233
  37.4 0.6 row_total_1.1.refs_0_
  38.0 1.5 %collective-permute-start.27 = (f32[136,128]{1,0:T(8,128)S(1)}, f32[136,128]{1,0:T(8,128)S(1)}, u32[]{:S(2)}, u32[]{:S(2)}) collective-permute-start(f32[136,128]{1,0:T(8,128)S(1)} %row_total_1.1.refs_0_), channel_id=1, source_target_pairs={{0,16},{2,18},{4,20},{6,22},{8,24},{10,26},{12,28},{14,30},{16,32}... | collective-permute-start | bytes 208904 | tf_op jit(solution)/shard_map/ppermute | solution.py:235
  39.6 2.6 %collective-permute-start.28 = (f32[136,128]{1,0:T(8,128)S(1)}, f32[136,128]{1,0:T(8,128)S(1)}, u32[]{:S(2)}, u32[]{:S(2)}) collective-permute-start(f32[136,128]{1,0:T(8,128)S(1)} %row_total_1.1.refs_0_), channel_id=1, source_target_pairs={{0,32},{2,34},{4,36},{6,38},{8,40},{10,42},{12,44},{14,46},{16,48}... | collective-permute-start | bytes 208904 | tf_op jit(solution)/shard_map/ppermute | solution.py:235
  42.2 1.1 collective-permute-start.29
  43.3 0.3 collective-permute-done.6.refs_7_.refs_11_
  43.5 0.6 row_total_0.1.refs_0_
  44.2 1.3 %collective-permute-start.7 = (f32[136,128]{1,0:T(8,128)S(1)}, f32[136,128]{1,0:T(8,128)S(1)}, u32[]{:S(2)}, u32[]{:S(2)}) collective-permute-start(f32[136,128]{1,0:T(8,128)S(1)} %row_total_0.1.refs_0_), channel_id=1, source_target_pairs={{0,16},{2,18},{4,20},{6,22},{8,24},{10,26},{12,28},{14,30},{16,32}... | collective-permute-start | bytes 208904 | tf_op jit(solution)/shard_map/ppermute | solution.py:235
  45.5 2.7 %collective-permute-start.8 = (f32[136,128]{1,0:T(8,128)S(1)}, f32[136,128]{1,0:T(8,128)S(1)}, u32[]{:S(2)}, u32[]{:S(2)}) collective-permute-start(f32[136,128]{1,0:T(8,128)S(1)} %row_total_0.1.refs_0_), channel_id=1, source_target_pairs={{0,32},{2,34},{4,36},{6,38},{8,40},{10,42},{12,44},{14,46},{16,48}... | collective-permute-start | bytes 208904 | tf_op jit(solution)/shard_map/ppermute | solution.py:235
  48.2 1.1 collective-permute-start.9
  49.3 0.6 plane_1.1
  49.9 1.4 %collective-permute-start.30 = (f32[136,128]{1,0:T(8,128)S(1)}, f32[136,128]{1,0:T(8,128)S(1)}, u32[]{:S(2)}, u32[]{:S(2)}) collective-permute-start(f32[136,128]{1,0:T(8,128)S(1)} %get-tuple-element.71), channel_id=1, source_target_pairs={{0,64},{2,66},{4,68},{6,70},{8,72},{10,74},{12,76},{14,78},{16,80}... | collective-permute-start | bytes 208904 | tf_op jit(solution)/shard_map/ppermute | solution.py:239
  51.2 2.4 %collective-permute-start.31 = (f32[136,128]{1,0:T(8,128)S(1)}, f32[136,128]{1,0:T(8,128)S(1)}, u32[]{:S(2)}, u32[]{:S(2)}) collective-permute-start(f32[136,128]{1,0:T(8,128)S(1)} %get-tuple-element.71), channel_id=1, source_target_pairs={{0,128},{2,130},{4,132},{6,134},{8,136},{10,138},{12,140},{14,142}... | collective-permute-start | bytes 208904 | tf_op jit(solution)/shard_map/ppermute | solution.py:239
  53.7 1.1 %collective-permute-start.32 = (f32[136,128]{1,0:T(8,128)S(1)}, f32[136,128]{1,0:T(8,128)S(1)}, u32[]{:S(2)}, u32[]{:S(2)}) collective-permute-start(f32[136,128]{1,0:T(8,128)S(1)} %get-tuple-element.71), channel_id=1, source_target_pairs={{0,192},{2,194},{4,196},{6,198},{8,200},{10,202},{12,204},{14,206}... | collective-permute-start | bytes 208904 | tf_op jit(solution)/shard_map/ppermute | solution.py:239
  54.8 0.6 plane_0.1
  55.4 0.4 collective-permute-start.10
  55.8 0.9 collective-permute-start.11
  56.7 1.6 %collective-permute-start.12 = (f32[136,128]{1,0:T(8,128)S(1)}, f32[136,128]{1,0:T(8,128)S(1)}, u32[]{:S(2)}, u32[]{:S(2)}) collective-permute-start(f32[136,128]{1,0:T(8,128)S(1)} %get-tuple-element.51), channel_id=1, source_target_pairs={{0,192},{2,194},{4,196},{6,198},{8,200},{10,202},{12,204},{14,206}... | collective-permute-start | bytes 208904 | tf_op jit(solution)/shard_map/ppermute | solution.py:239
  58.3 0.7 entering_1.1
  59.0 2.2 %collective-permute-start.33 = (f32[128,128]{1,0:T(8,128)S(1)}, f32[128,128]{1,0:T(8,128)S(1)}, u32[]{:S(2)}, u32[]{:S(2)}) collective-permute-start(f32[128,128]{1,0:T(8,128)S(1)} %get-tuple-element.74), channel_id=1, source_target_pairs={{0,2},{2,4},{4,6},{6,8},{8,10},{10,12},{12,14},{14,0},{16,18},{18,... | collective-permute-start | bytes 196616 | tf_op jit(solution)/shard_map/ppermute | solution.py:244
  61.2 1.0 collective-permute-start.34
  62.2 3.4 %collective-permute-start.35 = (f32[128,128]{1,0:T(8,128)S(1)}, f32[128,128]{1,0:T(8,128)S(1)}, u32[]{:S(2)}, u32[]{:S(2)}) collective-permute-start(f32[128,128]{1,0:T(8,128)S(1)} %get-tuple-element.76), channel_id=1, source_target_pairs={{0,6},{2,8},{4,10},{6,12},{8,14},{10,0},{12,2},{14,4},{16,22},{18,... | collective-permute-start | bytes 196616 | tf_op jit(solution)/shard_map/ppermute | solution.py:244
  65.7 2.2 %collective-permute-start.36 = (f32[128,128]{1,0:T(8,128)S(1)}, f32[128,128]{1,0:T(8,128)S(1)}, u32[]{:S(2)}, u32[]{:S(2)}) collective-permute-start(f32[128,128]{1,0:T(8,128)S(1)} %get-tuple-element.77), channel_id=1, source_target_pairs={{0,8},{2,10},{4,12},{6,14},{8,0},{10,2},{12,4},{14,6},{16,24},{18,... | collective-permute-start | bytes 196616 | tf_op jit(solution)/shard_map/ppermute | solution.py:244
  67.9 2.9 %collective-permute-start.37 = (f32[128,128]{1,0:T(8,128)S(1)}, f32[128,128]{1,0:T(8,128)S(1)}, u32[]{:S(2)}, u32[]{:S(2)}) collective-permute-start(f32[128,128]{1,0:T(8,128)S(1)} %get-tuple-element.78), channel_id=1, source_target_pairs={{0,10},{2,12},{4,14},{6,0},{8,2},{10,4},{12,6},{14,8},{16,26},{18,... | collective-permute-start | bytes 196616 | tf_op jit(solution)/shard_map/ppermute | solution.py:244
  70.8 2.9 %collective-permute-start.38 = (f32[128,128]{1,0:T(8,128)S(1)}, f32[128,128]{1,0:T(8,128)S(1)}, u32[]{:S(2)}, u32[]{:S(2)}) collective-permute-start(f32[128,128]{1,0:T(8,128)S(1)} %get-tuple-element.79), channel_id=1, source_target_pairs={{0,12},{2,14},{4,0},{6,2},{8,4},{10,6},{12,8},{14,10},{16,28},{18,... | collective-permute-start | bytes 196616 | tf_op jit(solution)/shard_map/ppermute | solution.py:244
  73.7 0.7 entering_0.1
  74.4 1.5 %collective-permute-start.13 = (f32[128,128]{1,0:T(8,128)S(1)}, f32[128,128]{1,0:T(8,128)S(1)}, u32[]{:S(2)}, u32[]{:S(2)}) collective-permute-start(f32[128,128]{1,0:T(8,128)S(1)} %get-tuple-element.54), channel_id=1, source_target_pairs={{0,2},{2,4},{4,6},{6,8},{8,10},{10,12},{12,14},{14,0},{16,18},{18,... | collective-permute-start | bytes 196616 | tf_op jit(solution)/shard_map/ppermute | solution.py:244
  75.9 0.8 copy-done
  76.7 0.8 copy-done.3
  77.4 0.7 copy-done.5
  78.1 0.7 copy-done.7
  78.8 1.6 %inside.1 = (f32[128,2048]{1,0:T(8,128)S(1)}, f32[128,2048]{1,0:T(8,128)S(1)}) custom-call(f32[16]{0:T(128)S(1)} %copy-done.7, bf16[128,2048]{1,0:T(8,128)(2,1)S(1)} %get-tuple-element.82.x, bf16[128,2048]{1,0:T(8,128)(2,1)S(1)} %get-tuple-element.81.z, bf16[128,128]{1,0:T(8,128)(2,1)S(1)} %copy-done.3, bf16[128,128]{1,0:T(8,128)(2,1)S(1)} %copy-done, ...), custom_call_target="tpu_custom_call" | custom-call | bytes 8388608 | tf_op jit(solution)/shard_map/inside/pallas_call | solution.py:228
  80.4 1.3 %collective-permute-start.15 = (f32[128,128]{1,0:T(8,128)S(1)}, f32[128,128]{1,0:T(8,128)S(1)}, u32[]{:S(2)}, u32[]{:S(2)}) collective-permute-start(f32[128,128]{1,0:T(8,128)S(1)} %get-tuple-element.56), channel_id=1, source_target_pairs={{0,6},{2,8},{4,10},{6,12},{8,14},{10,0},{12,2},{14,4},{16,22},{18,... | collective-permute-start | bytes 196616 | tf_op jit(solution)/shard_map/ppermute | solution.py:244
  81.8 4.2 %collective-permute-start.16 = (f32[128,128]{1,0:T(8,128)S(1)}, f32[128,128]{1,0:T(8,128)S(1)}, u32[]{:S(2)}, u32[]{:S(2)}) collective-permute-start(f32[128,128]{1,0:T(8,128)S(1)} %get-tuple-element.57), channel_id=1, source_target_pairs={{0,8},{2,10},{4,12},{6,14},{8,0},{10,2},{12,4},{14,6},{16,24},{18,... | collective-permute-start | bytes 196616 | tf_op jit(solution)/shard_map/ppermute | solution.py:244
  86.0 2.6 %collective-permute-start.17 = (f32[128,128]{1,0:T(8,128)S(1)}, f32[128,128]{1,0:T(8,128)S(1)}, u32[]{:S(2)}, u32[]{:S(2)}) collective-permute-start(f32[128,128]{1,0:T(8,128)S(1)} %get-tuple-element.58), channel_id=1, source_target_pairs={{0,10},{2,12},{4,14},{6,0},{8,2},{10,4},{12,6},{14,8},{16,26},{18,... | collective-permute-start | bytes 196616 | tf_op jit(solution)/shard_map/ppermute | solution.py:244
  88.5 0.8 copy-done.1
  89.3 0.7 copy-done.6
  90.0 1.0 head_norm_1.1
  91.0 2.1 %collective-permute-start.18 = (f32[128,128]{1,0:T(8,128)S(1)}, f32[128,128]{1,0:T(8,128)S(1)}, u32[]{:S(2)}, u32[]{:S(2)}) collective-permute-start(f32[128,128]{1,0:T(8,128)S(1)} %get-tuple-element.59), channel_id=1, source_target_pairs={{0,12},{2,14},{4,0},{6,2},{8,4},{10,6},{12,8},{14,10},{16,28},{18,... | collective-permute-start | bytes 196616 | tf_op jit(solution)/shard_map/ppermute | solution.py:244
  93.1 0.4 collective-permute-start.19
  93.5 2.9 %fusion = f32[128,2048]{1,0:T(8,128)S(1)} fusion(bf16[128,1024]{1,0:T(8,128)(2,1)S(1)} %head_norm_1.1, bf16[2048,2048]{1,0:T(8,128)(2,1)} %param.15), kind=kOutput, calls=%fused_computation | convolution fusion | flops 536870912 | bytes 5505024 | tf_op jit(solution)/shard_map/dot_general | solution.py:250
  96.5 0.5 collective-permute-done.19.refs_7_
  97.0 1.0 head_norm_0.1
  98.0 0.7 fusion.4
  98.8 7.4 %collective-permute-start.40 = (f32[64,2048]{1,0:T(8,128)S(1)}, f32[64,2048]{1,0:T(8,128)S(1)}, u32[]{:S(2)}, u32[]{:S(2)}) collective-permute-start(f32[64,2048]{1,0:T(8,128)S(1)} %constant_dynamic-slice_fusion), channel_id=1, source_target_pairs={{0,1},{1,0},{2,3},{3,2},{4,5},{5,4},{6,7},{7,6},{8,9},{9,8},{10,11... | collective-permute-start | bytes 1572872 | tf_op jit(solution)/shard_map/ppermute | solution.py:260
  106.2 1.5 %collective-permute-done.40 = f32[64,2048]{1,0:T(8,128)S(1)} collective-permute-done((f32[64,2048]{1,0:T(8,128)S(1)}, f32[64,2048]{1,0:T(8,128)S(1)}, u32[]{:S(2)}, u32[]{:S(2)}) %collective-permute-start.40) | collective-permute-done | bytes 524320 | tf_op jit(solution)/shard_map/ppermute | solution.py:260
  107.7 0.8 add_convert_fusion
  (53 shorter events, 0.7 us)
Async XLA Ops:
  1.5 0.8 copy-start.2
  2.3 0.7 copy-start.4
  4.3 11.5 %collective-permute-start = (f32[136,128]{1,0:T(8,128)S(1)}, f32[136,128]{1,0:T(8,128)S(1)}, u32[]{:S(2)}, u32[]{:S(2)}) collective-permute-start(f32[136,128]{1,0:T(8,128)S(1)} %get-tuple-element.44), channel_id=1, source_target_pairs={{0,2},{2,4},{4,6},{6,8},{8,10},{10,12},{12,14},{14,0},{16,18},{18,... | collective-permute-start | bytes 208904 | tf_op jit(solution)/shard_map/ppermute | solution.py:233
  6.9 13.4 %collective-permute-start.1 = (f32[136,128]{1,0:T(8,128)S(1)}, f32[136,128]{1,0:T(8,128)S(1)}, u32[]{:S(2)}, u32[]{:S(2)}) collective-permute-start(f32[136,128]{1,0:T(8,128)S(1)} %get-tuple-element.45), channel_id=1, source_target_pairs={{0,4},{2,6},{4,8},{6,10},{8,12},{10,14},{12,0},{14,2},{16,20},{18,... | collective-permute-start | bytes 208904 | tf_op jit(solution)/shard_map/ppermute | solution.py:233
  11.2 9.1 %collective-permute-start.20 = (f32[136,128]{1,0:T(8,128)S(1)}, f32[136,128]{1,0:T(8,128)S(1)}, u32[]{:S(2)}, u32[]{:S(2)}) collective-permute-start(f32[136,128]{1,0:T(8,128)S(1)} %get-tuple-element.64), channel_id=1, source_target_pairs={{0,2},{2,4},{4,6},{6,8},{8,10},{10,12},{12,14},{14,0},{16,18},{18,... | collective-permute-start | bytes 208904 | tf_op jit(solution)/shard_map/ppermute | solution.py:233
  14.1 9.5 %collective-permute-start.21 = (f32[136,128]{1,0:T(8,128)S(1)}, f32[136,128]{1,0:T(8,128)S(1)}, u32[]{:S(2)}, u32[]{:S(2)}) collective-permute-start(f32[136,128]{1,0:T(8,128)S(1)} %get-tuple-element.65), channel_id=1, source_target_pairs={{0,4},{2,6},{4,8},{6,10},{8,12},{10,14},{12,0},{14,2},{16,20},{18,... | collective-permute-start | bytes 208904 | tf_op jit(solution)/shard_map/ppermute | solution.py:233
  15.3 10.1 %collective-permute-start.22 = (f32[136,128]{1,0:T(8,128)S(1)}, f32[136,128]{1,0:T(8,128)S(1)}, u32[]{:S(2)}, u32[]{:S(2)}) collective-permute-start(f32[136,128]{1,0:T(8,128)S(1)} %get-tuple-element.66), channel_id=1, source_target_pairs={{0,6},{2,8},{4,10},{6,12},{8,14},{10,0},{12,2},{14,4},{16,22},{18,... | collective-permute-start | bytes 208904 | tf_op jit(solution)/shard_map/ppermute | solution.py:233
  15.8 10.0 %collective-permute-start.23 = (f32[136,128]{1,0:T(8,128)S(1)}, f32[136,128]{1,0:T(8,128)S(1)}, u32[]{:S(2)}, u32[]{:S(2)}) collective-permute-start(f32[136,128]{1,0:T(8,128)S(1)} %get-tuple-element.67), channel_id=1, source_target_pairs={{0,8},{2,10},{4,12},{6,14},{8,0},{10,2},{12,4},{14,6},{16,24},{18,... | collective-permute-start | bytes 208904 | tf_op jit(solution)/shard_map/ppermute | solution.py:233
  20.2 10.1 %collective-permute-start.24 = (f32[136,128]{1,0:T(8,128)S(1)}, f32[136,128]{1,0:T(8,128)S(1)}, u32[]{:S(2)}, u32[]{:S(2)}) collective-permute-start(f32[136,128]{1,0:T(8,128)S(1)} %get-tuple-element.68), channel_id=1, source_target_pairs={{0,10},{2,12},{4,14},{6,0},{8,2},{10,4},{12,6},{14,8},{16,26},{18,... | collective-permute-start | bytes 208904 | tf_op jit(solution)/shard_map/ppermute | solution.py:233
  20.3 11.9 %collective-permute-start.25 = (f32[136,128]{1,0:T(8,128)S(1)}, f32[136,128]{1,0:T(8,128)S(1)}, u32[]{:S(2)}, u32[]{:S(2)}) collective-permute-start(f32[136,128]{1,0:T(8,128)S(1)} %get-tuple-element.69), channel_id=1, source_target_pairs={{0,12},{2,14},{4,0},{6,2},{8,4},{10,6},{12,8},{14,10},{16,28},{18,... | collective-permute-start | bytes 208904 | tf_op jit(solution)/shard_map/ppermute | solution.py:233
  23.6 11.7 %collective-permute-start.26 = (f32[136,128]{1,0:T(8,128)S(1)}, f32[136,128]{1,0:T(8,128)S(1)}, u32[]{:S(2)}, u32[]{:S(2)}) collective-permute-start(f32[136,128]{1,0:T(8,128)S(1)} %get-tuple-element.70), channel_id=1, source_target_pairs={{0,14},{2,0},{4,2},{6,4},{8,6},{10,8},{12,10},{14,12},{16,30},{18,... | collective-permute-start | bytes 208904 | tf_op jit(solution)/shard_map/ppermute | solution.py:233
  25.4 12.6 %collective-permute-start.2 = (f32[136,128]{1,0:T(8,128)S(1)}, f32[136,128]{1,0:T(8,128)S(1)}, u32[]{:S(2)}, u32[]{:S(2)}) collective-permute-start(f32[136,128]{1,0:T(8,128)S(1)} %get-tuple-element.46), channel_id=1, source_target_pairs={{0,6},{2,8},{4,10},{6,12},{8,14},{10,0},{12,2},{14,4},{16,22},{18,... | collective-permute-start | bytes 208904 | tf_op jit(solution)/shard_map/ppermute | solution.py:233
  25.8 13.8 %collective-permute-start.3 = (f32[136,128]{1,0:T(8,128)S(1)}, f32[136,128]{1,0:T(8,128)S(1)}, u32[]{:S(2)}, u32[]{:S(2)}) collective-permute-start(f32[136,128]{1,0:T(8,128)S(1)} %get-tuple-element.47), channel_id=1, source_target_pairs={{0,8},{2,10},{4,12},{6,14},{8,0},{10,2},{12,4},{14,6},{16,24},{18,... | collective-permute-start | bytes 208904 | tf_op jit(solution)/shard_map/ppermute | solution.py:233
  30.4 11.8 %collective-permute-start.4 = (f32[136,128]{1,0:T(8,128)S(1)}, f32[136,128]{1,0:T(8,128)S(1)}, u32[]{:S(2)}, u32[]{:S(2)}) collective-permute-start(f32[136,128]{1,0:T(8,128)S(1)} %get-tuple-element.48), channel_id=1, source_target_pairs={{0,10},{2,12},{4,14},{6,0},{8,2},{10,4},{12,6},{14,8},{16,26},{18,... | collective-permute-start | bytes 208904 | tf_op jit(solution)/shard_map/ppermute | solution.py:233
  32.1 11.1 %collective-permute-start.5 = (f32[136,128]{1,0:T(8,128)S(1)}, f32[136,128]{1,0:T(8,128)S(1)}, u32[]{:S(2)}, u32[]{:S(2)}) collective-permute-start(f32[136,128]{1,0:T(8,128)S(1)} %get-tuple-element.49), channel_id=1, source_target_pairs={{0,12},{2,14},{4,0},{6,2},{8,4},{10,6},{12,8},{14,10},{16,28},{18,... | collective-permute-start | bytes 208904 | tf_op jit(solution)/shard_map/ppermute | solution.py:233
  35.4 8.1 %collective-permute-start.6 = (f32[136,128]{1,0:T(8,128)S(1)}, f32[136,128]{1,0:T(8,128)S(1)}, u32[]{:S(2)}, u32[]{:S(2)}) collective-permute-start(f32[136,128]{1,0:T(8,128)S(1)} %get-tuple-element.50), channel_id=1, source_target_pairs={{0,14},{2,0},{4,2},{6,4},{8,6},{10,8},{12,10},{14,12},{16,30},{18,... | collective-permute-start | bytes 208904 | tf_op jit(solution)/shard_map/ppermute | solution.py:233
  38.0 10.1 %collective-permute-start.27 = (f32[136,128]{1,0:T(8,128)S(1)}, f32[136,128]{1,0:T(8,128)S(1)}, u32[]{:S(2)}, u32[]{:S(2)}) collective-permute-start(f32[136,128]{1,0:T(8,128)S(1)} %row_total_1.1.refs_0_), channel_id=1, source_target_pairs={{0,16},{2,18},{4,20},{6,22},{8,24},{10,26},{12,28},{14,30},{16,32}... | collective-permute-start | bytes 208904 | tf_op jit(solution)/shard_map/ppermute | solution.py:235
  39.6 9.7 %collective-permute-start.28 = (f32[136,128]{1,0:T(8,128)S(1)}, f32[136,128]{1,0:T(8,128)S(1)}, u32[]{:S(2)}, u32[]{:S(2)}) collective-permute-start(f32[136,128]{1,0:T(8,128)S(1)} %row_total_1.1.refs_0_), channel_id=1, source_target_pairs={{0,32},{2,34},{4,36},{6,38},{8,40},{10,42},{12,44},{14,46},{16,48}... | collective-permute-start | bytes 208904 | tf_op jit(solution)/shard_map/ppermute | solution.py:235
  42.2 7.1 %collective-permute-start.29 = (f32[136,128]{1,0:T(8,128)S(1)}, f32[136,128]{1,0:T(8,128)S(1)}, u32[]{:S(2)}, u32[]{:S(2)}) collective-permute-start(f32[136,128]{1,0:T(8,128)S(1)} %row_total_1.1.refs_0_), channel_id=1, source_target_pairs={{0,48},{2,50},{4,52},{6,54},{8,56},{10,58},{12,60},{14,62},{16,0},... | collective-permute-start | bytes 208904 | tf_op jit(solution)/shard_map/ppermute | solution.py:235
  44.2 9.5 %collective-permute-start.7 = (f32[136,128]{1,0:T(8,128)S(1)}, f32[136,128]{1,0:T(8,128)S(1)}, u32[]{:S(2)}, u32[]{:S(2)}) collective-permute-start(f32[136,128]{1,0:T(8,128)S(1)} %row_total_0.1.refs_0_), channel_id=1, source_target_pairs={{0,16},{2,18},{4,20},{6,22},{8,24},{10,26},{12,28},{14,30},{16,32}... | collective-permute-start | bytes 208904 | tf_op jit(solution)/shard_map/ppermute | solution.py:235
  45.5 9.3 %collective-permute-start.8 = (f32[136,128]{1,0:T(8,128)S(1)}, f32[136,128]{1,0:T(8,128)S(1)}, u32[]{:S(2)}, u32[]{:S(2)}) collective-permute-start(f32[136,128]{1,0:T(8,128)S(1)} %row_total_0.1.refs_0_), channel_id=1, source_target_pairs={{0,32},{2,34},{4,36},{6,38},{8,40},{10,42},{12,44},{14,46},{16,48}... | collective-permute-start | bytes 208904 | tf_op jit(solution)/shard_map/ppermute | solution.py:235
  48.2 6.6 %collective-permute-start.9 = (f32[136,128]{1,0:T(8,128)S(1)}, f32[136,128]{1,0:T(8,128)S(1)}, u32[]{:S(2)}, u32[]{:S(2)}) collective-permute-start(f32[136,128]{1,0:T(8,128)S(1)} %row_total_0.1.refs_0_), channel_id=1, source_target_pairs={{0,48},{2,50},{4,52},{6,54},{8,56},{10,58},{12,60},{14,62},{16,0},... | collective-permute-start | bytes 208904 | tf_op jit(solution)/shard_map/ppermute | solution.py:235
  49.9 6.8 %collective-permute-start.30 = (f32[136,128]{1,0:T(8,128)S(1)}, f32[136,128]{1,0:T(8,128)S(1)}, u32[]{:S(2)}, u32[]{:S(2)}) collective-permute-start(f32[136,128]{1,0:T(8,128)S(1)} %get-tuple-element.71), channel_id=1, source_target_pairs={{0,64},{2,66},{4,68},{6,70},{8,72},{10,74},{12,76},{14,78},{16,80}... | collective-permute-start | bytes 208904 | tf_op jit(solution)/shard_map/ppermute | solution.py:239
  51.2 7.1 %collective-permute-start.31 = (f32[136,128]{1,0:T(8,128)S(1)}, f32[136,128]{1,0:T(8,128)S(1)}, u32[]{:S(2)}, u32[]{:S(2)}) collective-permute-start(f32[136,128]{1,0:T(8,128)S(1)} %get-tuple-element.71), channel_id=1, source_target_pairs={{0,128},{2,130},{4,132},{6,134},{8,136},{10,138},{12,140},{14,142}... | collective-permute-start | bytes 208904 | tf_op jit(solution)/shard_map/ppermute | solution.py:239
  53.7 4.7 %collective-permute-start.32 = (f32[136,128]{1,0:T(8,128)S(1)}, f32[136,128]{1,0:T(8,128)S(1)}, u32[]{:S(2)}, u32[]{:S(2)}) collective-permute-start(f32[136,128]{1,0:T(8,128)S(1)} %get-tuple-element.71), channel_id=1, source_target_pairs={{0,192},{2,194},{4,196},{6,198},{8,200},{10,202},{12,204},{14,206}... | collective-permute-start | bytes 208904 | tf_op jit(solution)/shard_map/ppermute | solution.py:239
  55.4 6.8 %collective-permute-start.10 = (f32[136,128]{1,0:T(8,128)S(1)}, f32[136,128]{1,0:T(8,128)S(1)}, u32[]{:S(2)}, u32[]{:S(2)}) collective-permute-start(f32[136,128]{1,0:T(8,128)S(1)} %get-tuple-element.51), channel_id=1, source_target_pairs={{0,64},{2,66},{4,68},{6,70},{8,72},{10,74},{12,76},{14,78},{16,80}... | collective-permute-start | bytes 208904 | tf_op jit(solution)/shard_map/ppermute | solution.py:239
  55.8 9.9 %collective-permute-start.11 = (f32[136,128]{1,0:T(8,128)S(1)}, f32[136,128]{1,0:T(8,128)S(1)}, u32[]{:S(2)}, u32[]{:S(2)}) collective-permute-start(f32[136,128]{1,0:T(8,128)S(1)} %get-tuple-element.51), channel_id=1, source_target_pairs={{0,128},{2,130},{4,132},{6,134},{8,136},{10,138},{12,140},{14,142}... | collective-permute-start | bytes 208904 | tf_op jit(solution)/shard_map/ppermute | solution.py:239
  56.7 11.2 %collective-permute-start.12 = (f32[136,128]{1,0:T(8,128)S(1)}, f32[136,128]{1,0:T(8,128)S(1)}, u32[]{:S(2)}, u32[]{:S(2)}) collective-permute-start(f32[136,128]{1,0:T(8,128)S(1)} %get-tuple-element.51), channel_id=1, source_target_pairs={{0,192},{2,194},{4,196},{6,198},{8,200},{10,202},{12,204},{14,206}... | collective-permute-start | bytes 208904 | tf_op jit(solution)/shard_map/ppermute | solution.py:239
  59.0 11.8 %collective-permute-start.33 = (f32[128,128]{1,0:T(8,128)S(1)}, f32[128,128]{1,0:T(8,128)S(1)}, u32[]{:S(2)}, u32[]{:S(2)}) collective-permute-start(f32[128,128]{1,0:T(8,128)S(1)} %get-tuple-element.74), channel_id=1, source_target_pairs={{0,2},{2,4},{4,6},{6,8},{8,10},{10,12},{12,14},{14,0},{16,18},{18,... | collective-permute-start | bytes 196616 | tf_op jit(solution)/shard_map/ppermute | solution.py:244
  61.2 12.4 %collective-permute-start.34 = (f32[128,128]{1,0:T(8,128)S(1)}, f32[128,128]{1,0:T(8,128)S(1)}, u32[]{:S(2)}, u32[]{:S(2)}) collective-permute-start(f32[128,128]{1,0:T(8,128)S(1)} %get-tuple-element.75), channel_id=1, source_target_pairs={{0,4},{2,6},{4,8},{6,10},{8,12},{10,14},{12,0},{14,2},{16,20},{18,... | collective-permute-start | bytes 196616 | tf_op jit(solution)/shard_map/ppermute | solution.py:244
  62.2 12.1 %collective-permute-start.35 = (f32[128,128]{1,0:T(8,128)S(1)}, f32[128,128]{1,0:T(8,128)S(1)}, u32[]{:S(2)}, u32[]{:S(2)}) collective-permute-start(f32[128,128]{1,0:T(8,128)S(1)} %get-tuple-element.76), channel_id=1, source_target_pairs={{0,6},{2,8},{4,10},{6,12},{8,14},{10,0},{12,2},{14,4},{16,22},{18,... | collective-permute-start | bytes 196616 | tf_op jit(solution)/shard_map/ppermute | solution.py:244
  65.7 10.2 %collective-permute-start.36 = (f32[128,128]{1,0:T(8,128)S(1)}, f32[128,128]{1,0:T(8,128)S(1)}, u32[]{:S(2)}, u32[]{:S(2)}) collective-permute-start(f32[128,128]{1,0:T(8,128)S(1)} %get-tuple-element.77), channel_id=1, source_target_pairs={{0,8},{2,10},{4,12},{6,14},{8,0},{10,2},{12,4},{14,6},{16,24},{18,... | collective-permute-start | bytes 196616 | tf_op jit(solution)/shard_map/ppermute | solution.py:244
  67.9 12.5 %collective-permute-start.37 = (f32[128,128]{1,0:T(8,128)S(1)}, f32[128,128]{1,0:T(8,128)S(1)}, u32[]{:S(2)}, u32[]{:S(2)}) collective-permute-start(f32[128,128]{1,0:T(8,128)S(1)} %get-tuple-element.78), channel_id=1, source_target_pairs={{0,10},{2,12},{4,14},{6,0},{8,2},{10,4},{12,6},{14,8},{16,26},{18,... | collective-permute-start | bytes 196616 | tf_op jit(solution)/shard_map/ppermute | solution.py:244
  70.8 11.0 %collective-permute-start.38 = (f32[128,128]{1,0:T(8,128)S(1)}, f32[128,128]{1,0:T(8,128)S(1)}, u32[]{:S(2)}, u32[]{:S(2)}) collective-permute-start(f32[128,128]{1,0:T(8,128)S(1)} %get-tuple-element.79), channel_id=1, source_target_pairs={{0,12},{2,14},{4,0},{6,2},{8,4},{10,6},{12,8},{14,10},{16,28},{18,... | collective-permute-start | bytes 196616 | tf_op jit(solution)/shard_map/ppermute | solution.py:244
  73.6 12.3 %collective-permute-start.39 = (f32[128,128]{1,0:T(8,128)S(1)}, f32[128,128]{1,0:T(8,128)S(1)}, u32[]{:S(2)}, u32[]{:S(2)}) collective-permute-start(f32[128,128]{1,0:T(8,128)S(1)} %get-tuple-element.80), channel_id=1, source_target_pairs={{0,14},{2,0},{4,2},{6,4},{8,6},{10,8},{12,10},{14,12},{16,30},{18,... | collective-permute-start | bytes 196616 | tf_op jit(solution)/shard_map/ppermute | solution.py:244
  74.4 16.6 %collective-permute-start.13 = (f32[128,128]{1,0:T(8,128)S(1)}, f32[128,128]{1,0:T(8,128)S(1)}, u32[]{:S(2)}, u32[]{:S(2)}) collective-permute-start(f32[128,128]{1,0:T(8,128)S(1)} %get-tuple-element.54), channel_id=1, source_target_pairs={{0,2},{2,4},{4,6},{6,8},{8,10},{10,12},{12,14},{14,0},{16,18},{18,... | collective-permute-start | bytes 196616 | tf_op jit(solution)/shard_map/ppermute | solution.py:244
  75.9 17.2 %collective-permute-start.14 = (f32[128,128]{1,0:T(8,128)S(1)}, f32[128,128]{1,0:T(8,128)S(1)}, u32[]{:S(2)}, u32[]{:S(2)}) collective-permute-start(f32[128,128]{1,0:T(8,128)S(1)} %get-tuple-element.55), channel_id=1, source_target_pairs={{0,4},{2,6},{4,8},{6,10},{8,12},{10,14},{12,0},{14,2},{16,20},{18,... | collective-permute-start | bytes 196616 | tf_op jit(solution)/shard_map/ppermute | solution.py:244
  75.9 0.8 copy-start
  76.6 0.8 copy-start.3
  77.4 0.7 copy-start.5
  78.1 0.7 copy-start.7
  80.4 16.0 %collective-permute-start.15 = (f32[128,128]{1,0:T(8,128)S(1)}, f32[128,128]{1,0:T(8,128)S(1)}, u32[]{:S(2)}, u32[]{:S(2)}) collective-permute-start(f32[128,128]{1,0:T(8,128)S(1)} %get-tuple-element.56), channel_id=1, source_target_pairs={{0,6},{2,8},{4,10},{6,12},{8,14},{10,0},{12,2},{14,4},{16,22},{18,... | collective-permute-start | bytes 196616 | tf_op jit(solution)/shard_map/ppermute | solution.py:244
  81.8 14.7 %collective-permute-start.16 = (f32[128,128]{1,0:T(8,128)S(1)}, f32[128,128]{1,0:T(8,128)S(1)}, u32[]{:S(2)}, u32[]{:S(2)}) collective-permute-start(f32[128,128]{1,0:T(8,128)S(1)} %get-tuple-element.57), channel_id=1, source_target_pairs={{0,8},{2,10},{4,12},{6,14},{8,0},{10,2},{12,4},{14,6},{16,24},{18,... | collective-permute-start | bytes 196616 | tf_op jit(solution)/shard_map/ppermute | solution.py:244
  86.0 10.5 %collective-permute-start.17 = (f32[128,128]{1,0:T(8,128)S(1)}, f32[128,128]{1,0:T(8,128)S(1)}, u32[]{:S(2)}, u32[]{:S(2)}) collective-permute-start(f32[128,128]{1,0:T(8,128)S(1)} %get-tuple-element.58), channel_id=1, source_target_pairs={{0,10},{2,12},{4,14},{6,0},{8,2},{10,4},{12,6},{14,8},{16,26},{18,... | collective-permute-start | bytes 196616 | tf_op jit(solution)/shard_map/ppermute | solution.py:244
  88.5 0.8 copy-start.1
  89.3 0.7 copy-start.6
  90.0 8.0 %copy-start.8 = (bf16[2048,2048]{1,0:T(8,128)(2,1)S(1)}, bf16[2048,2048]{1,0:T(8,128)(2,1)}, u32[]{:S(2)}) copy-start(bf16[2048,2048]{1,0:T(8,128)(2,1)} %param.15) | copy-start | bytes 25165828
  91.0 5.5 %collective-permute-start.18 = (f32[128,128]{1,0:T(8,128)S(1)}, f32[128,128]{1,0:T(8,128)S(1)}, u32[]{:S(2)}, u32[]{:S(2)}) collective-permute-start(f32[128,128]{1,0:T(8,128)S(1)} %get-tuple-element.59), channel_id=1, source_target_pairs={{0,12},{2,14},{4,0},{6,2},{8,4},{10,6},{12,8},{14,10},{16,28},{18,... | collective-permute-start | bytes 196616 | tf_op jit(solution)/shard_map/ppermute | solution.py:244
  93.1 3.9 %collective-permute-start.19 = (f32[128,128]{1,0:T(8,128)S(1)}, f32[128,128]{1,0:T(8,128)S(1)}, u32[]{:S(2)}, u32[]{:S(2)}) collective-permute-start(f32[128,128]{1,0:T(8,128)S(1)} %get-tuple-element.60), channel_id=1, source_target_pairs={{0,14},{2,0},{4,2},{6,4},{8,6},{10,8},{12,10},{14,12},{16,30},{18,... | collective-permute-start | bytes 196616 | tf_op jit(solution)/shard_map/ppermute | solution.py:244
  98.8 8.9 %collective-permute-start.40 = (f32[64,2048]{1,0:T(8,128)S(1)}, f32[64,2048]{1,0:T(8,128)S(1)}, u32[]{:S(2)}, u32[]{:S(2)}) collective-permute-start(f32[64,2048]{1,0:T(8,128)S(1)} %constant_dynamic-slice_fusion), channel_id=1, source_target_pairs={{0,1},{1,0},{2,3},{3,2},{4,5},{5,4},{6,7},{7,6},{8,9},{9,8},{10,11... | collective-permute-start | bytes 1572872 | tf_op jit(solution)/shard_map/ppermute | solution.py:260

commit v2 on v1

--- a/solution.py
+++ b/solution.py
@@ -13,7 +13,7 @@
 NX, NY, NZ = 4, 4, 8
 HEADS = 16
 W = 128
-CHUNKS = 2
+CHUNKS = 1
 PER_CHUNK = HEADS // CHUNKS
 OWN = PER_CHUNK // NZ
 ROWS = OWN * W

time: 109 us -> 106 us (0.972)
  starting transfers between devices: 83.5 us -> 42 us
  waiting for transfers between devices: 3.01 us -> 43.7 us
  Pallas kernels: 10.1 us -> 6.5 us
    ppermute x14 -> x7, waiting for transfers between devices: 0.89 us -> 18.3 us  [per_device(): lax.ppermute(out[k], 'ctx', z_shift(k))]
    ppermute x14 -> x7, starting transfers between devices: 26.8 us -> 12.2 us  [per_device(): lax.ppermute(back[k], 'ctx', z_shift(k))]
    ppermute x14 -> x7, waiting for transfers between devices: 0.56 us -> 15 us  [per_device(): lax.ppermute(back[k], 'ctx', z_shift(k))]
    ppermute x14 -> x7, starting transfers between devices: 31.1 us -> 17.5 us  [per_device(): lax.ppermute(out[k], 'ctx', z_shift(k))]
    ppermute x6 -> x3, starting transfers between devices: 10.3 us -> 5.05 us  [per_device(): lax.ppermute(total, 'ctx', y_shift(k))]
    ppermute x1, starting transfers between devices: 7.41 us -> 2.31 us  [per_device(): return (mine + lax.ppermute(other, 'tp', [(0, 1), (1, 0)])).astype(BF16)]
    ppermute x6 -> x3, waiting for transfers between devices: 0.02 us -> 4.79 us  [per_device(): lax.ppermute(total, 'ctx', y_shift(k))]
    ppermute x6 -> x3, waiting for transfers between devices: 0.02 us -> 4.03 us  [per_device(): planes = [lax.ppermute(plane, 'ctx', x_shift(k)) for k in range(1, NX)]]
  transfers between devices with their start and end apart: 41 -> 21, of which waited for: 5 -> 14; matrix products, arithmetic and copies ran while one was open for 3% -> 0% of each run, Pallas kernels for 7% -> 2%
where the time goes in v2:
time: 106 us; the launch traced here: 105 us
  waiting for transfers between devices  43.7 us (41%)
  starting transfers between devices  42 us (40%)
  local copies, waits for them, and re-layouts  7.26 us (7%)
  Pallas kernels  6.5 us (6%)
  matrix products  4.66 us (4%)
    ppermute x7, waiting for transfers between devices, per_device(): lax.ppermute(out[k], 'ctx', z_shift(k))  18.3 us
    ppermute x7, starting transfers between devices, per_device(): lax.ppermute(out[k], 'ctx', z_shift(k))  17.5 us
    ppermute x7, waiting for transfers between devices, per_device(): lax.ppermute(back[k], 'ctx', z_shift(k))  15 us
    ppermute x7, starting transfers between devices, per_device(): lax.ppermute(back[k], 'ctx', z_shift(k))  12.2 us
    unnamed x16, local copies, waits for them, and re-layouts  5.78 us
    ppermute x3, starting transfers between devices, per_device(): lax.ppermute(total, 'ctx', y_shift(k))  5.05 us
    ppermute x3, starting transfers between devices, per_device(): planes = [lax.ppermute(plane, 'ctx', x_shift(k)) for k in range(1, NX)]  4.89 us
    ppermute x3, waiting for transfers between devices, per_device(): lax.ppermute(total, 'ctx', y_shift(k))  4.79 us
  transfers between devices with their start and end apart: 21, of which 14 were waited for; matrix products, arithmetic and copies ran while one was open for 0% of the time, Pallas kernels for 2%

profile of v2, /device:TPU:1, one launch (start us, length us, event | category | flops | bytes accessed | tf_op | source)
XLA Modules:
  0.0 105.0 jit_solution(8192650700955336456)
XLA Ops:
  0.0 1.4 %copy_bitcast_fusion = (bf16[128,2048]{1,0:T(8,128)(2,1)S(1)}, bf16[128,2048]{1,0:T(8,128)(2,1)S(1)}) fusion(bf16[16,8,16,128]{3,2,1,0:T(8,128)(2,1)} %bitcast.11, bf16[16,8,16,128]{3,2,1,0:T(8,128)(2,1)} %bitcast.12), kind=kLoop, calls=%fused_computation | loop fusion | bytes 2097152 | tf_op jit(solution)/shard_map/reshape | solution.py:227
  1.4 0.1 pad_add_fusion.pos
  1.5 0.0 copy-start.2
  1.5 0.8 copy-done.2
  2.3 0.0 copy-start.4
  2.3 0.7 copy-done.4
  3.0 1.5 %local_state_0.1 = (f32[264,128]{1,0:T(8,128)S(1)}, f32[264,128]{1,0:T(8,128)S(1)}, f32[264,128]{1,0:T(8,128)S(1)}, f32[264,128]{1,0:T(8,128)S(1)}, f32[264,128]...) custom-call(s32[3]{0:T(128)S(1)} %pad_add_fusion.pos, ...), custom_call_target="tpu_custom_call" | custom-call | bytes 1048576 | tf_op jit(solution)/shard_map/local_state_0/pallas_call | solution.py:223
  4.5 2.5 %collective-permute-start = (f32[264,128]{1,0:T(8,128)S(1)}, f32[264,128]{1,0:T(8,128)S(1)}, u32[]{:S(2)}, u32[]{:S(2)}) collective-permute-start(f32[264,128]{1,0:T(8,128)S(1)} %get-tuple-element.26), channel_id=1, source_target_pairs={{0,2},{2,4},{4,6},{6,8},{8,10},{10,12},{12,14},{14,0},{16,18},{18,... | collective-permute-start | bytes 405512 | tf_op jit(solution)/shard_map/ppermute | solution.py:233
  7.0 3.0 %collective-permute-start.1 = (f32[264,128]{1,0:T(8,128)S(1)}, f32[264,128]{1,0:T(8,128)S(1)}, u32[]{:S(2)}, u32[]{:S(2)}) collective-permute-start(f32[264,128]{1,0:T(8,128)S(1)} %get-tuple-element.27), channel_id=1, source_target_pairs={{0,4},{2,6},{4,8},{6,10},{8,12},{10,14},{12,0},{14,2},{16,20},{18,... | collective-permute-start | bytes 405512 | tf_op jit(solution)/shard_map/ppermute | solution.py:233
  10.0 3.8 %collective-permute-start.2 = (f32[264,128]{1,0:T(8,128)S(1)}, f32[264,128]{1,0:T(8,128)S(1)}, u32[]{:S(2)}, u32[]{:S(2)}) collective-permute-start(f32[264,128]{1,0:T(8,128)S(1)} %get-tuple-element.28), channel_id=1, source_target_pairs={{0,6},{2,8},{4,10},{6,12},{8,14},{10,0},{12,2},{14,4},{16,22},{18,... | collective-permute-start | bytes 405512 | tf_op jit(solution)/shard_map/ppermute | solution.py:233
  13.8 0.5 collective-permute-start.3
  14.2 4.5 %collective-permute-start.4 = (f32[264,128]{1,0:T(8,128)S(1)}, f32[264,128]{1,0:T(8,128)S(1)}, u32[]{:S(2)}, u32[]{:S(2)}) collective-permute-start(f32[264,128]{1,0:T(8,128)S(1)} %get-tuple-element.30), channel_id=1, source_target_pairs={{0,10},{2,12},{4,14},{6,0},{8,2},{10,4},{12,6},{14,8},{16,26},{18,... | collective-permute-start | bytes 405512 | tf_op jit(solution)/shard_map/ppermute | solution.py:233
  18.7 0.0 collective-permute-done.refs_1_.refs_5_
  18.7 2.4 %collective-permute-start.5 = (f32[264,128]{1,0:T(8,128)S(1)}, f32[264,128]{1,0:T(8,128)S(1)}, u32[]{:S(2)}, u32[]{:S(2)}) collective-permute-start(f32[264,128]{1,0:T(8,128)S(1)} %get-tuple-element.31), channel_id=1, source_target_pairs={{0,12},{2,14},{4,0},{6,2},{8,4},{10,6},{12,8},{14,10},{16,28},{18,... | collective-permute-start | bytes 405512 | tf_op jit(solution)/shard_map/ppermute | solution.py:233
  21.1 0.0 collective-permute-done.1.refs_2_.refs_6_
  21.1 0.9 collective-permute-start.6
  22.0 8.0 %collective-permute-done.2.refs_3_.refs_7_ = f32[264,128]{1,0:T(8,128)S(1)} collective-permute-done((f32[264,128]{1,0:T(8,128)S(1)}, f32[264,128]{1,0:T(8,128)S(1)}, u32[]{:S(2)}, u32[]{:S(2)}) %collective-permute-start.2) | collective-permute-done | bytes 135200 | tf_op jit(solution)/shard_map/ppermute | solution.py:233
  30.0 1.3 %collective-permute-done.3.refs_4_.refs_8_ = f32[264,128]{1,0:T(8,128)S(1)} collective-permute-done((f32[264,128]{1,0:T(8,128)S(1)}, f32[264,128]{1,0:T(8,128)S(1)}, u32[]{:S(2)}, u32[]{:S(2)}) %collective-permute-start.3) | collective-permute-done | bytes 135200 | tf_op jit(solution)/shard_map/ppermute | solution.py:233
  31.3 0.0 collective-permute-done.4.refs_5_.refs_9_
  31.3 7.9 %collective-permute-done.5.refs_6_.refs_10_ = f32[264,128]{1,0:T(8,128)S(1)} collective-permute-done((f32[264,128]{1,0:T(8,128)S(1)}, f32[264,128]{1,0:T(8,128)S(1)}, u32[]{:S(2)}, u32[]{:S(2)}) %collective-permute-start.5) | collective-permute-done | bytes 135200 | tf_op jit(solution)/shard_map/ppermute | solution.py:233
  39.2 1.1 %collective-permute-done.6.refs_7_.refs_11_ = f32[264,128]{1,0:T(8,128)S(1)} collective-permute-done((f32[264,128]{1,0:T(8,128)S(1)}, f32[264,128]{1,0:T(8,128)S(1)}, u32[]{:S(2)}, u32[]{:S(2)}) %collective-permute-start.6) | collective-permute-done | bytes 135200 | tf_op jit(solution)/shard_map/ppermute | solution.py:233
  40.3 0.7 row_total_0.1.refs_0_
  41.0 1.4 %collective-permute-start.7 = (f32[264,128]{1,0:T(8,128)S(1)}, f32[264,128]{1,0:T(8,128)S(1)}, u32[]{:S(2)}, u32[]{:S(2)}) collective-permute-start(f32[264,128]{1,0:T(8,128)S(1)} %row_total_0.1.refs_0_), channel_id=1, source_target_pairs={{0,16},{2,18},{4,20},{6,22},{8,24},{10,26},{12,28},{14,30},{16,32}... | collective-permute-start | bytes 405512 | tf_op jit(solution)/shard_map/ppermute | solution.py:235
  42.4 2.6 %collective-permute-start.8 = (f32[264,128]{1,0:T(8,128)S(1)}, f32[264,128]{1,0:T(8,128)S(1)}, u32[]{:S(2)}, u32[]{:S(2)}) collective-permute-start(f32[264,128]{1,0:T(8,128)S(1)} %row_total_0.1.refs_0_), channel_id=1, source_target_pairs={{0,32},{2,34},{4,36},{6,38},{8,40},{10,42},{12,44},{14,46},{16,48}... | collective-permute-start | bytes 405512 | tf_op jit(solution)/shard_map/ppermute | solution.py:235
  45.0 1.1 %collective-permute-start.9 = (f32[264,128]{1,0:T(8,128)S(1)}, f32[264,128]{1,0:T(8,128)S(1)}, u32[]{:S(2)}, u32[]{:S(2)}) collective-permute-start(f32[264,128]{1,0:T(8,128)S(1)} %row_total_0.1.refs_0_), channel_id=1, source_target_pairs={{0,48},{2,50},{4,52},{6,54},{8,56},{10,58},{12,60},{14,62},{16,0},... | collective-permute-start | bytes 405512 | tf_op jit(solution)/shard_map/ppermute | solution.py:235
  46.1 0.8 collective-permute-done.7.refs_1_
  46.8 4.0 %collective-permute-done.8.refs_2_ = f32[264,128]{1,0:T(8,128)S(1)} collective-permute-done((f32[264,128]{1,0:T(8,128)S(1)}, f32[264,128]{1,0:T(8,128)S(1)}, u32[]{:S(2)}, u32[]{:S(2)}) %collective-permute-start.8) | collective-permute-done | bytes 135200 | tf_op jit(solution)/shard_map/ppermute | solution.py:235
  50.9 0.0 collective-permute-done.9.refs_3_
  50.9 0.6 plane_0.1
  51.5 1.3 %collective-permute-start.10 = (f32[264,128]{1,0:T(8,128)S(1)}, f32[264,128]{1,0:T(8,128)S(1)}, u32[]{:S(2)}, u32[]{:S(2)}) collective-permute-start(f32[264,128]{1,0:T(8,128)S(1)} %get-tuple-element.33), channel_id=1, source_target_pairs={{0,64},{2,66},{4,68},{6,70},{8,72},{10,74},{12,76},{14,78},{16,80}... | collective-permute-start | bytes 405512 | tf_op jit(solution)/shard_map/ppermute | solution.py:239
  52.8 2.4 %collective-permute-start.11 = (f32[264,128]{1,0:T(8,128)S(1)}, f32[264,128]{1,0:T(8,128)S(1)}, u32[]{:S(2)}, u32[]{:S(2)}) collective-permute-start(f32[264,128]{1,0:T(8,128)S(1)} %get-tuple-element.33), channel_id=1, source_target_pairs={{0,128},{2,130},{4,132},{6,134},{8,136},{10,138},{12,140},{14,142}... | collective-permute-start | bytes 405512 | tf_op jit(solution)/shard_map/ppermute | solution.py:239
  55.2 1.2 %collective-permute-start.12 = (f32[264,128]{1,0:T(8,128)S(1)}, f32[264,128]{1,0:T(8,128)S(1)}, u32[]{:S(2)}, u32[]{:S(2)}) collective-permute-start(f32[264,128]{1,0:T(8,128)S(1)} %get-tuple-element.33), channel_id=1, source_target_pairs={{0,192},{2,194},{4,196},{6,198},{8,200},{10,202},{12,204},{14,206}... | collective-permute-start | bytes 405512 | tf_op jit(solution)/shard_map/ppermute | solution.py:239
  56.4 0.3 collective-permute-done.10.refs_0_
  56.6 3.2 %collective-permute-done.11.refs_1_ = f32[264,128]{1,0:T(8,128)S(1)} collective-permute-done((f32[264,128]{1,0:T(8,128)S(1)}, f32[264,128]{1,0:T(8,128)S(1)}, u32[]{:S(2)}, u32[]{:S(2)}) %collective-permute-start.11) | collective-permute-done | bytes 135200 | tf_op jit(solution)/shard_map/ppermute | solution.py:239
  59.9 0.5 collective-permute-done.12.refs_2_
  60.4 0.8 entering_0.1
  61.2 3.2 %collective-permute-start.13 = (f32[256,128]{1,0:T(8,128)S(1)}, f32[256,128]{1,0:T(8,128)S(1)}, u32[]{:S(2)}, u32[]{:S(2)}) collective-permute-start(f32[256,128]{1,0:T(8,128)S(1)} %get-tuple-element.36), channel_id=1, source_target_pairs={{0,2},{2,4},{4,6},{6,8},{8,10},{10,12},{12,14},{14,0},{16,18},{18,... | collective-permute-start | bytes 393224 | tf_op jit(solution)/shard_map/ppermute | solution.py:244
  64.5 0.9 collective-permute-start.14
  65.3 0.3 collective-permute-start.15
  65.6 4.5 %collective-permute-start.16 = (f32[256,128]{1,0:T(8,128)S(1)}, f32[256,128]{1,0:T(8,128)S(1)}, u32[]{:S(2)}, u32[]{:S(2)}) collective-permute-start(f32[256,128]{1,0:T(8,128)S(1)} %get-tuple-element.39), channel_id=1, source_target_pairs={{0,8},{2,10},{4,12},{6,14},{8,0},{10,2},{12,4},{14,6},{16,24},{18,... | collective-permute-start | bytes 393224 | tf_op jit(solution)/shard_map/ppermute | solution.py:244
  70.1 0.7 collective-permute-start.17
  70.8 0.0 collective-permute-done.13.refs_1_
  70.8 2.6 %collective-permute-start.18 = (f32[256,128]{1,0:T(8,128)S(1)}, f32[256,128]{1,0:T(8,128)S(1)}, u32[]{:S(2)}, u32[]{:S(2)}) collective-permute-start(f32[256,128]{1,0:T(8,128)S(1)} %get-tuple-element.41), channel_id=1, source_target_pairs={{0,12},{2,14},{4,0},{6,2},{8,4},{10,6},{12,8},{14,10},{16,28},{18,... | collective-permute-start | bytes 393224 | tf_op jit(solution)/shard_map/ppermute | solution.py:244
  73.4 1.4 %collective-permute-done.14.refs_2_ = f32[256,128]{1,0:T(8,128)S(1)} collective-permute-done((f32[256,128]{1,0:T(8,128)S(1)}, f32[256,128]{1,0:T(8,128)S(1)}, u32[]{:S(2)}, u32[]{:S(2)}) %collective-permute-start.14) | collective-permute-done | bytes 131104 | tf_op jit(solution)/shard_map/ppermute | solution.py:244
  74.8 0.0 collective-permute-start.19
  74.8 0.0 copy-start
  74.8 0.8 copy-done
  75.5 0.0 copy-start.3
  75.5 0.8 copy-done.3
  76.3 0.7 copy-done.5
  77.0 0.7 copy-done.7
  77.6 1.6 %inside.1 = (f32[128,2048]{1,0:T(8,128)S(1)}, f32[128,2048]{1,0:T(8,128)S(1)}) custom-call(f32[16]{0:T(128)S(1)} %copy-done.7, bf16[128,2048]{1,0:T(8,128)(2,1)S(1)} %get-tuple-element.46.x, bf16[128,2048]{1,0:T(8,128)(2,1)S(1)} %get-tuple-element.45.z, bf16[128,128]{1,0:T(8,128)(2,1)S(1)} %copy-done.3, bf16[128,128]{1,0:T(8,128)(2,1)S(1)} %copy-done, ...), custom_call_target="tpu_custom_call" | custom-call | bytes 8388608 | tf_op jit(solution)/shard_map/inside/pallas_call | solution.py:228
  79.3 0.0 collective-permute-done.15.refs_3_
  79.3 2.7 %collective-permute-done.16.refs_4_ = f32[256,128]{1,0:T(8,128)S(1)} collective-permute-done((f32[256,128]{1,0:T(8,128)S(1)}, f32[256,128]{1,0:T(8,128)S(1)}, u32[]{:S(2)}, u32[]{:S(2)}) %collective-permute-start.16) | collective-permute-done | bytes 131104 | tf_op jit(solution)/shard_map/ppermute | solution.py:244
  82.0 0.0 collective-permute-done.17.refs_5_
  82.0 8.7 %collective-permute-done.18.refs_6_ = f32[256,128]{1,0:T(8,128)S(1)} collective-permute-done((f32[256,128]{1,0:T(8,128)S(1)}, f32[256,128]{1,0:T(8,128)S(1)}, u32[]{:S(2)}, u32[]{:S(2)}) %collective-permute-start.18) | collective-permute-done | bytes 131104 | tf_op jit(solution)/shard_map/ppermute | solution.py:244
  90.7 2.2 %collective-permute-done.19.refs_7_ = f32[256,128]{1,0:T(8,128)S(1)} collective-permute-done((f32[256,128]{1,0:T(8,128)S(1)}, f32[256,128]{1,0:T(8,128)S(1)}, u32[]{:S(2)}, u32[]{:S(2)}) %collective-permute-start.19) | collective-permute-done | bytes 131104 | tf_op jit(solution)/shard_map/ppermute | solution.py:244
  92.9 0.8 copy-done.1
  93.7 0.7 copy-done.6
  94.4 1.2 %head_norm_0.1 = bf16[128,2048]{1,0:T(8,128)(2,1)S(1)} custom-call(s32[3]{0:T(128)S(1)} %pad_add_fusion.pos, f32[256,128]{1,0:T(8,128)S(1)} %get-tuple-element.35.refs_0_, f32[256,128]{1,0:T(8,128)S(1)} %collective-permute-done.13.refs_1_, f32[256,128]{1,0:T(8,128)S(1)} %collective-permute-done.14.refs_2_, f32[256,128]{1,0:T(8,128)S(1)} %collective-permute-done.15.refs_3_, ...), custom_call_target="tpu_custom_call" | custom-call | tf_op jit(solution)/shard_map/head_norm_0/pallas_call | solution.py:245
  95.6 4.7 %fusion = f32[128,2048]{1,0:T(8,128)S(1)} fusion(bf16[128,2048]{1,0:T(8,128)(2,1)S(1)} %head_norm_0.1, bf16[2048,2048]{1,0:T(8,128)(2,1)} %param.15), kind=kOutput, calls=%fused_computation.5 | convolution fusion | flops 1073741824 | bytes 9961472 | tf_op jit(solution)/shard_map/dot_general | solution.py:250
  100.4 2.3 %collective-permute-start.20 = (f32[64,2048]{1,0:T(8,128)S(1)}, f32[64,2048]{1,0:T(8,128)S(1)}, u32[]{:S(2)}, u32[]{:S(2)}) collective-permute-start(f32[64,2048]{1,0:T(8,128)S(1)} %constant_dynamic-slice_fusion), channel_id=1, source_target_pairs={{0,1},{1,0},{2,3},{3,2},{4,5},{5,4},{6,7},{7,6},{8,9},{9,8},{10,11... | collective-permute-start | bytes 1572872 | tf_op jit(solution)/shard_map/ppermute | solution.py:260
  102.7 1.5 %collective-permute-done.20 = f32[64,2048]{1,0:T(8,128)S(1)} collective-permute-done((f32[64,2048]{1,0:T(8,128)S(1)}, f32[64,2048]{1,0:T(8,128)S(1)}, u32[]{:S(2)}, u32[]{:S(2)}) %collective-permute-start.20) | collective-permute-done | bytes 524320 | tf_op jit(solution)/shard_map/ppermute | solution.py:260
  104.2 0.8 add_convert_fusion
  (5 shorter events, 0.1 us)
Async XLA Ops:
  1.5 0.8 copy-start.2
  2.3 0.7 copy-start.4
  4.5 14.2 %collective-permute-start = (f32[264,128]{1,0:T(8,128)S(1)}, f32[264,128]{1,0:T(8,128)S(1)}, u32[]{:S(2)}, u32[]{:S(2)}) collective-permute-start(f32[264,128]{1,0:T(8,128)S(1)} %get-tuple-element.26), channel_id=1, source_target_pairs={{0,2},{2,4},{4,6},{6,8},{8,10},{10,12},{12,14},{14,0},{16,18},{18,... | collective-permute-start | bytes 405512 | tf_op jit(solution)/shard_map/ppermute | solution.py:233
  7.0 14.1 %collective-permute-start.1 = (f32[264,128]{1,0:T(8,128)S(1)}, f32[264,128]{1,0:T(8,128)S(1)}, u32[]{:S(2)}, u32[]{:S(2)}) collective-permute-start(f32[264,128]{1,0:T(8,128)S(1)} %get-tuple-element.27), channel_id=1, source_target_pairs={{0,4},{2,6},{4,8},{6,10},{8,12},{10,14},{12,0},{14,2},{16,20},{18,... | collective-permute-start | bytes 405512 | tf_op jit(solution)/shard_map/ppermute | solution.py:233
  10.0 20.0 %collective-permute-start.2 = (f32[264,128]{1,0:T(8,128)S(1)}, f32[264,128]{1,0:T(8,128)S(1)}, u32[]{:S(2)}, u32[]{:S(2)}) collective-permute-start(f32[264,128]{1,0:T(8,128)S(1)} %get-tuple-element.28), channel_id=1, source_target_pairs={{0,6},{2,8},{4,10},{6,12},{8,14},{10,0},{12,2},{14,4},{16,22},{18,... | collective-permute-start | bytes 405512 | tf_op jit(solution)/shard_map/ppermute | solution.py:233
  13.8 17.5 %collective-permute-start.3 = (f32[264,128]{1,0:T(8,128)S(1)}, f32[264,128]{1,0:T(8,128)S(1)}, u32[]{:S(2)}, u32[]{:S(2)}) collective-permute-start(f32[264,128]{1,0:T(8,128)S(1)} %get-tuple-element.29), channel_id=1, source_target_pairs={{0,8},{2,10},{4,12},{6,14},{8,0},{10,2},{12,4},{14,6},{16,24},{18,... | collective-permute-start | bytes 405512 | tf_op jit(solution)/shard_map/ppermute | solution.py:233
  14.2 17.1 %collective-permute-start.4 = (f32[264,128]{1,0:T(8,128)S(1)}, f32[264,128]{1,0:T(8,128)S(1)}, u32[]{:S(2)}, u32[]{:S(2)}) collective-permute-start(f32[264,128]{1,0:T(8,128)S(1)} %get-tuple-element.30), channel_id=1, source_target_pairs={{0,10},{2,12},{4,14},{6,0},{8,2},{10,4},{12,6},{14,8},{16,26},{18,... | collective-permute-start | bytes 405512 | tf_op jit(solution)/shard_map/ppermute | solution.py:233
  18.7 20.5 %collective-permute-start.5 = (f32[264,128]{1,0:T(8,128)S(1)}, f32[264,128]{1,0:T(8,128)S(1)}, u32[]{:S(2)}, u32[]{:S(2)}) collective-permute-start(f32[264,128]{1,0:T(8,128)S(1)} %get-tuple-element.31), channel_id=1, source_target_pairs={{0,12},{2,14},{4,0},{6,2},{8,4},{10,6},{12,8},{14,10},{16,28},{18,... | collective-permute-start | bytes 405512 | tf_op jit(solution)/shard_map/ppermute | solution.py:233
  21.1 19.2 %collective-permute-start.6 = (f32[264,128]{1,0:T(8,128)S(1)}, f32[264,128]{1,0:T(8,128)S(1)}, u32[]{:S(2)}, u32[]{:S(2)}) collective-permute-start(f32[264,128]{1,0:T(8,128)S(1)} %get-tuple-element.32), channel_id=1, source_target_pairs={{0,14},{2,0},{4,2},{6,4},{8,6},{10,8},{12,10},{14,12},{16,30},{18,... | collective-permute-start | bytes 405512 | tf_op jit(solution)/shard_map/ppermute | solution.py:233
  41.0 5.8 %collective-permute-start.7 = (f32[264,128]{1,0:T(8,128)S(1)}, f32[264,128]{1,0:T(8,128)S(1)}, u32[]{:S(2)}, u32[]{:S(2)}) collective-permute-start(f32[264,128]{1,0:T(8,128)S(1)} %row_total_0.1.refs_0_), channel_id=1, source_target_pairs={{0,16},{2,18},{4,20},{6,22},{8,24},{10,26},{12,28},{14,30},{16,32}... | collective-permute-start | bytes 405512 | tf_op jit(solution)/shard_map/ppermute | solution.py:235
  42.4 8.5 %collective-permute-start.8 = (f32[264,128]{1,0:T(8,128)S(1)}, f32[264,128]{1,0:T(8,128)S(1)}, u32[]{:S(2)}, u32[]{:S(2)}) collective-permute-start(f32[264,128]{1,0:T(8,128)S(1)} %row_total_0.1.refs_0_), channel_id=1, source_target_pairs={{0,32},{2,34},{4,36},{6,38},{8,40},{10,42},{12,44},{14,46},{16,48}... | collective-permute-start | bytes 405512 | tf_op jit(solution)/shard_map/ppermute | solution.py:235
  45.0 5.9 %collective-permute-start.9 = (f32[264,128]{1,0:T(8,128)S(1)}, f32[264,128]{1,0:T(8,128)S(1)}, u32[]{:S(2)}, u32[]{:S(2)}) collective-permute-start(f32[264,128]{1,0:T(8,128)S(1)} %row_total_0.1.refs_0_), channel_id=1, source_target_pairs={{0,48},{2,50},{4,52},{6,54},{8,56},{10,58},{12,60},{14,62},{16,0},... | collective-permute-start | bytes 405512 | tf_op jit(solution)/shard_map/ppermute | solution.py:235
  51.5 5.2 %collective-permute-start.10 = (f32[264,128]{1,0:T(8,128)S(1)}, f32[264,128]{1,0:T(8,128)S(1)}, u32[]{:S(2)}, u32[]{:S(2)}) collective-permute-start(f32[264,128]{1,0:T(8,128)S(1)} %get-tuple-element.33), channel_id=1, source_target_pairs={{0,64},{2,66},{4,68},{6,70},{8,72},{10,74},{12,76},{14,78},{16,80}... | collective-permute-start | bytes 405512 | tf_op jit(solution)/shard_map/ppermute | solution.py:239
  52.8 7.1 %collective-permute-start.11 = (f32[264,128]{1,0:T(8,128)S(1)}, f32[264,128]{1,0:T(8,128)S(1)}, u32[]{:S(2)}, u32[]{:S(2)}) collective-permute-start(f32[264,128]{1,0:T(8,128)S(1)} %get-tuple-element.33), channel_id=1, source_target_pairs={{0,128},{2,130},{4,132},{6,134},{8,136},{10,138},{12,140},{14,142}... | collective-permute-start | bytes 405512 | tf_op jit(solution)/shard_map/ppermute | solution.py:239
  55.2 5.2 %collective-permute-start.12 = (f32[264,128]{1,0:T(8,128)S(1)}, f32[264,128]{1,0:T(8,128)S(1)}, u32[]{:S(2)}, u32[]{:S(2)}) collective-permute-start(f32[264,128]{1,0:T(8,128)S(1)} %get-tuple-element.33), channel_id=1, source_target_pairs={{0,192},{2,194},{4,196},{6,198},{8,200},{10,202},{12,204},{14,206}... | collective-permute-start | bytes 405512 | tf_op jit(solution)/shard_map/ppermute | solution.py:239
  61.2 9.6 %collective-permute-start.13 = (f32[256,128]{1,0:T(8,128)S(1)}, f32[256,128]{1,0:T(8,128)S(1)}, u32[]{:S(2)}, u32[]{:S(2)}) collective-permute-start(f32[256,128]{1,0:T(8,128)S(1)} %get-tuple-element.36), channel_id=1, source_target_pairs={{0,2},{2,4},{4,6},{6,8},{8,10},{10,12},{12,14},{14,0},{16,18},{18,... | collective-permute-start | bytes 393224 | tf_op jit(solution)/shard_map/ppermute | solution.py:244
  64.5 10.3 %collective-permute-start.14 = (f32[256,128]{1,0:T(8,128)S(1)}, f32[256,128]{1,0:T(8,128)S(1)}, u32[]{:S(2)}, u32[]{:S(2)}) collective-permute-start(f32[256,128]{1,0:T(8,128)S(1)} %get-tuple-element.37), channel_id=1, source_target_pairs={{0,4},{2,6},{4,8},{6,10},{8,12},{10,14},{12,0},{14,2},{16,20},{18,... | collective-permute-start | bytes 393224 | tf_op jit(solution)/shard_map/ppermute | solution.py:244
  65.3 13.9 %collective-permute-start.15 = (f32[256,128]{1,0:T(8,128)S(1)}, f32[256,128]{1,0:T(8,128)S(1)}, u32[]{:S(2)}, u32[]{:S(2)}) collective-permute-start(f32[256,128]{1,0:T(8,128)S(1)} %get-tuple-element.38), channel_id=1, source_target_pairs={{0,6},{2,8},{4,10},{6,12},{8,14},{10,0},{12,2},{14,4},{16,22},{18,... | collective-permute-start | bytes 393224 | tf_op jit(solution)/shard_map/ppermute | solution.py:244
  65.6 16.4 %collective-permute-start.16 = (f32[256,128]{1,0:T(8,128)S(1)}, f32[256,128]{1,0:T(8,128)S(1)}, u32[]{:S(2)}, u32[]{:S(2)}) collective-permute-start(f32[256,128]{1,0:T(8,128)S(1)} %get-tuple-element.39), channel_id=1, source_target_pairs={{0,8},{2,10},{4,12},{6,14},{8,0},{10,2},{12,4},{14,6},{16,24},{18,... | collective-permute-start | bytes 393224 | tf_op jit(solution)/shard_map/ppermute | solution.py:244
  70.1 11.9 %collective-permute-start.17 = (f32[256,128]{1,0:T(8,128)S(1)}, f32[256,128]{1,0:T(8,128)S(1)}, u32[]{:S(2)}, u32[]{:S(2)}) collective-permute-start(f32[256,128]{1,0:T(8,128)S(1)} %get-tuple-element.40), channel_id=1, source_target_pairs={{0,10},{2,12},{4,14},{6,0},{8,2},{10,4},{12,6},{14,8},{16,26},{18,... | collective-permute-start | bytes 393224 | tf_op jit(solution)/shard_map/ppermute | solution.py:244
  70.8 19.9 %collective-permute-start.18 = (f32[256,128]{1,0:T(8,128)S(1)}, f32[256,128]{1,0:T(8,128)S(1)}, u32[]{:S(2)}, u32[]{:S(2)}) collective-permute-start(f32[256,128]{1,0:T(8,128)S(1)} %get-tuple-element.41), channel_id=1, source_target_pairs={{0,12},{2,14},{4,0},{6,2},{8,4},{10,6},{12,8},{14,10},{16,28},{18,... | collective-permute-start | bytes 393224 | tf_op jit(solution)/shard_map/ppermute | solution.py:244
  74.8 18.2 %collective-permute-start.19 = (f32[256,128]{1,0:T(8,128)S(1)}, f32[256,128]{1,0:T(8,128)S(1)}, u32[]{:S(2)}, u32[]{:S(2)}) collective-permute-start(f32[256,128]{1,0:T(8,128)S(1)} %get-tuple-element.42), channel_id=1, source_target_pairs={{0,14},{2,0},{4,2},{6,4},{8,6},{10,8},{12,10},{14,12},{16,30},{18,... | collective-permute-start | bytes 393224 | tf_op jit(solution)/shard_map/ppermute | solution.py:244
  74.8 0.8 copy-start
  75.5 0.8 copy-start.3
  76.3 0.7 copy-start.5
  77.0 0.7 copy-start.7
  92.9 0.8 copy-start.1
  93.7 0.7 copy-start.6
  100.4 3.8 %collective-permute-start.20 = (f32[64,2048]{1,0:T(8,128)S(1)}, f32[64,2048]{1,0:T(8,128)S(1)}, u32[]{:S(2)}, u32[]{:S(2)}) collective-permute-start(f32[64,2048]{1,0:T(8,128)S(1)} %constant_dynamic-slice_fusion), channel_id=1, source_target_pairs={{0,1},{1,0},{2,3},{3,2},{4,5},{5,4},{6,7},{7,6},{8,9},{9,8},{10,11... | collective-permute-start | bytes 1572872 | tf_op jit(solution)/shard_map/ppermute | solution.py:260

commit v3 on v2

--- a/solution.py
+++ b/solution.py
@@ -18,6 +18,10 @@
 OWN = PER_CHUNK // NZ
 ROWS = OWN * W
 MSG = ROWS + 8
+ORDER = (0, 1, 7, 2, 6, 3, 5, 4)
+EARLY = 5
+TILE = 512
+HBM = pl.BlockSpec(memory_space=pltpu.HBM)
 VMEM = pl.BlockSpec(memory_space=pltpu.VMEM)
 SMEM = pl.BlockSpec(memory_space=pltpu.SMEM)
 
@@ -26,14 +30,8 @@
     return [(i, i // NZ * NZ + (i + k) % NZ) for i in range(NX * NY * NZ)]
 
 
-def y_shift(k):
-    span = NY * NZ
-    return [(i, i // span * span + (i + k * NZ) % span) for i in range(NX * NY * NZ)]
-
-
-def x_shift(k):
-    total = NX * NY * NZ
-    return [(i, (i + k * NY * NZ) % total) for i in range(total)]
+def partners(stride, k):
+    return [(i, i ^ (stride * k)) for i in range(NX * NY * NZ)]
 
 
 def split(value):
@@ -60,12 +58,20 @@
     return tile
 
 
-def local_state_kernel(chunk, pos, x, b, log_decay, *refs):
-    outs, cum_ref = refs[:NZ], refs[NZ]
+def local_state_kernel(chunk, pos, x, b_hbm, log_decay_hbm, *refs):
+    outs, (cum_ref, b, log_decay, sems) = refs[:NZ], refs[NZ:]
+    copies = [
+        pltpu.make_async_copy(log_decay_hbm, log_decay, sems.at[0]),
+        pltpu.make_async_copy(b_hbm, b, sems.at[1]),
+    ]
+    for copy in copies:
+        copy.start()
+    for copy in copies:
+        copy.wait()
     cum_ref[...] = running_sum(log_decay[...])
     b_t = b[...].astype(F32).T
-    for k in range(NZ):
-        owner = (pos[0] + k) & (NZ - 1)
+    for k, shift in enumerate(ORDER):
+        owner = (pos[0] + shift) & (NZ - 1)
         lasts = []
         for i in range(OWN):
             head = chunk * PER_CHUNK + owner * OWN + i
@@ -82,7 +88,7 @@
 
 def row_total_kernel(pos, *refs):
     parts, out = refs[:NZ], refs[NZ]
-    places = [(pos[0] - k) & (NZ - 1) for k in range(NZ)]
+    places = [(pos[0] - shift) & (NZ - 1) for shift in ORDER]
     totals = []
     for i in range(OWN):
         logs = [part[ROWS + i : ROWS + i + 1, :] for part in parts]
@@ -100,7 +106,7 @@
 
 def plane_kernel(pos, *refs):
     parts, plane, before = refs[:NY], refs[NY], refs[NY + 1]
-    places = [(pos[1] - k) & (NY - 1) for k in range(NY)]
+    places = [pos[1] ^ k for k in range(NY)]
     plane_logs, before_logs = [], []
     for i in range(OWN):
         logs = [part[ROWS + i : ROWS + i + 1, :] for part in parts]
@@ -134,16 +140,19 @@
     parts = refs[NX : NX + NZ]
     outs = refs[NX + NZ : NX + 2 * NZ]
     ordered, entering = refs[NX + 2 * NZ :]
-    for k in range(NZ):
-        ordered[(pos[0] - k) & (NZ - 1)] = parts[k][...]
+    for k, shift in enumerate(ORDER):
+        ordered[(pos[0] - shift) & (NZ - 1)] = parts[k][...]
     for i in range(OWN):
         carry = jnp.zeros((W, W), F32)
-        between = jnp.zeros((1, W), F32)
+        logs = [plane[ROWS + i : ROWS + i + 1, :] for plane in planes]
         for k in range(1, NX):
-            earlier = k <= pos[2]
-            piece = planes[k - 1][i * W : (i + 1) * W, :]
-            carry += jnp.where(earlier, jnp.exp(between), 0.0) * piece
-            between += jnp.where(earlier, planes[k - 1][ROWS + i : ROWS + i + 1, :], 0.0)
+            after = jnp.zeros((1, W), F32)
+            for j in range(1, NX):
+                if j != k:
+                    between = jnp.logical_and(pos[2] ^ j > pos[2] ^ k, pos[2] ^ j < pos[2])
+                    after += jnp.where(between, logs[j - 1], 0.0)
+            weight = jnp.where(pos[2] ^ k < pos[2], jnp.exp(after), 0.0)
+            carry += weight * planes[k - 1][i * W : (i + 1) * W, :]
         carry = jnp.exp(before[ROWS + i : ROWS + i + 1, :]) * carry
         carry += before[i * W : (i + 1) * W, :]
         for place in range(NZ):
@@ -151,11 +160,13 @@
             if place < NZ - 1:
                 decay = jnp.exp(ordered[place, ROWS + i : ROWS + i + 1, :])
                 carry = decay * carry + ordered[place, i * W : (i + 1) * W, :]
-    for k in range(NZ):
-        outs[k][...] = entering[(pos[0] + k) & (NZ - 1)]
-
-
-def inside_kernel(skip, x, z, b, c, log_decay, fixed, slope):
+    for k, shift in enumerate(ORDER):
+        outs[k][...] = entering[(pos[0] + shift) & (NZ - 1)]
+
+
+def inside_kernel(skip, x, z, b, c, log_decay, gain, fixed, slope, read, gain_out):
+    read[...] = c[...]
+    gain_out[...] = gain[...]
     lower = lower_mask()
     logs = log_decay[...]
     cum = running_sum(logs)
@@ -177,23 +188,48 @@
         slope[:, at] = jnp.exp(column) * gate
 
 
-def head_norm_kernel(chunk, pos, *refs):
-    states = refs[:NZ]
-    c, fixed, slope, gain, normed = refs[NZ:]
-    read = c[...]
-    for k in range(NZ):
-        owner = (pos[0] - k) & (NZ - 1)
+def finish_kernel(shifts, last, pos, *refs):
+    count = len(shifts)
+    states, refs = refs[:count], refs[count:]
+    read, fixed, slope, gain, w_hbm = refs[:5]
+    if last:
+        so_far, mine, other, normed, w, sems, tile = refs[5:]
+    else:
+        total, normed, w, sems = refs[5:]
+    owners = [(pos[0] - shift) & (NZ - 1) for shift in shifts]
+    copies = []
+    for k, owner in enumerate(owners):
+        rows = pl.ds(pl.multiple_of(owner * ROWS, ROWS), ROWS)
+        copies.append(
+            pltpu.make_async_copy(w_hbm.at[rows, :], w.at[k * ROWS : (k + 1) * ROWS, :], sems.at[k])
+        )
+        copies[k].start()
+    for k, owner in enumerate(owners):
         for i in range(OWN):
-            local = owner * OWN + i
-            head = chunk * PER_CHUNK + local
+            head = owner * OWN + i
             high, low = split(states[k][i * W : (i + 1) * W, :])
-            carried = jnp.dot(read, high, preferred_element_type=F32)
-            carried += jnp.dot(read, low, preferred_element_type=F32)
+            carried = jnp.dot(read[...], high, preferred_element_type=F32)
+            carried += jnp.dot(read[...], low, preferred_element_type=F32)
             at = pl.ds(pl.multiple_of(head * W, W), W)
             gated = fixed[:, at] + slope[:, at] * carried
             meansq = jnp.mean(gated * gated, axis=-1, keepdims=True)
             value = gated * lax.rsqrt(meansq + 1e-05) * gain[pl.ds(head, 1), :]
-            normed[:, pl.ds(pl.multiple_of(local * W, W), W)] = value.astype(BF16)
+            place = k * ROWS + i * W
+            normed[:, place : place + W] = value.astype(BF16)
+    for copy in copies:
+        copy.wait()
+    for at in range(0, w.shape[1], TILE):
+        columns = slice(at, at + TILE)
+        part = jnp.dot(normed[...], w[:, columns], preferred_element_type=F32)
+        if last:
+            half = W // 2
+            near = pl.ds(pl.multiple_of(pos[3] * half, half), half)
+            far = pl.ds(pl.multiple_of((1 - pos[3]) * half, half), half)
+            tile[...] = so_far[:, columns] + part
+            mine[:, columns] = tile[near, :]
+            other[:, columns] = tile[far, :]
+        else:
+            total[:, columns] = part
 
 
 def call(kernel, outs, specs, scratch=(), flops=0, moved=0, name=None):
@@ -215,48 +251,69 @@
 
 def per_device(x_in, z_in, b_in, c_in, log_decay, d_skip, norm_gain, w_out):
     index = lax.axis_index("ctx")
-    pos = jnp.stack([index % NZ, index // NZ % NY, index // (NZ * NY)]).astype(jnp.int32)
+    pos = jnp.stack([index % NZ, index // NZ % NY, index // (NZ * NY), lax.axis_index("tp")]).astype(jnp.int32)
     x = x_in.reshape(W, HEADS * W)
     message = [shaped(MSG, W)] * NZ
-    kept, normed_parts = {}, []
+    kept = {}
     for chunk in range(CHUNKS):
         kept[chunk] = call(
-            functools.partial(local_state_kernel, chunk), message, [SMEM, VMEM, VMEM, VMEM],
-            [pltpu.VMEM((HEADS, W), F32)], moved=1 << 20, name=f"local_state_{chunk}",
+            functools.partial(local_state_kernel, chunk), message, [SMEM, VMEM, HBM, HBM],
+            [
+                pltpu.VMEM((HEADS, W), F32), pltpu.VMEM((W, W), BF16),
+                pltpu.VMEM((HEADS, W), F32), pltpu.SemaphoreType.DMA((2,)),
+            ], moved=1 << 20, name=f"local_state_{chunk}",
         )(pos, x, b_in, log_decay)
     z = z_in.reshape(W, HEADS * W)
-    fixed, slope = call(
-        inside_kernel, [shaped(W, HEADS * W)] * 2, [SMEM] + [VMEM] * 5, moved=8 << 20, name="inside",
-    )(d_skip, x, z, b_in, c_in, log_decay)
+    fixed, slope, read, gain = call(
+        inside_kernel,
+        [shaped(W, HEADS * W), shaped(W, HEADS * W), shaped(W, W, dtype=BF16), shaped(HEADS, W)],
+        [SMEM] + [VMEM] * 6, moved=8 << 20, name="inside",
+    )(d_skip, x, z, b_in, c_in, log_decay, norm_gain)
+
+    def along_z(parts):
+        return [parts[0]] + [
+            lax.ppermute(part, "ctx", z_shift(shift)) for part, shift in zip(parts[1:], ORDER[1:])
+        ]
+
+    parts, totals, back, states = {}, {}, {}, {}
     for chunk in range(CHUNKS):
-        out = kept[chunk]
-        parts = [out[0]] + [lax.ppermute(out[k], "ctx", z_shift(k)) for k in range(1, NZ)]
-        total = call(row_total_kernel, shaped(MSG, W), [SMEM] + [VMEM] * NZ, name=f"row_total_{chunk}")(pos, *parts)
-        rows = [total] + [lax.ppermute(total, "ctx", y_shift(k)) for k in range(1, NY)]
+        parts[chunk] = along_z(kept[chunk])
+        totals[chunk] = call(
+            row_total_kernel, shaped(MSG, W), [SMEM] + [VMEM] * NZ, name=f"row_total_{chunk}"
+        )(pos, *parts[chunk])
+    totals[0], fixed, slope, read, gain = lax.optimization_barrier(
+        (totals[0], fixed, slope, read, gain)
+    )
+    for chunk in range(CHUNKS):
+        total = totals[chunk]
+        rows = [total] + [lax.ppermute(total, "ctx", partners(NZ, k)) for k in range(1, NY)]
         plane, before = call(
             plane_kernel, [shaped(MSG, W)] * 2, [SMEM] + [VMEM] * NY, name=f"plane_{chunk}"
         )(pos, *rows)
-        planes = [lax.ppermute(plane, "ctx", x_shift(k)) for k in range(1, NX)]
-        back = call(
+        planes = [lax.ppermute(plane, "ctx", partners(NY * NZ, k)) for k in range(1, NX)]
+        back[chunk] = call(
             entering_kernel, [shaped(ROWS, W)] * NZ, [SMEM] + [VMEM] * (NX + NZ),
             [pltpu.VMEM((NZ, MSG, W), F32), pltpu.VMEM((NZ, ROWS, W), F32)], name=f"entering_{chunk}",
-        )(pos, *planes, before, *parts)
-        states = [back[0]] + [lax.ppermute(back[k], "ctx", z_shift(k)) for k in range(1, NZ)]
-        normed_parts.append(call(
-            functools.partial(head_norm_kernel, chunk), shaped(W, PER_CHUNK * W, dtype=BF16),
-            [SMEM] + [VMEM] * (NZ + 4), name=f"head_norm_{chunk}",
-        )(pos, *states, c_in, fixed, slope, norm_gain))
-    mixed = sum(
-        jnp.dot(
-            normed, w_out[chunk * PER_CHUNK * W : (chunk + 1) * PER_CHUNK * W],
-            preferred_element_type=F32,
-        )
-        for chunk, normed in enumerate(normed_parts)
-    )
-    core = lax.axis_index("tp")
-    half = W // 2
-    mine = lax.dynamic_slice_in_dim(mixed, core * half, half, 0)
-    other = lax.dynamic_slice_in_dim(mixed, (1 - core) * half, half, 0)
+        )(pos, *planes, before, *parts[chunk])
+        states[chunk] = along_z(back[chunk])
+    width = w_out.shape[1]
+
+    def finish(shifts, parts, last, outs, extra):
+        rows = len(shifts) * ROWS
+        return call(
+            functools.partial(finish_kernel, shifts, last), outs,
+            [SMEM] + [VMEM] * (len(shifts) + 4) + [HBM] + [VMEM] * len(extra),
+            [
+                pltpu.VMEM((W, rows), BF16), pltpu.VMEM((rows, width), BF16),
+                pltpu.SemaphoreType.DMA((len(shifts),)),
+            ] + ([pltpu.VMEM((W, TILE), F32)] if last else []),
+            name="finish_late" if last else "finish_early",
+        )(pos, *parts, read, fixed, slope, gain, w_out, *extra)
+
+    so_far = finish(ORDER[:EARLY], states[0][:EARLY], False, shaped(W, width), [])
+    mine, other = finish(
+        ORDER[EARLY:], states[0][EARLY:], True, [shaped(W // 2, width)] * 2, [so_far]
+    )
     return (mine + lax.ppermute(other, "tp", [(0, 1), (1, 0)])).astype(BF16)
 
 

time: 106 us -> 91.5 us (0.86)
  waiting for transfers between devices: 43.7 us -> 18.7 us
  starting transfers between devices: 42 us -> 53.4 us
  matrix products: 4.66 us -> 0 us
  Pallas kernels: 6.5 us -> 9.47 us
  local copies, waits for them, and re-layouts: 7.26 us -> 8.38 us
    ppermute x20, waiting for transfers between devices: 42.1 us -> 17.2 us  [the longest x14 7.79 us: along_z(): lax.ppermute(part, 'ctx', z_shift(shift))]
    ppermute x1, starting transfers between devices: 2.31 us -> 9.13 us  [per_device(): return (mine + lax.ppermute(other, 'tp', [(0, 1), (1, 0)])).astype(BF16)]
    dot_general x1 -> x0, matrix products: 4.66 us -> none  [per_device(): jnp.dot(normed, w_out[chunk * PER_CHUNK * W:(chunk + 1) * PER_CHUNK * W],...]
    ppermute x20, starting transfers between devices: 39.7 us -> 44.3 us  [the longest x14 37.5 us: along_z(): lax.ppermute(part, 'ctx', z_shift(shift))]
    pallas_call x2 -> x3, Pallas kernels: 2.88 us -> 5.76 us  [the longest x2 4.11 us: finish(): call(functools.partial(finish_kernel, shifts, last), outs, [SMEM] + [VMEM...]
    unnamed x16 -> x14, local copies, waits for them, and re-layouts: 5.78 us -> 6.95 us
  transfers between devices with their start and end apart: 21 -> 21, of which waited for: 14 -> 7; matrix products, arithmetic and copies ran while one was open for 0% -> 0% of each run, Pallas kernels for 2% -> 4%
where the time goes in v3:
time: 91.5 us; the launch traced here: 91 us
  starting transfers between devices  53.4 us (58%)
  waiting for transfers between devices  18.7 us (20%)
  Pallas kernels  9.47 us (10%)
  local copies, waits for them, and re-layouts  8.38 us (9%)
    ppermute x14, starting transfers between devices, along_z(): lax.ppermute(part, 'ctx', z_shift(shift))  37.5 us
    ppermute x1, starting transfers between devices, per_device(): return (mine + lax.ppermute(other, 'tp', [(0, 1), (1, 0)])).astype(BF16)  9.13 us
    ppermute x14, waiting for transfers between devices, along_z(): lax.ppermute(part, 'ctx', z_shift(shift))  7.79 us
    unnamed x14, local copies, waits for them, and re-layouts  6.95 us
    ppermute x3, waiting for transfers between devices, per_device(): lax.ppermute(total, 'ctx', partners(NZ, k))  4.8 us
    ppermute x3, waiting for transfers between devices, per_device(): lax.ppermute(plane, 'ctx', partners(NY * NZ, k))  4.61 us
    pallas_call x2, Pallas kernels, finish(): call(functools.partial(finish_kernel, shifts, last), outs, [SMEM] + [VMEM...  4.11 us
    ppermute x3, starting transfers between devices, per_device(): lax.ppermute(total, 'ctx', partners(NZ, k))  3.49 us
  transfers between devices with their start and end apart: 21, of which 7 were waited for; matrix products, arithmetic and copies ran while one was open for 0% of the time, Pallas kernels for 4%

profile of v3, /device:TPU:1, one launch (start us, length us, event | category | flops | bytes accessed | tf_op | source)
XLA Modules:
  0.0 91.0 jit_solution(17736443433392957520)
XLA Ops:
  0.0 1.4 %copy_bitcast_fusion = (bf16[128,2048]{1,0:T(8,128)(2,1)S(1)}, bf16[128,2048]{1,0:T(8,128)(2,1)S(1)}) fusion(bf16[16,8,16,128]{3,2,1,0:T(8,128)(2,1)} %bitcast.10, bf16[16,8,16,128]{3,2,1,0:T(8,128)(2,1)} %bitcast.11), kind=kLoop, calls=%fused_computation | loop fusion | bytes 2097152 | tf_op jit(solution)/shard_map/reshape | solution.py:266
  1.4 0.1 pad_add_fusion.pos
  1.5 0.0 copy-start.2
  1.5 0.8 copy-done.2
  2.3 0.0 copy-start.3
  2.3 0.7 copy-done.3
  3.0 1.6 %local_state_0.1 = (f32[264,128]{1,0:T(8,128)S(1)}, f32[264,128]{1,0:T(8,128)S(1)}, f32[264,128]{1,0:T(8,128)S(1)}, f32[264,128]{1,0:T(8,128)S(1)}, f32[264,128]...) custom-call(s32[4]{0:T(128)S(1)} %pad_add_fusion.pos, ...), custom_call_target="tpu_custom_call" | custom-call | bytes 1048576 | tf_op jit(solution)/shard_map/local_state_0/pallas_call | solution.py:259
  4.5 2.5 %collective-permute-start = (f32[264,128]{1,0:T(8,128)S(1)}, f32[264,128]{1,0:T(8,128)S(1)}, u32[]{:S(2)}, u32[]{:S(2)}) collective-permute-start(f32[264,128]{1,0:T(8,128)S(1)} %get-tuple-element.35), channel_id=1, source_target_pairs={{0,2},{2,4},{4,6},{6,8},{8,10},{10,12},{12,14},{14,0},{16,18},{18,... | collective-permute-start | bytes 405512 | tf_op jit(solution)/shard_map/ppermute | solution.py:275
  7.1 4.0 %collective-permute-start.1 = (f32[264,128]{1,0:T(8,128)S(1)}, f32[264,128]{1,0:T(8,128)S(1)}, u32[]{:S(2)}, u32[]{:S(2)}) collective-permute-start(f32[264,128]{1,0:T(8,128)S(1)} %get-tuple-element.36), channel_id=1, source_target_pairs={{0,14},{2,0},{4,2},{6,4},{8,6},{10,8},{12,10},{14,12},{16,30},{18,... | collective-permute-start | bytes 405512 | tf_op jit(solution)/shard_map/ppermute | solution.py:275
  11.1 0.0 collective-permute-start.2
  11.1 3.6 %collective-permute-start.3 = (f32[264,128]{1,0:T(8,128)S(1)}, f32[264,128]{1,0:T(8,128)S(1)}, u32[]{:S(2)}, u32[]{:S(2)}) collective-permute-start(f32[264,128]{1,0:T(8,128)S(1)} %get-tuple-element.38), channel_id=1, source_target_pairs={{0,12},{2,14},{4,0},{6,2},{8,4},{10,6},{12,8},{14,10},{16,28},{18,... | collective-permute-start | bytes 405512 | tf_op jit(solution)/shard_map/ppermute | solution.py:275
  14.7 0.3 collective-permute-start.4
  15.0 0.0 collective-permute-done.refs_1_.refs_5_
  15.0 4.1 %collective-permute-start.5 = (f32[264,128]{1,0:T(8,128)S(1)}, f32[264,128]{1,0:T(8,128)S(1)}, u32[]{:S(2)}, u32[]{:S(2)}) collective-permute-start(f32[264,128]{1,0:T(8,128)S(1)} %get-tuple-element.40), channel_id=1, source_target_pairs={{0,10},{2,12},{4,14},{6,0},{8,2},{10,4},{12,6},{14,8},{16,26},{18,... | collective-permute-start | bytes 405512 | tf_op jit(solution)/shard_map/ppermute | solution.py:275
  19.2 0.0 collective-permute-done.1.refs_2_.refs_6_
  19.2 3.9 %collective-permute-start.6 = (f32[264,128]{1,0:T(8,128)S(1)}, f32[264,128]{1,0:T(8,128)S(1)}, u32[]{:S(2)}, u32[]{:S(2)}) collective-permute-start(f32[264,128]{1,0:T(8,128)S(1)} %get-tuple-element.41), channel_id=1, source_target_pairs={{0,8},{2,10},{4,12},{6,14},{8,0},{10,2},{12,4},{14,6},{16,24},{18,... | collective-permute-start | bytes 405512 | tf_op jit(solution)/shard_map/ppermute | solution.py:275
  23.1 0.0 copy-start.4
  23.1 0.8 copy-done.4
  23.9 0.0 copy-start.5
  23.9 0.7 copy-done.5
  24.6 0.0 copy-start.6
  24.6 0.7 copy-done.6
  25.2 1.7 %inside.1 = (f32[128,2048]{1,0:T(8,128)S(1)}, f32[128,2048]{1,0:T(8,128)S(1)}, bf16[128,128]{1,0:T(8,128)(2,1)S(1)}, f32[16,128]{1,0:T(8,128)S(1)}) custom-call(f32[16]{0:T(128)S(1)} %copy-done.6, bf16[128,2048]{1,0:T(8,128)(2,1)S(1)} %get-tuple-element.64.x, bf16[128,2048]{1,0:T(8,128)(2,1)S(1)} %get-tuple-element.63.z, bf16[128,128]{1,0:T(8,128)(2,1)S(1)} %copy-done.2, ...), custom_call_target="tpu_custom_call" | custom-call | bytes 8388608 | tf_op jit(solution)/shard_map/inside/pallas_call | solution.py:267
  26.9 0.0 collective-permute-done.2.refs_3_.refs_7_
  26.9 0.0 collective-permute-done.3.refs_4_.refs_8_
  26.9 5.6 %collective-permute-done.4.refs_5_.refs_9_ = f32[264,128]{1,0:T(8,128)S(1)} collective-permute-done((f32[264,128]{1,0:T(8,128)S(1)}, f32[264,128]{1,0:T(8,128)S(1)}, u32[]{:S(2)}, u32[]{:S(2)}) %collective-permute-start.4) | collective-permute-done | bytes 135200 | tf_op jit(solution)/shard_map/ppermute | solution.py:275
  32.5 0.0 collective-permute-done.5.refs_6_.refs_10_
  32.5 0.0 collective-permute-done.6.refs_7_.refs_11_
  32.5 0.7 row_total_0.1.refs_0_
  33.2 2.8 %collective-permute-start.9 = (f32[264,128]{1,0:T(8,128)S(1)}, f32[264,128]{1,0:T(8,128)S(1)}, u32[]{:S(2)}, u32[]{:S(2)}) collective-permute-start(f32[264,128]{1,0:T(8,128)S(1)} %row_total_0.1.refs_0_), channel_id=1, source_target_pairs={{0,48},{2,50},{4,52},{6,54},{8,56},{10,58},{12,60},{14,62},{16,32}... | collective-permute-start | bytes 405512 | tf_op jit(solution)/shard_map/ppermute | solution.py:289
  36.0 0.4 collective-permute-start.8
  36.4 0.3 collective-permute-start.7
  36.7 2.9 %collective-permute-done.9.refs_3_ = f32[264,128]{1,0:T(8,128)S(1)} collective-permute-done((f32[264,128]{1,0:T(8,128)S(1)}, f32[264,128]{1,0:T(8,128)S(1)}, u32[]{:S(2)}, u32[]{:S(2)}) %collective-permute-start.9) | collective-permute-done | bytes 135200 | tf_op jit(solution)/shard_map/ppermute | solution.py:289
  39.6 1.9 %collective-permute-done.8.refs_2_ = f32[264,128]{1,0:T(8,128)S(1)} collective-permute-done((f32[264,128]{1,0:T(8,128)S(1)}, f32[264,128]{1,0:T(8,128)S(1)}, u32[]{:S(2)}, u32[]{:S(2)}) %collective-permute-start.8) | collective-permute-done | bytes 135200 | tf_op jit(solution)/shard_map/ppermute | solution.py:289
  41.5 0.0 collective-permute-done.7.refs_1_
  41.5 0.6 plane_0.1
  42.1 2.6 %collective-permute-start.12 = (f32[264,128]{1,0:T(8,128)S(1)}, f32[264,128]{1,0:T(8,128)S(1)}, u32[]{:S(2)}, u32[]{:S(2)}) collective-permute-start(f32[264,128]{1,0:T(8,128)S(1)} %get-tuple-element.47), channel_id=1, source_target_pairs={{0,192},{2,194},{4,196},{6,198},{8,200},{10,202},{12,204},{14,206}... | collective-permute-start | bytes 405512 | tf_op jit(solution)/shard_map/ppermute | solution.py:293
  44.7 0.5 collective-permute-start.11
  45.2 0.2 collective-permute-start.10
  45.5 2.6 %collective-permute-done.12.refs_2_ = f32[264,128]{1,0:T(8,128)S(1)} collective-permute-done((f32[264,128]{1,0:T(8,128)S(1)}, f32[264,128]{1,0:T(8,128)S(1)}, u32[]{:S(2)}, u32[]{:S(2)}) %collective-permute-start.12) | collective-permute-done | bytes 135200 | tf_op jit(solution)/shard_map/ppermute | solution.py:293
  48.1 2.0 %collective-permute-done.11.refs_1_ = f32[264,128]{1,0:T(8,128)S(1)} collective-permute-done((f32[264,128]{1,0:T(8,128)S(1)}, f32[264,128]{1,0:T(8,128)S(1)}, u32[]{:S(2)}, u32[]{:S(2)}) %collective-permute-start.11) | collective-permute-done | bytes 135200 | tf_op jit(solution)/shard_map/ppermute | solution.py:293
  50.1 0.0 collective-permute-done.10.refs_0_
  50.1 0.8 entering_0.1
  50.9 8.4 %collective-permute-start.16 = (f32[256,128]{1,0:T(8,128)S(1)}, f32[256,128]{1,0:T(8,128)S(1)}, u32[]{:S(2)}, u32[]{:S(2)}) collective-permute-start(f32[256,128]{1,0:T(8,128)S(1)} %get-tuple-element.57), channel_id=1, source_target_pairs={{0,2},{2,4},{4,6},{6,8},{8,10},{10,12},{12,14},{14,0},{16,18},{18,... | collective-permute-start | bytes 393224 | tf_op jit(solution)/shard_map/ppermute | solution.py:275
  59.3 0.0 collective-permute-start.17
  59.3 1.4 %collective-permute-start.18 = (f32[256,128]{1,0:T(8,128)S(1)}, f32[256,128]{1,0:T(8,128)S(1)}, u32[]{:S(2)}, u32[]{:S(2)}) collective-permute-start(f32[256,128]{1,0:T(8,128)S(1)} %get-tuple-element.59), channel_id=1, source_target_pairs={{0,4},{2,6},{4,8},{6,10},{8,12},{10,14},{12,0},{14,2},{16,20},{18,... | collective-permute-start | bytes 393224 | tf_op jit(solution)/shard_map/ppermute | solution.py:275
  60.7 2.1 %collective-permute-start.19 = (f32[256,128]{1,0:T(8,128)S(1)}, f32[256,128]{1,0:T(8,128)S(1)}, u32[]{:S(2)}, u32[]{:S(2)}) collective-permute-start(f32[256,128]{1,0:T(8,128)S(1)} %get-tuple-element.60), channel_id=1, source_target_pairs={{0,12},{2,14},{4,0},{6,2},{8,4},{10,6},{12,8},{14,10},{16,28},{18,... | collective-permute-start | bytes 393224 | tf_op jit(solution)/shard_map/ppermute | solution.py:275
  62.8 0.4 collective-permute-start.13
  63.3 0.0 collective-permute-done.16.refs_1_
  63.3 4.1 %collective-permute-start.14 = (f32[256,128]{1,0:T(8,128)S(1)}, f32[256,128]{1,0:T(8,128)S(1)}, u32[]{:S(2)}, u32[]{:S(2)}) collective-permute-start(f32[256,128]{1,0:T(8,128)S(1)} %get-tuple-element.50), channel_id=1, source_target_pairs={{0,10},{2,12},{4,14},{6,0},{8,2},{10,4},{12,6},{14,8},{16,26},{18,... | collective-permute-start | bytes 393224 | tf_op jit(solution)/shard_map/ppermute | solution.py:275
  67.3 0.0 collective-permute-done.17.refs_2_
  67.3 2.5 %collective-permute-start.15 = (f32[256,128]{1,0:T(8,128)S(1)}, f32[256,128]{1,0:T(8,128)S(1)}, u32[]{:S(2)}, u32[]{:S(2)}) collective-permute-start(f32[256,128]{1,0:T(8,128)S(1)} %get-tuple-element.51), channel_id=1, source_target_pairs={{0,8},{2,10},{4,12},{6,14},{8,0},{10,2},{12,4},{14,6},{16,24},{18,... | collective-permute-start | bytes 393224 | tf_op jit(solution)/shard_map/ppermute | solution.py:275
  69.8 0.0 collective-permute-done.18.refs_3_
  69.9 0.0 collective-permute-done.19.refs_4_
  69.9 3.4 %copy-done = bf16[2048,2048]{1,0:T(8,128)(2,1)S(1)} copy-done((bf16[2048,2048]{1,0:T(8,128)(2,1)S(1)}, bf16[2048,2048]{1,0:T(8,128)(2,1)}, u32[]{:S(2)}) %copy-start) | copy-done | bytes 8388632
  73.2 2.3 %finish_early.1.refs_8_ = f32[128,2048]{1,0:T(8,128)S(1)} custom-call(s32[4]{0:T(128)S(1)} %pad_add_fusion.pos, f32[256,128]{1,0:T(8,128)S(1)} %get-tuple-element.56.refs_0_, f32[256,128]{1,0:T(8,128)S(1)} %collective-permute-done.16.refs_1_, f32[256,128]{1,0:T(8,128)S(1)} %collective-permute-done.17.refs_2_, ...), custom_call_target="tpu_custom_call" | custom-call | tf_op jit(solution)/shard_map/finish_early/pallas_call | solution.py:303
  75.6 0.0 collective-permute-done.13.refs_0_
  75.6 0.0 collective-permute-done.14.refs_1_
  75.6 2.2 %collective-permute-done.15.refs_2_ = f32[256,128]{1,0:T(8,128)S(1)} collective-permute-done((f32[256,128]{1,0:T(8,128)S(1)}, f32[256,128]{1,0:T(8,128)S(1)}, u32[]{:S(2)}, u32[]{:S(2)}) %collective-permute-start.15) | collective-permute-done | bytes 131104 | tf_op jit(solution)/shard_map/ppermute | solution.py:275
  77.7 0.0 copy-done.1
  77.7 1.8 %finish_late.1 = (f32[64,2048]{1,0:T(8,128)S(1)}, f32[64,2048]{1,0:T(8,128)S(1)}) custom-call(s32[4]{0:T(128)S(1)} %pad_add_fusion.pos, f32[256,128]{1,0:T(8,128)S(1)} %collective-permute-done.13.refs_0_, f32[256,128]{1,0:T(8,128)S(1)} %collective-permute-done.14.refs_1_, f32[256,128]{1,0:T(8,128)S(1)} %collective-permute-done.15.refs_2_, ...), custom_call_target="tpu_custom_call" | custom-call | tf_op jit(solution)/shard_map/finish_late/pallas_call | solution.py:303
  79.5 9.1 %collective-permute-start.20 = (f32[64,2048]{1,0:T(8,128)S(1)}, f32[64,2048]{1,0:T(8,128)S(1)}, u32[]{:S(2)}, u32[]{:S(2)}) collective-permute-start(f32[64,2048]{1,0:T(8,128)S(1)} %get-tuple-element.62), channel_id=1, source_target_pairs={{0,1},{1,0},{2,3},{3,2},{4,5},{5,4},{6,7},{7,6},{8,9},{9,8},{10,11... | collective-permute-start | bytes 1572872 | tf_op jit(solution)/shard_map/ppermute | solution.py:317
  88.7 1.5 %collective-permute-done.20 = f32[64,2048]{1,0:T(8,128)S(1)} collective-permute-done((f32[64,2048]{1,0:T(8,128)S(1)}, f32[64,2048]{1,0:T(8,128)S(1)}, u32[]{:S(2)}, u32[]{:S(2)}) %collective-permute-start.20) | collective-permute-done | bytes 524320 | tf_op jit(solution)/shard_map/ppermute | solution.py:317
  90.2 0.8 add_convert_fusion
  (2 shorter events, 0.0 us)
Async XLA Ops:
  1.5 0.8 copy-start.2
  2.3 0.7 copy-start.3
  4.5 10.5 %collective-permute-start = (f32[264,128]{1,0:T(8,128)S(1)}, f32[264,128]{1,0:T(8,128)S(1)}, u32[]{:S(2)}, u32[]{:S(2)}) collective-permute-start(f32[264,128]{1,0:T(8,128)S(1)} %get-tuple-element.35), channel_id=1, source_target_pairs={{0,2},{2,4},{4,6},{6,8},{8,10},{10,12},{12,14},{14,0},{16,18},{18,... | collective-permute-start | bytes 405512 | tf_op jit(solution)/shard_map/ppermute | solution.py:275
  7.1 12.1 %collective-permute-start.1 = (f32[264,128]{1,0:T(8,128)S(1)}, f32[264,128]{1,0:T(8,128)S(1)}, u32[]{:S(2)}, u32[]{:S(2)}) collective-permute-start(f32[264,128]{1,0:T(8,128)S(1)} %get-tuple-element.36), channel_id=1, source_target_pairs={{0,14},{2,0},{4,2},{6,4},{8,6},{10,8},{12,10},{14,12},{16,30},{18,... | collective-permute-start | bytes 405512 | tf_op jit(solution)/shard_map/ppermute | solution.py:275
  11.1 15.8 %collective-permute-start.2 = (f32[264,128]{1,0:T(8,128)S(1)}, f32[264,128]{1,0:T(8,128)S(1)}, u32[]{:S(2)}, u32[]{:S(2)}) collective-permute-start(f32[264,128]{1,0:T(8,128)S(1)} %get-tuple-element.37), channel_id=1, source_target_pairs={{0,4},{2,6},{4,8},{6,10},{8,12},{10,14},{12,0},{14,2},{16,20},{18,... | collective-permute-start | bytes 405512 | tf_op jit(solution)/shard_map/ppermute | solution.py:275
  11.1 15.8 %collective-permute-start.3 = (f32[264,128]{1,0:T(8,128)S(1)}, f32[264,128]{1,0:T(8,128)S(1)}, u32[]{:S(2)}, u32[]{:S(2)}) collective-permute-start(f32[264,128]{1,0:T(8,128)S(1)} %get-tuple-element.38), channel_id=1, source_target_pairs={{0,12},{2,14},{4,0},{6,2},{8,4},{10,6},{12,8},{14,10},{16,28},{18,... | collective-permute-start | bytes 405512 | tf_op jit(solution)/shard_map/ppermute | solution.py:275
  14.7 17.8 %collective-permute-start.4 = (f32[264,128]{1,0:T(8,128)S(1)}, f32[264,128]{1,0:T(8,128)S(1)}, u32[]{:S(2)}, u32[]{:S(2)}) collective-permute-start(f32[264,128]{1,0:T(8,128)S(1)} %get-tuple-element.39), channel_id=1, source_target_pairs={{0,6},{2,8},{4,10},{6,12},{8,14},{10,0},{12,2},{14,4},{16,22},{18,... | collective-permute-start | bytes 405512 | tf_op jit(solution)/shard_map/ppermute | solution.py:275
  15.0 17.5 %collective-permute-start.5 = (f32[264,128]{1,0:T(8,128)S(1)}, f32[264,128]{1,0:T(8,128)S(1)}, u32[]{:S(2)}, u32[]{:S(2)}) collective-permute-start(f32[264,128]{1,0:T(8,128)S(1)} %get-tuple-element.40), channel_id=1, source_target_pairs={{0,10},{2,12},{4,14},{6,0},{8,2},{10,4},{12,6},{14,8},{16,26},{18,... | collective-permute-start | bytes 405512 | tf_op jit(solution)/shard_map/ppermute | solution.py:275
  19.2 13.3 %collective-permute-start.6 = (f32[264,128]{1,0:T(8,128)S(1)}, f32[264,128]{1,0:T(8,128)S(1)}, u32[]{:S(2)}, u32[]{:S(2)}) collective-permute-start(f32[264,128]{1,0:T(8,128)S(1)} %get-tuple-element.41), channel_id=1, source_target_pairs={{0,8},{2,10},{4,12},{6,14},{8,0},{10,2},{12,4},{14,6},{16,24},{18,... | collective-permute-start | bytes 405512 | tf_op jit(solution)/shard_map/ppermute | solution.py:275
  23.1 0.8 copy-start.4
  23.9 0.7 copy-start.5
  24.6 0.7 copy-start.6
  33.2 6.4 %collective-permute-start.9 = (f32[264,128]{1,0:T(8,128)S(1)}, f32[264,128]{1,0:T(8,128)S(1)}, u32[]{:S(2)}, u32[]{:S(2)}) collective-permute-start(f32[264,128]{1,0:T(8,128)S(1)} %row_total_0.1.refs_0_), channel_id=1, source_target_pairs={{0,48},{2,50},{4,52},{6,54},{8,56},{10,58},{12,60},{14,62},{16,32}... | collective-permute-start | bytes 405512 | tf_op jit(solution)/shard_map/ppermute | solution.py:289
  36.0 5.5 %collective-permute-start.8 = (f32[264,128]{1,0:T(8,128)S(1)}, f32[264,128]{1,0:T(8,128)S(1)}, u32[]{:S(2)}, u32[]{:S(2)}) collective-permute-start(f32[264,128]{1,0:T(8,128)S(1)} %row_total_0.1.refs_0_), channel_id=1, source_target_pairs={{0,32},{2,34},{4,36},{6,38},{8,40},{10,42},{12,44},{14,46},{16,48}... | collective-permute-start | bytes 405512 | tf_op jit(solution)/shard_map/ppermute | solution.py:289
  36.4 5.1 %collective-permute-start.7 = (f32[264,128]{1,0:T(8,128)S(1)}, f32[264,128]{1,0:T(8,128)S(1)}, u32[]{:S(2)}, u32[]{:S(2)}) collective-permute-start(f32[264,128]{1,0:T(8,128)S(1)} %row_total_0.1.refs_0_), channel_id=1, source_target_pairs={{0,16},{2,18},{4,20},{6,22},{8,24},{10,26},{12,28},{14,30},{16,0},... | collective-permute-start | bytes 405512 | tf_op jit(solution)/shard_map/ppermute | solution.py:289
  42.1 6.0 %collective-permute-start.12 = (f32[264,128]{1,0:T(8,128)S(1)}, f32[264,128]{1,0:T(8,128)S(1)}, u32[]{:S(2)}, u32[]{:S(2)}) collective-permute-start(f32[264,128]{1,0:T(8,128)S(1)} %get-tuple-element.47), channel_id=1, source_target_pairs={{0,192},{2,194},{4,196},{6,198},{8,200},{10,202},{12,204},{14,206}... | collective-permute-start | bytes 405512 | tf_op jit(solution)/shard_map/ppermute | solution.py:293
  44.7 5.4 %collective-permute-start.11 = (f32[264,128]{1,0:T(8,128)S(1)}, f32[264,128]{1,0:T(8,128)S(1)}, u32[]{:S(2)}, u32[]{:S(2)}) collective-permute-start(f32[264,128]{1,0:T(8,128)S(1)} %get-tuple-element.47), channel_id=1, source_target_pairs={{0,128},{2,130},{4,132},{6,134},{8,136},{10,138},{12,140},{14,142}... | collective-permute-start | bytes 405512 | tf_op jit(solution)/shard_map/ppermute | solution.py:293
  45.2 4.9 %collective-permute-start.10 = (f32[264,128]{1,0:T(8,128)S(1)}, f32[264,128]{1,0:T(8,128)S(1)}, u32[]{:S(2)}, u32[]{:S(2)}) collective-permute-start(f32[264,128]{1,0:T(8,128)S(1)} %get-tuple-element.47), channel_id=1, source_target_pairs={{0,64},{2,66},{4,68},{6,70},{8,72},{10,74},{12,76},{14,78},{16,80}... | collective-permute-start | bytes 405512 | tf_op jit(solution)/shard_map/ppermute | solution.py:293
  50.9 12.4 %collective-permute-start.16 = (f32[256,128]{1,0:T(8,128)S(1)}, f32[256,128]{1,0:T(8,128)S(1)}, u32[]{:S(2)}, u32[]{:S(2)}) collective-permute-start(f32[256,128]{1,0:T(8,128)S(1)} %get-tuple-element.57), channel_id=1, source_target_pairs={{0,2},{2,4},{4,6},{6,8},{8,10},{10,12},{12,14},{14,0},{16,18},{18,... | collective-permute-start | bytes 393224 | tf_op jit(solution)/shard_map/ppermute | solution.py:275
  59.3 8.1 %collective-permute-start.17 = (f32[256,128]{1,0:T(8,128)S(1)}, f32[256,128]{1,0:T(8,128)S(1)}, u32[]{:S(2)}, u32[]{:S(2)}) collective-permute-start(f32[256,128]{1,0:T(8,128)S(1)} %get-tuple-element.58), channel_id=1, source_target_pairs={{0,14},{2,0},{4,2},{6,4},{8,6},{10,8},{12,10},{14,12},{16,30},{18,... | collective-permute-start | bytes 393224 | tf_op jit(solution)/shard_map/ppermute | solution.py:275
  59.3 10.6 %collective-permute-start.18 = (f32[256,128]{1,0:T(8,128)S(1)}, f32[256,128]{1,0:T(8,128)S(1)}, u32[]{:S(2)}, u32[]{:S(2)}) collective-permute-start(f32[256,128]{1,0:T(8,128)S(1)} %get-tuple-element.59), channel_id=1, source_target_pairs={{0,4},{2,6},{4,8},{6,10},{8,12},{10,14},{12,0},{14,2},{16,20},{18,... | collective-permute-start | bytes 393224 | tf_op jit(solution)/shard_map/ppermute | solution.py:275
  60.7 9.1 %collective-permute-start.19 = (f32[256,128]{1,0:T(8,128)S(1)}, f32[256,128]{1,0:T(8,128)S(1)}, u32[]{:S(2)}, u32[]{:S(2)}) collective-permute-start(f32[256,128]{1,0:T(8,128)S(1)} %get-tuple-element.60), channel_id=1, source_target_pairs={{0,12},{2,14},{4,0},{6,2},{8,4},{10,6},{12,8},{14,10},{16,28},{18,... | collective-permute-start | bytes 393224 | tf_op jit(solution)/shard_map/ppermute | solution.py:275
  62.8 12.7 %collective-permute-start.13 = (f32[256,128]{1,0:T(8,128)S(1)}, f32[256,128]{1,0:T(8,128)S(1)}, u32[]{:S(2)}, u32[]{:S(2)}) collective-permute-start(f32[256,128]{1,0:T(8,128)S(1)} %get-tuple-element.49), channel_id=1, source_target_pairs={{0,6},{2,8},{4,10},{6,12},{8,14},{10,0},{12,2},{14,4},{16,22},{18,... | collective-permute-start | bytes 393224 | tf_op jit(solution)/shard_map/ppermute | solution.py:275
  63.3 12.3 %collective-permute-start.14 = (f32[256,128]{1,0:T(8,128)S(1)}, f32[256,128]{1,0:T(8,128)S(1)}, u32[]{:S(2)}, u32[]{:S(2)}) collective-permute-start(f32[256,128]{1,0:T(8,128)S(1)} %get-tuple-element.50), channel_id=1, source_target_pairs={{0,10},{2,12},{4,14},{6,0},{8,2},{10,4},{12,6},{14,8},{16,26},{18,... | collective-permute-start | bytes 393224 | tf_op jit(solution)/shard_map/ppermute | solution.py:275
  67.3 10.4 %collective-permute-start.15 = (f32[256,128]{1,0:T(8,128)S(1)}, f32[256,128]{1,0:T(8,128)S(1)}, u32[]{:S(2)}, u32[]{:S(2)}) collective-permute-start(f32[256,128]{1,0:T(8,128)S(1)} %get-tuple-element.51), channel_id=1, source_target_pairs={{0,8},{2,10},{4,12},{6,14},{8,0},{10,2},{12,4},{14,6},{16,24},{18,... | collective-permute-start | bytes 393224 | tf_op jit(solution)/shard_map/ppermute | solution.py:275
  69.9 3.4 %copy-start = (bf16[2048,2048]{1,0:T(8,128)(2,1)S(1)}, bf16[2048,2048]{1,0:T(8,128)(2,1)}, u32[]{:S(2)}) copy-start(bf16[2048,2048]{1,0:T(8,128)(2,1)} %refs_7_.1) | copy-start | bytes 25165828
  73.2 4.5 %copy-start.1 = (bf16[2048,2048]{1,0:T(8,128)(2,1)S(1)}, bf16[2048,2048]{1,0:T(8,128)(2,1)}, u32[]{:S(2)}) copy-start(bf16[2048,2048]{1,0:T(8,128)(2,1)} %refs_7_.1) | copy-start | bytes 25165828
  79.5 10.7 %collective-permute-start.20 = (f32[64,2048]{1,0:T(8,128)S(1)}, f32[64,2048]{1,0:T(8,128)S(1)}, u32[]{:S(2)}, u32[]{:S(2)}) collective-permute-start(f32[64,2048]{1,0:T(8,128)S(1)} %get-tuple-element.62), channel_id=1, source_target_pairs={{0,1},{1,0},{2,3},{3,2},{4,5},{5,4},{6,7},{7,6},{8,9},{9,8},{10,11... | collective-permute-start | bytes 1572872 | tf_op jit(solution)/shard_map/ppermute | solution.py:317

commit v4 on v0

v4 whole, which is shorter than its diff:
```python
import functools

import jax
import jax.numpy as jnp
from jax import lax
from jax.experimental import pallas as pl
from jax.experimental.pallas import tpu as pltpu
from jax.sharding import PartitionSpec as P

F32 = jnp.float32
BF16 = jnp.bfloat16
HIGHEST = lax.Precision.HIGHEST
NX, NY, NZ = 4, 4, 8
PAIRS = NZ // 2
HEADS = 16
W = 128
GROUPS = 2
HALF = HEADS // GROUPS // 2
ROWS = HALF * W
TILE = 512
WORK = 10**10
VMEM = pl.BlockSpec(memory_space=pltpu.VMEM)
SMEM = pl.BlockSpec(memory_space=pltpu.SMEM)


def partners(stride, k):
    return [(i, i ^ (stride * k)) for i in range(NX * NY * NZ)]


def split(value):
    high = value.astype(BF16)
    return high, (value - high.astype(F32)).astype(BF16)


def lower_mask():
    rows = lax.broadcasted_iota(jnp.int32, (W, W), 0)
    columns = lax.broadcasted_iota(jnp.int32, (W, W), 1)
    return rows >= columns


def running_sum(log_decay):
    upper = jnp.where(lower_mask(), 1.0, 0.0).T
    return jnp.dot(log_decay, upper, precision=HIGHEST, preferred_element_type=F32)


def decay_tile(rows):
    place = lax.broadcasted_iota(jnp.int32, (8, W), 0)
    tile = jnp.zeros((8, W), F32)
    for i, row in enumerate(rows):
        tile = jnp.where(place == i, jnp.broadcast_to(row, (8, W)), tile)
    return tile


def running_sum_t(log_decay):
    lower = jnp.where(lower_mask(), 1.0, 0.0)
    return lax.dot_general(
        lower, log_decay, (((1,), (1,)), ((), ())), precision=HIGHEST, preferred_element_type=F32
    )


def rows_of(index):
    return pl.ds(pl.multiple_of(index * W, W), W)


def local_state_kernel(group, pos, x, b, log_decay, keep, send, cum_ref):
    cum_ref[...] = running_sum(log_decay[...])
    b_t = b[...].astype(F32).T
    role = pos[0] & 1
    for out, side in ((send, 1 - role), (keep, role)):
        lasts = []
        for j in range(HALF):
            head = (group * 2 + side) * HALF + j
            cum = cum_ref[pl.ds(head, 1), :]
            last = jnp.broadcast_to(cum[:, W - 1 :], (1, W))
            parts = jnp.concatenate(split(b_t * jnp.exp(last - cum)), axis=1)
            x_head = x[:, rows_of(head)]
            out[j * W : (j + 1) * W, :] = jnp.dot(
                parts, jnp.concatenate([x_head, x_head]), preferred_element_type=F32
            )
            lasts.append(last)
        out[ROWS:, :] = decay_tile(lasts)


def pair_kernel(pos, keep, got, *outs):
    first = pos[0] & 1 == 0
    for m in range(PAIRS):
        j = (pos[0] >> 1) ^ m
        state, log = rows_of(j), pl.ds(ROWS + j, 1)
        earlier = jnp.where(first, keep[state, :], got[state, :])
        later = jnp.where(first, got[state, :], keep[state, :])
        decay = jnp.exp(jnp.where(first, got[log, :], keep[log, :]))
        outs[m][:W, :] = decay * earlier + later
        outs[m][W:, :] = decay_tile([keep[log, :] + got[log, :]])


def row_total_kernel(pos, *refs):
    parts, out = refs[:PAIRS], refs[PAIRS]
    places = [(pos[0] >> 1) ^ m for m in range(PAIRS)]
    logs = [part[W : W + 1, :] for part in parts]
    total = jnp.zeros((W, W), F32)
    for k in range(PAIRS):
        after = jnp.zeros((1, W), F32)
        for j in range(PAIRS):
            if j != k:
                after += jnp.where(places[j] > places[k], logs[j], 0.0)
        total += jnp.exp(after) * parts[k][:W, :]
    out[:W, :] = total
    out[W:, :] = decay_tile([sum(logs)])


def plane_kernel(pos, *refs):
    parts, plane, before = refs[:NY], refs[NY], refs[NY + 1]
    places = [pos[1] ^ k for k in range(NY)]
    logs = [part[W : W + 1, :] for part in parts]
    total = jnp.zeros((W, W), F32)
    earlier = jnp.zeros((W, W), F32)
    to_row = jnp.zeros((1, W), F32)
    for k in range(NY):
        after = jnp.zeros((1, W), F32)
        between = jnp.zeros((1, W), F32)
        for j in range(NY):
            if j != k:
                later = jnp.where(places[j] > places[k], logs[j], 0.0)
                after += later
                between += jnp.where(places[j] < pos[1], later, 0.0)
        piece = parts[k][:W, :]
        total += jnp.exp(after) * piece
        if k > 0:
            mine = places[k] < pos[1]
            earlier += jnp.where(mine, jnp.exp(between), 0.0) * piece
            to_row += jnp.where(mine, logs[k], 0.0)
    plane[:W, :] = total
    before[:W, :] = earlier
    plane[W:, :] = decay_tile([sum(logs)])
    before[W:, :] = decay_tile([to_row])


def entering_kernel(pos, *refs):
    planes, before = refs[: NX - 1], refs[NX - 1]
    parts = refs[NX : NX + PAIRS]
    outs = refs[NX + PAIRS : NX + 2 * PAIRS]
    ordered, entering = refs[NX + 2 * PAIRS :]
    for m in range(PAIRS):
        ordered[(pos[0] >> 1) ^ m] = parts[m][...]
    carry = jnp.zeros((W, W), F32)
    logs = [plane[W : W + 1, :] for plane in planes]
    for k in range(1, NX):
        after = jnp.zeros((1, W), F32)
        for j in range(1, NX):
            if j != k:
                between = jnp.logical_and(pos[2] ^ j > pos[2] ^ k, pos[2] ^ j < pos[2])
                after += jnp.where(between, logs[j - 1], 0.0)
        weight = jnp.where(pos[2] ^ k < pos[2], jnp.exp(after), 0.0)
        carry += weight * planes[k - 1][:W, :]
    carry = jnp.exp(before[W : W + 1, :]) * carry + before[:W, :]
    for place in range(PAIRS):
        entering[place] = carry
        if place < PAIRS - 1:
            carry = jnp.exp(ordered[place, W : W + 1, :]) * carry + ordered[place, :W, :]
    for m in range(PAIRS):
        outs[m][...] = entering[(pos[0] >> 1) ^ m]


def spread_kernel(pos, keep, got, *refs):
    carries, mine, send = refs[:PAIRS], refs[PAIRS], refs[PAIRS + 1]
    first = pos[0] & 1 == 0
    for m in range(PAIRS):
        j = (pos[0] >> 1) ^ m
        state, log = rows_of(j), pl.ds(ROWS + j, 1)
        carry = carries[m][...]
        decay = jnp.exp(jnp.where(first, keep[log, :], got[log, :]))
        after = decay * carry + jnp.where(first, keep[state, :], got[state, :])
        mine[state, :] = jnp.where(first, carry, after)
        send[state, :] = jnp.where(first, after, carry)


def inside_kernel(skip, x, z, b, c, log_decay, gain, fixed, slope, read, gain_out):
    read[...] = c[...]
    gain_out[...] = gain[...]
    lower = lower_mask()
    logs = log_decay[...]
    cum = running_sum(logs)
    cum_t = running_sum_t(logs)
    scores = lax.dot_general(c[...], b[...], (((1,), (1,)), ((), ())), preferred_element_type=F32)
    for head in range(HEADS):
        at = slice(head * W, (head + 1) * W)
        column = cum_t[:, head : head + 1]
        differ = column - cum[head : head + 1, :]
        within = jnp.where(lower, jnp.exp(jnp.where(lower, differ, 0.0)), 0.0)
        x_head = x[:, at]
        inner = jnp.dot((within * scores).astype(BF16), x_head, preferred_element_type=F32)
        gate = z[:, at].astype(F32)
        gate = gate / (1.0 + jnp.exp(-gate))
        fixed[:, at] = (inner + skip[head] * x_head.astype(F32)) * gate
        slope[:, at] = jnp.exp(column) * gate


def finish_kernel(group, sides, stage, pos, *refs):
    count = len(sides)
    states, refs = refs[:count], refs[count:]
    read, fixed, slope, gain, w = refs[:5]
    first_row = 0
    if stage == 0:
        total, w_next, normed, sem = refs[5:]
        fetch = pltpu.make_async_copy(w.at[w_next.shape[0] :, :], w_next, sem)
        fetch.start()
    elif stage == 1:
        so_far, total, normed = refs[5:]
        first_row = w.shape[0]
    else:
        so_far, mine, other, normed, tile = refs[5:]
        first_row = w.shape[0]
    role = pos[0] & 1
    bases = [(group * 2 + (1 - role if side else role)) * HALF for side in sides]
    twice = jnp.concatenate([read[...], read[...]], axis=1)
    for k, base in enumerate(bases):
        for i in range(0, HALF, 2):
            parts = [split(states[k][(i + n) * W : (i + n + 1) * W, :]) for n in range(2)]
            both = [jnp.concatenate(half, axis=1) for half in zip(*parts)]
            carried = jnp.dot(twice, jnp.concatenate(both), preferred_element_type=F32)
            for n in range(2):
                head = base + i + n
                at = rows_of(head)
                gated = fixed[:, at] + slope[:, at] * carried[:, n * W : (n + 1) * W]
                meansq = jnp.mean(gated * gated, axis=-1, keepdims=True)
                value = gated * lax.rsqrt(meansq + 1e-05) * gain[pl.ds(head, 1), :]
                place = k * ROWS + (i + n) * W
                normed[:, place : place + W] = value.astype(BF16)
    for at in range(0, w.shape[1], TILE):
        columns = slice(at, at + TILE)
        part = jnp.zeros((W, TILE), F32) if stage == 0 else so_far[:, columns]
        for k, base in enumerate(bases):
            rows = pl.ds(pl.multiple_of(base * W - first_row, ROWS), ROWS)
            part += jnp.dot(
                normed[:, k * ROWS : (k + 1) * ROWS], w[rows, columns], preferred_element_type=F32
            )
        if stage < 2:
            total[:, columns] = part
        else:
            half = W // 2
            tile[...] = part
            mine[:, columns] = tile[pl.ds(pl.multiple_of(pos[3] * half, half), half), :]
            other[:, columns] = tile[pl.ds(pl.multiple_of((1 - pos[3]) * half, half), half), :]
    if stage == 0:
        fetch.wait()


def call(kernel, outs, specs, scratch=(), name=None, grant=16, work=0):
    return pl.pallas_call(
        kernel,
        out_shape=outs,
        in_specs=specs,
        out_specs=jax.tree.map(lambda _: VMEM, outs),
        scratch_shapes=scratch,
        compiler_params=pltpu.CompilerParams(vmem_limit_bytes=grant * 1024 * 1024),
        cost_estimate=pl.CostEstimate(flops=work, bytes_accessed=0, transcendentals=0),
        name=name,
    )


def shaped(*shape, dtype=F32):
    return jax.ShapeDtypeStruct(shape, dtype)


def per_device(x_in, z_in, b_in, c_in, log_decay, d_skip, norm_gain, w_out):
    index = lax.axis_index("ctx")
    pos = jnp.stack([index % NZ, index // NZ % NY, index // (NZ * NY), lax.axis_index("tp")]).astype(jnp.int32)
    x = x_in.reshape(W, HEADS * W)
    width = w_out.shape[1]
    full, single = shaped(ROWS + 8, W), shaped(W + 8, W)
    keep, got, parts, totals, planes, mine, states = {}, {}, {}, {}, {}, {}, {}
    for g in range(GROUPS):
        keep[g], send = call(
            functools.partial(local_state_kernel, g), [full] * 2, [SMEM, VMEM, VMEM, VMEM],
            [pltpu.VMEM((HEADS, W), F32)], name=f"local_state_{g}",
        )(pos, x, b_in, log_decay)
        got[g] = lax.ppermute(send, "ctx", partners(1, 1))
    keep[1], z = lax.optimization_barrier((keep[1], z_in))
    fixed, slope, read, gain = call(
        inside_kernel,
        [shaped(W, HEADS * W), shaped(W, HEADS * W), shaped(W, W, dtype=BF16), shaped(HEADS, W)],
        [SMEM] + [VMEM] * 6, name="inside",
    )(d_skip, x, z.reshape(W, HEADS * W), b_in, c_in, log_decay, norm_gain)
    keep[0], fixed, slope, read, gain = lax.optimization_barrier(
        (keep[0], fixed, slope, read, gain)
    )
    for g in range(GROUPS):
        pair = call(pair_kernel, [single] * PAIRS, [SMEM, VMEM, VMEM], name=f"pair_{g}")(
            pos, keep[g], got[g]
        )
        parts[g] = [pair[0]] + [lax.ppermute(pair[m], "ctx", partners(2, m)) for m in range(1, PAIRS)]
    for g in range(GROUPS):
        total = call(
            row_total_kernel, single, [SMEM] + [VMEM] * PAIRS, name=f"row_total_{g}"
        )(pos, *parts[g])
        totals[g] = [total] + [lax.ppermute(total, "ctx", partners(NZ, k)) for k in range(1, NY)]
    for g in range(GROUPS):
        plane, before = call(
            plane_kernel, [single] * 2, [SMEM] + [VMEM] * NY, name=f"plane_{g}"
        )(pos, *totals[g])
        planes[g] = [lax.ppermute(plane, "ctx", partners(NY * NZ, k)) for k in range(1, NX)] + [before]
    for g in range(GROUPS):
        back = call(
            entering_kernel, [shaped(W, W)] * PAIRS, [SMEM] + [VMEM] * (NX + PAIRS),
            [pltpu.VMEM((PAIRS, W + 8, W), F32), pltpu.VMEM((PAIRS, W, W), F32)],
            name=f"entering_{g}", work=WORK,
        )(pos, *planes[g], *parts[g])
        states[g] = [back[0]] + [lax.ppermute(back[m], "ctx", partners(2, m)) for m in range(1, PAIRS)]
    for g in range(GROUPS):
        mine[g], send = call(
            spread_kernel, [shaped(ROWS, W)] * 2, [SMEM] + [VMEM] * (2 + PAIRS), name=f"spread_{g}"
        )(pos, keep[g], got[g], *states[g])
        states[g] = lax.ppermute(send, "ctx", partners(1, 1))

    def finish(group, sides, stage, parts, w, outs, extra):
        scratch = [pltpu.VMEM((W, len(sides) * ROWS), BF16)]
        scratch += [[pltpu.SemaphoreType.DMA(())], [], [pltpu.VMEM((W, TILE), F32)]][stage]
        return call(
            functools.partial(finish_kernel, group, sides, stage), outs,
            [SMEM] + [VMEM] * (len(sides) + 5 + len(extra)), scratch, name=f"finish_{stage}",
        )(pos, *parts, read, fixed, slope, gain, w, *extra)

    so_far, w = finish(
        0, (0, 1), 0, [mine[0], states[0]], w_out,
        [shaped(W, width), shaped(w_out.shape[0] // 2, width, dtype=BF16)], [],
    )
    so_far = finish(1, (0,), 1, [mine[1]], w, shaped(W, width), [so_far])
    near, far = finish(1, (1,), 2, [states[1]], w, [shaped(W // 2, width)] * 2, [so_far])
    return (near + lax.ppermute(far, "tp", [(0, 1), (1, 0)])).astype(BF16)


def solution(mesh):
    return jax.shard_map(
        per_device,
        mesh=mesh,
        in_specs=(
            P("ctx", "tp", None),
            P("ctx", "tp", None),
            P("ctx", None),
            P("ctx", None),
            P("tp", "ctx"),
            P("tp"),
            P("tp", None),
            P("tp", None),
        ),
        out_specs=P(("ctx", "tp"), None),
        check_vma=False,
    )
```

time: 853 us -> 84.1 us (0.10)
  blocking collectives: 310 us -> 0 us
  waiting for transfers between devices: 313 us -> 10.7 us
  other arithmetic: 189 us -> 0.84 us
  starting transfers between devices: 0.04 us -> 51.2 us
  Pallas kernels: 0 us -> 14.9 us
  between operations: 14.2 us -> 0.18 us
  matrix products: 10.5 us -> 0 us
    unnamed x1 -> x0, blocking collectives: 310 us -> none
    all_gather x1 -> x0, waiting for transfers between devices: 301 us -> none  [prefix(): pieces = jax.tree.map(lambda part: lax.all_gather(part, axis), value)]
    select_n x127 -> x0, other arithmetic: 185 us -> none  [hop(): jnp.where(position < mine, new, old)]
    ppermute x0 -> x29, starting transfers between devices: none -> 51.2 us  [the longest x6 13.7 us: per_device(): lax.ppermute(pair[m], 'ctx', partners(2, m))]
    pallas_call x0 -> x16, Pallas kernels: none -> 14.9 us  [the longest x3 4.55 us: finish(): call(functools.partial(finish_kernel, group, sides, stage), outs, [SMEM]...]
    reduce_scatter x1 -> x0, waiting for transfers between devices: 11.2 us -> none  [per_device(): lax.psum_scatter(jnp.dot(normed, w_out, preferred_element_type=jnp.float3...]
    ppermute x0 -> x29, waiting for transfers between devices: none -> 10.7 us  [the longest x2 3.27 us: per_device(): states[g] = lax.ppermute(send, 'ctx', partners(1, 1))]
    dot_general x6 -> x0, matrix products: 10.5 us -> none  [the longest x1 5.65 us: per_device(): jnp.dot(normed, w_out, preferred_element_type=jnp.float32)]
  transfers between devices with their start and end apart: 2 -> 29, of which waited for: 2 -> 8; matrix products, arithmetic and copies ran while one was open for 1% -> 1% of each run, Pallas kernels for 0% -> 15%
where the time goes in v4:
time: 84.1 us; the launch traced here: 83.7 us
  starting transfers between devices  51.2 us (61%)
  Pallas kernels  14.9 us (18%)
  waiting for transfers between devices  10.7 us (13%)
  local copies, waits for them, and re-layouts  5.93 us (7%)
    ppermute x6, starting transfers between devices, per_device(): lax.ppermute(pair[m], 'ctx', partners(2, m))  13.7 us
    ppermute x6, starting transfers between devices, per_device(): lax.ppermute(back[m], 'ctx', partners(2, m))  11.5 us
    ppermute x6, starting transfers between devices, per_device(): lax.ppermute(total, 'ctx', partners(NZ, k))  7 us
    ppermute x6, starting transfers between devices, per_device(): lax.ppermute(plane, 'ctx', partners(NY * NZ, k))  6.86 us
    unnamed x16, local copies, waits for them, and re-layouts  5.93 us
    ppermute x1, starting transfers between devices, per_device(): return (near + lax.ppermute(far, 'tp', [(0, 1), (1, 0)])).astype(BF16)  5.15 us
    pallas_call x3, Pallas kernels, finish(): call(functools.partial(finish_kernel, group, sides, stage), outs, [SMEM]...  4.55 us
    ppermute x2, starting transfers between devices, per_device(): states[g] = lax.ppermute(send, 'ctx', partners(1, 1))  4.31 us
  transfers between devices with their start and end apart: 29, of which 8 were waited for; matrix products, arithmetic and copies ran while one was open for 1% of the time, Pallas kernels for 15%

profile of v4, /device:TPU:1, one launch (start us, length us, event | category | flops | bytes accessed | tf_op | source)
XLA Modules:
  0.0 83.7 jit_solution(10525576385603593473)
XLA Ops:
  0.0 1.2 %copy.14 = bf16[16,8,16,128]{3,1,2,0:T(8,128)(2,1)S(1)} copy(bf16[16,8,16,128]{3,2,1,0:T(8,128)(2,1)} %bitcast.18) | data formatting | bytes 1048576
  1.2 0.1 pad_add_fusion.pos
  1.3 0.8 copy-done
  2.0 0.7 copy-done.1
  2.7 1.3 %local_state_0.1 = (f32[520,128]{1,0:T(8,128)S(1)}, f32[520,128]{1,0:T(8,128)S(1)}) custom-call(s32[4]{0:T(128)S(1)} %pad_add_fusion.pos, bf16[128,2048]{1,0:T(8,128)(2,1)S(1)} %bitcast.14, bf16[128,128]{1,0:T(8,128)(2,1)S(1)} %copy-done, f32[16,128]{1,0:T(8,128)S(1)} %copy-done.1), custom_call_target="tpu_custom_call" | custom-call | tf_op jit(solution)/shard_map/local_state_0/pallas_call | solution.py:273
  4.1 2.6 %collective-permute-start.14 = (f32[520,128]{1,0:T(8,128)S(1)}, f32[520,128]{1,0:T(8,128)S(1)}, u32[]{:S(2)}, u32[]{:S(2)}) collective-permute-start(f32[520,128]{1,0:T(8,128)S(1)} %get-tuple-element.73), channel_id=1, source_target_pairs={{0,2},{2,0},{4,6},{6,4},{8,10},{10,8},{12,14},{14,12},{16,18},{18,... | collective-permute-start | bytes 798728 | tf_op jit(solution)/shard_map/ppermute | solution.py:277
  6.6 1.3 %local_state_1.1 = (f32[520,128]{1,0:T(8,128)S(1)}, f32[520,128]{1,0:T(8,128)S(1)}) custom-call(s32[4]{0:T(128)S(1)} %pad_add_fusion.pos, bf16[128,2048]{1,0:T(8,128)(2,1)S(1)} %bitcast.15, bf16[128,128]{1,0:T(8,128)(2,1)S(1)} %copy-done, f32[16,128]{1,0:T(8,128)S(1)} %copy-done.1), custom_call_target="tpu_custom_call" | custom-call | tf_op jit(solution)/shard_map/local_state_1/pallas_call | solution.py:273
  7.9 0.1 collective-permute-start
  8.0 1.2 %copy.13 = bf16[16,8,16,128]{3,1,2,0:T(8,128)(2,1)S(1)} copy(bf16[16,8,16,128]{3,2,1,0:T(8,128)(2,1)} %bitcast.19) | data formatting | bytes 1048576
  9.2 0.0 copy-start.2
  9.2 0.7 copy-done.2
  10.0 0.7 copy-done.3
  10.7 0.7 copy-done.4
  11.3 1.6 %inside.1 = (f32[128,2048]{1,0:T(8,128)S(1)}, f32[128,2048]{1,0:T(8,128)S(1)}, bf16[128,128]{1,0:T(8,128)(2,1)S(1)}, f32[16,128]{1,0:T(8,128)S(1)}) custom-call(f32[16]{0:T(128)S(1)} %copy-done.4, bf16[128,2048]{1,0:T(8,128)(2,1)S(1)} %bitcast.16, bf16[128,2048]{1,0:T(8,128)(2,1)S(1)} %bitcast.17, bf16[128,128]{1,0:T(8,128)(2,1)S(1)} %copy-done, ...), custom_call_target="tpu_custom_call" | custom-call | tf_op jit(solution)/shard_map/inside/pallas_call | solution.py:279
  13.0 0.6 pair_0.1
  13.6 3.1 %collective-permute-start.15 = (f32[136,128]{1,0:T(8,128)S(1)}, f32[136,128]{1,0:T(8,128)S(1)}, u32[]{:S(2)}, u32[]{:S(2)}) collective-permute-start(f32[136,128]{1,0:T(8,128)S(1)} %get-tuple-element.75), channel_id=1, source_target_pairs={{0,4},{2,6},{4,0},{6,2},{8,12},{10,14},{12,8},{14,10},{16,20},{18,... | collective-permute-start | bytes 208904 | tf_op jit(solution)/shard_map/ppermute | solution.py:291
  16.7 4.9 %collective-permute-start.16 = (f32[136,128]{1,0:T(8,128)S(1)}, f32[136,128]{1,0:T(8,128)S(1)}, u32[]{:S(2)}, u32[]{:S(2)}) collective-permute-start(f32[136,128]{1,0:T(8,128)S(1)} %get-tuple-element.76), channel_id=1, source_target_pairs={{0,8},{2,10},{4,12},{6,14},{8,0},{10,2},{12,4},{14,6},{16,24},{18,... | collective-permute-start | bytes 208904 | tf_op jit(solution)/shard_map/ppermute | solution.py:291
  21.6 0.0 collective-permute-start.17
  21.6 0.6 pair_1.1
  22.2 1.3 %collective-permute-start.1 = (f32[136,128]{1,0:T(8,128)S(1)}, f32[136,128]{1,0:T(8,128)S(1)}, u32[]{:S(2)}, u32[]{:S(2)}) collective-permute-start(f32[136,128]{1,0:T(8,128)S(1)} %get-tuple-element.52), channel_id=1, source_target_pairs={{0,4},{2,6},{4,0},{6,2},{8,12},{10,14},{12,8},{14,10},{16,20},{18,... | collective-permute-start | bytes 208904 | tf_op jit(solution)/shard_map/ppermute | solution.py:291
  23.5 4.5 %collective-permute-start.2 = (f32[136,128]{1,0:T(8,128)S(1)}, f32[136,128]{1,0:T(8,128)S(1)}, u32[]{:S(2)}, u32[]{:S(2)}) collective-permute-start(f32[136,128]{1,0:T(8,128)S(1)} %get-tuple-element.53), channel_id=1, source_target_pairs={{0,8},{2,10},{4,12},{6,14},{8,0},{10,2},{12,4},{14,6},{16,24},{18,... | collective-permute-start | bytes 208904 | tf_op jit(solution)/shard_map/ppermute | solution.py:291
  27.9 0.0 collective-permute-start.3
  27.9 0.0 collective-permute-done.16.refs_2_.refs_6_
  27.9 0.5 collective-permute-done.17.refs_3_.refs_7_
  28.5 0.6 row_total_0.1.refs_0_
  29.1 2.8 %collective-permute-start.20 = (f32[136,128]{1,0:T(8,128)S(1)}, f32[136,128]{1,0:T(8,128)S(1)}, u32[]{:S(2)}, u32[]{:S(2)}) collective-permute-start(f32[136,128]{1,0:T(8,128)S(1)} %row_total_0.1.refs_0_), channel_id=1, source_target_pairs={{0,48},{2,50},{4,52},{6,54},{8,56},{10,58},{12,60},{14,62},{16,32}... | collective-permute-start | bytes 208904 | tf_op jit(solution)/shard_map/ppermute | solution.py:296
  31.9 0.3 collective-permute-start.19
  32.2 0.3 collective-permute-start.18
  32.6 2.0 %collective-permute-done.3.refs_3_.refs_7_ = f32[136,128]{1,0:T(8,128)S(1)} collective-permute-done((f32[136,128]{1,0:T(8,128)S(1)}, f32[136,128]{1,0:T(8,128)S(1)}, u32[]{:S(2)}, u32[]{:S(2)}) %collective-permute-start.3) | collective-permute-done | bytes 69664 | tf_op jit(solution)/shard_map/ppermute | solution.py:291
  34.6 0.6 row_total_1.1.refs_0_
  35.2 2.8 %collective-permute-start.6 = (f32[136,128]{1,0:T(8,128)S(1)}, f32[136,128]{1,0:T(8,128)S(1)}, u32[]{:S(2)}, u32[]{:S(2)}) collective-permute-start(f32[136,128]{1,0:T(8,128)S(1)} %row_total_1.1.refs_0_), channel_id=1, source_target_pairs={{0,48},{2,50},{4,52},{6,54},{8,56},{10,58},{12,60},{14,62},{16,32}... | collective-permute-start | bytes 208904 | tf_op jit(solution)/shard_map/ppermute | solution.py:296
  38.0 0.3 collective-permute-start.5
  38.3 0.3 collective-permute-start.4
  38.7 0.6 plane_0.1
  39.3 2.6 %collective-permute-start.23 = (f32[136,128]{1,0:T(8,128)S(1)}, f32[136,128]{1,0:T(8,128)S(1)}, u32[]{:S(2)}, u32[]{:S(2)}) collective-permute-start(f32[136,128]{1,0:T(8,128)S(1)} %get-tuple-element.78), channel_id=1, source_target_pairs={{0,192},{2,194},{4,196},{6,198},{8,200},{10,202},{12,204},{14,206}... | collective-permute-start | bytes 208904 | tf_op jit(solution)/shard_map/ppermute | solution.py:301
  41.8 0.5 collective-permute-start.22
  42.4 0.3 collective-permute-start.21
  42.6 0.8 collective-permute-done.5.refs_2_
  43.4 0.6 plane_1.1
  44.0 2.7 %collective-permute-start.9 = (f32[136,128]{1,0:T(8,128)S(1)}, f32[136,128]{1,0:T(8,128)S(1)}, u32[]{:S(2)}, u32[]{:S(2)}) collective-permute-start(f32[136,128]{1,0:T(8,128)S(1)} %get-tuple-element.55), channel_id=1, source_target_pairs={{0,192},{2,194},{4,196},{6,198},{8,200},{10,202},{12,204},{14,206}... | collective-permute-start | bytes 208904 | tf_op jit(solution)/shard_map/ppermute | solution.py:301
  46.8 0.5 collective-permute-start.8
  47.3 0.3 collective-permute-start.7
  47.6 0.6 entering_0.1
  48.2 1.0 %collective-permute-start.24 = (f32[128,128]{1,0:T(8,128)S(1)}, f32[128,128]{1,0:T(8,128)S(1)}, u32[]{:S(2)}, u32[]{:S(2)}) collective-permute-start(f32[128,128]{1,0:T(8,128)S(1)} %get-tuple-element.81), channel_id=1, source_target_pairs={{0,4},{2,6},{4,0},{6,2},{8,12},{10,14},{12,8},{14,10},{16,20},{18,... | collective-permute-start | bytes 196616 | tf_op jit(solution)/shard_map/ppermute | solution.py:308
  49.2 1.8 %collective-permute-start.25 = (f32[128,128]{1,0:T(8,128)S(1)}, f32[128,128]{1,0:T(8,128)S(1)}, u32[]{:S(2)}, u32[]{:S(2)}) collective-permute-start(f32[128,128]{1,0:T(8,128)S(1)} %get-tuple-element.82), channel_id=1, source_target_pairs={{0,8},{2,10},{4,12},{6,14},{8,0},{10,2},{12,4},{14,6},{16,24},{18,... | collective-permute-start | bytes 196616 | tf_op jit(solution)/shard_map/ppermute | solution.py:308
  50.9 3.0 %collective-permute-start.26 = (f32[128,128]{1,0:T(8,128)S(1)}, f32[128,128]{1,0:T(8,128)S(1)}, u32[]{:S(2)}, u32[]{:S(2)}) collective-permute-start(f32[128,128]{1,0:T(8,128)S(1)} %get-tuple-element.83), channel_id=1, source_target_pairs={{0,12},{2,14},{4,8},{6,10},{8,4},{10,6},{12,0},{14,2},{16,28},{18,... | collective-permute-start | bytes 196616 | tf_op jit(solution)/shard_map/ppermute | solution.py:308
  53.9 0.6 entering_1.1
  54.6 1.0 %collective-permute-start.10 = (f32[128,128]{1,0:T(8,128)S(1)}, f32[128,128]{1,0:T(8,128)S(1)}, u32[]{:S(2)}, u32[]{:S(2)}) collective-permute-start(f32[128,128]{1,0:T(8,128)S(1)} %get-tuple-element.58), channel_id=1, source_target_pairs={{0,4},{2,6},{4,0},{6,2},{8,12},{10,14},{12,8},{14,10},{16,20},{18,... | collective-permute-start | bytes 196616 | tf_op jit(solution)/shard_map/ppermute | solution.py:308
  55.6 1.8 %collective-permute-start.11 = (f32[128,128]{1,0:T(8,128)S(1)}, f32[128,128]{1,0:T(8,128)S(1)}, u32[]{:S(2)}, u32[]{:S(2)}) collective-permute-start(f32[128,128]{1,0:T(8,128)S(1)} %get-tuple-element.59), channel_id=1, source_target_pairs={{0,8},{2,10},{4,12},{6,14},{8,0},{10,2},{12,4},{14,6},{16,24},{18,... | collective-permute-start | bytes 196616 | tf_op jit(solution)/shard_map/ppermute | solution.py:308
  57.3 3.0 %collective-permute-start.12 = (f32[128,128]{1,0:T(8,128)S(1)}, f32[128,128]{1,0:T(8,128)S(1)}, u32[]{:S(2)}, u32[]{:S(2)}) collective-permute-start(f32[128,128]{1,0:T(8,128)S(1)} %get-tuple-element.60), channel_id=1, source_target_pairs={{0,12},{2,14},{4,8},{6,10},{8,4},{10,6},{12,0},{14,2},{16,28},{18,... | collective-permute-start | bytes 196616 | tf_op jit(solution)/shard_map/ppermute | solution.py:308
  60.3 0.6 spread_0.1
  61.0 1.2 %collective-permute-start.27 = (f32[512,128]{1,0:T(8,128)S(1)}, f32[512,128]{1,0:T(8,128)S(1)}, u32[]{:S(2)}, u32[]{:S(2)}) collective-permute-start(f32[512,128]{1,0:T(8,128)S(1)} %get-tuple-element.85), channel_id=1, source_target_pairs={{0,2},{2,0},{4,6},{6,4},{8,10},{10,8},{12,14},{14,12},{16,18},{18,... | collective-permute-start | bytes 786440 | tf_op jit(solution)/shard_map/ppermute | solution.py:313
  62.2 1.5 %collective-permute-done.11.refs_2_ = f32[128,128]{1,0:T(8,128)S(1)} collective-permute-done((f32[128,128]{1,0:T(8,128)S(1)}, f32[128,128]{1,0:T(8,128)S(1)}, u32[]{:S(2)}, u32[]{:S(2)}) %collective-permute-start.11) | collective-permute-done | bytes 65568 | tf_op jit(solution)/shard_map/ppermute | solution.py:308
  63.7 1.0 %collective-permute-done.12.refs_3_ = f32[128,128]{1,0:T(8,128)S(1)} collective-permute-done((f32[128,128]{1,0:T(8,128)S(1)}, f32[128,128]{1,0:T(8,128)S(1)}, u32[]{:S(2)}, u32[]{:S(2)}) %collective-permute-start.12) | collective-permute-done | bytes 65568 | tf_op jit(solution)/shard_map/ppermute | solution.py:308
  64.7 0.6 spread_1.1
  65.3 3.1 %collective-permute-start.13 = (f32[512,128]{1,0:T(8,128)S(1)}, f32[512,128]{1,0:T(8,128)S(1)}, u32[]{:S(2)}, u32[]{:S(2)}) collective-permute-start(f32[512,128]{1,0:T(8,128)S(1)} %get-tuple-element.61), channel_id=1, source_target_pairs={{0,2},{2,0},{4,6},{6,4},{8,10},{10,8},{12,14},{14,12},{16,18},{18,... | collective-permute-start | bytes 786440 | tf_op jit(solution)/shard_map/ppermute | solution.py:313
  68.4 0.4 collective-permute-done.27.refs_1_
  68.9 2.0 %finish_0.1 = (f32[128,2048]{1,0:T(8,128)S(1)}, bf16[1024,2048]{1,0:T(8,128)(2,1)S(1)}) custom-call(s32[4]{0:T(128)S(1)} %pad_add_fusion.pos, f32[512,128]{1,0:T(8,128)S(1)} %get-tuple-element.84.refs_0_, f32[512,128]{1,0:T(8,128)S(1)} %collective-permute-done.27.refs_1_, bf16[128,128]{1,0:T(8,128)(2,1)S(1)} %get-tuple-element.68.refs_2_.refs_1_, ...), custom_call_target="tpu_custom_call" | custom-call | tf_op jit(solution)/shard_map/finish_0/pallas_call | solution.py:318
  70.8 1.3 %finish_1.1.refs_6_ = f32[128,2048]{1,0:T(8,128)S(1)} custom-call(s32[4]{0:T(128)S(1)} %pad_add_fusion.pos, f32[512,128]{1,0:T(8,128)S(1)} %get-tuple-element.87.refs_0_, bf16[128,128]{1,0:T(8,128)(2,1)S(1)} %get-tuple-element.68.refs_2_.refs_1_, f32[128,2048]{1,0:T(8,128)S(1)} %get-tuple-element.69.refs_3_.refs_2_, ...), custom_call_target="tpu_custom_call" | custom-call | tf_op jit(solution)/shard_map/finish_1/pallas_call | solution.py:318
  72.1 2.8 %collective-permute-done.13.refs_0_ = f32[512,128]{1,0:T(8,128)S(1)} collective-permute-done((f32[512,128]{1,0:T(8,128)S(1)}, f32[512,128]{1,0:T(8,128)S(1)}, u32[]{:S(2)}, u32[]{:S(2)}) %collective-permute-start.13) | collective-permute-done | bytes 262176 | tf_op jit(solution)/shard_map/ppermute | solution.py:313
  75.0 1.3 %finish_2.1 = (f32[64,2048]{1,0:T(8,128)S(1)}, f32[64,2048]{1,0:T(8,128)S(1)}) custom-call(s32[4]{0:T(128)S(1)} %pad_add_fusion.pos, f32[512,128]{1,0:T(8,128)S(1)} %collective-permute-done.13.refs_0_, bf16[128,128]{1,0:T(8,128)(2,1)S(1)} %get-tuple-element.68.refs_2_.refs_1_, f32[128,2048]{1,0:T(8,128)S(1)} %get-tuple-element.69.refs_3_.refs_2_, ...), custom_call_target="tpu_custom_call" | custom-call | tf_op jit(solution)/shard_map/finish_2/pallas_call | solution.py:318
  76.3 5.2 %collective-permute-start.28 = (f32[64,2048]{1,0:T(8,128)S(1)}, f32[64,2048]{1,0:T(8,128)S(1)}, u32[]{:S(2)}, u32[]{:S(2)}) collective-permute-start(f32[64,2048]{1,0:T(8,128)S(1)} %get-tuple-element.90), channel_id=1, source_target_pairs={{0,1},{1,0},{2,3},{3,2},{4,5},{5,4},{6,7},{7,6},{8,9},{9,8},{10,11... | collective-permute-start | bytes 1572872 | tf_op jit(solution)/shard_map/ppermute | solution.py:329
  81.4 1.5 %collective-permute-done.28 = f32[64,2048]{1,0:T(8,128)S(1)} collective-permute-done((f32[64,2048]{1,0:T(8,128)S(1)}, f32[64,2048]{1,0:T(8,128)S(1)}, u32[]{:S(2)}, u32[]{:S(2)}) %collective-permute-start.28) | collective-permute-done | bytes 524320 | tf_op jit(solution)/shard_map/ppermute | solution.py:329
  83.0 0.8 add_convert_fusion
  (29 shorter events, 0.1 us)
Async XLA Ops:
  1.3 0.8 copy-start
  2.0 0.7 copy-start.1
  4.1 8.9 %collective-permute-start.14 = (f32[520,128]{1,0:T(8,128)S(1)}, f32[520,128]{1,0:T(8,128)S(1)}, u32[]{:S(2)}, u32[]{:S(2)}) collective-permute-start(f32[520,128]{1,0:T(8,128)S(1)} %get-tuple-element.73), channel_id=1, source_target_pairs={{0,2},{2,0},{4,6},{6,4},{8,10},{10,8},{12,14},{14,12},{16,18},{18,... | collective-permute-start | bytes 798728 | tf_op jit(solution)/shard_map/ppermute | solution.py:277
  7.9 13.6 %collective-permute-start = (f32[520,128]{1,0:T(8,128)S(1)}, f32[520,128]{1,0:T(8,128)S(1)}, u32[]{:S(2)}, u32[]{:S(2)}) collective-permute-start(f32[520,128]{1,0:T(8,128)S(1)} %get-tuple-element.50), channel_id=1, source_target_pairs={{0,2},{2,0},{4,6},{6,4},{8,10},{10,8},{12,14},{14,12},{16,18},{18,... | collective-permute-start | bytes 798728 | tf_op jit(solution)/shard_map/ppermute | solution.py:277
  9.2 0.8 copy-start.2
  10.0 0.7 copy-start.3
  10.7 0.7 copy-start.4
  13.6 14.4 %collective-permute-start.15 = (f32[136,128]{1,0:T(8,128)S(1)}, f32[136,128]{1,0:T(8,128)S(1)}, u32[]{:S(2)}, u32[]{:S(2)}) collective-permute-start(f32[136,128]{1,0:T(8,128)S(1)} %get-tuple-element.75), channel_id=1, source_target_pairs={{0,4},{2,6},{4,0},{6,2},{8,12},{10,14},{12,8},{14,10},{16,20},{18,... | collective-permute-start | bytes 208904 | tf_op jit(solution)/shard_map/ppermute | solution.py:291
  16.7 11.3 %collective-permute-start.16 = (f32[136,128]{1,0:T(8,128)S(1)}, f32[136,128]{1,0:T(8,128)S(1)}, u32[]{:S(2)}, u32[]{:S(2)}) collective-permute-start(f32[136,128]{1,0:T(8,128)S(1)} %get-tuple-element.76), channel_id=1, source_target_pairs={{0,8},{2,10},{4,12},{6,14},{8,0},{10,2},{12,4},{14,6},{16,24},{18,... | collective-permute-start | bytes 208904 | tf_op jit(solution)/shard_map/ppermute | solution.py:291
  21.6 6.9 %collective-permute-start.17 = (f32[136,128]{1,0:T(8,128)S(1)}, f32[136,128]{1,0:T(8,128)S(1)}, u32[]{:S(2)}, u32[]{:S(2)}) collective-permute-start(f32[136,128]{1,0:T(8,128)S(1)} %get-tuple-element.77), channel_id=1, source_target_pairs={{0,12},{2,14},{4,8},{6,10},{8,4},{10,6},{12,0},{14,2},{16,28},{18,... | collective-permute-start | bytes 208904 | tf_op jit(solution)/shard_map/ppermute | solution.py:291
  22.2 10.0 %collective-permute-start.1 = (f32[136,128]{1,0:T(8,128)S(1)}, f32[136,128]{1,0:T(8,128)S(1)}, u32[]{:S(2)}, u32[]{:S(2)}) collective-permute-start(f32[136,128]{1,0:T(8,128)S(1)} %get-tuple-element.52), channel_id=1, source_target_pairs={{0,4},{2,6},{4,0},{6,2},{8,12},{10,14},{12,8},{14,10},{16,20},{18,... | collective-permute-start | bytes 208904 | tf_op jit(solution)/shard_map/ppermute | solution.py:291
  23.5 9.1 %collective-permute-start.2 = (f32[136,128]{1,0:T(8,128)S(1)}, f32[136,128]{1,0:T(8,128)S(1)}, u32[]{:S(2)}, u32[]{:S(2)}) collective-permute-start(f32[136,128]{1,0:T(8,128)S(1)} %get-tuple-element.53), channel_id=1, source_target_pairs={{0,8},{2,10},{4,12},{6,14},{8,0},{10,2},{12,4},{14,6},{16,24},{18,... | collective-permute-start | bytes 208904 | tf_op jit(solution)/shard_map/ppermute | solution.py:291
  27.9 6.6 %collective-permute-start.3 = (f32[136,128]{1,0:T(8,128)S(1)}, f32[136,128]{1,0:T(8,128)S(1)}, u32[]{:S(2)}, u32[]{:S(2)}) collective-permute-start(f32[136,128]{1,0:T(8,128)S(1)} %get-tuple-element.54), channel_id=1, source_target_pairs={{0,12},{2,14},{4,8},{6,10},{8,4},{10,6},{12,0},{14,2},{16,28},{18,... | collective-permute-start | bytes 208904 | tf_op jit(solution)/shard_map/ppermute | solution.py:291
  29.1 9.3 %collective-permute-start.20 = (f32[136,128]{1,0:T(8,128)S(1)}, f32[136,128]{1,0:T(8,128)S(1)}, u32[]{:S(2)}, u32[]{:S(2)}) collective-permute-start(f32[136,128]{1,0:T(8,128)S(1)} %row_total_0.1.refs_0_), channel_id=1, source_target_pairs={{0,48},{2,50},{4,52},{6,54},{8,56},{10,58},{12,60},{14,62},{16,32}... | collective-permute-start | bytes 208904 | tf_op jit(solution)/shard_map/ppermute | solution.py:296
  31.9 6.8 %collective-permute-start.19 = (f32[136,128]{1,0:T(8,128)S(1)}, f32[136,128]{1,0:T(8,128)S(1)}, u32[]{:S(2)}, u32[]{:S(2)}) collective-permute-start(f32[136,128]{1,0:T(8,128)S(1)} %row_total_0.1.refs_0_), channel_id=1, source_target_pairs={{0,32},{2,34},{4,36},{6,38},{8,40},{10,42},{12,44},{14,46},{16,48}... | collective-permute-start | bytes 208904 | tf_op jit(solution)/shard_map/ppermute | solution.py:296
  32.2 6.4 %collective-permute-start.18 = (f32[136,128]{1,0:T(8,128)S(1)}, f32[136,128]{1,0:T(8,128)S(1)}, u32[]{:S(2)}, u32[]{:S(2)}) collective-permute-start(f32[136,128]{1,0:T(8,128)S(1)} %row_total_0.1.refs_0_), channel_id=1, source_target_pairs={{0,16},{2,18},{4,20},{6,22},{8,24},{10,26},{12,28},{14,30},{16,0},... | collective-permute-start | bytes 208904 | tf_op jit(solution)/shard_map/ppermute | solution.py:296
  35.2 7.2 %collective-permute-start.6 = (f32[136,128]{1,0:T(8,128)S(1)}, f32[136,128]{1,0:T(8,128)S(1)}, u32[]{:S(2)}, u32[]{:S(2)}) collective-permute-start(f32[136,128]{1,0:T(8,128)S(1)} %row_total_1.1.refs_0_), channel_id=1, source_target_pairs={{0,48},{2,50},{4,52},{6,54},{8,56},{10,58},{12,60},{14,62},{16,32}... | collective-permute-start | bytes 208904 | tf_op jit(solution)/shard_map/ppermute | solution.py:296
  38.0 5.4 %collective-permute-start.5 = (f32[136,128]{1,0:T(8,128)S(1)}, f32[136,128]{1,0:T(8,128)S(1)}, u32[]{:S(2)}, u32[]{:S(2)}) collective-permute-start(f32[136,128]{1,0:T(8,128)S(1)} %row_total_1.1.refs_0_), channel_id=1, source_target_pairs={{0,32},{2,34},{4,36},{6,38},{8,40},{10,42},{12,44},{14,46},{16,48}... | collective-permute-start | bytes 208904 | tf_op jit(solution)/shard_map/ppermute | solution.py:296
  38.3 5.1 %collective-permute-start.4 = (f32[136,128]{1,0:T(8,128)S(1)}, f32[136,128]{1,0:T(8,128)S(1)}, u32[]{:S(2)}, u32[]{:S(2)}) collective-permute-start(f32[136,128]{1,0:T(8,128)S(1)} %row_total_1.1.refs_0_), channel_id=1, source_target_pairs={{0,16},{2,18},{4,20},{6,22},{8,24},{10,26},{12,28},{14,30},{16,0},... | collective-permute-start | bytes 208904 | tf_op jit(solution)/shard_map/ppermute | solution.py:296
  39.3 8.0 %collective-permute-start.23 = (f32[136,128]{1,0:T(8,128)S(1)}, f32[136,128]{1,0:T(8,128)S(1)}, u32[]{:S(2)}, u32[]{:S(2)}) collective-permute-start(f32[136,128]{1,0:T(8,128)S(1)} %get-tuple-element.78), channel_id=1, source_target_pairs={{0,192},{2,194},{4,196},{6,198},{8,200},{10,202},{12,204},{14,206}... | collective-permute-start | bytes 208904 | tf_op jit(solution)/shard_map/ppermute | solution.py:301
  41.8 5.7 %collective-permute-start.22 = (f32[136,128]{1,0:T(8,128)S(1)}, f32[136,128]{1,0:T(8,128)S(1)}, u32[]{:S(2)}, u32[]{:S(2)}) collective-permute-start(f32[136,128]{1,0:T(8,128)S(1)} %get-tuple-element.78), channel_id=1, source_target_pairs={{0,128},{2,130},{4,132},{6,134},{8,136},{10,138},{12,140},{14,142}... | collective-permute-start | bytes 208904 | tf_op jit(solution)/shard_map/ppermute | solution.py:301
  42.4 5.2 %collective-permute-start.21 = (f32[136,128]{1,0:T(8,128)S(1)}, f32[136,128]{1,0:T(8,128)S(1)}, u32[]{:S(2)}, u32[]{:S(2)}) collective-permute-start(f32[136,128]{1,0:T(8,128)S(1)} %get-tuple-element.78), channel_id=1, source_target_pairs={{0,64},{2,66},{4,68},{6,70},{8,72},{10,74},{12,76},{14,78},{16,80}... | collective-permute-start | bytes 208904 | tf_op jit(solution)/shard_map/ppermute | solution.py:301
  44.0 6.9 %collective-permute-start.9 = (f32[136,128]{1,0:T(8,128)S(1)}, f32[136,128]{1,0:T(8,128)S(1)}, u32[]{:S(2)}, u32[]{:S(2)}) collective-permute-start(f32[136,128]{1,0:T(8,128)S(1)} %get-tuple-element.55), channel_id=1, source_target_pairs={{0,192},{2,194},{4,196},{6,198},{8,200},{10,202},{12,204},{14,206}... | collective-permute-start | bytes 208904 | tf_op jit(solution)/shard_map/ppermute | solution.py:301
  46.8 7.2 %collective-permute-start.8 = (f32[136,128]{1,0:T(8,128)S(1)}, f32[136,128]{1,0:T(8,128)S(1)}, u32[]{:S(2)}, u32[]{:S(2)}) collective-permute-start(f32[136,128]{1,0:T(8,128)S(1)} %get-tuple-element.55), channel_id=1, source_target_pairs={{0,128},{2,130},{4,132},{6,134},{8,136},{10,138},{12,140},{14,142}... | collective-permute-start | bytes 208904 | tf_op jit(solution)/shard_map/ppermute | solution.py:301
  47.3 6.7 %collective-permute-start.7 = (f32[136,128]{1,0:T(8,128)S(1)}, f32[136,128]{1,0:T(8,128)S(1)}, u32[]{:S(2)}, u32[]{:S(2)}) collective-permute-start(f32[136,128]{1,0:T(8,128)S(1)} %get-tuple-element.55), channel_id=1, source_target_pairs={{0,64},{2,66},{4,68},{6,70},{8,72},{10,74},{12,76},{14,78},{16,80}... | collective-permute-start | bytes 208904 | tf_op jit(solution)/shard_map/ppermute | solution.py:301
  47.5 21.3 %slice-start = ((s8[8388608]{0:T(1024)(128)(4,1)}), s8[4194304]{0:T(1024)(128)(4,1)S(1)}, s32[]{:S(2)}) async-start(s8[8388608]{0:T(1024)(128)(4,1)} %bitcast.12), calls=%async_computation | async-start | bytes 8388608
  48.2 9.2 %collective-permute-start.24 = (f32[128,128]{1,0:T(8,128)S(1)}, f32[128,128]{1,0:T(8,128)S(1)}, u32[]{:S(2)}, u32[]{:S(2)}) collective-permute-start(f32[128,128]{1,0:T(8,128)S(1)} %get-tuple-element.81), channel_id=1, source_target_pairs={{0,4},{2,6},{4,0},{6,2},{8,12},{10,14},{12,8},{14,10},{16,20},{18,... | collective-permute-start | bytes 196616 | tf_op jit(solution)/shard_map/ppermute | solution.py:308
  49.2 11.2 %collective-permute-start.25 = (f32[128,128]{1,0:T(8,128)S(1)}, f32[128,128]{1,0:T(8,128)S(1)}, u32[]{:S(2)}, u32[]{:S(2)}) collective-permute-start(f32[128,128]{1,0:T(8,128)S(1)} %get-tuple-element.82), channel_id=1, source_target_pairs={{0,8},{2,10},{4,12},{6,14},{8,0},{10,2},{12,4},{14,6},{16,24},{18,... | collective-permute-start | bytes 196616 | tf_op jit(solution)/shard_map/ppermute | solution.py:308
  50.9 9.4 %collective-permute-start.26 = (f32[128,128]{1,0:T(8,128)S(1)}, f32[128,128]{1,0:T(8,128)S(1)}, u32[]{:S(2)}, u32[]{:S(2)}) collective-permute-start(f32[128,128]{1,0:T(8,128)S(1)} %get-tuple-element.83), channel_id=1, source_target_pairs={{0,12},{2,14},{4,8},{6,10},{8,4},{10,6},{12,0},{14,2},{16,28},{18,... | collective-permute-start | bytes 196616 | tf_op jit(solution)/shard_map/ppermute | solution.py:308
  53.9 14.9 %slice-start.1 = ((s8[8388608]{0:T(1024)(128)(4,1)}), s8[4194304]{0:T(1024)(128)(4,1)S(1)}, s32[]{:S(2)}) async-start(s8[8388608]{0:T(1024)(128)(4,1)} %bitcast.12), calls=%async_computation.1 | async-start | bytes 8388608
  54.6 7.6 %collective-permute-start.10 = (f32[128,128]{1,0:T(8,128)S(1)}, f32[128,128]{1,0:T(8,128)S(1)}, u32[]{:S(2)}, u32[]{:S(2)}) collective-permute-start(f32[128,128]{1,0:T(8,128)S(1)} %get-tuple-element.58), channel_id=1, source_target_pairs={{0,4},{2,6},{4,0},{6,2},{8,12},{10,14},{12,8},{14,10},{16,20},{18,... | collective-permute-start | bytes 196616 | tf_op jit(solution)/shard_map/ppermute | solution.py:308
  55.6 8.1 %collective-permute-start.11 = (f32[128,128]{1,0:T(8,128)S(1)}, f32[128,128]{1,0:T(8,128)S(1)}, u32[]{:S(2)}, u32[]{:S(2)}) collective-permute-start(f32[128,128]{1,0:T(8,128)S(1)} %get-tuple-element.59), channel_id=1, source_target_pairs={{0,8},{2,10},{4,12},{6,14},{8,0},{10,2},{12,4},{14,6},{16,24},{18,... | collective-permute-start | bytes 196616 | tf_op jit(solution)/shard_map/ppermute | solution.py:308
  57.3 7.4 %collective-permute-start.12 = (f32[128,128]{1,0:T(8,128)S(1)}, f32[128,128]{1,0:T(8,128)S(1)}, u32[]{:S(2)}, u32[]{:S(2)}) collective-permute-start(f32[128,128]{1,0:T(8,128)S(1)} %get-tuple-element.60), channel_id=1, source_target_pairs={{0,12},{2,14},{4,8},{6,10},{8,4},{10,6},{12,0},{14,2},{16,28},{18,... | collective-permute-start | bytes 196616 | tf_op jit(solution)/shard_map/ppermute | solution.py:308
  61.0 7.9 %collective-permute-start.27 = (f32[512,128]{1,0:T(8,128)S(1)}, f32[512,128]{1,0:T(8,128)S(1)}, u32[]{:S(2)}, u32[]{:S(2)}) collective-permute-start(f32[512,128]{1,0:T(8,128)S(1)} %get-tuple-element.85), channel_id=1, source_target_pairs={{0,2},{2,0},{4,6},{6,4},{8,10},{10,8},{12,14},{14,12},{16,18},{18,... | collective-permute-start | bytes 786440 | tf_op jit(solution)/shard_map/ppermute | solution.py:313
  65.3 9.6 %collective-permute-start.13 = (f32[512,128]{1,0:T(8,128)S(1)}, f32[512,128]{1,0:T(8,128)S(1)}, u32[]{:S(2)}, u32[]{:S(2)}) collective-permute-start(f32[512,128]{1,0:T(8,128)S(1)} %get-tuple-element.61), channel_id=1, source_target_pairs={{0,2},{2,0},{4,6},{6,4},{8,10},{10,8},{12,14},{14,12},{16,18},{18,... | collective-permute-start | bytes 786440 | tf_op jit(solution)/shard_map/ppermute | solution.py:313
  76.3 6.7 %collective-permute-start.28 = (f32[64,2048]{1,0:T(8,128)S(1)}, f32[64,2048]{1,0:T(8,128)S(1)}, u32[]{:S(2)}, u32[]{:S(2)}) collective-permute-start(f32[64,2048]{1,0:T(8,128)S(1)} %get-tuple-element.90), channel_id=1, source_target_pairs={{0,1},{1,0},{2,3},{3,2},{4,5},{5,4},{6,7},{7,6},{8,9},{9,8},{10,11... | collective-permute-start | bytes 1572872 | tf_op jit(solution)/shard_map/ppermute | solution.py:329

commit v5 on v4

--- a/solution.py
+++ b/solution.py
@@ -19,6 +19,7 @@
 ROWS = HALF * W
 TILE = 512
 WORK = 10**10
+UP, DOWN, ACROSS = (0, 3, 2, 1), (0, 3, 2, 1), (0, 1, 2, 3)
 VMEM = pl.BlockSpec(memory_space=pltpu.VMEM)
 SMEM = pl.BlockSpec(memory_space=pltpu.SMEM)
 
@@ -58,11 +59,17 @@
     )
 
 
+def position():
+    index = lax.axis_index("ctx")
+    return index & (NZ - 1), (index >> 3) & (NY - 1), index >> 5, lax.axis_index("tp")
+
+
 def rows_of(index):
     return pl.ds(pl.multiple_of(index * W, W), W)
 
 
-def local_state_kernel(group, pos, x, b, log_decay, keep, send, cum_ref):
+def local_state_kernel(group, x, b, log_decay, keep, send, cum_ref):
+    pos = position()
     cum_ref[...] = running_sum(log_decay[...])
     b_t = b[...].astype(F32).T
     role = pos[0] & 1
@@ -81,21 +88,23 @@
         out[ROWS:, :] = decay_tile(lasts)
 
 
-def pair_kernel(pos, keep, got, *outs):
+def pair_kernel(keep, got, *outs):
+    pos = position()
     first = pos[0] & 1 == 0
-    for m in range(PAIRS):
+    for k, m in enumerate(UP):
         j = (pos[0] >> 1) ^ m
         state, log = rows_of(j), pl.ds(ROWS + j, 1)
         earlier = jnp.where(first, keep[state, :], got[state, :])
         later = jnp.where(first, got[state, :], keep[state, :])
         decay = jnp.exp(jnp.where(first, got[log, :], keep[log, :]))
-        outs[m][:W, :] = decay * earlier + later
-        outs[m][W:, :] = decay_tile([keep[log, :] + got[log, :]])
-
-
-def row_total_kernel(pos, *refs):
+        outs[k][:W, :] = decay * earlier + later
+        outs[k][W:, :] = decay_tile([keep[log, :] + got[log, :]])
+
+
+def row_total_kernel(*refs):
+    pos = position()
     parts, out = refs[:PAIRS], refs[PAIRS]
-    places = [(pos[0] >> 1) ^ m for m in range(PAIRS)]
+    places = [(pos[0] >> 1) ^ m for m in UP]
     logs = [part[W : W + 1, :] for part in parts]
     total = jnp.zeros((W, W), F32)
     for k in range(PAIRS):
@@ -108,9 +117,10 @@
     out[W:, :] = decay_tile([sum(logs)])
 
 
-def plane_kernel(pos, *refs):
+def plane_kernel(*refs):
+    pos = position()
     parts, plane, before = refs[:NY], refs[NY], refs[NY + 1]
-    places = [pos[1] ^ k for k in range(NY)]
+    places = [pos[1] ^ m for m in ACROSS]
     logs = [part[W : W + 1, :] for part in parts]
     total = jnp.zeros((W, W), F32)
     earlier = jnp.zeros((W, W), F32)
@@ -135,39 +145,42 @@
     before[W:, :] = decay_tile([to_row])
 
 
-def entering_kernel(pos, *refs):
+def entering_kernel(*refs):
+    pos = position()
     planes, before = refs[: NX - 1], refs[NX - 1]
     parts = refs[NX : NX + PAIRS]
     outs = refs[NX + PAIRS : NX + 2 * PAIRS]
     ordered, entering = refs[NX + 2 * PAIRS :]
-    for m in range(PAIRS):
-        ordered[(pos[0] >> 1) ^ m] = parts[m][...]
+    for k, m in enumerate(UP):
+        ordered[(pos[0] >> 1) ^ m] = parts[k][...]
     carry = jnp.zeros((W, W), F32)
     logs = [plane[W : W + 1, :] for plane in planes]
-    for k in range(1, NX):
+    places = [pos[2] ^ m for m in ACROSS[1:]]
+    for k in range(NX - 1):
         after = jnp.zeros((1, W), F32)
-        for j in range(1, NX):
+        for j in range(NX - 1):
             if j != k:
-                between = jnp.logical_and(pos[2] ^ j > pos[2] ^ k, pos[2] ^ j < pos[2])
-                after += jnp.where(between, logs[j - 1], 0.0)
-        weight = jnp.where(pos[2] ^ k < pos[2], jnp.exp(after), 0.0)
-        carry += weight * planes[k - 1][:W, :]
+                between = jnp.logical_and(places[j] > places[k], places[j] < pos[2])
+                after += jnp.where(between, logs[j], 0.0)
+        weight = jnp.where(places[k] < pos[2], jnp.exp(after), 0.0)
+        carry += weight * planes[k][:W, :]
     carry = jnp.exp(before[W : W + 1, :]) * carry + before[:W, :]
     for place in range(PAIRS):
         entering[place] = carry
         if place < PAIRS - 1:
             carry = jnp.exp(ordered[place, W : W + 1, :]) * carry + ordered[place, :W, :]
-    for m in range(PAIRS):
-        outs[m][...] = entering[(pos[0] >> 1) ^ m]
-
-
-def spread_kernel(pos, keep, got, *refs):
+    for k, m in enumerate(DOWN):
+        outs[k][...] = entering[(pos[0] >> 1) ^ m]
+
+
+def spread_kernel(keep, got, *refs):
+    pos = position()
     carries, mine, send = refs[:PAIRS], refs[PAIRS], refs[PAIRS + 1]
     first = pos[0] & 1 == 0
-    for m in range(PAIRS):
+    for k, m in enumerate(DOWN):
         j = (pos[0] >> 1) ^ m
         state, log = rows_of(j), pl.ds(ROWS + j, 1)
-        carry = carries[m][...]
+        carry = carries[k][...]
         decay = jnp.exp(jnp.where(first, keep[log, :], got[log, :]))
         after = decay * carry + jnp.where(first, keep[state, :], got[state, :])
         mine[state, :] = jnp.where(first, carry, after)
@@ -195,7 +208,8 @@
         slope[:, at] = jnp.exp(column) * gate
 
 
-def finish_kernel(group, sides, stage, pos, *refs):
+def finish_kernel(group, sides, stage, *refs):
+    pos = position()
     count = len(sides)
     states, refs = refs[:count], refs[count:]
     read, fixed, slope, gain, w = refs[:5]
@@ -262,18 +276,22 @@
     return jax.ShapeDtypeStruct(shape, dtype)
 
 
+def exchange(values, stride, order):
+    return [values[0]] + [
+        lax.ppermute(value, "ctx", partners(stride, m)) for value, m in zip(values[1:], order[1:])
+    ]
+
+
 def per_device(x_in, z_in, b_in, c_in, log_decay, d_skip, norm_gain, w_out):
-    index = lax.axis_index("ctx")
-    pos = jnp.stack([index % NZ, index // NZ % NY, index // (NZ * NY), lax.axis_index("tp")]).astype(jnp.int32)
     x = x_in.reshape(W, HEADS * W)
     width = w_out.shape[1]
     full, single = shaped(ROWS + 8, W), shaped(W + 8, W)
     keep, got, parts, totals, planes, mine, states = {}, {}, {}, {}, {}, {}, {}
     for g in range(GROUPS):
         keep[g], send = call(
-            functools.partial(local_state_kernel, g), [full] * 2, [SMEM, VMEM, VMEM, VMEM],
+            functools.partial(local_state_kernel, g), [full] * 2, [VMEM] * 3,
             [pltpu.VMEM((HEADS, W), F32)], name=f"local_state_{g}",
-        )(pos, x, b_in, log_decay)
+        )(x, b_in, log_decay)
         got[g] = lax.ppermute(send, "ctx", partners(1, 1))
     keep[1], z = lax.optimization_barrier((keep[1], z_in))
     fixed, slope, read, gain = call(
@@ -285,31 +303,31 @@
         (keep[0], fixed, slope, read, gain)
     )
     for g in range(GROUPS):
-        pair = call(pair_kernel, [single] * PAIRS, [SMEM, VMEM, VMEM], name=f"pair_{g}")(
-            pos, keep[g], got[g]
+        pair = call(pair_kernel, [single] * PAIRS, [VMEM] * 2, name=f"pair_{g}")(
+            keep[g], got[g]
         )
-        parts[g] = [pair[0]] + [lax.ppermute(pair[m], "ctx", partners(2, m)) for m in range(1, PAIRS)]
+        parts[g] = exchange(pair, 2, UP)
     for g in range(GROUPS):
         total = call(
-            row_total_kernel, single, [SMEM] + [VMEM] * PAIRS, name=f"row_total_{g}"
-        )(pos, *parts[g])
-        totals[g] = [total] + [lax.ppermute(total, "ctx", partners(NZ, k)) for k in range(1, NY)]
+            row_total_kernel, single, [VMEM] * PAIRS, name=f"row_total_{g}"
+        )(*parts[g])
+        totals[g] = exchange([total] * NY, NZ, ACROSS)
     for g in range(GROUPS):
         plane, before = call(
-            plane_kernel, [single] * 2, [SMEM] + [VMEM] * NY, name=f"plane_{g}"
-        )(pos, *totals[g])
-        planes[g] = [lax.ppermute(plane, "ctx", partners(NY * NZ, k)) for k in range(1, NX)] + [before]
+            plane_kernel, [single] * 2, [VMEM] * NY, name=f"plane_{g}"
+        )(*totals[g])
+        planes[g] = exchange([plane] * NX, NY * NZ, ACROSS)[1:] + [before]
     for g in range(GROUPS):
         back = call(
-            entering_kernel, [shaped(W, W)] * PAIRS, [SMEM] + [VMEM] * (NX + PAIRS),
+            entering_kernel, [shaped(W, W)] * PAIRS, [VMEM] * (NX + PAIRS),
             [pltpu.VMEM((PAIRS, W + 8, W), F32), pltpu.VMEM((PAIRS, W, W), F32)],
             name=f"entering_{g}", work=WORK,
-        )(pos, *planes[g], *parts[g])
-        states[g] = [back[0]] + [lax.ppermute(back[m], "ctx", partners(2, m)) for m in range(1, PAIRS)]
+        )(*planes[g], *parts[g])
+        states[g] = exchange(back, 2, DOWN)
     for g in range(GROUPS):
         mine[g], send = call(
-            spread_kernel, [shaped(ROWS, W)] * 2, [SMEM] + [VMEM] * (2 + PAIRS), name=f"spread_{g}"
-        )(pos, keep[g], got[g], *states[g])
+            spread_kernel, [shaped(ROWS, W)] * 2, [VMEM] * (2 + PAIRS), name=f"spread_{g}"
+        )(keep[g], got[g], *states[g])
         states[g] = lax.ppermute(send, "ctx", partners(1, 1))
 
     def finish(group, sides, stage, parts, w, outs, extra):
@@ -317,8 +335,8 @@
         scratch += [[pltpu.SemaphoreType.DMA(())], [], [pltpu.VMEM((W, TILE), F32)]][stage]
         return call(
             functools.partial(finish_kernel, group, sides, stage), outs,
-            [SMEM] + [VMEM] * (len(sides) + 5 + len(extra)), scratch, name=f"finish_{stage}",
-        )(pos, *parts, read, fixed, slope, gain, w, *extra)
+            [VMEM] * (len(sides) + 5 + len(extra)), scratch, name=f"finish_{stage}",
+        )(*parts, read, fixed, slope, gain, w, *extra)
 
     so_far, w = finish(
         0, (0, 1), 0, [mine[0], states[0]], w_out,

time: 84.1 us -> 80.8 us (0.961)
  Pallas kernels: 14.9 us -> 6.81 us
  waiting for transfers between devices: 10.7 us -> 16.3 us
  starting transfers between devices: 51.2 us -> 48.1 us
  local copies, waits for them, and re-layouts: 5.93 us -> 8.07 us
    pallas_call x15, Pallas kernels: 13.2 us -> 5.17 us  [the longest x3 2.91 us: finish(): call(functools.partial(finish_kernel, group, sides, stage), outs, [VMEM]...]
    ppermute x24, waiting for transfers between devices: 5.9 us -> 9.28 us  [exchange(): lax.ppermute(value, 'ctx', partners(stride, m))]
    ppermute x2, waiting for transfers between devices: 3.27 us -> 5.49 us  [per_device(): states[g] = lax.ppermute(send, 'ctx', partners(1, 1))]
    unnamed x16 -> x22, local copies, waits for them, and re-layouts: 5.93 us -> 8.07 us
    ppermute x2, starting transfers between devices: 4.31 us -> 2.17 us  [per_device(): states[g] = lax.ppermute(send, 'ctx', partners(1, 1))]
    ppermute x1, starting transfers between devices: 5.15 us -> 3.97 us  [per_device(): return (near + lax.ppermute(far, 'tp', [(0, 1), (1, 0)])).astype(BF16)]
  transfers between devices with their start and end apart: 29 -> 29, of which waited for: 8 -> 9; matrix products, arithmetic and copies ran while one was open for 1% -> 1% of each run, Pallas kernels for 15% -> 7%
where the time goes in v5:
time: 80.8 us; the launch traced here: 80.3 us
  starting transfers between devices  48.1 us (60%)
  waiting for transfers between devices  16.3 us (20%)
  local copies, waits for them, and re-layouts  8.07 us (10%)
  Pallas kernels  6.81 us (8%)
    ppermute x24, starting transfers between devices, exchange(): lax.ppermute(value, 'ctx', partners(stride, m))  39.3 us
    ppermute x24, waiting for transfers between devices, exchange(): lax.ppermute(value, 'ctx', partners(stride, m))  9.28 us
    unnamed x22, local copies, waits for them, and re-layouts  8.07 us
    ppermute x2, waiting for transfers between devices, per_device(): states[g] = lax.ppermute(send, 'ctx', partners(1, 1))  5.49 us
    ppermute x1, starting transfers between devices, per_device(): return (near + lax.ppermute(far, 'tp', [(0, 1), (1, 0)])).astype(BF16)  3.97 us
    pallas_call x3, Pallas kernels, finish(): call(functools.partial(finish_kernel, group, sides, stage), outs, [VMEM]...  2.91 us
    ppermute x2, starting transfers between devices, per_device(): got[g] = lax.ppermute(send, 'ctx', partners(1, 1))  2.66 us
    ppermute x2, starting transfers between devices, per_device(): states[g] = lax.ppermute(send, 'ctx', partners(1, 1))  2.17 us
  transfers between devices with their start and end apart: 29, of which 9 were waited for; matrix products, arithmetic and copies ran while one was open for 1% of the time, Pallas kernels for 7%

profile of v5, /device:TPU:1, one launch (start us, length us, event | category | flops | bytes accessed | tf_op | source)
XLA Modules:
  0.0 80.3 jit_solution(16192632144699671488)
XLA Ops:
  0.0 1.2 %copy.14 = bf16[16,8,16,128]{3,1,2,0:T(8,128)(2,1)S(1)} copy(bf16[16,8,16,128]{3,2,1,0:T(8,128)(2,1)} %bitcast.14) | data formatting | bytes 1048576
  1.2 0.7 copy-done
  1.9 0.7 copy-done.2
  2.6 0.8 local_state_0.1
  3.4 2.6 %collective-permute-start.14 = (f32[520,128]{1,0:T(8,128)S(1)}, f32[520,128]{1,0:T(8,128)S(1)}, u32[]{:S(2)}, u32[]{:S(2)}) collective-permute-start(f32[520,128]{1,0:T(8,128)S(1)} %get-tuple-element.73), channel_id=1, source_target_pairs={{0,2},{2,0},{4,6},{6,4},{8,10},{10,8},{12,14},{14,12},{16,18},{18,... | collective-permute-start | bytes 798728 | tf_op jit(solution)/shard_map/ppermute | solution.py:295
  6.0 0.7 copy-done.3
  6.7 0.8 local_state_1.1
  7.5 0.1 collective-permute-start
  7.6 1.2 %copy.13 = bf16[16,8,16,128]{3,1,2,0:T(8,128)(2,1)S(1)} copy(bf16[16,8,16,128]{3,2,1,0:T(8,128)(2,1)} %bitcast.15) | data formatting | bytes 1048576
  8.8 0.7 copy-done.1
  9.5 0.7 copy-done.4
  10.2 0.8 copy-done.5
  11.0 0.7 copy-done.6
  11.7 0.7 copy-done.7
  12.3 1.6 %inside.1 = (f32[128,2048]{1,0:T(8,128)S(1)}, f32[128,2048]{1,0:T(8,128)S(1)}, bf16[128,128]{1,0:T(8,128)(2,1)S(1)}, f32[16,128]{1,0:T(8,128)S(1)}) custom-call(f32[16]{0:T(128)S(1)} %copy-done.7, bf16[128,2048]{1,0:T(8,128)(2,1)S(1)} %bitcast.12, bf16[128,2048]{1,0:T(8,128)(2,1)S(1)} %bitcast.13, bf16[128,128]{1,0:T(8,128)(2,1)S(1)} %copy-done.1, ...), custom_call_target="tpu_custom_call" | custom-call | tf_op jit(solution)/shard_map/inside/pallas_call | solution.py:297
  14.0 0.1 pair_0.1
  14.0 5.9 %collective-permute-start.15 = (f32[136,128]{1,0:T(8,128)S(1)}, f32[136,128]{1,0:T(8,128)S(1)}, u32[]{:S(2)}, u32[]{:S(2)}) collective-permute-start(f32[136,128]{1,0:T(8,128)S(1)} %get-tuple-element.75), channel_id=1, source_target_pairs={{0,12},{2,14},{4,8},{6,10},{8,4},{10,6},{12,0},{14,2},{16,28},{18,... | collective-permute-start | bytes 208904 | tf_op jit(solution)/shard_map/ppermute | solution.py:281
  20.0 1.0 %collective-permute-start.16 = (f32[136,128]{1,0:T(8,128)S(1)}, f32[136,128]{1,0:T(8,128)S(1)}, u32[]{:S(2)}, u32[]{:S(2)}) collective-permute-start(f32[136,128]{1,0:T(8,128)S(1)} %get-tuple-element.76), channel_id=1, source_target_pairs={{0,8},{2,10},{4,12},{6,14},{8,0},{10,2},{12,4},{14,6},{16,24},{18,... | collective-permute-start | bytes 208904 | tf_op jit(solution)/shard_map/ppermute | solution.py:281
  21.0 1.2 %collective-permute-start.17 = (f32[136,128]{1,0:T(8,128)S(1)}, f32[136,128]{1,0:T(8,128)S(1)}, u32[]{:S(2)}, u32[]{:S(2)}) collective-permute-start(f32[136,128]{1,0:T(8,128)S(1)} %get-tuple-element.77), channel_id=1, source_target_pairs={{0,4},{2,6},{4,0},{6,2},{8,12},{10,14},{12,8},{14,10},{16,20},{18,... | collective-permute-start | bytes 208904 | tf_op jit(solution)/shard_map/ppermute | solution.py:281
  22.1 0.1 pair_1.1
  22.2 3.6 %collective-permute-start.1 = (f32[136,128]{1,0:T(8,128)S(1)}, f32[136,128]{1,0:T(8,128)S(1)}, u32[]{:S(2)}, u32[]{:S(2)}) collective-permute-start(f32[136,128]{1,0:T(8,128)S(1)} %get-tuple-element.52), channel_id=1, source_target_pairs={{0,12},{2,14},{4,8},{6,10},{8,4},{10,6},{12,0},{14,2},{16,28},{18,... | collective-permute-start | bytes 208904 | tf_op jit(solution)/shard_map/ppermute | solution.py:281
  25.8 1.0 %collective-permute-start.2 = (f32[136,128]{1,0:T(8,128)S(1)}, f32[136,128]{1,0:T(8,128)S(1)}, u32[]{:S(2)}, u32[]{:S(2)}) collective-permute-start(f32[136,128]{1,0:T(8,128)S(1)} %get-tuple-element.53), channel_id=1, source_target_pairs={{0,8},{2,10},{4,12},{6,14},{8,0},{10,2},{12,4},{14,6},{16,24},{18,... | collective-permute-start | bytes 208904 | tf_op jit(solution)/shard_map/ppermute | solution.py:281
  26.8 1.2 %collective-permute-start.3 = (f32[136,128]{1,0:T(8,128)S(1)}, f32[136,128]{1,0:T(8,128)S(1)}, u32[]{:S(2)}, u32[]{:S(2)}) collective-permute-start(f32[136,128]{1,0:T(8,128)S(1)} %get-tuple-element.54), channel_id=1, source_target_pairs={{0,4},{2,6},{4,0},{6,2},{8,12},{10,14},{12,8},{14,10},{16,20},{18,... | collective-permute-start | bytes 208904 | tf_op jit(solution)/shard_map/ppermute | solution.py:281
  28.0 1.3 %collective-permute-done.17.refs_3_.refs_7_ = f32[136,128]{1,0:T(8,128)S(1)} collective-permute-done((f32[136,128]{1,0:T(8,128)S(1)}, f32[136,128]{1,0:T(8,128)S(1)}, u32[]{:S(2)}, u32[]{:S(2)}) %collective-permute-start.17) | collective-permute-done | bytes 69664 | tf_op jit(solution)/shard_map/ppermute | solution.py:281
  29.3 2.8 %collective-permute-start.20 = (f32[136,128]{1,0:T(8,128)S(1)}, f32[136,128]{1,0:T(8,128)S(1)}, u32[]{:S(2)}, u32[]{:S(2)}) collective-permute-start(f32[136,128]{1,0:T(8,128)S(1)} %row_total_0.1.refs_0_), channel_id=1, source_target_pairs={{0,48},{2,50},{4,52},{6,54},{8,56},{10,58},{12,60},{14,62},{16,32}... | collective-permute-start | bytes 208904 | tf_op jit(solution)/shard_map/ppermute | solution.py:281
  32.2 0.3 collective-permute-start.19
  32.5 0.3 collective-permute-start.18
  32.8 0.4 collective-permute-done.2.refs_2_.refs_6_
  33.3 2.8 %collective-permute-start.6 = (f32[136,128]{1,0:T(8,128)S(1)}, f32[136,128]{1,0:T(8,128)S(1)}, u32[]{:S(2)}, u32[]{:S(2)}) collective-permute-start(f32[136,128]{1,0:T(8,128)S(1)} %row_total_1.1.refs_0_), channel_id=1, source_target_pairs={{0,48},{2,50},{4,52},{6,54},{8,56},{10,58},{12,60},{14,62},{16,32}... | collective-permute-start | bytes 208904 | tf_op jit(solution)/shard_map/ppermute | solution.py:281
  36.1 0.3 collective-permute-start.5
  36.4 0.3 collective-permute-start.4
  36.8 0.3 collective-permute-done.19.refs_2_
  37.1 0.1 plane_0.1
  37.1 2.6 %collective-permute-start.23 = (f32[136,128]{1,0:T(8,128)S(1)}, f32[136,128]{1,0:T(8,128)S(1)}, u32[]{:S(2)}, u32[]{:S(2)}) collective-permute-start(f32[136,128]{1,0:T(8,128)S(1)} %get-tuple-element.78), channel_id=1, source_target_pairs={{0,192},{2,194},{4,196},{6,198},{8,200},{10,202},{12,204},{14,206}... | collective-permute-start | bytes 208904 | tf_op jit(solution)/shard_map/ppermute | solution.py:281
  39.7 0.5 collective-permute-start.22
  40.2 0.3 collective-permute-start.21
  40.5 0.3 collective-permute-done.5.refs_2_
  40.7 0.1 plane_1.1
  40.8 2.7 %collective-permute-start.9 = (f32[136,128]{1,0:T(8,128)S(1)}, f32[136,128]{1,0:T(8,128)S(1)}, u32[]{:S(2)}, u32[]{:S(2)}) collective-permute-start(f32[136,128]{1,0:T(8,128)S(1)} %get-tuple-element.55), channel_id=1, source_target_pairs={{0,192},{2,194},{4,196},{6,198},{8,200},{10,202},{12,204},{14,206}... | collective-permute-start | bytes 208904 | tf_op jit(solution)/shard_map/ppermute | solution.py:281
  43.6 0.5 collective-permute-start.8
  44.1 0.3 collective-permute-start.7
  44.3 0.0 collective-permute-done.22.refs_1_
  44.4 0.1 entering_0.1
  44.5 2.9 %collective-permute-start.24 = (f32[128,128]{1,0:T(8,128)S(1)}, f32[128,128]{1,0:T(8,128)S(1)}, u32[]{:S(2)}, u32[]{:S(2)}) collective-permute-start(f32[128,128]{1,0:T(8,128)S(1)} %get-tuple-element.81), channel_id=1, source_target_pairs={{0,12},{2,14},{4,8},{6,10},{8,4},{10,6},{12,0},{14,2},{16,28},{18,... | collective-permute-start | bytes 196616 | tf_op jit(solution)/shard_map/ppermute | solution.py:281
  47.4 2.9 %collective-permute-start.25 = (f32[128,128]{1,0:T(8,128)S(1)}, f32[128,128]{1,0:T(8,128)S(1)}, u32[]{:S(2)}, u32[]{:S(2)}) collective-permute-start(f32[128,128]{1,0:T(8,128)S(1)} %get-tuple-element.82), channel_id=1, source_target_pairs={{0,8},{2,10},{4,12},{6,14},{8,0},{10,2},{12,4},{14,6},{16,24},{18,... | collective-permute-start | bytes 196616 | tf_op jit(solution)/shard_map/ppermute | solution.py:281
  50.4 0.0 slice-start.1
  50.4 0.1 entering_1.1
  50.5 2.8 %collective-permute-start.10 = (f32[128,128]{1,0:T(8,128)S(1)}, f32[128,128]{1,0:T(8,128)S(1)}, u32[]{:S(2)}, u32[]{:S(2)}) collective-permute-start(f32[128,128]{1,0:T(8,128)S(1)} %get-tuple-element.58), channel_id=1, source_target_pairs={{0,12},{2,14},{4,8},{6,10},{8,4},{10,6},{12,0},{14,2},{16,28},{18,... | collective-permute-start | bytes 196616 | tf_op jit(solution)/shard_map/ppermute | solution.py:281
  53.3 2.9 %collective-permute-start.11 = (f32[128,128]{1,0:T(8,128)S(1)}, f32[128,128]{1,0:T(8,128)S(1)}, u32[]{:S(2)}, u32[]{:S(2)}) collective-permute-start(f32[128,128]{1,0:T(8,128)S(1)} %get-tuple-element.59), channel_id=1, source_target_pairs={{0,8},{2,10},{4,12},{6,14},{8,0},{10,2},{12,4},{14,6},{16,24},{18,... | collective-permute-start | bytes 196616 | tf_op jit(solution)/shard_map/ppermute | solution.py:281
  56.2 0.0 collective-permute-start.12
  56.2 0.1 spread_0.1
  56.3 2.1 %collective-permute-start.27 = (f32[512,128]{1,0:T(8,128)S(1)}, f32[512,128]{1,0:T(8,128)S(1)}, u32[]{:S(2)}, u32[]{:S(2)}) collective-permute-start(f32[512,128]{1,0:T(8,128)S(1)} %get-tuple-element.85), channel_id=1, source_target_pairs={{0,2},{2,0},{4,6},{6,4},{8,10},{10,8},{12,14},{14,12},{16,18},{18,... | collective-permute-start | bytes 786440 | tf_op jit(solution)/shard_map/ppermute | solution.py:331
  58.4 2.0 %collective-permute-done.11.refs_2_ = f32[128,128]{1,0:T(8,128)S(1)} collective-permute-done((f32[128,128]{1,0:T(8,128)S(1)}, f32[128,128]{1,0:T(8,128)S(1)}, u32[]{:S(2)}, u32[]{:S(2)}) %collective-permute-start.11) | collective-permute-done | bytes 65568 | tf_op jit(solution)/shard_map/ppermute | solution.py:281
  60.4 5.0 %collective-permute-done.12.refs_3_ = f32[128,128]{1,0:T(8,128)S(1)} collective-permute-done((f32[128,128]{1,0:T(8,128)S(1)}, f32[128,128]{1,0:T(8,128)S(1)}, u32[]{:S(2)}, u32[]{:S(2)}) %collective-permute-start.12) | collective-permute-done | bytes 65568 | tf_op jit(solution)/shard_map/ppermute | solution.py:281
  65.4 0.1 spread_1.1
  65.5 0.1 collective-permute-start.13
  65.6 1.7 %collective-permute-done.27.refs_1_ = f32[512,128]{1,0:T(8,128)S(1)} collective-permute-done((f32[512,128]{1,0:T(8,128)S(1)}, f32[512,128]{1,0:T(8,128)S(1)}, u32[]{:S(2)}, u32[]{:S(2)}) %collective-permute-start.27) | collective-permute-done | bytes 262176 | tf_op jit(solution)/shard_map/ppermute | solution.py:331
  67.3 1.4 %finish_0.1 = (f32[128,2048]{1,0:T(8,128)S(1)}, bf16[1024,2048]{1,0:T(8,128)(2,1)S(1)}) custom-call(f32[512,128]{1,0:T(8,128)S(1)} %get-tuple-element.84.refs_0_, f32[512,128]{1,0:T(8,128)S(1)} %collective-permute-done.27.refs_1_, bf16[128,128]{1,0:T(8,128)(2,1)S(1)} %get-tuple-element.68.refs_2_.refs_1_, f32[128,2048]{1,0:T(8,128)S(1)} %get-tuple-element.69.refs_3_.refs_2_, ...), custom_call_target="tpu_custom_call" | custom-call | tf_op jit(solution)/shard_map/finish_0/pallas_call | solution.py:336
  68.7 0.7 finish_1.1.refs_6_
  69.4 3.8 %collective-permute-done.13.refs_0_ = f32[512,128]{1,0:T(8,128)S(1)} collective-permute-done((f32[512,128]{1,0:T(8,128)S(1)}, f32[512,128]{1,0:T(8,128)S(1)}, u32[]{:S(2)}, u32[]{:S(2)}) %collective-permute-start.13) | collective-permute-done | bytes 262176 | tf_op jit(solution)/shard_map/ppermute | solution.py:331
  73.2 0.8 finish_2.1
  74.0 4.0 %collective-permute-start.28 = (f32[64,2048]{1,0:T(8,128)S(1)}, f32[64,2048]{1,0:T(8,128)S(1)}, u32[]{:S(2)}, u32[]{:S(2)}) collective-permute-start(f32[64,2048]{1,0:T(8,128)S(1)} %get-tuple-element.90), channel_id=1, source_target_pairs={{0,1},{1,0},{2,3},{3,2},{4,5},{5,4},{6,7},{7,6},{8,9},{9,8},{10,11... | collective-permute-start | bytes 1572872 | tf_op jit(solution)/shard_map/ppermute | solution.py:347
  78.0 1.5 %collective-permute-done.28 = f32[64,2048]{1,0:T(8,128)S(1)} collective-permute-done((f32[64,2048]{1,0:T(8,128)S(1)}, f32[64,2048]{1,0:T(8,128)S(1)}, u32[]{:S(2)}, u32[]{:S(2)}) %collective-permute-start.28) | collective-permute-done | bytes 524320 | tf_op jit(solution)/shard_map/ppermute | solution.py:347
  79.5 0.8 add_convert_fusion
  (34 shorter events, 0.2 us)
Async XLA Ops:
  1.2 0.8 copy-start
  1.9 0.7 copy-start.2
  3.4 10.5 %collective-permute-start.14 = (f32[520,128]{1,0:T(8,128)S(1)}, f32[520,128]{1,0:T(8,128)S(1)}, u32[]{:S(2)}, u32[]{:S(2)}) collective-permute-start(f32[520,128]{1,0:T(8,128)S(1)} %get-tuple-element.73), channel_id=1, source_target_pairs={{0,2},{2,0},{4,6},{6,4},{8,10},{10,8},{12,14},{14,12},{16,18},{18,... | collective-permute-start | bytes 798728 | tf_op jit(solution)/shard_map/ppermute | solution.py:295
  6.0 0.7 copy-start.3
  7.5 14.7 %collective-permute-start = (f32[520,128]{1,0:T(8,128)S(1)}, f32[520,128]{1,0:T(8,128)S(1)}, u32[]{:S(2)}, u32[]{:S(2)}) collective-permute-start(f32[520,128]{1,0:T(8,128)S(1)} %get-tuple-element.50), channel_id=1, source_target_pairs={{0,2},{2,0},{4,6},{6,4},{8,10},{10,8},{12,14},{14,12},{16,18},{18,... | collective-permute-start | bytes 798728 | tf_op jit(solution)/shard_map/ppermute | solution.py:295
  8.7 0.8 copy-start.1
  9.5 0.7 copy-start.4
  10.2 0.8 copy-start.5
  11.0 0.7 copy-start.6
  11.7 0.7 copy-start.7
  14.0 12.7 %collective-permute-start.15 = (f32[136,128]{1,0:T(8,128)S(1)}, f32[136,128]{1,0:T(8,128)S(1)}, u32[]{:S(2)}, u32[]{:S(2)}) collective-permute-start(f32[136,128]{1,0:T(8,128)S(1)} %get-tuple-element.75), channel_id=1, source_target_pairs={{0,12},{2,14},{4,8},{6,10},{8,4},{10,6},{12,0},{14,2},{16,28},{18,... | collective-permute-start | bytes 208904 | tf_op jit(solution)/shard_map/ppermute | solution.py:281
  20.0 8.0 %collective-permute-start.16 = (f32[136,128]{1,0:T(8,128)S(1)}, f32[136,128]{1,0:T(8,128)S(1)}, u32[]{:S(2)}, u32[]{:S(2)}) collective-permute-start(f32[136,128]{1,0:T(8,128)S(1)} %get-tuple-element.76), channel_id=1, source_target_pairs={{0,8},{2,10},{4,12},{6,14},{8,0},{10,2},{12,4},{14,6},{16,24},{18,... | collective-permute-start | bytes 208904 | tf_op jit(solution)/shard_map/ppermute | solution.py:281
  21.0 8.3 %collective-permute-start.17 = (f32[136,128]{1,0:T(8,128)S(1)}, f32[136,128]{1,0:T(8,128)S(1)}, u32[]{:S(2)}, u32[]{:S(2)}) collective-permute-start(f32[136,128]{1,0:T(8,128)S(1)} %get-tuple-element.77), channel_id=1, source_target_pairs={{0,4},{2,6},{4,0},{6,2},{8,12},{10,14},{12,8},{14,10},{16,20},{18,... | collective-permute-start | bytes 208904 | tf_op jit(solution)/shard_map/ppermute | solution.py:281
  22.2 10.3 %collective-permute-start.1 = (f32[136,128]{1,0:T(8,128)S(1)}, f32[136,128]{1,0:T(8,128)S(1)}, u32[]{:S(2)}, u32[]{:S(2)}) collective-permute-start(f32[136,128]{1,0:T(8,128)S(1)} %get-tuple-element.52), channel_id=1, source_target_pairs={{0,12},{2,14},{4,8},{6,10},{8,4},{10,6},{12,0},{14,2},{16,28},{18,... | collective-permute-start | bytes 208904 | tf_op jit(solution)/shard_map/ppermute | solution.py:281
  25.8 7.4 %collective-permute-start.2 = (f32[136,128]{1,0:T(8,128)S(1)}, f32[136,128]{1,0:T(8,128)S(1)}, u32[]{:S(2)}, u32[]{:S(2)}) collective-permute-start(f32[136,128]{1,0:T(8,128)S(1)} %get-tuple-element.53), channel_id=1, source_target_pairs={{0,8},{2,10},{4,12},{6,14},{8,0},{10,2},{12,4},{14,6},{16,24},{18,... | collective-permute-start | bytes 208904 | tf_op jit(solution)/shard_map/ppermute | solution.py:281
  26.8 6.4 %collective-permute-start.3 = (f32[136,128]{1,0:T(8,128)S(1)}, f32[136,128]{1,0:T(8,128)S(1)}, u32[]{:S(2)}, u32[]{:S(2)}) collective-permute-start(f32[136,128]{1,0:T(8,128)S(1)} %get-tuple-element.54), channel_id=1, source_target_pairs={{0,4},{2,6},{4,0},{6,2},{8,12},{10,14},{12,8},{14,10},{16,20},{18,... | collective-permute-start | bytes 208904 | tf_op jit(solution)/shard_map/ppermute | solution.py:281
  29.3 7.1 %collective-permute-start.20 = (f32[136,128]{1,0:T(8,128)S(1)}, f32[136,128]{1,0:T(8,128)S(1)}, u32[]{:S(2)}, u32[]{:S(2)}) collective-permute-start(f32[136,128]{1,0:T(8,128)S(1)} %row_total_0.1.refs_0_), channel_id=1, source_target_pairs={{0,48},{2,50},{4,52},{6,54},{8,56},{10,58},{12,60},{14,62},{16,32}... | collective-permute-start | bytes 208904 | tf_op jit(solution)/shard_map/ppermute | solution.py:281
  32.2 4.9 %collective-permute-start.19 = (f32[136,128]{1,0:T(8,128)S(1)}, f32[136,128]{1,0:T(8,128)S(1)}, u32[]{:S(2)}, u32[]{:S(2)}) collective-permute-start(f32[136,128]{1,0:T(8,128)S(1)} %row_total_0.1.refs_0_), channel_id=1, source_target_pairs={{0,32},{2,34},{4,36},{6,38},{8,40},{10,42},{12,44},{14,46},{16,48}... | collective-permute-start | bytes 208904 | tf_op jit(solution)/shard_map/ppermute | solution.py:281
  32.5 4.5 %collective-permute-start.18 = (f32[136,128]{1,0:T(8,128)S(1)}, f32[136,128]{1,0:T(8,128)S(1)}, u32[]{:S(2)}, u32[]{:S(2)}) collective-permute-start(f32[136,128]{1,0:T(8,128)S(1)} %row_total_0.1.refs_0_), channel_id=1, source_target_pairs={{0,16},{2,18},{4,20},{6,22},{8,24},{10,26},{12,28},{14,30},{16,0},... | collective-permute-start | bytes 208904 | tf_op jit(solution)/shard_map/ppermute | solution.py:281
  33.3 7.0 %collective-permute-start.6 = (f32[136,128]{1,0:T(8,128)S(1)}, f32[136,128]{1,0:T(8,128)S(1)}, u32[]{:S(2)}, u32[]{:S(2)}) collective-permute-start(f32[136,128]{1,0:T(8,128)S(1)} %row_total_1.1.refs_0_), channel_id=1, source_target_pairs={{0,48},{2,50},{4,52},{6,54},{8,56},{10,58},{12,60},{14,62},{16,32}... | collective-permute-start | bytes 208904 | tf_op jit(solution)/shard_map/ppermute | solution.py:281
  36.1 4.7 %collective-permute-start.5 = (f32[136,128]{1,0:T(8,128)S(1)}, f32[136,128]{1,0:T(8,128)S(1)}, u32[]{:S(2)}, u32[]{:S(2)}) collective-permute-start(f32[136,128]{1,0:T(8,128)S(1)} %row_total_1.1.refs_0_), channel_id=1, source_target_pairs={{0,32},{2,34},{4,36},{6,38},{8,40},{10,42},{12,44},{14,46},{16,48}... | collective-permute-start | bytes 208904 | tf_op jit(solution)/shard_map/ppermute | solution.py:281
  36.4 4.3 %collective-permute-start.4 = (f32[136,128]{1,0:T(8,128)S(1)}, f32[136,128]{1,0:T(8,128)S(1)}, u32[]{:S(2)}, u32[]{:S(2)}) collective-permute-start(f32[136,128]{1,0:T(8,128)S(1)} %row_total_1.1.refs_0_), channel_id=1, source_target_pairs={{0,16},{2,18},{4,20},{6,22},{8,24},{10,26},{12,28},{14,30},{16,0},... | collective-permute-start | bytes 208904 | tf_op jit(solution)/shard_map/ppermute | solution.py:281
  37.1 7.0 %collective-permute-start.23 = (f32[136,128]{1,0:T(8,128)S(1)}, f32[136,128]{1,0:T(8,128)S(1)}, u32[]{:S(2)}, u32[]{:S(2)}) collective-permute-start(f32[136,128]{1,0:T(8,128)S(1)} %get-tuple-element.78), channel_id=1, source_target_pairs={{0,192},{2,194},{4,196},{6,198},{8,200},{10,202},{12,204},{14,206}... | collective-permute-start | bytes 208904 | tf_op jit(solution)/shard_map/ppermute | solution.py:281
  39.7 4.7 %collective-permute-start.22 = (f32[136,128]{1,0:T(8,128)S(1)}, f32[136,128]{1,0:T(8,128)S(1)}, u32[]{:S(2)}, u32[]{:S(2)}) collective-permute-start(f32[136,128]{1,0:T(8,128)S(1)} %get-tuple-element.78), channel_id=1, source_target_pairs={{0,128},{2,130},{4,132},{6,134},{8,136},{10,138},{12,140},{14,142}... | collective-permute-start | bytes 208904 | tf_op jit(solution)/shard_map/ppermute | solution.py:281
  40.2 4.2 %collective-permute-start.21 = (f32[136,128]{1,0:T(8,128)S(1)}, f32[136,128]{1,0:T(8,128)S(1)}, u32[]{:S(2)}, u32[]{:S(2)}) collective-permute-start(f32[136,128]{1,0:T(8,128)S(1)} %get-tuple-element.78), channel_id=1, source_target_pairs={{0,64},{2,66},{4,68},{6,70},{8,72},{10,74},{12,76},{14,78},{16,80}... | collective-permute-start | bytes 208904 | tf_op jit(solution)/shard_map/ppermute | solution.py:281
  40.8 9.5 %collective-permute-start.9 = (f32[136,128]{1,0:T(8,128)S(1)}, f32[136,128]{1,0:T(8,128)S(1)}, u32[]{:S(2)}, u32[]{:S(2)}) collective-permute-start(f32[136,128]{1,0:T(8,128)S(1)} %get-tuple-element.55), channel_id=1, source_target_pairs={{0,192},{2,194},{4,196},{6,198},{8,200},{10,202},{12,204},{14,206}... | collective-permute-start | bytes 208904 | tf_op jit(solution)/shard_map/ppermute | solution.py:281
  43.6 6.8 %collective-permute-start.8 = (f32[136,128]{1,0:T(8,128)S(1)}, f32[136,128]{1,0:T(8,128)S(1)}, u32[]{:S(2)}, u32[]{:S(2)}) collective-permute-start(f32[136,128]{1,0:T(8,128)S(1)} %get-tuple-element.55), channel_id=1, source_target_pairs={{0,128},{2,130},{4,132},{6,134},{8,136},{10,138},{12,140},{14,142}... | collective-permute-start | bytes 208904 | tf_op jit(solution)/shard_map/ppermute | solution.py:281
  44.1 6.3 %collective-permute-start.7 = (f32[136,128]{1,0:T(8,128)S(1)}, f32[136,128]{1,0:T(8,128)S(1)}, u32[]{:S(2)}, u32[]{:S(2)}) collective-permute-start(f32[136,128]{1,0:T(8,128)S(1)} %get-tuple-element.55), channel_id=1, source_target_pairs={{0,64},{2,66},{4,68},{6,70},{8,72},{10,74},{12,76},{14,78},{16,80}... | collective-permute-start | bytes 208904 | tf_op jit(solution)/shard_map/ppermute | solution.py:281
  44.4 22.9 %slice-start = ((s8[8388608]{0:T(1024)(128)(4,1)}), s8[4194304]{0:T(1024)(128)(4,1)S(1)}, s32[]{:S(2)}) async-start(s8[8388608]{0:T(1024)(128)(4,1)} %bitcast.8), calls=%async_computation | async-start | bytes 8388608
  44.5 11.7 %collective-permute-start.24 = (f32[128,128]{1,0:T(8,128)S(1)}, f32[128,128]{1,0:T(8,128)S(1)}, u32[]{:S(2)}, u32[]{:S(2)}) collective-permute-start(f32[128,128]{1,0:T(8,128)S(1)} %get-tuple-element.81), channel_id=1, source_target_pairs={{0,12},{2,14},{4,8},{6,10},{8,4},{10,6},{12,0},{14,2},{16,28},{18,... | collective-permute-start | bytes 196616 | tf_op jit(solution)/shard_map/ppermute | solution.py:281
  47.4 8.8 %collective-permute-start.25 = (f32[128,128]{1,0:T(8,128)S(1)}, f32[128,128]{1,0:T(8,128)S(1)}, u32[]{:S(2)}, u32[]{:S(2)}) collective-permute-start(f32[128,128]{1,0:T(8,128)S(1)} %get-tuple-element.82), channel_id=1, source_target_pairs={{0,8},{2,10},{4,12},{6,14},{8,0},{10,2},{12,4},{14,6},{16,24},{18,... | collective-permute-start | bytes 196616 | tf_op jit(solution)/shard_map/ppermute | solution.py:281
  50.4 5.9 %collective-permute-start.26 = (f32[128,128]{1,0:T(8,128)S(1)}, f32[128,128]{1,0:T(8,128)S(1)}, u32[]{:S(2)}, u32[]{:S(2)}) collective-permute-start(f32[128,128]{1,0:T(8,128)S(1)} %get-tuple-element.83), channel_id=1, source_target_pairs={{0,4},{2,6},{4,0},{6,2},{8,12},{10,14},{12,8},{14,10},{16,20},{18,... | collective-permute-start | bytes 196616 | tf_op jit(solution)/shard_map/ppermute | solution.py:281
  50.4 16.9 %slice-start.1 = ((s8[8388608]{0:T(1024)(128)(4,1)}), s8[4194304]{0:T(1024)(128)(4,1)S(1)}, s32[]{:S(2)}) async-start(s8[8388608]{0:T(1024)(128)(4,1)} %bitcast.8), calls=%async_computation.1 | async-start | bytes 8388608
  50.5 7.9 %collective-permute-start.10 = (f32[128,128]{1,0:T(8,128)S(1)}, f32[128,128]{1,0:T(8,128)S(1)}, u32[]{:S(2)}, u32[]{:S(2)}) collective-permute-start(f32[128,128]{1,0:T(8,128)S(1)} %get-tuple-element.58), channel_id=1, source_target_pairs={{0,12},{2,14},{4,8},{6,10},{8,4},{10,6},{12,0},{14,2},{16,28},{18,... | collective-permute-start | bytes 196616 | tf_op jit(solution)/shard_map/ppermute | solution.py:281
  53.3 7.1 %collective-permute-start.11 = (f32[128,128]{1,0:T(8,128)S(1)}, f32[128,128]{1,0:T(8,128)S(1)}, u32[]{:S(2)}, u32[]{:S(2)}) collective-permute-start(f32[128,128]{1,0:T(8,128)S(1)} %get-tuple-element.59), channel_id=1, source_target_pairs={{0,8},{2,10},{4,12},{6,14},{8,0},{10,2},{12,4},{14,6},{16,24},{18,... | collective-permute-start | bytes 196616 | tf_op jit(solution)/shard_map/ppermute | solution.py:281
  56.2 9.2 %collective-permute-start.12 = (f32[128,128]{1,0:T(8,128)S(1)}, f32[128,128]{1,0:T(8,128)S(1)}, u32[]{:S(2)}, u32[]{:S(2)}) collective-permute-start(f32[128,128]{1,0:T(8,128)S(1)} %get-tuple-element.60), channel_id=1, source_target_pairs={{0,4},{2,6},{4,0},{6,2},{8,12},{10,14},{12,8},{14,10},{16,20},{18,... | collective-permute-start | bytes 196616 | tf_op jit(solution)/shard_map/ppermute | solution.py:281
  56.3 10.9 %collective-permute-start.27 = (f32[512,128]{1,0:T(8,128)S(1)}, f32[512,128]{1,0:T(8,128)S(1)}, u32[]{:S(2)}, u32[]{:S(2)}) collective-permute-start(f32[512,128]{1,0:T(8,128)S(1)} %get-tuple-element.85), channel_id=1, source_target_pairs={{0,2},{2,0},{4,6},{6,4},{8,10},{10,8},{12,14},{14,12},{16,18},{18,... | collective-permute-start | bytes 786440 | tf_op jit(solution)/shard_map/ppermute | solution.py:331
  65.5 7.7 %collective-permute-start.13 = (f32[512,128]{1,0:T(8,128)S(1)}, f32[512,128]{1,0:T(8,128)S(1)}, u32[]{:S(2)}, u32[]{:S(2)}) collective-permute-start(f32[512,128]{1,0:T(8,128)S(1)} %get-tuple-element.61), channel_id=1, source_target_pairs={{0,2},{2,0},{4,6},{6,4},{8,10},{10,8},{12,14},{14,12},{16,18},{18,... | collective-permute-start | bytes 786440 | tf_op jit(solution)/shard_map/ppermute | solution.py:331
  74.0 5.5 %collective-permute-start.28 = (f32[64,2048]{1,0:T(8,128)S(1)}, f32[64,2048]{1,0:T(8,128)S(1)}, u32[]{:S(2)}, u32[]{:S(2)}) collective-permute-start(f32[64,2048]{1,0:T(8,128)S(1)} %get-tuple-element.90), channel_id=1, source_target_pairs={{0,1},{1,0},{2,3},{3,2},{4,5},{5,4},{6,7},{7,6},{8,9},{9,8},{10,11... | collective-permute-start | bytes 1572872 | tf_op jit(solution)/shard_map/ppermute | solution.py:347

commit v6 on v5

--- a/solution.py
+++ b/solution.py
@@ -39,9 +39,10 @@
     return rows >= columns
 
 
-def running_sum(log_decay):
-    upper = jnp.where(lower_mask(), 1.0, 0.0).T
-    return jnp.dot(log_decay, upper, precision=HIGHEST, preferred_element_type=F32)
+def running_sum(log_decay, lower):
+    return lax.dot_general(
+        log_decay, lower, (((1,), (1,)), ((), ())), precision=HIGHEST, preferred_element_type=F32
+    )
 
 
 def decay_tile(rows):
@@ -52,11 +53,14 @@
     return tile
 
 
-def running_sum_t(log_decay):
-    lower = jnp.where(lower_mask(), 1.0, 0.0)
+def running_sum_t(log_decay, lower):
     return lax.dot_general(
         lower, log_decay, (((1,), (1,)), ((), ())), precision=HIGHEST, preferred_element_type=F32
     )
+
+
+def lower_kernel(out):
+    out[...] = jnp.where(lower_mask(), 1.0, 0.0)
 
 
 def position():
@@ -68,9 +72,9 @@
     return pl.ds(pl.multiple_of(index * W, W), W)
 
 
-def local_state_kernel(group, x, b, log_decay, keep, send, cum_ref):
-    pos = position()
-    cum_ref[...] = running_sum(log_decay[...])
+def local_state_kernel(group, lower, x, b, log_decay, keep, send, cum_ref):
+    pos = position()
+    cum_ref[...] = running_sum(log_decay[...], lower[...])
     b_t = b[...].astype(F32).T
     role = pos[0] & 1
     for out, side in ((send, 1 - role), (keep, role)):
@@ -187,13 +191,13 @@
         send[state, :] = jnp.where(first, after, carry)
 
 
-def inside_kernel(skip, x, z, b, c, log_decay, gain, fixed, slope, read, gain_out):
+def inside_kernel(skip, ones, x, z, b, c, log_decay, gain, fixed, slope, read, gain_out):
     read[...] = c[...]
     gain_out[...] = gain[...]
     lower = lower_mask()
     logs = log_decay[...]
-    cum = running_sum(logs)
-    cum_t = running_sum_t(logs)
+    cum = running_sum(logs, ones[...])
+    cum_t = running_sum_t(logs, ones[...])
     scores = lax.dot_general(c[...], b[...], (((1,), (1,)), ((), ())), preferred_element_type=F32)
     for head in range(HEADS):
         at = slice(head * W, (head + 1) * W)
@@ -283,22 +287,26 @@
 
 
 def per_device(x_in, z_in, b_in, c_in, log_decay, d_skip, norm_gain, w_out):
+    lower = call(lower_kernel, shaped(W, W), [], name="lower", work=WORK)()
+    lower, x_in, z_in, b_in, c_in, log_decay, d_skip, norm_gain = lax.optimization_barrier(
+        (lower, x_in, z_in, b_in, c_in, log_decay, d_skip, norm_gain)
+    )
     x = x_in.reshape(W, HEADS * W)
     width = w_out.shape[1]
     full, single = shaped(ROWS + 8, W), shaped(W + 8, W)
     keep, got, parts, totals, planes, mine, states = {}, {}, {}, {}, {}, {}, {}
     for g in range(GROUPS):
         keep[g], send = call(
-            functools.partial(local_state_kernel, g), [full] * 2, [VMEM] * 3,
+            functools.partial(local_state_kernel, g), [full] * 2, [VMEM] * 4,
             [pltpu.VMEM((HEADS, W), F32)], name=f"local_state_{g}",
-        )(x, b_in, log_decay)
+        )(lower, x, b_in, log_decay)
         got[g] = lax.ppermute(send, "ctx", partners(1, 1))
     keep[1], z = lax.optimization_barrier((keep[1], z_in))
     fixed, slope, read, gain = call(
         inside_kernel,
         [shaped(W, HEADS * W), shaped(W, HEADS * W), shaped(W, W, dtype=BF16), shaped(HEADS, W)],
-        [SMEM] + [VMEM] * 6, name="inside",
-    )(d_skip, x, z.reshape(W, HEADS * W), b_in, c_in, log_decay, norm_gain)
+        [SMEM] + [VMEM] * 7, name="inside",
+    )(d_skip, lower, x, z.reshape(W, HEADS * W), b_in, c_in, log_decay, norm_gain)
     keep[0], fixed, slope, read, gain = lax.optimization_barrier(
         (keep[0], fixed, slope, read, gain)
     )

time: 80.8 us -> 77.8 us (0.963)
  local copies, waits for them, and re-layouts: 8.07 us -> 1.38 us
  starting transfers between devices: 48.1 us -> 51.8 us
    unnamed x22 -> x20, local copies, waits for them, and re-layouts: 8.07 us -> 1.38 us
    ppermute x2, waiting for transfers between devices: 0.01 us -> 2.34 us  [per_device(): got[g] = lax.ppermute(send, 'ctx', partners(1, 1))]
    ppermute x24, waiting for transfers between devices: 9.28 us -> 7.11 us  [exchange(): lax.ppermute(value, 'ctx', partners(stride, m))]
    ppermute x2, starting transfers between devices: 2.17 us -> 3.9 us  [per_device(): states[g] = lax.ppermute(send, 'ctx', partners(1, 1))]
    ppermute x24, starting transfers between devices: 39.3 us -> 40.8 us  [exchange(): lax.ppermute(value, 'ctx', partners(stride, m))]
  transfers between devices with their start and end apart: 29 -> 29, of which waited for: 9 -> 9; matrix products, arithmetic and copies ran while one was open for 1% -> 0% of each run, Pallas kernels for 7% -> 7%
where the time goes in v6:
time: 77.8 us; the launch traced here: 77.7 us
  starting transfers between devices  51.8 us (67%)
  waiting for transfers between devices  16.7 us (21%)
  Pallas kernels  6.83 us (9%)
  local copies, waits for them, and re-layouts  1.38 us (2%)
    ppermute x24, starting transfers between devices, exchange(): lax.ppermute(value, 'ctx', partners(stride, m))  40.8 us
    ppermute x24, waiting for transfers between devices, exchange(): lax.ppermute(value, 'ctx', partners(stride, m))  7.11 us
    ppermute x2, waiting for transfers between devices, per_device(): states[g] = lax.ppermute(send, 'ctx', partners(1, 1))  5.76 us
    ppermute x1, starting transfers between devices, per_device(): return (near + lax.ppermute(far, 'tp', [(0, 1), (1, 0)])).astype(BF16)  4.39 us
    ppermute x2, starting transfers between devices, per_device(): states[g] = lax.ppermute(send, 'ctx', partners(1, 1))  3.9 us
    pallas_call x3, Pallas kernels, finish(): call(functools.partial(finish_kernel, group, sides, stage), outs, [VMEM]...  2.91 us
    ppermute x2, starting transfers between devices, per_device(): got[g] = lax.ppermute(send, 'ctx', partners(1, 1))  2.66 us
    ppermute x2, waiting for transfers between devices, per_device(): got[g] = lax.ppermute(send, 'ctx', partners(1, 1))  2.34 us
  transfers between devices with their start and end apart: 29, of which 9 were waited for; matrix products, arithmetic and copies ran while one was open for 0% of the time, Pallas kernels for 7%

profile of v6, /device:TPU:1, one launch (start us, length us, event | category | flops | bytes accessed | tf_op | source)
XLA Modules:
  0.0 77.7 jit_solution(15185833883855660343)
XLA Ops:
  0.1 1.1 %copy-done.5 = bf16[128,16,128]{2,1,0:T(8,128)(2,1)S(1)} copy-done((bf16[128,16,128]{2,1,0:T(8,128)(2,1)S(1)}, bf16[128,16,128]{2,1,0:T(8,128)(2,1)}, u32[]{:S(2)}) %copy-start.5) | copy-done | bytes 524312
  1.1 0.1 copy.14
  1.3 0.8 %local_state_0.1 = (f32[520,128]{1,0:T(8,128)S(1)}, f32[520,128]{1,0:T(8,128)S(1)}) custom-call(f32[128,128]{1,0:T(8,128)S(1)} %lower.1.ones, bf16[128,2048]{1,0:T(8,128)(2,1)S(1)} %bitcast.10, bf16[128,128]{1,0:T(8,128)(2,1)S(1)} %copy-done, f32[16,128]{1,0:T(8,128)S(1)} %copy-done.1), custom_call_target="tpu_custom_call" | custom-call | tf_op jit(solution)/shard_map/local_state_0/pallas_call | solution.py:299
  2.1 2.6 %collective-permute-start.14 = (f32[520,128]{1,0:T(8,128)S(1)}, f32[520,128]{1,0:T(8,128)S(1)}, u32[]{:S(2)}, u32[]{:S(2)}) collective-permute-start(f32[520,128]{1,0:T(8,128)S(1)} %get-tuple-element.89), channel_id=1, source_target_pairs={{0,2},{2,0},{4,6},{6,4},{8,10},{10,8},{12,14},{14,12},{16,18},{18,... | collective-permute-start | bytes 798728 | tf_op jit(solution)/shard_map/ppermute | solution.py:303
  4.6 0.8 %local_state_1.1 = (f32[520,128]{1,0:T(8,128)S(1)}, f32[520,128]{1,0:T(8,128)S(1)}) custom-call(f32[128,128]{1,0:T(8,128)S(1)} %lower.1.ones, bf16[128,2048]{1,0:T(8,128)(2,1)S(1)} %bitcast.11, bf16[128,128]{1,0:T(8,128)(2,1)S(1)} %copy-done, f32[16,128]{1,0:T(8,128)S(1)} %copy-done.1), custom_call_target="tpu_custom_call" | custom-call | tf_op jit(solution)/shard_map/local_state_1/pallas_call | solution.py:299
  5.4 0.1 collective-permute-start
  5.5 0.1 copy.13
  5.7 1.6 %inside.1 = (f32[128,2048]{1,0:T(8,128)S(1)}, f32[128,2048]{1,0:T(8,128)S(1)}, bf16[128,128]{1,0:T(8,128)(2,1)S(1)}, f32[16,128]{1,0:T(8,128)S(1)}) custom-call(f32[16]{0:T(128)S(1)} %copy-done.4, f32[128,128]{1,0:T(8,128)S(1)} %lower.1.ones, bf16[128,2048]{1,0:T(8,128)(2,1)S(1)} %bitcast.12, bf16[128,2048]{1,0:T(8,128)(2,1)S(1)} %bitcast.13, ...), custom_call_target="tpu_custom_call" | custom-call | tf_op jit(solution)/shard_map/inside/pallas_call | solution.py:305
  7.4 2.3 %collective-permute-done.14.got = f32[520,128]{1,0:T(8,128)S(1)} collective-permute-done((f32[520,128]{1,0:T(8,128)S(1)}, f32[520,128]{1,0:T(8,128)S(1)}, u32[]{:S(2)}, u32[]{:S(2)}) %collective-permute-start.14) | collective-permute-done | bytes 266272 | tf_op jit(solution)/shard_map/ppermute | solution.py:303
  9.7 0.1 pair_0.1
  9.8 6.7 %collective-permute-start.15 = (f32[136,128]{1,0:T(8,128)S(1)}, f32[136,128]{1,0:T(8,128)S(1)}, u32[]{:S(2)}, u32[]{:S(2)}) collective-permute-start(f32[136,128]{1,0:T(8,128)S(1)} %get-tuple-element.91), channel_id=1, source_target_pairs={{0,12},{2,14},{4,8},{6,10},{8,4},{10,6},{12,0},{14,2},{16,28},{18,... | collective-permute-start | bytes 208904 | tf_op jit(solution)/shard_map/ppermute | solution.py:285
  16.4 1.0 %collective-permute-start.16 = (f32[136,128]{1,0:T(8,128)S(1)}, f32[136,128]{1,0:T(8,128)S(1)}, u32[]{:S(2)}, u32[]{:S(2)}) collective-permute-start(f32[136,128]{1,0:T(8,128)S(1)} %get-tuple-element.92), channel_id=1, source_target_pairs={{0,8},{2,10},{4,12},{6,14},{8,0},{10,2},{12,4},{14,6},{16,24},{18,... | collective-permute-start | bytes 208904 | tf_op jit(solution)/shard_map/ppermute | solution.py:285
  17.4 1.2 %collective-permute-start.17 = (f32[136,128]{1,0:T(8,128)S(1)}, f32[136,128]{1,0:T(8,128)S(1)}, u32[]{:S(2)}, u32[]{:S(2)}) collective-permute-start(f32[136,128]{1,0:T(8,128)S(1)} %get-tuple-element.93), channel_id=1, source_target_pairs={{0,4},{2,6},{4,0},{6,2},{8,12},{10,14},{12,8},{14,10},{16,20},{18,... | collective-permute-start | bytes 208904 | tf_op jit(solution)/shard_map/ppermute | solution.py:285
  18.6 0.1 pair_1.1
  18.7 4.0 %collective-permute-start.1 = (f32[136,128]{1,0:T(8,128)S(1)}, f32[136,128]{1,0:T(8,128)S(1)}, u32[]{:S(2)}, u32[]{:S(2)}) collective-permute-start(f32[136,128]{1,0:T(8,128)S(1)} %get-tuple-element.65), channel_id=1, source_target_pairs={{0,12},{2,14},{4,8},{6,10},{8,4},{10,6},{12,0},{14,2},{16,28},{18,... | collective-permute-start | bytes 208904 | tf_op jit(solution)/shard_map/ppermute | solution.py:285
  22.7 0.8 %collective-permute-start.2 = (f32[136,128]{1,0:T(8,128)S(1)}, f32[136,128]{1,0:T(8,128)S(1)}, u32[]{:S(2)}, u32[]{:S(2)}) collective-permute-start(f32[136,128]{1,0:T(8,128)S(1)} %get-tuple-element.66), channel_id=1, source_target_pairs={{0,8},{2,10},{4,12},{6,14},{8,0},{10,2},{12,4},{14,6},{16,24},{18,... | collective-permute-start | bytes 208904 | tf_op jit(solution)/shard_map/ppermute | solution.py:285
  23.5 0.0 collective-permute-done.15.refs_1_.refs_5_
  23.5 1.3 %collective-permute-start.3 = (f32[136,128]{1,0:T(8,128)S(1)}, f32[136,128]{1,0:T(8,128)S(1)}, u32[]{:S(2)}, u32[]{:S(2)}) collective-permute-start(f32[136,128]{1,0:T(8,128)S(1)} %get-tuple-element.67), channel_id=1, source_target_pairs={{0,4},{2,6},{4,0},{6,2},{8,12},{10,14},{12,8},{14,10},{16,20},{18,... | collective-permute-start | bytes 208904 | tf_op jit(solution)/shard_map/ppermute | solution.py:285
  24.9 0.4 collective-permute-done.16.refs_2_.refs_6_
  25.3 2.8 %collective-permute-start.20 = (f32[136,128]{1,0:T(8,128)S(1)}, f32[136,128]{1,0:T(8,128)S(1)}, u32[]{:S(2)}, u32[]{:S(2)}) collective-permute-start(f32[136,128]{1,0:T(8,128)S(1)} %row_total_0.1.refs_0_), channel_id=1, source_target_pairs={{0,48},{2,50},{4,52},{6,54},{8,56},{10,58},{12,60},{14,62},{16,32}... | collective-permute-start | bytes 208904 | tf_op jit(solution)/shard_map/ppermute | solution.py:285
  28.2 0.3 collective-permute-start.19
  28.5 0.8 collective-permute-start.18
  29.3 1.5 %collective-permute-done.2.refs_2_.refs_6_ = f32[136,128]{1,0:T(8,128)S(1)} collective-permute-done((f32[136,128]{1,0:T(8,128)S(1)}, f32[136,128]{1,0:T(8,128)S(1)}, u32[]{:S(2)}, u32[]{:S(2)}) %collective-permute-start.2) | collective-permute-done | bytes 69664 | tf_op jit(solution)/shard_map/ppermute | solution.py:285
  30.7 0.0 collective-permute-done.3.refs_3_.refs_7_
  30.8 2.8 %collective-permute-start.6 = (f32[136,128]{1,0:T(8,128)S(1)}, f32[136,128]{1,0:T(8,128)S(1)}, u32[]{:S(2)}, u32[]{:S(2)}) collective-permute-start(f32[136,128]{1,0:T(8,128)S(1)} %row_total_1.1.refs_0_), channel_id=1, source_target_pairs={{0,48},{2,50},{4,52},{6,54},{8,56},{10,58},{12,60},{14,62},{16,32}... | collective-permute-start | bytes 208904 | tf_op jit(solution)/shard_map/ppermute | solution.py:285
  33.6 0.3 collective-permute-start.5
  34.0 0.0 collective-permute-done.20.refs_3_
  34.0 0.3 collective-permute-start.4
  34.3 0.0 collective-permute-done.19.refs_2_
  34.3 0.0 collective-permute-done.18.refs_1_
  34.3 0.1 plane_0.1
  34.4 2.6 %collective-permute-start.23 = (f32[136,128]{1,0:T(8,128)S(1)}, f32[136,128]{1,0:T(8,128)S(1)}, u32[]{:S(2)}, u32[]{:S(2)}) collective-permute-start(f32[136,128]{1,0:T(8,128)S(1)} %get-tuple-element.94), channel_id=1, source_target_pairs={{0,192},{2,194},{4,196},{6,198},{8,200},{10,202},{12,204},{14,206}... | collective-permute-start | bytes 208904 | tf_op jit(solution)/shard_map/ppermute | solution.py:285
  36.9 0.5 collective-permute-start.22
  37.5 0.3 collective-permute-start.21
  37.7 1.2 %collective-permute-done.5.refs_2_ = f32[136,128]{1,0:T(8,128)S(1)} collective-permute-done((f32[136,128]{1,0:T(8,128)S(1)}, f32[136,128]{1,0:T(8,128)S(1)}, u32[]{:S(2)}, u32[]{:S(2)}) %collective-permute-start.5) | collective-permute-done | bytes 69664 | tf_op jit(solution)/shard_map/ppermute | solution.py:285
  39.0 0.0 collective-permute-done.4.refs_1_
  39.0 0.1 plane_1.1
  39.0 2.7 %collective-permute-start.9 = (f32[136,128]{1,0:T(8,128)S(1)}, f32[136,128]{1,0:T(8,128)S(1)}, u32[]{:S(2)}, u32[]{:S(2)}) collective-permute-start(f32[136,128]{1,0:T(8,128)S(1)} %get-tuple-element.68), channel_id=1, source_target_pairs={{0,192},{2,194},{4,196},{6,198},{8,200},{10,202},{12,204},{14,206}... | collective-permute-start | bytes 208904 | tf_op jit(solution)/shard_map/ppermute | solution.py:285
  41.8 0.5 collective-permute-start.8
  42.3 0.0 collective-permute-done.23.refs_2_
  42.3 0.3 collective-permute-start.7
  42.6 0.1 entering_0.1
  42.7 1.7 %collective-permute-start.24 = (f32[128,128]{1,0:T(8,128)S(1)}, f32[128,128]{1,0:T(8,128)S(1)}, u32[]{:S(2)}, u32[]{:S(2)}) collective-permute-start(f32[128,128]{1,0:T(8,128)S(1)} %get-tuple-element.97), channel_id=1, source_target_pairs={{0,12},{2,14},{4,8},{6,10},{8,4},{10,6},{12,0},{14,2},{16,28},{18,... | collective-permute-start | bytes 196616 | tf_op jit(solution)/shard_map/ppermute | solution.py:285
  44.3 3.3 %collective-permute-start.25 = (f32[128,128]{1,0:T(8,128)S(1)}, f32[128,128]{1,0:T(8,128)S(1)}, u32[]{:S(2)}, u32[]{:S(2)}) collective-permute-start(f32[128,128]{1,0:T(8,128)S(1)} %get-tuple-element.98), channel_id=1, source_target_pairs={{0,8},{2,10},{4,12},{6,14},{8,0},{10,2},{12,4},{14,6},{16,24},{18,... | collective-permute-start | bytes 196616 | tf_op jit(solution)/shard_map/ppermute | solution.py:285
  47.6 0.0 collective-permute-done.9.refs_2_
  47.6 0.8 %collective-permute-start.26 = (f32[128,128]{1,0:T(8,128)S(1)}, f32[128,128]{1,0:T(8,128)S(1)}, u32[]{:S(2)}, u32[]{:S(2)}) collective-permute-start(f32[128,128]{1,0:T(8,128)S(1)} %get-tuple-element.99), channel_id=1, source_target_pairs={{0,4},{2,6},{4,0},{6,2},{8,12},{10,14},{12,8},{14,10},{16,20},{18,... | collective-permute-start | bytes 196616 | tf_op jit(solution)/shard_map/ppermute | solution.py:285
  48.4 0.1 entering_1.1
  48.5 2.0 %collective-permute-start.10 = (f32[128,128]{1,0:T(8,128)S(1)}, f32[128,128]{1,0:T(8,128)S(1)}, u32[]{:S(2)}, u32[]{:S(2)}) collective-permute-start(f32[128,128]{1,0:T(8,128)S(1)} %get-tuple-element.71), channel_id=1, source_target_pairs={{0,12},{2,14},{4,8},{6,10},{8,4},{10,6},{12,0},{14,2},{16,28},{18,... | collective-permute-start | bytes 196616 | tf_op jit(solution)/shard_map/ppermute | solution.py:285
  50.5 3.0 %collective-permute-start.11 = (f32[128,128]{1,0:T(8,128)S(1)}, f32[128,128]{1,0:T(8,128)S(1)}, u32[]{:S(2)}, u32[]{:S(2)}) collective-permute-start(f32[128,128]{1,0:T(8,128)S(1)} %get-tuple-element.72), channel_id=1, source_target_pairs={{0,8},{2,10},{4,12},{6,14},{8,0},{10,2},{12,4},{14,6},{16,24},{18,... | collective-permute-start | bytes 196616 | tf_op jit(solution)/shard_map/ppermute | solution.py:285
  53.5 0.8 %collective-permute-start.12 = (f32[128,128]{1,0:T(8,128)S(1)}, f32[128,128]{1,0:T(8,128)S(1)}, u32[]{:S(2)}, u32[]{:S(2)}) collective-permute-start(f32[128,128]{1,0:T(8,128)S(1)} %get-tuple-element.73), channel_id=1, source_target_pairs={{0,4},{2,6},{4,0},{6,2},{8,12},{10,14},{12,8},{14,10},{16,20},{18,... | collective-permute-start | bytes 196616 | tf_op jit(solution)/shard_map/ppermute | solution.py:285
  54.3 0.1 spread_0.1
  54.4 1.0 %collective-permute-start.27 = (f32[512,128]{1,0:T(8,128)S(1)}, f32[512,128]{1,0:T(8,128)S(1)}, u32[]{:S(2)}, u32[]{:S(2)}) collective-permute-start(f32[512,128]{1,0:T(8,128)S(1)} %get-tuple-element.101), channel_id=1, source_target_pairs={{0,2},{2,0},{4,6},{6,4},{8,10},{10,8},{12,14},{14,12},{16,18},{18,... | collective-permute-start | bytes 786440 | tf_op jit(solution)/shard_map/ppermute | solution.py:339
  55.4 2.2 %collective-permute-done.11.refs_2_ = f32[128,128]{1,0:T(8,128)S(1)} collective-permute-done((f32[128,128]{1,0:T(8,128)S(1)}, f32[128,128]{1,0:T(8,128)S(1)}, u32[]{:S(2)}, u32[]{:S(2)}) %collective-permute-start.11) | collective-permute-done | bytes 65568 | tf_op jit(solution)/shard_map/ppermute | solution.py:285
  57.6 1.7 %collective-permute-done.12.refs_3_ = f32[128,128]{1,0:T(8,128)S(1)} collective-permute-done((f32[128,128]{1,0:T(8,128)S(1)}, f32[128,128]{1,0:T(8,128)S(1)}, u32[]{:S(2)}, u32[]{:S(2)}) %collective-permute-start.12) | collective-permute-done | bytes 65568 | tf_op jit(solution)/shard_map/ppermute | solution.py:285
  59.4 0.1 spread_1.1
  59.5 2.9 %collective-permute-start.13 = (f32[512,128]{1,0:T(8,128)S(1)}, f32[512,128]{1,0:T(8,128)S(1)}, u32[]{:S(2)}, u32[]{:S(2)}) collective-permute-start(f32[512,128]{1,0:T(8,128)S(1)} %get-tuple-element.74), channel_id=1, source_target_pairs={{0,2},{2,0},{4,6},{6,4},{8,10},{10,8},{12,14},{14,12},{16,18},{18,... | collective-permute-start | bytes 786440 | tf_op jit(solution)/shard_map/ppermute | solution.py:339
  62.3 0.9 %collective-permute-done.27.refs_1_ = f32[512,128]{1,0:T(8,128)S(1)} collective-permute-done((f32[512,128]{1,0:T(8,128)S(1)}, f32[512,128]{1,0:T(8,128)S(1)}, u32[]{:S(2)}, u32[]{:S(2)}) %collective-permute-start.27) | collective-permute-done | bytes 262176 | tf_op jit(solution)/shard_map/ppermute | solution.py:339
  63.3 1.4 %finish_0.1 = (f32[128,2048]{1,0:T(8,128)S(1)}, bf16[1024,2048]{1,0:T(8,128)(2,1)S(1)}) custom-call(f32[512,128]{1,0:T(8,128)S(1)} %get-tuple-element.100.refs_0_, f32[512,128]{1,0:T(8,128)S(1)} %collective-permute-done.27.refs_1_, bf16[128,128]{1,0:T(8,128)(2,1)S(1)} %get-tuple-element.84.refs_2_.refs_1_, ...), custom_call_target="tpu_custom_call" | custom-call | tf_op jit(solution)/shard_map/finish_0/pallas_call | solution.py:344
  64.7 0.7 finish_1.1.refs_6_
  65.4 4.8 %collective-permute-done.13.refs_0_ = f32[512,128]{1,0:T(8,128)S(1)} collective-permute-done((f32[512,128]{1,0:T(8,128)S(1)}, f32[512,128]{1,0:T(8,128)S(1)}, u32[]{:S(2)}, u32[]{:S(2)}) %collective-permute-start.13) | collective-permute-done | bytes 262176 | tf_op jit(solution)/shard_map/ppermute | solution.py:339
  70.2 0.8 %finish_2.1 = (f32[64,2048]{1,0:T(8,128)S(1)}, f32[64,2048]{1,0:T(8,128)S(1)}) custom-call(f32[512,128]{1,0:T(8,128)S(1)} %collective-permute-done.13.refs_0_, bf16[128,128]{1,0:T(8,128)(2,1)S(1)} %get-tuple-element.84.refs_2_.refs_1_, f32[128,2048]{1,0:T(8,128)S(1)} %get-tuple-element.85.refs_3_.refs_2_, f32[128,2048]{1,0:T(8,128)S(1)} %get-tuple-element.86.refs_4_.refs_3_, ...), custom_call_target="tpu_custom_call" | custom-call | tf_op jit(solution)/shard_map/finish_2/pallas_call | solution.py:344
  71.0 4.4 %collective-permute-start.28 = (f32[64,2048]{1,0:T(8,128)S(1)}, f32[64,2048]{1,0:T(8,128)S(1)}, u32[]{:S(2)}, u32[]{:S(2)}) collective-permute-start(f32[64,2048]{1,0:T(8,128)S(1)} %get-tuple-element.106), channel_id=1, source_target_pairs={{0,1},{1,0},{2,3},{3,2},{4,5},{5,4},{6,7},{7,6},{8,9},{9,8},{10,11... | collective-permute-start | bytes 1572872 | tf_op jit(solution)/shard_map/ppermute | solution.py:355
  75.4 1.5 %collective-permute-done.28 = f32[64,2048]{1,0:T(8,128)S(1)} collective-permute-done((f32[64,2048]{1,0:T(8,128)S(1)}, f32[64,2048]{1,0:T(8,128)S(1)}, u32[]{:S(2)}, u32[]{:S(2)}) %collective-permute-start.28) | collective-permute-done | bytes 524320 | tf_op jit(solution)/shard_map/ppermute | solution.py:355
  77.0 0.8 add_convert_fusion
  (33 shorter events, 0.2 us)
Async XLA Ops:
  0.0 5.7 %copy-start.3 = (f32[16,128]{1,0:T(8,128)S(1)}, f32[16,128]{1,0:T(8,128)}, u32[]{:S(2)}) copy-start(f32[16,128]{1,0:T(8,128)} %gain) | copy-start | bytes 24580
  0.0 5.7 %copy-start.4 = (f32[16]{0:T(128)S(1)}, f32[16]{0:T(128)}, u32[]{:S(2)}) copy-start(f32[16]{0:T(128)} %skip) | copy-start | bytes 196
  0.0 1.3 %copy-start.1 = (f32[16,128]{1,0:T(8,128)S(1)}, f32[16,128]{1,0:T(8,128)}, u32[]{:S(2)}) copy-start(f32[16,128]{1,0:T(8,128)} %log_decay.2) | copy-start | bytes 24580
  0.0 5.7 %copy-start.2 = (bf16[128,128]{1,0:T(8,128)(2,1)S(1)}, bf16[128,128]{1,0:T(8,128)(2,1)}, u32[]{:S(2)}) copy-start(bf16[128,128]{1,0:T(8,128)(2,1)} %c) | copy-start | bytes 98308
  0.0 1.3 %copy-start = (bf16[128,128]{1,0:T(8,128)(2,1)S(1)}, bf16[128,128]{1,0:T(8,128)(2,1)}, u32[]{:S(2)}) copy-start(bf16[128,128]{1,0:T(8,128)(2,1)} %b.2) | copy-start | bytes 98308
  0.0 5.5 %copy-start.6 = (bf16[128,16,128]{2,1,0:T(8,128)(2,1)S(1)}, bf16[128,16,128]{2,1,0:T(8,128)(2,1)}, u32[]{:S(2)}) copy-start(bf16[128,16,128]{2,1,0:T(8,128)(2,1)} %param.9) | copy-start | bytes 1572868
  0.0 1.1 %copy-start.5 = (bf16[128,16,128]{2,1,0:T(8,128)(2,1)S(1)}, bf16[128,16,128]{2,1,0:T(8,128)(2,1)}, u32[]{:S(2)}) copy-start(bf16[128,16,128]{2,1,0:T(8,128)(2,1)} %param.8) | copy-start | bytes 1572868
  2.1 7.6 %collective-permute-start.14 = (f32[520,128]{1,0:T(8,128)S(1)}, f32[520,128]{1,0:T(8,128)S(1)}, u32[]{:S(2)}, u32[]{:S(2)}) collective-permute-start(f32[520,128]{1,0:T(8,128)S(1)} %get-tuple-element.89), channel_id=1, source_target_pairs={{0,2},{2,0},{4,6},{6,4},{8,10},{10,8},{12,14},{14,12},{16,18},{18,... | collective-permute-start | bytes 798728 | tf_op jit(solution)/shard_map/ppermute | solution.py:303
  5.4 13.2 %collective-permute-start = (f32[520,128]{1,0:T(8,128)S(1)}, f32[520,128]{1,0:T(8,128)S(1)}, u32[]{:S(2)}, u32[]{:S(2)}) collective-permute-start(f32[520,128]{1,0:T(8,128)S(1)} %get-tuple-element.63), channel_id=1, source_target_pairs={{0,2},{2,0},{4,6},{6,4},{8,10},{10,8},{12,14},{14,12},{16,18},{18,... | collective-permute-start | bytes 798728 | tf_op jit(solution)/shard_map/ppermute | solution.py:303
  9.8 13.8 %collective-permute-start.15 = (f32[136,128]{1,0:T(8,128)S(1)}, f32[136,128]{1,0:T(8,128)S(1)}, u32[]{:S(2)}, u32[]{:S(2)}) collective-permute-start(f32[136,128]{1,0:T(8,128)S(1)} %get-tuple-element.91), channel_id=1, source_target_pairs={{0,12},{2,14},{4,8},{6,10},{8,4},{10,6},{12,0},{14,2},{16,28},{18,... | collective-permute-start | bytes 208904 | tf_op jit(solution)/shard_map/ppermute | solution.py:285
  16.4 8.8 %collective-permute-start.16 = (f32[136,128]{1,0:T(8,128)S(1)}, f32[136,128]{1,0:T(8,128)S(1)}, u32[]{:S(2)}, u32[]{:S(2)}) collective-permute-start(f32[136,128]{1,0:T(8,128)S(1)} %get-tuple-element.92), channel_id=1, source_target_pairs={{0,8},{2,10},{4,12},{6,14},{8,0},{10,2},{12,4},{14,6},{16,24},{18,... | collective-permute-start | bytes 208904 | tf_op jit(solution)/shard_map/ppermute | solution.py:285
  17.4 7.9 %collective-permute-start.17 = (f32[136,128]{1,0:T(8,128)S(1)}, f32[136,128]{1,0:T(8,128)S(1)}, u32[]{:S(2)}, u32[]{:S(2)}) collective-permute-start(f32[136,128]{1,0:T(8,128)S(1)} %get-tuple-element.93), channel_id=1, source_target_pairs={{0,4},{2,6},{4,0},{6,2},{8,12},{10,14},{12,8},{14,10},{16,20},{18,... | collective-permute-start | bytes 208904 | tf_op jit(solution)/shard_map/ppermute | solution.py:285
  18.7 9.8 %collective-permute-start.1 = (f32[136,128]{1,0:T(8,128)S(1)}, f32[136,128]{1,0:T(8,128)S(1)}, u32[]{:S(2)}, u32[]{:S(2)}) collective-permute-start(f32[136,128]{1,0:T(8,128)S(1)} %get-tuple-element.65), channel_id=1, source_target_pairs={{0,12},{2,14},{4,8},{6,10},{8,4},{10,6},{12,0},{14,2},{16,28},{18,... | collective-permute-start | bytes 208904 | tf_op jit(solution)/shard_map/ppermute | solution.py:285
  22.7 8.0 %collective-permute-start.2 = (f32[136,128]{1,0:T(8,128)S(1)}, f32[136,128]{1,0:T(8,128)S(1)}, u32[]{:S(2)}, u32[]{:S(2)}) collective-permute-start(f32[136,128]{1,0:T(8,128)S(1)} %get-tuple-element.66), channel_id=1, source_target_pairs={{0,8},{2,10},{4,12},{6,14},{8,0},{10,2},{12,4},{14,6},{16,24},{18,... | collective-permute-start | bytes 208904 | tf_op jit(solution)/shard_map/ppermute | solution.py:285
  23.5 7.2 %collective-permute-start.3 = (f32[136,128]{1,0:T(8,128)S(1)}, f32[136,128]{1,0:T(8,128)S(1)}, u32[]{:S(2)}, u32[]{:S(2)}) collective-permute-start(f32[136,128]{1,0:T(8,128)S(1)} %get-tuple-element.67), channel_id=1, source_target_pairs={{0,4},{2,6},{4,0},{6,2},{8,12},{10,14},{12,8},{14,10},{16,20},{18,... | collective-permute-start | bytes 208904 | tf_op jit(solution)/shard_map/ppermute | solution.py:285
  25.3 8.6 %collective-permute-start.20 = (f32[136,128]{1,0:T(8,128)S(1)}, f32[136,128]{1,0:T(8,128)S(1)}, u32[]{:S(2)}, u32[]{:S(2)}) collective-permute-start(f32[136,128]{1,0:T(8,128)S(1)} %row_total_0.1.refs_0_), channel_id=1, source_target_pairs={{0,48},{2,50},{4,52},{6,54},{8,56},{10,58},{12,60},{14,62},{16,32}... | collective-permute-start | bytes 208904 | tf_op jit(solution)/shard_map/ppermute | solution.py:285
  28.2 6.2 %collective-permute-start.19 = (f32[136,128]{1,0:T(8,128)S(1)}, f32[136,128]{1,0:T(8,128)S(1)}, u32[]{:S(2)}, u32[]{:S(2)}) collective-permute-start(f32[136,128]{1,0:T(8,128)S(1)} %row_total_0.1.refs_0_), channel_id=1, source_target_pairs={{0,32},{2,34},{4,36},{6,38},{8,40},{10,42},{12,44},{14,46},{16,48}... | collective-permute-start | bytes 208904 | tf_op jit(solution)/shard_map/ppermute | solution.py:285
  28.5 5.8 %collective-permute-start.18 = (f32[136,128]{1,0:T(8,128)S(1)}, f32[136,128]{1,0:T(8,128)S(1)}, u32[]{:S(2)}, u32[]{:S(2)}) collective-permute-start(f32[136,128]{1,0:T(8,128)S(1)} %row_total_0.1.refs_0_), channel_id=1, source_target_pairs={{0,16},{2,18},{4,20},{6,22},{8,24},{10,26},{12,28},{14,30},{16,0},... | collective-permute-start | bytes 208904 | tf_op jit(solution)/shard_map/ppermute | solution.py:285
  30.8 6.7 %collective-permute-start.6 = (f32[136,128]{1,0:T(8,128)S(1)}, f32[136,128]{1,0:T(8,128)S(1)}, u32[]{:S(2)}, u32[]{:S(2)}) collective-permute-start(f32[136,128]{1,0:T(8,128)S(1)} %row_total_1.1.refs_0_), channel_id=1, source_target_pairs={{0,48},{2,50},{4,52},{6,54},{8,56},{10,58},{12,60},{14,62},{16,32}... | collective-permute-start | bytes 208904 | tf_op jit(solution)/shard_map/ppermute | solution.py:285
  33.6 5.3 %collective-permute-start.5 = (f32[136,128]{1,0:T(8,128)S(1)}, f32[136,128]{1,0:T(8,128)S(1)}, u32[]{:S(2)}, u32[]{:S(2)}) collective-permute-start(f32[136,128]{1,0:T(8,128)S(1)} %row_total_1.1.refs_0_), channel_id=1, source_target_pairs={{0,32},{2,34},{4,36},{6,38},{8,40},{10,42},{12,44},{14,46},{16,48}... | collective-permute-start | bytes 208904 | tf_op jit(solution)/shard_map/ppermute | solution.py:285
  34.0 5.0 %collective-permute-start.4 = (f32[136,128]{1,0:T(8,128)S(1)}, f32[136,128]{1,0:T(8,128)S(1)}, u32[]{:S(2)}, u32[]{:S(2)}) collective-permute-start(f32[136,128]{1,0:T(8,128)S(1)} %row_total_1.1.refs_0_), channel_id=1, source_target_pairs={{0,16},{2,18},{4,20},{6,22},{8,24},{10,26},{12,28},{14,30},{16,0},... | collective-permute-start | bytes 208904 | tf_op jit(solution)/shard_map/ppermute | solution.py:285
  34.4 7.9 %collective-permute-start.23 = (f32[136,128]{1,0:T(8,128)S(1)}, f32[136,128]{1,0:T(8,128)S(1)}, u32[]{:S(2)}, u32[]{:S(2)}) collective-permute-start(f32[136,128]{1,0:T(8,128)S(1)} %get-tuple-element.94), channel_id=1, source_target_pairs={{0,192},{2,194},{4,196},{6,198},{8,200},{10,202},{12,204},{14,206}... | collective-permute-start | bytes 208904 | tf_op jit(solution)/shard_map/ppermute | solution.py:285
  36.9 5.6 %collective-permute-start.22 = (f32[136,128]{1,0:T(8,128)S(1)}, f32[136,128]{1,0:T(8,128)S(1)}, u32[]{:S(2)}, u32[]{:S(2)}) collective-permute-start(f32[136,128]{1,0:T(8,128)S(1)} %get-tuple-element.94), channel_id=1, source_target_pairs={{0,128},{2,130},{4,132},{6,134},{8,136},{10,138},{12,140},{14,142}... | collective-permute-start | bytes 208904 | tf_op jit(solution)/shard_map/ppermute | solution.py:285
  37.5 5.1 %collective-permute-start.21 = (f32[136,128]{1,0:T(8,128)S(1)}, f32[136,128]{1,0:T(8,128)S(1)}, u32[]{:S(2)}, u32[]{:S(2)}) collective-permute-start(f32[136,128]{1,0:T(8,128)S(1)} %get-tuple-element.94), channel_id=1, source_target_pairs={{0,64},{2,66},{4,68},{6,70},{8,72},{10,74},{12,76},{14,78},{16,80}... | collective-permute-start | bytes 208904 | tf_op jit(solution)/shard_map/ppermute | solution.py:285
  39.0 8.6 %collective-permute-start.9 = (f32[136,128]{1,0:T(8,128)S(1)}, f32[136,128]{1,0:T(8,128)S(1)}, u32[]{:S(2)}, u32[]{:S(2)}) collective-permute-start(f32[136,128]{1,0:T(8,128)S(1)} %get-tuple-element.68), channel_id=1, source_target_pairs={{0,192},{2,194},{4,196},{6,198},{8,200},{10,202},{12,204},{14,206}... | collective-permute-start | bytes 208904 | tf_op jit(solution)/shard_map/ppermute | solution.py:285
  41.8 6.6 %collective-permute-start.8 = (f32[136,128]{1,0:T(8,128)S(1)}, f32[136,128]{1,0:T(8,128)S(1)}, u32[]{:S(2)}, u32[]{:S(2)}) collective-permute-start(f32[136,128]{1,0:T(8,128)S(1)} %get-tuple-element.68), channel_id=1, source_target_pairs={{0,128},{2,130},{4,132},{6,134},{8,136},{10,138},{12,140},{14,142}... | collective-permute-start | bytes 208904 | tf_op jit(solution)/shard_map/ppermute | solution.py:285
  42.3 6.1 %collective-permute-start.7 = (f32[136,128]{1,0:T(8,128)S(1)}, f32[136,128]{1,0:T(8,128)S(1)}, u32[]{:S(2)}, u32[]{:S(2)}) collective-permute-start(f32[136,128]{1,0:T(8,128)S(1)} %get-tuple-element.68), channel_id=1, source_target_pairs={{0,64},{2,66},{4,68},{6,70},{8,72},{10,74},{12,76},{14,78},{16,80}... | collective-permute-start | bytes 208904 | tf_op jit(solution)/shard_map/ppermute | solution.py:285
  42.6 20.7 %slice-start = ((s8[8388608]{0:T(1024)(128)(4,1)}), s8[4194304]{0:T(1024)(128)(4,1)S(1)}, s32[]{:S(2)}) async-start(s8[8388608]{0:T(1024)(128)(4,1)} %bitcast.8), calls=%async_computation | async-start | bytes 8388608
  42.7 10.8 %collective-permute-start.24 = (f32[128,128]{1,0:T(8,128)S(1)}, f32[128,128]{1,0:T(8,128)S(1)}, u32[]{:S(2)}, u32[]{:S(2)}) collective-permute-start(f32[128,128]{1,0:T(8,128)S(1)} %get-tuple-element.97), channel_id=1, source_target_pairs={{0,12},{2,14},{4,8},{6,10},{8,4},{10,6},{12,0},{14,2},{16,28},{18,... | collective-permute-start | bytes 196616 | tf_op jit(solution)/shard_map/ppermute | solution.py:285
  44.3 9.9 %collective-permute-start.25 = (f32[128,128]{1,0:T(8,128)S(1)}, f32[128,128]{1,0:T(8,128)S(1)}, u32[]{:S(2)}, u32[]{:S(2)}) collective-permute-start(f32[128,128]{1,0:T(8,128)S(1)} %get-tuple-element.98), channel_id=1, source_target_pairs={{0,8},{2,10},{4,12},{6,14},{8,0},{10,2},{12,4},{14,6},{16,24},{18,... | collective-permute-start | bytes 196616 | tf_op jit(solution)/shard_map/ppermute | solution.py:285
  47.6 6.7 %collective-permute-start.26 = (f32[128,128]{1,0:T(8,128)S(1)}, f32[128,128]{1,0:T(8,128)S(1)}, u32[]{:S(2)}, u32[]{:S(2)}) collective-permute-start(f32[128,128]{1,0:T(8,128)S(1)} %get-tuple-element.99), channel_id=1, source_target_pairs={{0,4},{2,6},{4,0},{6,2},{8,12},{10,14},{12,8},{14,10},{16,20},{18,... | collective-permute-start | bytes 196616 | tf_op jit(solution)/shard_map/ppermute | solution.py:285
  48.4 14.9 %slice-start.1 = ((s8[8388608]{0:T(1024)(128)(4,1)}), s8[4194304]{0:T(1024)(128)(4,1)S(1)}, s32[]{:S(2)}) async-start(s8[8388608]{0:T(1024)(128)(4,1)} %bitcast.8), calls=%async_computation.1 | async-start | bytes 8388608
  48.5 6.9 %collective-permute-start.10 = (f32[128,128]{1,0:T(8,128)S(1)}, f32[128,128]{1,0:T(8,128)S(1)}, u32[]{:S(2)}, u32[]{:S(2)}) collective-permute-start(f32[128,128]{1,0:T(8,128)S(1)} %get-tuple-element.71), channel_id=1, source_target_pairs={{0,12},{2,14},{4,8},{6,10},{8,4},{10,6},{12,0},{14,2},{16,28},{18,... | collective-permute-start | bytes 196616 | tf_op jit(solution)/shard_map/ppermute | solution.py:285
  50.5 7.2 %collective-permute-start.11 = (f32[128,128]{1,0:T(8,128)S(1)}, f32[128,128]{1,0:T(8,128)S(1)}, u32[]{:S(2)}, u32[]{:S(2)}) collective-permute-start(f32[128,128]{1,0:T(8,128)S(1)} %get-tuple-element.72), channel_id=1, source_target_pairs={{0,8},{2,10},{4,12},{6,14},{8,0},{10,2},{12,4},{14,6},{16,24},{18,... | collective-permute-start | bytes 196616 | tf_op jit(solution)/shard_map/ppermute | solution.py:285
  53.5 5.9 %collective-permute-start.12 = (f32[128,128]{1,0:T(8,128)S(1)}, f32[128,128]{1,0:T(8,128)S(1)}, u32[]{:S(2)}, u32[]{:S(2)}) collective-permute-start(f32[128,128]{1,0:T(8,128)S(1)} %get-tuple-element.73), channel_id=1, source_target_pairs={{0,4},{2,6},{4,0},{6,2},{8,12},{10,14},{12,8},{14,10},{16,20},{18,... | collective-permute-start | bytes 196616 | tf_op jit(solution)/shard_map/ppermute | solution.py:285
  54.4 8.9 %collective-permute-start.27 = (f32[512,128]{1,0:T(8,128)S(1)}, f32[512,128]{1,0:T(8,128)S(1)}, u32[]{:S(2)}, u32[]{:S(2)}) collective-permute-start(f32[512,128]{1,0:T(8,128)S(1)} %get-tuple-element.101), channel_id=1, source_target_pairs={{0,2},{2,0},{4,6},{6,4},{8,10},{10,8},{12,14},{14,12},{16,18},{18,... | collective-permute-start | bytes 786440 | tf_op jit(solution)/shard_map/ppermute | solution.py:339
  59.5 10.8 %collective-permute-start.13 = (f32[512,128]{1,0:T(8,128)S(1)}, f32[512,128]{1,0:T(8,128)S(1)}, u32[]{:S(2)}, u32[]{:S(2)}) collective-permute-start(f32[512,128]{1,0:T(8,128)S(1)} %get-tuple-element.74), channel_id=1, source_target_pairs={{0,2},{2,0},{4,6},{6,4},{8,10},{10,8},{12,14},{14,12},{16,18},{18,... | collective-permute-start | bytes 786440 | tf_op jit(solution)/shard_map/ppermute | solution.py:339
  71.0 5.9 %collective-permute-start.28 = (f32[64,2048]{1,0:T(8,128)S(1)}, f32[64,2048]{1,0:T(8,128)S(1)}, u32[]{:S(2)}, u32[]{:S(2)}) collective-permute-start(f32[64,2048]{1,0:T(8,128)S(1)} %get-tuple-element.106), channel_id=1, source_target_pairs={{0,1},{1,0},{2,3},{3,2},{4,5},{5,4},{6,7},{7,6},{8,9},{9,8},{10,11... | collective-permute-start | bytes 1572872 | tf_op jit(solution)/shard_map/ppermute | solution.py:355

commit v7 on v6

--- a/solution.py
+++ b/solution.py
@@ -226,11 +226,15 @@
         so_far, total, normed = refs[5:]
         first_row = w.shape[0]
     else:
-        so_far, mine, other, normed, tile = refs[5:]
+        so_far, total, normed = refs[5:]
         first_row = w.shape[0]
     role = pos[0] & 1
     bases = [(group * 2 + (1 - role if side else role)) * HALF for side in sides]
-    twice = jnp.concatenate([read[...], read[...]], axis=1)
+    tokens = slice(None)
+    if stage >= 2:
+        core = pos[3] if stage == 3 else 1 - pos[3]
+        tokens = pl.ds(pl.multiple_of(core * (W // 2), W // 2), W // 2)
+    twice = jnp.concatenate([read[tokens, :], read[tokens, :]], axis=1)
     for k, base in enumerate(bases):
         for i in range(0, HALF, 2):
             parts = [split(states[k][(i + n) * W : (i + n + 1) * W, :]) for n in range(2)]
@@ -239,26 +243,20 @@
             for n in range(2):
                 head = base + i + n
                 at = rows_of(head)
-                gated = fixed[:, at] + slope[:, at] * carried[:, n * W : (n + 1) * W]
+                gated = fixed[tokens, at] + slope[tokens, at] * carried[:, n * W : (n + 1) * W]
                 meansq = jnp.mean(gated * gated, axis=-1, keepdims=True)
                 value = gated * lax.rsqrt(meansq + 1e-05) * gain[pl.ds(head, 1), :]
                 place = k * ROWS + (i + n) * W
                 normed[:, place : place + W] = value.astype(BF16)
     for at in range(0, w.shape[1], TILE):
         columns = slice(at, at + TILE)
-        part = jnp.zeros((W, TILE), F32) if stage == 0 else so_far[:, columns]
+        part = jnp.zeros((W, TILE), F32) if stage == 0 else so_far[tokens, columns]
         for k, base in enumerate(bases):
             rows = pl.ds(pl.multiple_of(base * W - first_row, ROWS), ROWS)
             part += jnp.dot(
                 normed[:, k * ROWS : (k + 1) * ROWS], w[rows, columns], preferred_element_type=F32
             )
-        if stage < 2:
-            total[:, columns] = part
-        else:
-            half = W // 2
-            tile[...] = part
-            mine[:, columns] = tile[pl.ds(pl.multiple_of(pos[3] * half, half), half), :]
-            other[:, columns] = tile[pl.ds(pl.multiple_of((1 - pos[3]) * half, half), half), :]
+        total[:, columns] = part
     if stage == 0:
         fetch.wait()
 
@@ -339,8 +337,8 @@
         states[g] = lax.ppermute(send, "ctx", partners(1, 1))
 
     def finish(group, sides, stage, parts, w, outs, extra):
-        scratch = [pltpu.VMEM((W, len(sides) * ROWS), BF16)]
-        scratch += [[pltpu.SemaphoreType.DMA(())], [], [pltpu.VMEM((W, TILE), F32)]][stage]
+        scratch = [pltpu.VMEM((W // 2 if stage >= 2 else W, len(sides) * ROWS), BF16)]
+        scratch += [pltpu.SemaphoreType.DMA(())] if stage == 0 else []
         return call(
             functools.partial(finish_kernel, group, sides, stage), outs,
             [VMEM] * (len(sides) + 5 + len(extra)), scratch, name=f"finish_{stage}",
@@ -351,8 +349,10 @@
         [shaped(W, width), shaped(w_out.shape[0] // 2, width, dtype=BF16)], [],
     )
     so_far = finish(1, (0,), 1, [mine[1]], w, shaped(W, width), [so_far])
-    near, far = finish(1, (1,), 2, [states[1]], w, [shaped(W // 2, width)] * 2, [so_far])
-    return (near + lax.ppermute(far, "tp", [(0, 1), (1, 0)])).astype(BF16)
+    far = finish(1, (1,), 2, [states[1]], w, shaped(W // 2, width), [so_far])
+    arrived = lax.ppermute(far, "tp", [(0, 1), (1, 0)])
+    near = finish(1, (1,), 3, [states[1]], w, shaped(W // 2, width), [so_far])
+    return (near + arrived).astype(BF16)
 
 
 def solution(mesh):

time: 77.8 us -> 77.7 us (level)
    pallas_call x3 -> x4, Pallas kernels: 2.91 us -> 3.55 us  [finish(): call(functools.partial(finish_kernel, group, sides, stage), outs, [VMEM]...]
  transfers between devices with their start and end apart: 29 -> 29, of which waited for: 9 -> 9; matrix products, arithmetic and copies ran while one was open for 0% -> 0% of each run, Pallas kernels for 7% -> 8%
where the time goes in v7:
time: 77.7 us
  starting transfers between devices  51.8 us (67%)
  waiting for transfers between devices  16 us (21%)
  Pallas kernels  7.47 us (10%)
  local copies, waits for them, and re-layouts  1.38 us (2%)
    ppermute x24, starting transfers between devices, exchange(): lax.ppermute(value, 'ctx', partners(stride, m))  40.8 us
    ppermute x24, waiting for transfers between devices, exchange(): lax.ppermute(value, 'ctx', partners(stride, m))  7.11 us
    ppermute x2, waiting for transfers between devices, per_device(): states[g] = lax.ppermute(send, 'ctx', partners(1, 1))  5.75 us
    ppermute x1, starting transfers between devices, per_device(): arrived = lax.ppermute(far, 'tp', [(0, 1), (1, 0)])  4.39 us
    ppermute x2, starting transfers between devices, per_device(): states[g] = lax.ppermute(send, 'ctx', partners(1, 1))  3.91 us
    pallas_call x4, Pallas kernels, finish(): call(functools.partial(finish_kernel, group, sides, stage), outs, [VMEM]...  3.55 us
    ppermute x2, starting transfers between devices, per_device(): got[g] = lax.ppermute(send, 'ctx', partners(1, 1))  2.66 us
    ppermute x2, waiting for transfers between devices, per_device(): got[g] = lax.ppermute(send, 'ctx', partners(1, 1))  2.34 us
  transfers between devices with their start and end apart: 29, of which 9 were waited for; matrix products, arithmetic and copies ran while one was open for 0% of the time, Pallas kernels for 8%

profile of v7, /device:TPU:1, one launch (start us, length us, event | category | flops | bytes accessed | tf_op | source)
XLA Modules:
  0.0 77.7 jit_solution(17017128542797245413)
XLA Ops:
  0.1 1.1 %copy-done.5 = bf16[128,16,128]{2,1,0:T(8,128)(2,1)S(1)} copy-done((bf16[128,16,128]{2,1,0:T(8,128)(2,1)S(1)}, bf16[128,16,128]{2,1,0:T(8,128)(2,1)}, u32[]{:S(2)}) %copy-start.5) | copy-done | bytes 524312
  1.1 0.1 copy.14
  1.3 0.8 %local_state_0.1 = (f32[520,128]{1,0:T(8,128)S(1)}, f32[520,128]{1,0:T(8,128)S(1)}) custom-call(f32[128,128]{1,0:T(8,128)S(1)} %lower.1.ones, bf16[128,2048]{1,0:T(8,128)(2,1)S(1)} %bitcast.10, bf16[128,128]{1,0:T(8,128)(2,1)S(1)} %copy-done, f32[16,128]{1,0:T(8,128)S(1)} %copy-done.1), custom_call_target="tpu_custom_call" | custom-call | tf_op jit(solution)/shard_map/local_state_0/pallas_call | solution.py:297
  2.1 2.6 %collective-permute-start.14 = (f32[520,128]{1,0:T(8,128)S(1)}, f32[520,128]{1,0:T(8,128)S(1)}, u32[]{:S(2)}, u32[]{:S(2)}) collective-permute-start(f32[520,128]{1,0:T(8,128)S(1)} %get-tuple-element.87), channel_id=1, source_target_pairs={{0,2},{2,0},{4,6},{6,4},{8,10},{10,8},{12,14},{14,12},{16,18},{18,... | collective-permute-start | bytes 798728 | tf_op jit(solution)/shard_map/ppermute | solution.py:301
  4.6 0.8 %local_state_1.1 = (f32[520,128]{1,0:T(8,128)S(1)}, f32[520,128]{1,0:T(8,128)S(1)}) custom-call(f32[128,128]{1,0:T(8,128)S(1)} %lower.1.ones, bf16[128,2048]{1,0:T(8,128)(2,1)S(1)} %bitcast.11, bf16[128,128]{1,0:T(8,128)(2,1)S(1)} %copy-done, f32[16,128]{1,0:T(8,128)S(1)} %copy-done.1), custom_call_target="tpu_custom_call" | custom-call | tf_op jit(solution)/shard_map/local_state_1/pallas_call | solution.py:297
  5.4 0.1 collective-permute-start
  5.5 0.1 copy.13
  5.7 1.6 %inside.1 = (f32[128,2048]{1,0:T(8,128)S(1)}, f32[128,2048]{1,0:T(8,128)S(1)}, bf16[128,128]{1,0:T(8,128)(2,1)S(1)}, f32[16,128]{1,0:T(8,128)S(1)}) custom-call(f32[16]{0:T(128)S(1)} %copy-done.4, f32[128,128]{1,0:T(8,128)S(1)} %lower.1.ones, bf16[128,2048]{1,0:T(8,128)(2,1)S(1)} %bitcast.12, bf16[128,2048]{1,0:T(8,128)(2,1)S(1)} %bitcast.13, ...), custom_call_target="tpu_custom_call" | custom-call | tf_op jit(solution)/shard_map/inside/pallas_call | solution.py:303
  7.4 2.3 %collective-permute-done.14.got = f32[520,128]{1,0:T(8,128)S(1)} collective-permute-done((f32[520,128]{1,0:T(8,128)S(1)}, f32[520,128]{1,0:T(8,128)S(1)}, u32[]{:S(2)}, u32[]{:S(2)}) %collective-permute-start.14) | collective-permute-done | bytes 266272 | tf_op jit(solution)/shard_map/ppermute | solution.py:301
  9.7 0.1 pair_0.1
  9.8 6.7 %collective-permute-start.15 = (f32[136,128]{1,0:T(8,128)S(1)}, f32[136,128]{1,0:T(8,128)S(1)}, u32[]{:S(2)}, u32[]{:S(2)}) collective-permute-start(f32[136,128]{1,0:T(8,128)S(1)} %get-tuple-element.89), channel_id=1, source_target_pairs={{0,12},{2,14},{4,8},{6,10},{8,4},{10,6},{12,0},{14,2},{16,28},{18,... | collective-permute-start | bytes 208904 | tf_op jit(solution)/shard_map/ppermute | solution.py:283
  16.4 1.0 %collective-permute-start.16 = (f32[136,128]{1,0:T(8,128)S(1)}, f32[136,128]{1,0:T(8,128)S(1)}, u32[]{:S(2)}, u32[]{:S(2)}) collective-permute-start(f32[136,128]{1,0:T(8,128)S(1)} %get-tuple-element.90), channel_id=1, source_target_pairs={{0,8},{2,10},{4,12},{6,14},{8,0},{10,2},{12,4},{14,6},{16,24},{18,... | collective-permute-start | bytes 208904 | tf_op jit(solution)/shard_map/ppermute | solution.py:283
  17.4 1.2 %collective-permute-start.17 = (f32[136,128]{1,0:T(8,128)S(1)}, f32[136,128]{1,0:T(8,128)S(1)}, u32[]{:S(2)}, u32[]{:S(2)}) collective-permute-start(f32[136,128]{1,0:T(8,128)S(1)} %get-tuple-element.91), channel_id=1, source_target_pairs={{0,4},{2,6},{4,0},{6,2},{8,12},{10,14},{12,8},{14,10},{16,20},{18,... | collective-permute-start | bytes 208904 | tf_op jit(solution)/shard_map/ppermute | solution.py:283
  18.6 0.0 collective-permute-done.got
  18.6 0.1 pair_1.1
  18.7 4.0 %collective-permute-start.1 = (f32[136,128]{1,0:T(8,128)S(1)}, f32[136,128]{1,0:T(8,128)S(1)}, u32[]{:S(2)}, u32[]{:S(2)}) collective-permute-start(f32[136,128]{1,0:T(8,128)S(1)} %get-tuple-element.63), channel_id=1, source_target_pairs={{0,12},{2,14},{4,8},{6,10},{8,4},{10,6},{12,0},{14,2},{16,28},{18,... | collective-permute-start | bytes 208904 | tf_op jit(solution)/shard_map/ppermute | solution.py:283
  22.7 0.8 %collective-permute-start.2 = (f32[136,128]{1,0:T(8,128)S(1)}, f32[136,128]{1,0:T(8,128)S(1)}, u32[]{:S(2)}, u32[]{:S(2)}) collective-permute-start(f32[136,128]{1,0:T(8,128)S(1)} %get-tuple-element.64), channel_id=1, source_target_pairs={{0,8},{2,10},{4,12},{6,14},{8,0},{10,2},{12,4},{14,6},{16,24},{18,... | collective-permute-start | bytes 208904 | tf_op jit(solution)/shard_map/ppermute | solution.py:283
  23.5 0.0 collective-permute-done.15.refs_1_.refs_5_
  23.5 1.3 %collective-permute-start.3 = (f32[136,128]{1,0:T(8,128)S(1)}, f32[136,128]{1,0:T(8,128)S(1)}, u32[]{:S(2)}, u32[]{:S(2)}) collective-permute-start(f32[136,128]{1,0:T(8,128)S(1)} %get-tuple-element.65), channel_id=1, source_target_pairs={{0,4},{2,6},{4,0},{6,2},{8,12},{10,14},{12,8},{14,10},{16,20},{18,... | collective-permute-start | bytes 208904 | tf_op jit(solution)/shard_map/ppermute | solution.py:283
  24.9 0.4 collective-permute-done.16.refs_2_.refs_6_
  25.3 2.8 %collective-permute-start.20 = (f32[136,128]{1,0:T(8,128)S(1)}, f32[136,128]{1,0:T(8,128)S(1)}, u32[]{:S(2)}, u32[]{:S(2)}) collective-permute-start(f32[136,128]{1,0:T(8,128)S(1)} %row_total_0.1.refs_0_), channel_id=1, source_target_pairs={{0,48},{2,50},{4,52},{6,54},{8,56},{10,58},{12,60},{14,62},{16,32}... | collective-permute-start | bytes 208904 | tf_op jit(solution)/shard_map/ppermute | solution.py:283
  28.2 0.3 collective-permute-start.19
  28.5 0.0 collective-permute-done.1.refs_1_.refs_5_
  28.5 0.8 collective-permute-start.18
  29.3 1.5 %collective-permute-done.2.refs_2_.refs_6_ = f32[136,128]{1,0:T(8,128)S(1)} collective-permute-done((f32[136,128]{1,0:T(8,128)S(1)}, f32[136,128]{1,0:T(8,128)S(1)}, u32[]{:S(2)}, u32[]{:S(2)}) %collective-permute-start.2) | collective-permute-done | bytes 69664 | tf_op jit(solution)/shard_map/ppermute | solution.py:283
  30.7 0.0 collective-permute-done.3.refs_3_.refs_7_
  30.8 2.8 %collective-permute-start.6 = (f32[136,128]{1,0:T(8,128)S(1)}, f32[136,128]{1,0:T(8,128)S(1)}, u32[]{:S(2)}, u32[]{:S(2)}) collective-permute-start(f32[136,128]{1,0:T(8,128)S(1)} %row_total_1.1.refs_0_), channel_id=1, source_target_pairs={{0,48},{2,50},{4,52},{6,54},{8,56},{10,58},{12,60},{14,62},{16,32}... | collective-permute-start | bytes 208904 | tf_op jit(solution)/shard_map/ppermute | solution.py:283
  33.6 0.3 collective-permute-start.5
  34.0 0.3 collective-permute-start.4
  34.3 0.0 collective-permute-done.19.refs_2_
  34.3 0.0 collective-permute-done.18.refs_1_
  34.3 0.1 plane_0.1
  34.4 2.6 %collective-permute-start.23 = (f32[136,128]{1,0:T(8,128)S(1)}, f32[136,128]{1,0:T(8,128)S(1)}, u32[]{:S(2)}, u32[]{:S(2)}) collective-permute-start(f32[136,128]{1,0:T(8,128)S(1)} %get-tuple-element.92), channel_id=1, source_target_pairs={{0,192},{2,194},{4,196},{6,198},{8,200},{10,202},{12,204},{14,206}... | collective-permute-start | bytes 208904 | tf_op jit(solution)/shard_map/ppermute | solution.py:283
  36.9 0.5 collective-permute-start.22
  37.5 0.0 collective-permute-done.6.refs_3_
  37.5 0.3 collective-permute-start.21
  37.7 1.2 %collective-permute-done.5.refs_2_ = f32[136,128]{1,0:T(8,128)S(1)} collective-permute-done((f32[136,128]{1,0:T(8,128)S(1)}, f32[136,128]{1,0:T(8,128)S(1)}, u32[]{:S(2)}, u32[]{:S(2)}) %collective-permute-start.5) | collective-permute-done | bytes 69664 | tf_op jit(solution)/shard_map/ppermute | solution.py:283
  39.0 0.1 plane_1.1
  39.0 2.7 %collective-permute-start.9 = (f32[136,128]{1,0:T(8,128)S(1)}, f32[136,128]{1,0:T(8,128)S(1)}, u32[]{:S(2)}, u32[]{:S(2)}) collective-permute-start(f32[136,128]{1,0:T(8,128)S(1)} %get-tuple-element.66), channel_id=1, source_target_pairs={{0,192},{2,194},{4,196},{6,198},{8,200},{10,202},{12,204},{14,206}... | collective-permute-start | bytes 208904 | tf_op jit(solution)/shard_map/ppermute | solution.py:283
  41.8 0.5 collective-permute-start.8
  42.3 0.3 collective-permute-start.7
  42.6 0.1 entering_0.1
  42.7 1.7 %collective-permute-start.24 = (f32[128,128]{1,0:T(8,128)S(1)}, f32[128,128]{1,0:T(8,128)S(1)}, u32[]{:S(2)}, u32[]{:S(2)}) collective-permute-start(f32[128,128]{1,0:T(8,128)S(1)} %get-tuple-element.95), channel_id=1, source_target_pairs={{0,12},{2,14},{4,8},{6,10},{8,4},{10,6},{12,0},{14,2},{16,28},{18,... | collective-permute-start | bytes 196616 | tf_op jit(solution)/shard_map/ppermute | solution.py:283
  44.3 3.3 %collective-permute-start.25 = (f32[128,128]{1,0:T(8,128)S(1)}, f32[128,128]{1,0:T(8,128)S(1)}, u32[]{:S(2)}, u32[]{:S(2)}) collective-permute-start(f32[128,128]{1,0:T(8,128)S(1)} %get-tuple-element.96), channel_id=1, source_target_pairs={{0,8},{2,10},{4,12},{6,14},{8,0},{10,2},{12,4},{14,6},{16,24},{18,... | collective-permute-start | bytes 196616 | tf_op jit(solution)/shard_map/ppermute | solution.py:283
  47.6 0.8 %collective-permute-start.26 = (f32[128,128]{1,0:T(8,128)S(1)}, f32[128,128]{1,0:T(8,128)S(1)}, u32[]{:S(2)}, u32[]{:S(2)}) collective-permute-start(f32[128,128]{1,0:T(8,128)S(1)} %get-tuple-element.97), channel_id=1, source_target_pairs={{0,4},{2,6},{4,0},{6,2},{8,12},{10,14},{12,8},{14,10},{16,20},{18,... | collective-permute-start | bytes 196616 | tf_op jit(solution)/shard_map/ppermute | solution.py:283
  48.4 0.1 entering_1.1
  48.5 2.0 %collective-permute-start.10 = (f32[128,128]{1,0:T(8,128)S(1)}, f32[128,128]{1,0:T(8,128)S(1)}, u32[]{:S(2)}, u32[]{:S(2)}) collective-permute-start(f32[128,128]{1,0:T(8,128)S(1)} %get-tuple-element.69), channel_id=1, source_target_pairs={{0,12},{2,14},{4,8},{6,10},{8,4},{10,6},{12,0},{14,2},{16,28},{18,... | collective-permute-start | bytes 196616 | tf_op jit(solution)/shard_map/ppermute | solution.py:283
  50.5 3.0 %collective-permute-start.11 = (f32[128,128]{1,0:T(8,128)S(1)}, f32[128,128]{1,0:T(8,128)S(1)}, u32[]{:S(2)}, u32[]{:S(2)}) collective-permute-start(f32[128,128]{1,0:T(8,128)S(1)} %get-tuple-element.70), channel_id=1, source_target_pairs={{0,8},{2,10},{4,12},{6,14},{8,0},{10,2},{12,4},{14,6},{16,24},{18,... | collective-permute-start | bytes 196616 | tf_op jit(solution)/shard_map/ppermute | solution.py:283
  53.5 0.8 %collective-permute-start.12 = (f32[128,128]{1,0:T(8,128)S(1)}, f32[128,128]{1,0:T(8,128)S(1)}, u32[]{:S(2)}, u32[]{:S(2)}) collective-permute-start(f32[128,128]{1,0:T(8,128)S(1)} %get-tuple-element.71), channel_id=1, source_target_pairs={{0,4},{2,6},{4,0},{6,2},{8,12},{10,14},{12,8},{14,10},{16,20},{18,... | collective-permute-start | bytes 196616 | tf_op jit(solution)/shard_map/ppermute | solution.py:283
  54.3 0.1 spread_0.1
  54.4 1.0 %collective-permute-start.27 = (f32[512,128]{1,0:T(8,128)S(1)}, f32[512,128]{1,0:T(8,128)S(1)}, u32[]{:S(2)}, u32[]{:S(2)}) collective-permute-start(f32[512,128]{1,0:T(8,128)S(1)} %get-tuple-element.99), channel_id=1, source_target_pairs={{0,2},{2,0},{4,6},{6,4},{8,10},{10,8},{12,14},{14,12},{16,18},{18,... | collective-permute-start | bytes 786440 | tf_op jit(solution)/shard_map/ppermute | solution.py:337
  55.4 2.2 %collective-permute-done.11.refs_2_ = f32[128,128]{1,0:T(8,128)S(1)} collective-permute-done((f32[128,128]{1,0:T(8,128)S(1)}, f32[128,128]{1,0:T(8,128)S(1)}, u32[]{:S(2)}, u32[]{:S(2)}) %collective-permute-start.11) | collective-permute-done | bytes 65568 | tf_op jit(solution)/shard_map/ppermute | solution.py:283
  57.6 1.7 %collective-permute-done.12.refs_3_ = f32[128,128]{1,0:T(8,128)S(1)} collective-permute-done((f32[128,128]{1,0:T(8,128)S(1)}, f32[128,128]{1,0:T(8,128)S(1)}, u32[]{:S(2)}, u32[]{:S(2)}) %collective-permute-start.12) | collective-permute-done | bytes 65568 | tf_op jit(solution)/shard_map/ppermute | solution.py:283
  59.4 0.1 spread_1.1
  59.5 2.9 %collective-permute-start.13 = (f32[512,128]{1,0:T(8,128)S(1)}, f32[512,128]{1,0:T(8,128)S(1)}, u32[]{:S(2)}, u32[]{:S(2)}) collective-permute-start(f32[512,128]{1,0:T(8,128)S(1)} %get-tuple-element.72), channel_id=1, source_target_pairs={{0,2},{2,0},{4,6},{6,4},{8,10},{10,8},{12,14},{14,12},{16,18},{18,... | collective-permute-start | bytes 786440 | tf_op jit(solution)/shard_map/ppermute | solution.py:337
  62.3 0.9 %collective-permute-done.27.refs_1_ = f32[512,128]{1,0:T(8,128)S(1)} collective-permute-done((f32[512,128]{1,0:T(8,128)S(1)}, f32[512,128]{1,0:T(8,128)S(1)}, u32[]{:S(2)}, u32[]{:S(2)}) %collective-permute-start.27) | collective-permute-done | bytes 262176 | tf_op jit(solution)/shard_map/ppermute | solution.py:337
  63.3 1.4 %finish_0.1 = (f32[128,2048]{1,0:T(8,128)S(1)}, bf16[1024,2048]{1,0:T(8,128)(2,1)S(1)}) custom-call(f32[512,128]{1,0:T(8,128)S(1)} %get-tuple-element.98.refs_0_, f32[512,128]{1,0:T(8,128)S(1)} %collective-permute-done.27.refs_1_, bf16[128,128]{1,0:T(8,128)(2,1)S(1)} %get-tuple-element.82.refs_2_.refs_1_, f32[128,2048]{1,0:T(8,128)S(1)} %get-tuple-element.83.refs_3_.refs_2_, ...), custom_call_target="tpu_custom_call" | custom-call | tf_op jit(solution)/shard_map/finish_0/pallas_call | solution.py:342
  64.7 0.7 finish_1.1.refs_6_
  65.4 4.8 %collective-permute-done.13.refs_0_ = f32[512,128]{1,0:T(8,128)S(1)} collective-permute-done((f32[512,128]{1,0:T(8,128)S(1)}, f32[512,128]{1,0:T(8,128)S(1)}, u32[]{:S(2)}, u32[]{:S(2)}) %collective-permute-start.13) | collective-permute-done | bytes 262176 | tf_op jit(solution)/shard_map/ppermute | solution.py:337
  70.2 0.7 finish_2.1
  71.0 4.4 %collective-permute-start.28 = (f32[64,2048]{1,0:T(8,128)S(1)}, f32[64,2048]{1,0:T(8,128)S(1)}, u32[]{:S(2)}, u32[]{:S(2)}) collective-permute-start(f32[64,2048]{1,0:T(8,128)S(1)} %finish_2.1), channel_id=1, source_target_pairs={{0,1},{1,0},{2,3},{3,2},{4,5},{5,4},{6,7},{7,6},{8,9},{9,8},{10,11... | collective-permute-start | bytes 1572872 | tf_op jit(solution)/shard_map/ppermute | solution.py:353
  75.3 0.7 finish_3.1
  76.1 0.8 %collective-permute-done.28 = f32[64,2048]{1,0:T(8,128)S(1)} collective-permute-done((f32[64,2048]{1,0:T(8,128)S(1)}, f32[64,2048]{1,0:T(8,128)S(1)}, u32[]{:S(2)}, u32[]{:S(2)}) %collective-permute-start.28) | collective-permute-done | bytes 524320 | tf_op jit(solution)/shard_map/ppermute | solution.py:353
  76.9 0.8 add_convert_fusion
  (34 shorter events, 0.2 us)
Async XLA Ops:
  0.0 5.7 %copy-start.3 = (f32[16,128]{1,0:T(8,128)S(1)}, f32[16,128]{1,0:T(8,128)}, u32[]{:S(2)}) copy-start(f32[16,128]{1,0:T(8,128)} %gain) | copy-start | bytes 24580
  0.0 5.7 %copy-start.4 = (f32[16]{0:T(128)S(1)}, f32[16]{0:T(128)}, u32[]{:S(2)}) copy-start(f32[16]{0:T(128)} %skip) | copy-start | bytes 196
  0.0 1.3 %copy-start.1 = (f32[16,128]{1,0:T(8,128)S(1)}, f32[16,128]{1,0:T(8,128)}, u32[]{:S(2)}) copy-start(f32[16,128]{1,0:T(8,128)} %log_decay.2) | copy-start | bytes 24580
  0.0 5.7 %copy-start.2 = (bf16[128,128]{1,0:T(8,128)(2,1)S(1)}, bf16[128,128]{1,0:T(8,128)(2,1)}, u32[]{:S(2)}) copy-start(bf16[128,128]{1,0:T(8,128)(2,1)} %c) | copy-start | bytes 98308
  0.0 1.3 %copy-start = (bf16[128,128]{1,0:T(8,128)(2,1)S(1)}, bf16[128,128]{1,0:T(8,128)(2,1)}, u32[]{:S(2)}) copy-start(bf16[128,128]{1,0:T(8,128)(2,1)} %b.2) | copy-start | bytes 98308
  0.0 5.5 %copy-start.6 = (bf16[128,16,128]{2,1,0:T(8,128)(2,1)S(1)}, bf16[128,16,128]{2,1,0:T(8,128)(2,1)}, u32[]{:S(2)}) copy-start(bf16[128,16,128]{2,1,0:T(8,128)(2,1)} %param.9) | copy-start | bytes 1572868
  0.0 1.1 %copy-start.5 = (bf16[128,16,128]{2,1,0:T(8,128)(2,1)S(1)}, bf16[128,16,128]{2,1,0:T(8,128)(2,1)}, u32[]{:S(2)}) copy-start(bf16[128,16,128]{2,1,0:T(8,128)(2,1)} %param.8) | copy-start | bytes 1572868
  2.1 7.6 %collective-permute-start.14 = (f32[520,128]{1,0:T(8,128)S(1)}, f32[520,128]{1,0:T(8,128)S(1)}, u32[]{:S(2)}, u32[]{:S(2)}) collective-permute-start(f32[520,128]{1,0:T(8,128)S(1)} %get-tuple-element.87), channel_id=1, source_target_pairs={{0,2},{2,0},{4,6},{6,4},{8,10},{10,8},{12,14},{14,12},{16,18},{18,... | collective-permute-start | bytes 798728 | tf_op jit(solution)/shard_map/ppermute | solution.py:301
  5.4 13.2 %collective-permute-start = (f32[520,128]{1,0:T(8,128)S(1)}, f32[520,128]{1,0:T(8,128)S(1)}, u32[]{:S(2)}, u32[]{:S(2)}) collective-permute-start(f32[520,128]{1,0:T(8,128)S(1)} %get-tuple-element.61), channel_id=1, source_target_pairs={{0,2},{2,0},{4,6},{6,4},{8,10},{10,8},{12,14},{14,12},{16,18},{18,... | collective-permute-start | bytes 798728 | tf_op jit(solution)/shard_map/ppermute | solution.py:301
  9.8 13.8 %collective-permute-start.15 = (f32[136,128]{1,0:T(8,128)S(1)}, f32[136,128]{1,0:T(8,128)S(1)}, u32[]{:S(2)}, u32[]{:S(2)}) collective-permute-start(f32[136,128]{1,0:T(8,128)S(1)} %get-tuple-element.89), channel_id=1, source_target_pairs={{0,12},{2,14},{4,8},{6,10},{8,4},{10,6},{12,0},{14,2},{16,28},{18,... | collective-permute-start | bytes 208904 | tf_op jit(solution)/shard_map/ppermute | solution.py:283
  16.4 8.8 %collective-permute-start.16 = (f32[136,128]{1,0:T(8,128)S(1)}, f32[136,128]{1,0:T(8,128)S(1)}, u32[]{:S(2)}, u32[]{:S(2)}) collective-permute-start(f32[136,128]{1,0:T(8,128)S(1)} %get-tuple-element.90), channel_id=1, source_target_pairs={{0,8},{2,10},{4,12},{6,14},{8,0},{10,2},{12,4},{14,6},{16,24},{18,... | collective-permute-start | bytes 208904 | tf_op jit(solution)/shard_map/ppermute | solution.py:283
  17.4 7.9 %collective-permute-start.17 = (f32[136,128]{1,0:T(8,128)S(1)}, f32[136,128]{1,0:T(8,128)S(1)}, u32[]{:S(2)}, u32[]{:S(2)}) collective-permute-start(f32[136,128]{1,0:T(8,128)S(1)} %get-tuple-element.91), channel_id=1, source_target_pairs={{0,4},{2,6},{4,0},{6,2},{8,12},{10,14},{12,8},{14,10},{16,20},{18,... | collective-permute-start | bytes 208904 | tf_op jit(solution)/shard_map/ppermute | solution.py:283
  18.7 9.8 %collective-permute-start.1 = (f32[136,128]{1,0:T(8,128)S(1)}, f32[136,128]{1,0:T(8,128)S(1)}, u32[]{:S(2)}, u32[]{:S(2)}) collective-permute-start(f32[136,128]{1,0:T(8,128)S(1)} %get-tuple-element.63), channel_id=1, source_target_pairs={{0,12},{2,14},{4,8},{6,10},{8,4},{10,6},{12,0},{14,2},{16,28},{18,... | collective-permute-start | bytes 208904 | tf_op jit(solution)/shard_map/ppermute | solution.py:283
  22.7 8.0 %collective-permute-start.2 = (f32[136,128]{1,0:T(8,128)S(1)}, f32[136,128]{1,0:T(8,128)S(1)}, u32[]{:S(2)}, u32[]{:S(2)}) collective-permute-start(f32[136,128]{1,0:T(8,128)S(1)} %get-tuple-element.64), channel_id=1, source_target_pairs={{0,8},{2,10},{4,12},{6,14},{8,0},{10,2},{12,4},{14,6},{16,24},{18,... | collective-permute-start | bytes 208904 | tf_op jit(solution)/shard_map/ppermute | solution.py:283
  23.5 7.2 %collective-permute-start.3 = (f32[136,128]{1,0:T(8,128)S(1)}, f32[136,128]{1,0:T(8,128)S(1)}, u32[]{:S(2)}, u32[]{:S(2)}) collective-permute-start(f32[136,128]{1,0:T(8,128)S(1)} %get-tuple-element.65), channel_id=1, source_target_pairs={{0,4},{2,6},{4,0},{6,2},{8,12},{10,14},{12,8},{14,10},{16,20},{18,... | collective-permute-start | bytes 208904 | tf_op jit(solution)/shard_map/ppermute | solution.py:283
  25.3 8.6 %collective-permute-start.20 = (f32[136,128]{1,0:T(8,128)S(1)}, f32[136,128]{1,0:T(8,128)S(1)}, u32[]{:S(2)}, u32[]{:S(2)}) collective-permute-start(f32[136,128]{1,0:T(8,128)S(1)} %row_total_0.1.refs_0_), channel_id=1, source_target_pairs={{0,48},{2,50},{4,52},{6,54},{8,56},{10,58},{12,60},{14,62},{16,32}... | collective-permute-start | bytes 208904 | tf_op jit(solution)/shard_map/ppermute | solution.py:283
  28.2 6.2 %collective-permute-start.19 = (f32[136,128]{1,0:T(8,128)S(1)}, f32[136,128]{1,0:T(8,128)S(1)}, u32[]{:S(2)}, u32[]{:S(2)}) collective-permute-start(f32[136,128]{1,0:T(8,128)S(1)} %row_total_0.1.refs_0_), channel_id=1, source_target_pairs={{0,32},{2,34},{4,36},{6,38},{8,40},{10,42},{12,44},{14,46},{16,48}... | collective-permute-start | bytes 208904 | tf_op jit(solution)/shard_map/ppermute | solution.py:283
  28.5 5.8 %collective-permute-start.18 = (f32[136,128]{1,0:T(8,128)S(1)}, f32[136,128]{1,0:T(8,128)S(1)}, u32[]{:S(2)}, u32[]{:S(2)}) collective-permute-start(f32[136,128]{1,0:T(8,128)S(1)} %row_total_0.1.refs_0_), channel_id=1, source_target_pairs={{0,16},{2,18},{4,20},{6,22},{8,24},{10,26},{12,28},{14,30},{16,0},... | collective-permute-start | bytes 208904 | tf_op jit(solution)/shard_map/ppermute | solution.py:283
  30.8 6.7 %collective-permute-start.6 = (f32[136,128]{1,0:T(8,128)S(1)}, f32[136,128]{1,0:T(8,128)S(1)}, u32[]{:S(2)}, u32[]{:S(2)}) collective-permute-start(f32[136,128]{1,0:T(8,128)S(1)} %row_total_1.1.refs_0_), channel_id=1, source_target_pairs={{0,48},{2,50},{4,52},{6,54},{8,56},{10,58},{12,60},{14,62},{16,32}... | collective-permute-start | bytes 208904 | tf_op jit(solution)/shard_map/ppermute | solution.py:283
  33.6 5.3 %collective-permute-start.5 = (f32[136,128]{1,0:T(8,128)S(1)}, f32[136,128]{1,0:T(8,128)S(1)}, u32[]{:S(2)}, u32[]{:S(2)}) collective-permute-start(f32[136,128]{1,0:T(8,128)S(1)} %row_total_1.1.refs_0_), channel_id=1, source_target_pairs={{0,32},{2,34},{4,36},{6,38},{8,40},{10,42},{12,44},{14,46},{16,48}... | collective-permute-start | bytes 208904 | tf_op jit(solution)/shard_map/ppermute | solution.py:283
  34.0 5.0 %collective-permute-start.4 = (f32[136,128]{1,0:T(8,128)S(1)}, f32[136,128]{1,0:T(8,128)S(1)}, u32[]{:S(2)}, u32[]{:S(2)}) collective-permute-start(f32[136,128]{1,0:T(8,128)S(1)} %row_total_1.1.refs_0_), channel_id=1, source_target_pairs={{0,16},{2,18},{4,20},{6,22},{8,24},{10,26},{12,28},{14,30},{16,0},... | collective-permute-start | bytes 208904 | tf_op jit(solution)/shard_map/ppermute | solution.py:283
  34.4 7.9 %collective-permute-start.23 = (f32[136,128]{1,0:T(8,128)S(1)}, f32[136,128]{1,0:T(8,128)S(1)}, u32[]{:S(2)}, u32[]{:S(2)}) collective-permute-start(f32[136,128]{1,0:T(8,128)S(1)} %get-tuple-element.92), channel_id=1, source_target_pairs={{0,192},{2,194},{4,196},{6,198},{8,200},{10,202},{12,204},{14,206}... | collective-permute-start | bytes 208904 | tf_op jit(solution)/shard_map/ppermute | solution.py:283
  36.9 5.6 %collective-permute-start.22 = (f32[136,128]{1,0:T(8,128)S(1)}, f32[136,128]{1,0:T(8,128)S(1)}, u32[]{:S(2)}, u32[]{:S(2)}) collective-permute-start(f32[136,128]{1,0:T(8,128)S(1)} %get-tuple-element.92), channel_id=1, source_target_pairs={{0,128},{2,130},{4,132},{6,134},{8,136},{10,138},{12,140},{14,142}... | collective-permute-start | bytes 208904 | tf_op jit(solution)/shard_map/ppermute | solution.py:283
  37.5 5.1 %collective-permute-start.21 = (f32[136,128]{1,0:T(8,128)S(1)}, f32[136,128]{1,0:T(8,128)S(1)}, u32[]{:S(2)}, u32[]{:S(2)}) collective-permute-start(f32[136,128]{1,0:T(8,128)S(1)} %get-tuple-element.92), channel_id=1, source_target_pairs={{0,64},{2,66},{4,68},{6,70},{8,72},{10,74},{12,76},{14,78},{16,80}... | collective-permute-start | bytes 208904 | tf_op jit(solution)/shard_map/ppermute | solution.py:283
  39.0 8.6 %collective-permute-start.9 = (f32[136,128]{1,0:T(8,128)S(1)}, f32[136,128]{1,0:T(8,128)S(1)}, u32[]{:S(2)}, u32[]{:S(2)}) collective-permute-start(f32[136,128]{1,0:T(8,128)S(1)} %get-tuple-element.66), channel_id=1, source_target_pairs={{0,192},{2,194},{4,196},{6,198},{8,200},{10,202},{12,204},{14,206}... | collective-permute-start | bytes 208904 | tf_op jit(solution)/shard_map/ppermute | solution.py:283
  41.8 6.6 %collective-permute-start.8 = (f32[136,128]{1,0:T(8,128)S(1)}, f32[136,128]{1,0:T(8,128)S(1)}, u32[]{:S(2)}, u32[]{:S(2)}) collective-permute-start(f32[136,128]{1,0:T(8,128)S(1)} %get-tuple-element.66), channel_id=1, source_target_pairs={{0,128},{2,130},{4,132},{6,134},{8,136},{10,138},{12,140},{14,142}... | collective-permute-start | bytes 208904 | tf_op jit(solution)/shard_map/ppermute | solution.py:283
  42.3 6.1 %collective-permute-start.7 = (f32[136,128]{1,0:T(8,128)S(1)}, f32[136,128]{1,0:T(8,128)S(1)}, u32[]{:S(2)}, u32[]{:S(2)}) collective-permute-start(f32[136,128]{1,0:T(8,128)S(1)} %get-tuple-element.66), channel_id=1, source_target_pairs={{0,64},{2,66},{4,68},{6,70},{8,72},{10,74},{12,76},{14,78},{16,80}... | collective-permute-start | bytes 208904 | tf_op jit(solution)/shard_map/ppermute | solution.py:283
  42.6 20.7 %slice-start = ((s8[8388608]{0:T(1024)(128)(4,1)}), s8[4194304]{0:T(1024)(128)(4,1)S(1)}, s32[]{:S(2)}) async-start(s8[8388608]{0:T(1024)(128)(4,1)} %bitcast.8), calls=%async_computation | async-start | bytes 8388608
  42.7 10.8 %collective-permute-start.24 = (f32[128,128]{1,0:T(8,128)S(1)}, f32[128,128]{1,0:T(8,128)S(1)}, u32[]{:S(2)}, u32[]{:S(2)}) collective-permute-start(f32[128,128]{1,0:T(8,128)S(1)} %get-tuple-element.95), channel_id=1, source_target_pairs={{0,12},{2,14},{4,8},{6,10},{8,4},{10,6},{12,0},{14,2},{16,28},{18,... | collective-permute-start | bytes 196616 | tf_op jit(solution)/shard_map/ppermute | solution.py:283
  44.3 9.9 %collective-permute-start.25 = (f32[128,128]{1,0:T(8,128)S(1)}, f32[128,128]{1,0:T(8,128)S(1)}, u32[]{:S(2)}, u32[]{:S(2)}) collective-permute-start(f32[128,128]{1,0:T(8,128)S(1)} %get-tuple-element.96), channel_id=1, source_target_pairs={{0,8},{2,10},{4,12},{6,14},{8,0},{10,2},{12,4},{14,6},{16,24},{18,... | collective-permute-start | bytes 196616 | tf_op jit(solution)/shard_map/ppermute | solution.py:283
  47.6 6.7 %collective-permute-start.26 = (f32[128,128]{1,0:T(8,128)S(1)}, f32[128,128]{1,0:T(8,128)S(1)}, u32[]{:S(2)}, u32[]{:S(2)}) collective-permute-start(f32[128,128]{1,0:T(8,128)S(1)} %get-tuple-element.97), channel_id=1, source_target_pairs={{0,4},{2,6},{4,0},{6,2},{8,12},{10,14},{12,8},{14,10},{16,20},{18,... | collective-permute-start | bytes 196616 | tf_op jit(solution)/shard_map/ppermute | solution.py:283
  48.4 14.9 %slice-start.1 = ((s8[8388608]{0:T(1024)(128)(4,1)}), s8[4194304]{0:T(1024)(128)(4,1)S(1)}, s32[]{:S(2)}) async-start(s8[8388608]{0:T(1024)(128)(4,1)} %bitcast.8), calls=%async_computation.1 | async-start | bytes 8388608
  48.5 6.9 %collective-permute-start.10 = (f32[128,128]{1,0:T(8,128)S(1)}, f32[128,128]{1,0:T(8,128)S(1)}, u32[]{:S(2)}, u32[]{:S(2)}) collective-permute-start(f32[128,128]{1,0:T(8,128)S(1)} %get-tuple-element.69), channel_id=1, source_target_pairs={{0,12},{2,14},{4,8},{6,10},{8,4},{10,6},{12,0},{14,2},{16,28},{18,... | collective-permute-start | bytes 196616 | tf_op jit(solution)/shard_map/ppermute | solution.py:283
  50.5 7.2 %collective-permute-start.11 = (f32[128,128]{1,0:T(8,128)S(1)}, f32[128,128]{1,0:T(8,128)S(1)}, u32[]{:S(2)}, u32[]{:S(2)}) collective-permute-start(f32[128,128]{1,0:T(8,128)S(1)} %get-tuple-element.70), channel_id=1, source_target_pairs={{0,8},{2,10},{4,12},{6,14},{8,0},{10,2},{12,4},{14,6},{16,24},{18,... | collective-permute-start | bytes 196616 | tf_op jit(solution)/shard_map/ppermute | solution.py:283
  53.5 5.9 %collective-permute-start.12 = (f32[128,128]{1,0:T(8,128)S(1)}, f32[128,128]{1,0:T(8,128)S(1)}, u32[]{:S(2)}, u32[]{:S(2)}) collective-permute-start(f32[128,128]{1,0:T(8,128)S(1)} %get-tuple-element.71), channel_id=1, source_target_pairs={{0,4},{2,6},{4,0},{6,2},{8,12},{10,14},{12,8},{14,10},{16,20},{18,... | collective-permute-start | bytes 196616 | tf_op jit(solution)/shard_map/ppermute | solution.py:283
  54.4 8.9 %collective-permute-start.27 = (f32[512,128]{1,0:T(8,128)S(1)}, f32[512,128]{1,0:T(8,128)S(1)}, u32[]{:S(2)}, u32[]{:S(2)}) collective-permute-start(f32[512,128]{1,0:T(8,128)S(1)} %get-tuple-element.99), channel_id=1, source_target_pairs={{0,2},{2,0},{4,6},{6,4},{8,10},{10,8},{12,14},{14,12},{16,18},{18,... | collective-permute-start | bytes 786440 | tf_op jit(solution)/shard_map/ppermute | solution.py:337
  59.5 10.8 %collective-permute-start.13 = (f32[512,128]{1,0:T(8,128)S(1)}, f32[512,128]{1,0:T(8,128)S(1)}, u32[]{:S(2)}, u32[]{:S(2)}) collective-permute-start(f32[512,128]{1,0:T(8,128)S(1)} %get-tuple-element.72), channel_id=1, source_target_pairs={{0,2},{2,0},{4,6},{6,4},{8,10},{10,8},{12,14},{14,12},{16,18},{18,... | collective-permute-start | bytes 786440 | tf_op jit(solution)/shard_map/ppermute | solution.py:337
  71.0 5.9 %collective-permute-start.28 = (f32[64,2048]{1,0:T(8,128)S(1)}, f32[64,2048]{1,0:T(8,128)S(1)}, u32[]{:S(2)}, u32[]{:S(2)}) collective-permute-start(f32[64,2048]{1,0:T(8,128)S(1)} %finish_2.1), channel_id=1, source_target_pairs={{0,1},{1,0},{2,3},{3,2},{4,5},{5,4},{6,7},{7,6},{8,9},{9,8},{10,11... | collective-permute-start | bytes 1572872 | tf_op jit(solution)/shard_map/ppermute | solution.py:353

commit v8 on v6

--- a/solution.py
+++ b/solution.py
@@ -227,6 +227,7 @@
         first_row = w.shape[0]
     else:
         so_far, mine, other, normed, tile = refs[5:]
+        left = w.shape[1] // 2
         first_row = w.shape[0]
     role = pos[0] & 1
     bases = [(group * 2 + (1 - role if side else role)) * HALF for side in sides]
@@ -244,7 +245,7 @@
                 value = gated * lax.rsqrt(meansq + 1e-05) * gain[pl.ds(head, 1), :]
                 place = k * ROWS + (i + n) * W
                 normed[:, place : place + W] = value.astype(BF16)
-    for at in range(0, w.shape[1], TILE):
+    for at in range(0, w.shape[1] if stage < 2 else left, TILE):
         columns = slice(at, at + TILE)
         part = jnp.zeros((W, TILE), F32) if stage == 0 else so_far[:, columns]
         for k, base in enumerate(bases):
@@ -263,6 +264,25 @@
         fetch.wait()
 
 
+def right_kernel(normed, w, so_far, mine, other, tile):
+    pos = position()
+    half, left = W // 2, mine.shape[1]
+    rows = pl.ds(pl.multiple_of((1 - (pos[0] & 1)) * ROWS, ROWS), ROWS)
+    for at in range(0, left, TILE):
+        columns, source = slice(at, at + TILE), slice(left + at, left + at + TILE)
+        tile[...] = so_far[:, source] + jnp.dot(
+            normed[...], w[rows, source], preferred_element_type=F32
+        )
+        mine[:, columns] = tile[pl.ds(pl.multiple_of(pos[3] * half, half), half), :]
+        other[:, columns] = tile[pl.ds(pl.multiple_of((1 - pos[3]) * half, half), half), :]
+
+
+def add_kernel(near_left, near_right, left, right, out):
+    middle = out.shape[1] // 2
+    out[:, :middle] = (near_left[...] + left[...]).astype(BF16)
+    out[:, middle:] = (near_right[...] + right[...]).astype(BF16)
+
+
 def call(kernel, outs, specs, scratch=(), name=None, grant=16, work=0):
     return pl.pallas_call(
         kernel,
@@ -339,7 +359,7 @@
         states[g] = lax.ppermute(send, "ctx", partners(1, 1))
 
     def finish(group, sides, stage, parts, w, outs, extra):
-        scratch = [pltpu.VMEM((W, len(sides) * ROWS), BF16)]
+        scratch = [pltpu.VMEM((W, len(sides) * ROWS), BF16)] if stage < 2 else []
         scratch += [[pltpu.SemaphoreType.DMA(())], [], [pltpu.VMEM((W, TILE), F32)]][stage]
         return call(
             functools.partial(finish_kernel, group, sides, stage), outs,
@@ -351,8 +371,19 @@
         [shaped(W, width), shaped(w_out.shape[0] // 2, width, dtype=BF16)], [],
     )
     so_far = finish(1, (0,), 1, [mine[1]], w, shaped(W, width), [so_far])
-    near, far = finish(1, (1,), 2, [states[1]], w, [shaped(W // 2, width)] * 2, [so_far])
-    return (near + lax.ppermute(far, "tp", [(0, 1), (1, 0)])).astype(BF16)
+    quarter = shaped(W // 2, width // 2)
+    swap = [(0, 1), (1, 0)]
+    near_left, far_left, normed = finish(
+        1, (1,), 2, [states[1]], w, [quarter, quarter, shaped(W, ROWS, dtype=BF16)], [so_far]
+    )
+    left = lax.ppermute(far_left, "tp", swap)
+    near_right, far_right = call(
+        right_kernel, [quarter] * 2, [VMEM] * 3, [pltpu.VMEM((W, TILE), F32)], name="finish_right"
+    )(normed, w, so_far)
+    right = lax.ppermute(far_right, "tp", swap)
+    return call(add_kernel, shaped(W // 2, width, dtype=BF16), [VMEM] * 4, name="add")(
+        near_left, near_right, left, right
+    )
 
 
 def solution(mesh):

time: 77.8 us -> 78 us (level)
  Pallas kernels: 6.83 us -> 7.76 us
    pallas_call x0 -> x2, Pallas kernels: none -> 1.12 us  [the longest x1 0.75 us: per_device(): call(add_kernel, shaped(W // 2, width, dtype=BF16), [VMEM] * 4, name='add')]
    ppermute x1 -> x2, starting transfers between devices: 4.39 us -> 4.49 us  [the longest x1 4.39 us: per_device(): right = lax.ppermute(far_right, 'tp', swap)]
  transfers between devices with their start and end apart: 29 -> 30, of which waited for: 9 -> 10; matrix products, arithmetic and copies ran while one was open for 0% -> 0% of each run, Pallas kernels for 7% -> 7%
where the time goes in v8:
time: 78 us; the launch traced here: 77.9 us
  starting transfers between devices  51.9 us (67%)
  waiting for transfers between devices  16.6 us (21%)
  Pallas kernels  7.76 us (10%)
  local copies, waits for them, and re-layouts  1.38 us (2%)
    ppermute x24, starting transfers between devices, exchange(): lax.ppermute(value, 'ctx', partners(stride, m))  40.8 us
    ppermute x24, waiting for transfers between devices, exchange(): lax.ppermute(value, 'ctx', partners(stride, m))  7.11 us
    ppermute x2, waiting for transfers between devices, per_device(): states[g] = lax.ppermute(send, 'ctx', partners(1, 1))  5.74 us
    ppermute x1, starting transfers between devices, per_device(): right = lax.ppermute(far_right, 'tp', swap)  4.39 us
    ppermute x2, starting transfers between devices, per_device(): states[g] = lax.ppermute(send, 'ctx', partners(1, 1))  3.91 us
    pallas_call x3, Pallas kernels, finish(): call(functools.partial(finish_kernel, group, sides, stage), outs, [VMEM]...  2.72 us
    ppermute x2, starting transfers between devices, per_device(): got[g] = lax.ppermute(send, 'ctx', partners(1, 1))  2.66 us
    ppermute x2, waiting for transfers between devices, per_device(): got[g] = lax.ppermute(send, 'ctx', partners(1, 1))  2.34 us
  transfers between devices with their start and end apart: 30, of which 10 were waited for; matrix products, arithmetic and copies ran while one was open for 0% of the time, Pallas kernels for 7%

profile of v8, /device:TPU:1, one launch (start us, length us, event | category | flops | bytes accessed | tf_op | source)
XLA Modules:
  0.0 77.9 jit_solution(3655413862246627232)
XLA Ops:
  0.1 1.1 %copy-done.5 = bf16[128,16,128]{2,1,0:T(8,128)(2,1)S(1)} copy-done((bf16[128,16,128]{2,1,0:T(8,128)(2,1)S(1)}, bf16[128,16,128]{2,1,0:T(8,128)(2,1)}, u32[]{:S(2)}) %copy-start.5) | copy-done | bytes 524312
  1.1 0.1 copy.14
  1.3 0.8 %local_state_0.1 = (f32[520,128]{1,0:T(8,128)S(1)}, f32[520,128]{1,0:T(8,128)S(1)}) custom-call(f32[128,128]{1,0:T(8,128)S(1)} %lower.1.ones, bf16[128,2048]{1,0:T(8,128)(2,1)S(1)} %bitcast.10, bf16[128,128]{1,0:T(8,128)(2,1)S(1)} %copy-done, f32[16,128]{1,0:T(8,128)S(1)} %copy-done.1), custom_call_target="tpu_custom_call" | custom-call | tf_op jit(solution)/shard_map/local_state_0/pallas_call | solution.py:319
  2.1 2.6 %collective-permute-start.14 = (f32[520,128]{1,0:T(8,128)S(1)}, f32[520,128]{1,0:T(8,128)S(1)}, u32[]{:S(2)}, u32[]{:S(2)}) collective-permute-start(f32[520,128]{1,0:T(8,128)S(1)} %get-tuple-element.92), channel_id=1, source_target_pairs={{0,2},{2,0},{4,6},{6,4},{8,10},{10,8},{12,14},{14,12},{16,18},{18,... | collective-permute-start | bytes 798728 | tf_op jit(solution)/shard_map/ppermute | solution.py:323
  4.6 0.8 local_state_1.1
  5.4 0.1 collective-permute-start
  5.5 0.1 copy.13
  5.7 1.6 %inside.1 = (f32[128,2048]{1,0:T(8,128)S(1)}, f32[128,2048]{1,0:T(8,128)S(1)}, bf16[128,128]{1,0:T(8,128)(2,1)S(1)}, f32[16,128]{1,0:T(8,128)S(1)}) custom-call(f32[16]{0:T(128)S(1)} %copy-done.4, f32[128,128]{1,0:T(8,128)S(1)} %lower.1.ones, bf16[128,2048]{1,0:T(8,128)(2,1)S(1)} %bitcast.12, bf16[128,2048]{1,0:T(8,128)(2,1)S(1)} %bitcast.13, ...), custom_call_target="tpu_custom_call" | custom-call | tf_op jit(solution)/shard_map/inside/pallas_call | solution.py:325
  7.4 2.3 %collective-permute-done.14.got = f32[520,128]{1,0:T(8,128)S(1)} collective-permute-done((f32[520,128]{1,0:T(8,128)S(1)}, f32[520,128]{1,0:T(8,128)S(1)}, u32[]{:S(2)}, u32[]{:S(2)}) %collective-permute-start.14) | collective-permute-done | bytes 266272 | tf_op jit(solution)/shard_map/ppermute | solution.py:323
  9.7 0.1 pair_0.1
  9.8 6.7 %collective-permute-start.15 = (f32[136,128]{1,0:T(8,128)S(1)}, f32[136,128]{1,0:T(8,128)S(1)}, u32[]{:S(2)}, u32[]{:S(2)}) collective-permute-start(f32[136,128]{1,0:T(8,128)S(1)} %get-tuple-element.94), channel_id=1, source_target_pairs={{0,12},{2,14},{4,8},{6,10},{8,4},{10,6},{12,0},{14,2},{16,28},{18,... | collective-permute-start | bytes 208904 | tf_op jit(solution)/shard_map/ppermute | solution.py:305
  16.4 1.0 %collective-permute-start.16 = (f32[136,128]{1,0:T(8,128)S(1)}, f32[136,128]{1,0:T(8,128)S(1)}, u32[]{:S(2)}, u32[]{:S(2)}) collective-permute-start(f32[136,128]{1,0:T(8,128)S(1)} %get-tuple-element.95), channel_id=1, source_target_pairs={{0,8},{2,10},{4,12},{6,14},{8,0},{10,2},{12,4},{14,6},{16,24},{18,... | collective-permute-start | bytes 208904 | tf_op jit(solution)/shard_map/ppermute | solution.py:305
  17.4 1.2 %collective-permute-start.17 = (f32[136,128]{1,0:T(8,128)S(1)}, f32[136,128]{1,0:T(8,128)S(1)}, u32[]{:S(2)}, u32[]{:S(2)}) collective-permute-start(f32[136,128]{1,0:T(8,128)S(1)} %get-tuple-element.96), channel_id=1, source_target_pairs={{0,4},{2,6},{4,0},{6,2},{8,12},{10,14},{12,8},{14,10},{16,20},{18,... | collective-permute-start | bytes 208904 | tf_op jit(solution)/shard_map/ppermute | solution.py:305
  18.6 0.0 collective-permute-done.got
  18.6 0.1 pair_1.1
  18.7 4.0 %collective-permute-start.1 = (f32[136,128]{1,0:T(8,128)S(1)}, f32[136,128]{1,0:T(8,128)S(1)}, u32[]{:S(2)}, u32[]{:S(2)}) collective-permute-start(f32[136,128]{1,0:T(8,128)S(1)} %get-tuple-element.68), channel_id=1, source_target_pairs={{0,12},{2,14},{4,8},{6,10},{8,4},{10,6},{12,0},{14,2},{16,28},{18,... | collective-permute-start | bytes 208904 | tf_op jit(solution)/shard_map/ppermute | solution.py:305
  22.7 0.8 %collective-permute-start.2 = (f32[136,128]{1,0:T(8,128)S(1)}, f32[136,128]{1,0:T(8,128)S(1)}, u32[]{:S(2)}, u32[]{:S(2)}) collective-permute-start(f32[136,128]{1,0:T(8,128)S(1)} %get-tuple-element.69), channel_id=1, source_target_pairs={{0,8},{2,10},{4,12},{6,14},{8,0},{10,2},{12,4},{14,6},{16,24},{18,... | collective-permute-start | bytes 208904 | tf_op jit(solution)/shard_map/ppermute | solution.py:305
  23.5 0.0 collective-permute-done.15.refs_1_.refs_5_
  23.5 1.3 %collective-permute-start.3 = (f32[136,128]{1,0:T(8,128)S(1)}, f32[136,128]{1,0:T(8,128)S(1)}, u32[]{:S(2)}, u32[]{:S(2)}) collective-permute-start(f32[136,128]{1,0:T(8,128)S(1)} %get-tuple-element.70), channel_id=1, source_target_pairs={{0,4},{2,6},{4,0},{6,2},{8,12},{10,14},{12,8},{14,10},{16,20},{18,... | collective-permute-start | bytes 208904 | tf_op jit(solution)/shard_map/ppermute | solution.py:305
  24.9 0.4 collective-permute-done.16.refs_2_.refs_6_
  25.3 2.8 %collective-permute-start.20 = (f32[136,128]{1,0:T(8,128)S(1)}, f32[136,128]{1,0:T(8,128)S(1)}, u32[]{:S(2)}, u32[]{:S(2)}) collective-permute-start(f32[136,128]{1,0:T(8,128)S(1)} %row_total_0.1.refs_0_), channel_id=1, source_target_pairs={{0,48},{2,50},{4,52},{6,54},{8,56},{10,58},{12,60},{14,62},{16,32}... | collective-permute-start | bytes 208904 | tf_op jit(solution)/shard_map/ppermute | solution.py:305
  28.2 0.3 collective-permute-start.19
  28.5 0.0 collective-permute-done.1.refs_1_.refs_5_
  28.5 0.8 collective-permute-start.18
  29.3 1.5 %collective-permute-done.2.refs_2_.refs_6_ = f32[136,128]{1,0:T(8,128)S(1)} collective-permute-done((f32[136,128]{1,0:T(8,128)S(1)}, f32[136,128]{1,0:T(8,128)S(1)}, u32[]{:S(2)}, u32[]{:S(2)}) %collective-permute-start.2) | collective-permute-done | bytes 69664 | tf_op jit(solution)/shard_map/ppermute | solution.py:305
  30.7 0.0 collective-permute-done.3.refs_3_.refs_7_
  30.8 2.8 %collective-permute-start.6 = (f32[136,128]{1,0:T(8,128)S(1)}, f32[136,128]{1,0:T(8,128)S(1)}, u32[]{:S(2)}, u32[]{:S(2)}) collective-permute-start(f32[136,128]{1,0:T(8,128)S(1)} %row_total_1.1.refs_0_), channel_id=1, source_target_pairs={{0,48},{2,50},{4,52},{6,54},{8,56},{10,58},{12,60},{14,62},{16,32}... | collective-permute-start | bytes 208904 | tf_op jit(solution)/shard_map/ppermute | solution.py:305
  33.6 0.3 collective-permute-start.5
  34.0 0.3 collective-permute-start.4
  34.3 0.0 collective-permute-done.19.refs_2_
  34.3 0.1 plane_0.1
  34.4 2.6 %collective-permute-start.23 = (f32[136,128]{1,0:T(8,128)S(1)}, f32[136,128]{1,0:T(8,128)S(1)}, u32[]{:S(2)}, u32[]{:S(2)}) collective-permute-start(f32[136,128]{1,0:T(8,128)S(1)} %get-tuple-element.97), channel_id=1, source_target_pairs={{0,192},{2,194},{4,196},{6,198},{8,200},{10,202},{12,204},{14,206}... | collective-permute-start | bytes 208904 | tf_op jit(solution)/shard_map/ppermute | solution.py:305
  36.9 0.5 collective-permute-start.22
  37.5 0.3 collective-permute-start.21
  37.7 1.2 %collective-permute-done.5.refs_2_ = f32[136,128]{1,0:T(8,128)S(1)} collective-permute-done((f32[136,128]{1,0:T(8,128)S(1)}, f32[136,128]{1,0:T(8,128)S(1)}, u32[]{:S(2)}, u32[]{:S(2)}) %collective-permute-start.5) | collective-permute-done | bytes 69664 | tf_op jit(solution)/shard_map/ppermute | solution.py:305
  39.0 0.1 plane_1.1
  39.0 2.7 %collective-permute-start.9 = (f32[136,128]{1,0:T(8,128)S(1)}, f32[136,128]{1,0:T(8,128)S(1)}, u32[]{:S(2)}, u32[]{:S(2)}) collective-permute-start(f32[136,128]{1,0:T(8,128)S(1)} %get-tuple-element.71), channel_id=1, source_target_pairs={{0,192},{2,194},{4,196},{6,198},{8,200},{10,202},{12,204},{14,206}... | collective-permute-start | bytes 208904 | tf_op jit(solution)/shard_map/ppermute | solution.py:305
  41.8 0.5 collective-permute-start.8
  42.3 0.3 collective-permute-start.7
  42.6 0.1 entering_0.1
  42.7 1.7 %collective-permute-start.24 = (f32[128,128]{1,0:T(8,128)S(1)}, f32[128,128]{1,0:T(8,128)S(1)}, u32[]{:S(2)}, u32[]{:S(2)}) collective-permute-start(f32[128,128]{1,0:T(8,128)S(1)} %get-tuple-element.100), channel_id=1, source_target_pairs={{0,12},{2,14},{4,8},{6,10},{8,4},{10,6},{12,0},{14,2},{16,28},{18,... | collective-permute-start | bytes 196616 | tf_op jit(solution)/shard_map/ppermute | solution.py:305
  44.3 3.3 %collective-permute-start.25 = (f32[128,128]{1,0:T(8,128)S(1)}, f32[128,128]{1,0:T(8,128)S(1)}, u32[]{:S(2)}, u32[]{:S(2)}) collective-permute-start(f32[128,128]{1,0:T(8,128)S(1)} %get-tuple-element.101), channel_id=1, source_target_pairs={{0,8},{2,10},{4,12},{6,14},{8,0},{10,2},{12,4},{14,6},{16,24},{18,... | collective-permute-start | bytes 196616 | tf_op jit(solution)/shard_map/ppermute | solution.py:305
  47.6 0.8 %collective-permute-start.26 = (f32[128,128]{1,0:T(8,128)S(1)}, f32[128,128]{1,0:T(8,128)S(1)}, u32[]{:S(2)}, u32[]{:S(2)}) collective-permute-start(f32[128,128]{1,0:T(8,128)S(1)} %get-tuple-element.102), channel_id=1, source_target_pairs={{0,4},{2,6},{4,0},{6,2},{8,12},{10,14},{12,8},{14,10},{16,20},{18,... | collective-permute-start | bytes 196616 | tf_op jit(solution)/shard_map/ppermute | solution.py:305
  48.4 0.1 entering_1.1
  48.5 2.0 %collective-permute-start.10 = (f32[128,128]{1,0:T(8,128)S(1)}, f32[128,128]{1,0:T(8,128)S(1)}, u32[]{:S(2)}, u32[]{:S(2)}) collective-permute-start(f32[128,128]{1,0:T(8,128)S(1)} %get-tuple-element.74), channel_id=1, source_target_pairs={{0,12},{2,14},{4,8},{6,10},{8,4},{10,6},{12,0},{14,2},{16,28},{18,... | collective-permute-start | bytes 196616 | tf_op jit(solution)/shard_map/ppermute | solution.py:305
  50.5 3.0 %collective-permute-start.11 = (f32[128,128]{1,0:T(8,128)S(1)}, f32[128,128]{1,0:T(8,128)S(1)}, u32[]{:S(2)}, u32[]{:S(2)}) collective-permute-start(f32[128,128]{1,0:T(8,128)S(1)} %get-tuple-element.75), channel_id=1, source_target_pairs={{0,8},{2,10},{4,12},{6,14},{8,0},{10,2},{12,4},{14,6},{16,24},{18,... | collective-permute-start | bytes 196616 | tf_op jit(solution)/shard_map/ppermute | solution.py:305
  53.5 0.8 %collective-permute-start.12 = (f32[128,128]{1,0:T(8,128)S(1)}, f32[128,128]{1,0:T(8,128)S(1)}, u32[]{:S(2)}, u32[]{:S(2)}) collective-permute-start(f32[128,128]{1,0:T(8,128)S(1)} %get-tuple-element.76), channel_id=1, source_target_pairs={{0,4},{2,6},{4,0},{6,2},{8,12},{10,14},{12,8},{14,10},{16,20},{18,... | collective-permute-start | bytes 196616 | tf_op jit(solution)/shard_map/ppermute | solution.py:305
  54.3 0.1 spread_0.1
  54.4 1.0 %collective-permute-start.27 = (f32[512,128]{1,0:T(8,128)S(1)}, f32[512,128]{1,0:T(8,128)S(1)}, u32[]{:S(2)}, u32[]{:S(2)}) collective-permute-start(f32[512,128]{1,0:T(8,128)S(1)} %get-tuple-element.104), channel_id=1, source_target_pairs={{0,2},{2,0},{4,6},{6,4},{8,10},{10,8},{12,14},{14,12},{16,18},{18,... | collective-permute-start | bytes 786440 | tf_op jit(solution)/shard_map/ppermute | solution.py:359
  55.4 2.2 %collective-permute-done.11.refs_2_ = f32[128,128]{1,0:T(8,128)S(1)} collective-permute-done((f32[128,128]{1,0:T(8,128)S(1)}, f32[128,128]{1,0:T(8,128)S(1)}, u32[]{:S(2)}, u32[]{:S(2)}) %collective-permute-start.11) | collective-permute-done | bytes 65568 | tf_op jit(solution)/shard_map/ppermute | solution.py:305
  57.6 1.7 %collective-permute-done.12.refs_3_ = f32[128,128]{1,0:T(8,128)S(1)} collective-permute-done((f32[128,128]{1,0:T(8,128)S(1)}, f32[128,128]{1,0:T(8,128)S(1)}, u32[]{:S(2)}, u32[]{:S(2)}) %collective-permute-start.12) | collective-permute-done | bytes 65568 | tf_op jit(solution)/shard_map/ppermute | solution.py:305
  59.4 0.1 spread_1.1
  59.5 2.9 %collective-permute-start.13 = (f32[512,128]{1,0:T(8,128)S(1)}, f32[512,128]{1,0:T(8,128)S(1)}, u32[]{:S(2)}, u32[]{:S(2)}) collective-permute-start(f32[512,128]{1,0:T(8,128)S(1)} %get-tuple-element.77), channel_id=1, source_target_pairs={{0,2},{2,0},{4,6},{6,4},{8,10},{10,8},{12,14},{14,12},{16,18},{18,... | collective-permute-start | bytes 786440 | tf_op jit(solution)/shard_map/ppermute | solution.py:359
  62.3 0.9 %collective-permute-done.27.refs_1_ = f32[512,128]{1,0:T(8,128)S(1)} collective-permute-done((f32[512,128]{1,0:T(8,128)S(1)}, f32[512,128]{1,0:T(8,128)S(1)}, u32[]{:S(2)}, u32[]{:S(2)}) %collective-permute-start.27) | collective-permute-done | bytes 262176 | tf_op jit(solution)/shard_map/ppermute | solution.py:359
  63.3 1.4 %finish_0.1 = (f32[128,2048]{1,0:T(8,128)S(1)}, bf16[1024,2048]{1,0:T(8,128)(2,1)S(1)}) custom-call(f32[512,128]{1,0:T(8,128)S(1)} %get-tuple-element.103.refs_0_, f32[512,128]{1,0:T(8,128)S(1)} %collective-permute-done.27.refs_1_, bf16[128,128]{1,0:T(8,128)(2,1)S(1)} %get-tuple-element.87.refs_2_.refs_1_, ...), custom_call_target="tpu_custom_call" | custom-call | tf_op jit(solution)/shard_map/finish_0/pallas_call | solution.py:364
  64.7 0.7 finish_1.1.refs_6_.so_far
  65.4 4.8 %collective-permute-done.13.refs_0_ = f32[512,128]{1,0:T(8,128)S(1)} collective-permute-done((f32[512,128]{1,0:T(8,128)S(1)}, f32[512,128]{1,0:T(8,128)S(1)}, u32[]{:S(2)}, u32[]{:S(2)}) %collective-permute-start.13) | collective-permute-done | bytes 262176 | tf_op jit(solution)/shard_map/ppermute | solution.py:359
  70.2 0.6 finish_2.1
  70.8 0.4 finish_right.1
  71.2 4.4 %collective-permute-start.29 = (f32[64,1024]{1,0:T(8,128)S(1)}, f32[64,1024]{1,0:T(8,128)S(1)}, u32[]{:S(2)}, u32[]{:S(2)}) collective-permute-start(f32[64,1024]{1,0:T(8,128)S(1)} %get-tuple-element.112), channel_id=1, source_target_pairs={{0,1},{1,0},{2,3},{3,2},{4,5},{5,4},{6,7},{7,6},{8,9},{9,8},{10,11... | collective-permute-start | bytes 786440 | tf_op jit(solution)/shard_map/ppermute | solution.py:383
  75.6 0.1 collective-permute-start.28
  75.7 1.1 %collective-permute-done.29.right = f32[64,1024]{1,0:T(8,128)S(1)} collective-permute-done((f32[64,1024]{1,0:T(8,128)S(1)}, f32[64,1024]{1,0:T(8,128)S(1)}, u32[]{:S(2)}, u32[]{:S(2)}) %collective-permute-start.29) | collective-permute-done | bytes 262176 | tf_op jit(solution)/shard_map/ppermute | solution.py:383
  76.8 0.4 collective-permute-done.28.left
  77.1 0.7 add.1
  (36 shorter events, 0.2 us)
Async XLA Ops:
  0.0 5.7 %copy-start.3 = (f32[16,128]{1,0:T(8,128)S(1)}, f32[16,128]{1,0:T(8,128)}, u32[]{:S(2)}) copy-start(f32[16,128]{1,0:T(8,128)} %gain) | copy-start | bytes 24580
  0.0 5.7 %copy-start.4 = (f32[16]{0:T(128)S(1)}, f32[16]{0:T(128)}, u32[]{:S(2)}) copy-start(f32[16]{0:T(128)} %skip) | copy-start | bytes 196
  0.0 1.3 %copy-start.1 = (f32[16,128]{1,0:T(8,128)S(1)}, f32[16,128]{1,0:T(8,128)}, u32[]{:S(2)}) copy-start(f32[16,128]{1,0:T(8,128)} %log_decay.2) | copy-start | bytes 24580
  0.0 5.7 %copy-start.2 = (bf16[128,128]{1,0:T(8,128)(2,1)S(1)}, bf16[128,128]{1,0:T(8,128)(2,1)}, u32[]{:S(2)}) copy-start(bf16[128,128]{1,0:T(8,128)(2,1)} %c) | copy-start | bytes 98308
  0.0 1.3 %copy-start = (bf16[128,128]{1,0:T(8,128)(2,1)S(1)}, bf16[128,128]{1,0:T(8,128)(2,1)}, u32[]{:S(2)}) copy-start(bf16[128,128]{1,0:T(8,128)(2,1)} %b.2) | copy-start | bytes 98308
  0.0 5.5 %copy-start.6 = (bf16[128,16,128]{2,1,0:T(8,128)(2,1)S(1)}, bf16[128,16,128]{2,1,0:T(8,128)(2,1)}, u32[]{:S(2)}) copy-start(bf16[128,16,128]{2,1,0:T(8,128)(2,1)} %param.9) | copy-start | bytes 1572868
  0.0 1.1 %copy-start.5 = (bf16[128,16,128]{2,1,0:T(8,128)(2,1)S(1)}, bf16[128,16,128]{2,1,0:T(8,128)(2,1)}, u32[]{:S(2)}) copy-start(bf16[128,16,128]{2,1,0:T(8,128)(2,1)} %param.8) | copy-start | bytes 1572868
  2.1 7.6 %collective-permute-start.14 = (f32[520,128]{1,0:T(8,128)S(1)}, f32[520,128]{1,0:T(8,128)S(1)}, u32[]{:S(2)}, u32[]{:S(2)}) collective-permute-start(f32[520,128]{1,0:T(8,128)S(1)} %get-tuple-element.92), channel_id=1, source_target_pairs={{0,2},{2,0},{4,6},{6,4},{8,10},{10,8},{12,14},{14,12},{16,18},{18,... | collective-permute-start | bytes 798728 | tf_op jit(solution)/shard_map/ppermute | solution.py:323
  5.4 13.2 %collective-permute-start = (f32[520,128]{1,0:T(8,128)S(1)}, f32[520,128]{1,0:T(8,128)S(1)}, u32[]{:S(2)}, u32[]{:S(2)}) collective-permute-start(f32[520,128]{1,0:T(8,128)S(1)} %get-tuple-element.66), channel_id=1, source_target_pairs={{0,2},{2,0},{4,6},{6,4},{8,10},{10,8},{12,14},{14,12},{16,18},{18,... | collective-permute-start | bytes 798728 | tf_op jit(solution)/shard_map/ppermute | solution.py:323
  9.8 13.8 %collective-permute-start.15 = (f32[136,128]{1,0:T(8,128)S(1)}, f32[136,128]{1,0:T(8,128)S(1)}, u32[]{:S(2)}, u32[]{:S(2)}) collective-permute-start(f32[136,128]{1,0:T(8,128)S(1)} %get-tuple-element.94), channel_id=1, source_target_pairs={{0,12},{2,14},{4,8},{6,10},{8,4},{10,6},{12,0},{14,2},{16,28},{18,... | collective-permute-start | bytes 208904 | tf_op jit(solution)/shard_map/ppermute | solution.py:305
  16.4 8.8 %collective-permute-start.16 = (f32[136,128]{1,0:T(8,128)S(1)}, f32[136,128]{1,0:T(8,128)S(1)}, u32[]{:S(2)}, u32[]{:S(2)}) collective-permute-start(f32[136,128]{1,0:T(8,128)S(1)} %get-tuple-element.95), channel_id=1, source_target_pairs={{0,8},{2,10},{4,12},{6,14},{8,0},{10,2},{12,4},{14,6},{16,24},{18,... | collective-permute-start | bytes 208904 | tf_op jit(solution)/shard_map/ppermute | solution.py:305
  17.4 7.9 %collective-permute-start.17 = (f32[136,128]{1,0:T(8,128)S(1)}, f32[136,128]{1,0:T(8,128)S(1)}, u32[]{:S(2)}, u32[]{:S(2)}) collective-permute-start(f32[136,128]{1,0:T(8,128)S(1)} %get-tuple-element.96), channel_id=1, source_target_pairs={{0,4},{2,6},{4,0},{6,2},{8,12},{10,14},{12,8},{14,10},{16,20},{18,... | collective-permute-start | bytes 208904 | tf_op jit(solution)/shard_map/ppermute | solution.py:305
  18.7 9.8 %collective-permute-start.1 = (f32[136,128]{1,0:T(8,128)S(1)}, f32[136,128]{1,0:T(8,128)S(1)}, u32[]{:S(2)}, u32[]{:S(2)}) collective-permute-start(f32[136,128]{1,0:T(8,128)S(1)} %get-tuple-element.68), channel_id=1, source_target_pairs={{0,12},{2,14},{4,8},{6,10},{8,4},{10,6},{12,0},{14,2},{16,28},{18,... | collective-permute-start | bytes 208904 | tf_op jit(solution)/shard_map/ppermute | solution.py:305
  22.7 8.0 %collective-permute-start.2 = (f32[136,128]{1,0:T(8,128)S(1)}, f32[136,128]{1,0:T(8,128)S(1)}, u32[]{:S(2)}, u32[]{:S(2)}) collective-permute-start(f32[136,128]{1,0:T(8,128)S(1)} %get-tuple-element.69), channel_id=1, source_target_pairs={{0,8},{2,10},{4,12},{6,14},{8,0},{10,2},{12,4},{14,6},{16,24},{18,... | collective-permute-start | bytes 208904 | tf_op jit(solution)/shard_map/ppermute | solution.py:305
  23.5 7.2 %collective-permute-start.3 = (f32[136,128]{1,0:T(8,128)S(1)}, f32[136,128]{1,0:T(8,128)S(1)}, u32[]{:S(2)}, u32[]{:S(2)}) collective-permute-start(f32[136,128]{1,0:T(8,128)S(1)} %get-tuple-element.70), channel_id=1, source_target_pairs={{0,4},{2,6},{4,0},{6,2},{8,12},{10,14},{12,8},{14,10},{16,20},{18,... | collective-permute-start | bytes 208904 | tf_op jit(solution)/shard_map/ppermute | solution.py:305
  25.3 8.6 %collective-permute-start.20 = (f32[136,128]{1,0:T(8,128)S(1)}, f32[136,128]{1,0:T(8,128)S(1)}, u32[]{:S(2)}, u32[]{:S(2)}) collective-permute-start(f32[136,128]{1,0:T(8,128)S(1)} %row_total_0.1.refs_0_), channel_id=1, source_target_pairs={{0,48},{2,50},{4,52},{6,54},{8,56},{10,58},{12,60},{14,62},{16,32}... | collective-permute-start | bytes 208904 | tf_op jit(solution)/shard_map/ppermute | solution.py:305
  28.2 6.2 %collective-permute-start.19 = (f32[136,128]{1,0:T(8,128)S(1)}, f32[136,128]{1,0:T(8,128)S(1)}, u32[]{:S(2)}, u32[]{:S(2)}) collective-permute-start(f32[136,128]{1,0:T(8,128)S(1)} %row_total_0.1.refs_0_), channel_id=1, source_target_pairs={{0,32},{2,34},{4,36},{6,38},{8,40},{10,42},{12,44},{14,46},{16,48}... | collective-permute-start | bytes 208904 | tf_op jit(solution)/shard_map/ppermute | solution.py:305
  28.5 5.8 %collective-permute-start.18 = (f32[136,128]{1,0:T(8,128)S(1)}, f32[136,128]{1,0:T(8,128)S(1)}, u32[]{:S(2)}, u32[]{:S(2)}) collective-permute-start(f32[136,128]{1,0:T(8,128)S(1)} %row_total_0.1.refs_0_), channel_id=1, source_target_pairs={{0,16},{2,18},{4,20},{6,22},{8,24},{10,26},{12,28},{14,30},{16,0},... | collective-permute-start | bytes 208904 | tf_op jit(solution)/shard_map/ppermute | solution.py:305
  30.8 6.7 %collective-permute-start.6 = (f32[136,128]{1,0:T(8,128)S(1)}, f32[136,128]{1,0:T(8,128)S(1)}, u32[]{:S(2)}, u32[]{:S(2)}) collective-permute-start(f32[136,128]{1,0:T(8,128)S(1)} %row_total_1.1.refs_0_), channel_id=1, source_target_pairs={{0,48},{2,50},{4,52},{6,54},{8,56},{10,58},{12,60},{14,62},{16,32}... | collective-permute-start | bytes 208904 | tf_op jit(solution)/shard_map/ppermute | solution.py:305
  33.6 5.3 %collective-permute-start.5 = (f32[136,128]{1,0:T(8,128)S(1)}, f32[136,128]{1,0:T(8,128)S(1)}, u32[]{:S(2)}, u32[]{:S(2)}) collective-permute-start(f32[136,128]{1,0:T(8,128)S(1)} %row_total_1.1.refs_0_), channel_id=1, source_target_pairs={{0,32},{2,34},{4,36},{6,38},{8,40},{10,42},{12,44},{14,46},{16,48}... | collective-permute-start | bytes 208904 | tf_op jit(solution)/shard_map/ppermute | solution.py:305
  34.0 5.0 %collective-permute-start.4 = (f32[136,128]{1,0:T(8,128)S(1)}, f32[136,128]{1,0:T(8,128)S(1)}, u32[]{:S(2)}, u32[]{:S(2)}) collective-permute-start(f32[136,128]{1,0:T(8,128)S(1)} %row_total_1.1.refs_0_), channel_id=1, source_target_pairs={{0,16},{2,18},{4,20},{6,22},{8,24},{10,26},{12,28},{14,30},{16,0},... | collective-permute-start | bytes 208904 | tf_op jit(solution)/shard_map/ppermute | solution.py:305
  34.4 7.9 %collective-permute-start.23 = (f32[136,128]{1,0:T(8,128)S(1)}, f32[136,128]{1,0:T(8,128)S(1)}, u32[]{:S(2)}, u32[]{:S(2)}) collective-permute-start(f32[136,128]{1,0:T(8,128)S(1)} %get-tuple-element.97), channel_id=1, source_target_pairs={{0,192},{2,194},{4,196},{6,198},{8,200},{10,202},{12,204},{14,206}... | collective-permute-start | bytes 208904 | tf_op jit(solution)/shard_map/ppermute | solution.py:305
  36.9 5.6 %collective-permute-start.22 = (f32[136,128]{1,0:T(8,128)S(1)}, f32[136,128]{1,0:T(8,128)S(1)}, u32[]{:S(2)}, u32[]{:S(2)}) collective-permute-start(f32[136,128]{1,0:T(8,128)S(1)} %get-tuple-element.97), channel_id=1, source_target_pairs={{0,128},{2,130},{4,132},{6,134},{8,136},{10,138},{12,140},{14,142}... | collective-permute-start | bytes 208904 | tf_op jit(solution)/shard_map/ppermute | solution.py:305
  37.5 5.1 %collective-permute-start.21 = (f32[136,128]{1,0:T(8,128)S(1)}, f32[136,128]{1,0:T(8,128)S(1)}, u32[]{:S(2)}, u32[]{:S(2)}) collective-permute-start(f32[136,128]{1,0:T(8,128)S(1)} %get-tuple-element.97), channel_id=1, source_target_pairs={{0,64},{2,66},{4,68},{6,70},{8,72},{10,74},{12,76},{14,78},{16,80}... | collective-permute-start | bytes 208904 | tf_op jit(solution)/shard_map/ppermute | solution.py:305
  39.0 8.6 %collective-permute-start.9 = (f32[136,128]{1,0:T(8,128)S(1)}, f32[136,128]{1,0:T(8,128)S(1)}, u32[]{:S(2)}, u32[]{:S(2)}) collective-permute-start(f32[136,128]{1,0:T(8,128)S(1)} %get-tuple-element.71), channel_id=1, source_target_pairs={{0,192},{2,194},{4,196},{6,198},{8,200},{10,202},{12,204},{14,206}... | collective-permute-start | bytes 208904 | tf_op jit(solution)/shard_map/ppermute | solution.py:305
  41.8 6.6 %collective-permute-start.8 = (f32[136,128]{1,0:T(8,128)S(1)}, f32[136,128]{1,0:T(8,128)S(1)}, u32[]{:S(2)}, u32[]{:S(2)}) collective-permute-start(f32[136,128]{1,0:T(8,128)S(1)} %get-tuple-element.71), channel_id=1, source_target_pairs={{0,128},{2,130},{4,132},{6,134},{8,136},{10,138},{12,140},{14,142}... | collective-permute-start | bytes 208904 | tf_op jit(solution)/shard_map/ppermute | solution.py:305
  42.3 6.1 %collective-permute-start.7 = (f32[136,128]{1,0:T(8,128)S(1)}, f32[136,128]{1,0:T(8,128)S(1)}, u32[]{:S(2)}, u32[]{:S(2)}) collective-permute-start(f32[136,128]{1,0:T(8,128)S(1)} %get-tuple-element.71), channel_id=1, source_target_pairs={{0,64},{2,66},{4,68},{6,70},{8,72},{10,74},{12,76},{14,78},{16,80}... | collective-permute-start | bytes 208904 | tf_op jit(solution)/shard_map/ppermute | solution.py:305
  42.6 20.7 %slice-start = ((s8[8388608]{0:T(1024)(128)(4,1)}), s8[4194304]{0:T(1024)(128)(4,1)S(1)}, s32[]{:S(2)}) async-start(s8[8388608]{0:T(1024)(128)(4,1)} %bitcast.8), calls=%async_computation | async-start | bytes 8388608
  42.7 10.8 %collective-permute-start.24 = (f32[128,128]{1,0:T(8,128)S(1)}, f32[128,128]{1,0:T(8,128)S(1)}, u32[]{:S(2)}, u32[]{:S(2)}) collective-permute-start(f32[128,128]{1,0:T(8,128)S(1)} %get-tuple-element.100), channel_id=1, source_target_pairs={{0,12},{2,14},{4,8},{6,10},{8,4},{10,6},{12,0},{14,2},{16,28},{18,... | collective-permute-start | bytes 196616 | tf_op jit(solution)/shard_map/ppermute | solution.py:305
  44.3 9.9 %collective-permute-start.25 = (f32[128,128]{1,0:T(8,128)S(1)}, f32[128,128]{1,0:T(8,128)S(1)}, u32[]{:S(2)}, u32[]{:S(2)}) collective-permute-start(f32[128,128]{1,0:T(8,128)S(1)} %get-tuple-element.101), channel_id=1, source_target_pairs={{0,8},{2,10},{4,12},{6,14},{8,0},{10,2},{12,4},{14,6},{16,24},{18,... | collective-permute-start | bytes 196616 | tf_op jit(solution)/shard_map/ppermute | solution.py:305
  47.6 6.7 %collective-permute-start.26 = (f32[128,128]{1,0:T(8,128)S(1)}, f32[128,128]{1,0:T(8,128)S(1)}, u32[]{:S(2)}, u32[]{:S(2)}) collective-permute-start(f32[128,128]{1,0:T(8,128)S(1)} %get-tuple-element.102), channel_id=1, source_target_pairs={{0,4},{2,6},{4,0},{6,2},{8,12},{10,14},{12,8},{14,10},{16,20},{18,... | collective-permute-start | bytes 196616 | tf_op jit(solution)/shard_map/ppermute | solution.py:305
  48.4 14.9 %slice-start.1 = ((s8[8388608]{0:T(1024)(128)(4,1)}), s8[4194304]{0:T(1024)(128)(4,1)S(1)}, s32[]{:S(2)}) async-start(s8[8388608]{0:T(1024)(128)(4,1)} %bitcast.8), calls=%async_computation.1 | async-start | bytes 8388608
  48.5 6.9 %collective-permute-start.10 = (f32[128,128]{1,0:T(8,128)S(1)}, f32[128,128]{1,0:T(8,128)S(1)}, u32[]{:S(2)}, u32[]{:S(2)}) collective-permute-start(f32[128,128]{1,0:T(8,128)S(1)} %get-tuple-element.74), channel_id=1, source_target_pairs={{0,12},{2,14},{4,8},{6,10},{8,4},{10,6},{12,0},{14,2},{16,28},{18,... | collective-permute-start | bytes 196616 | tf_op jit(solution)/shard_map/ppermute | solution.py:305
  50.5 7.2 %collective-permute-start.11 = (f32[128,128]{1,0:T(8,128)S(1)}, f32[128,128]{1,0:T(8,128)S(1)}, u32[]{:S(2)}, u32[]{:S(2)}) collective-permute-start(f32[128,128]{1,0:T(8,128)S(1)} %get-tuple-element.75), channel_id=1, source_target_pairs={{0,8},{2,10},{4,12},{6,14},{8,0},{10,2},{12,4},{14,6},{16,24},{18,... | collective-permute-start | bytes 196616 | tf_op jit(solution)/shard_map/ppermute | solution.py:305
  53.5 5.9 %collective-permute-start.12 = (f32[128,128]{1,0:T(8,128)S(1)}, f32[128,128]{1,0:T(8,128)S(1)}, u32[]{:S(2)}, u32[]{:S(2)}) collective-permute-start(f32[128,128]{1,0:T(8,128)S(1)} %get-tuple-element.76), channel_id=1, source_target_pairs={{0,4},{2,6},{4,0},{6,2},{8,12},{10,14},{12,8},{14,10},{16,20},{18,... | collective-permute-start | bytes 196616 | tf_op jit(solution)/shard_map/ppermute | solution.py:305
  54.4 8.9 %collective-permute-start.27 = (f32[512,128]{1,0:T(8,128)S(1)}, f32[512,128]{1,0:T(8,128)S(1)}, u32[]{:S(2)}, u32[]{:S(2)}) collective-permute-start(f32[512,128]{1,0:T(8,128)S(1)} %get-tuple-element.104), channel_id=1, source_target_pairs={{0,2},{2,0},{4,6},{6,4},{8,10},{10,8},{12,14},{14,12},{16,18},{18,... | collective-permute-start | bytes 786440 | tf_op jit(solution)/shard_map/ppermute | solution.py:359
  59.5 10.8 %collective-permute-start.13 = (f32[512,128]{1,0:T(8,128)S(1)}, f32[512,128]{1,0:T(8,128)S(1)}, u32[]{:S(2)}, u32[]{:S(2)}) collective-permute-start(f32[512,128]{1,0:T(8,128)S(1)} %get-tuple-element.77), channel_id=1, source_target_pairs={{0,2},{2,0},{4,6},{6,4},{8,10},{10,8},{12,14},{14,12},{16,18},{18,... | collective-permute-start | bytes 786440 | tf_op jit(solution)/shard_map/ppermute | solution.py:359
  71.2 5.6 %collective-permute-start.29 = (f32[64,1024]{1,0:T(8,128)S(1)}, f32[64,1024]{1,0:T(8,128)S(1)}, u32[]{:S(2)}, u32[]{:S(2)}) collective-permute-start(f32[64,1024]{1,0:T(8,128)S(1)} %get-tuple-element.112), channel_id=1, source_target_pairs={{0,1},{1,0},{2,3},{3,2},{4,5},{5,4},{6,7},{7,6},{8,9},{9,8},{10,11... | collective-permute-start | bytes 786440 | tf_op jit(solution)/shard_map/ppermute | solution.py:383
  75.6 1.5 %collective-permute-start.28 = (f32[64,1024]{1,0:T(8,128)S(1)}, f32[64,1024]{1,0:T(8,128)S(1)}, u32[]{:S(2)}, u32[]{:S(2)}) collective-permute-start(f32[64,1024]{1,0:T(8,128)S(1)} %get-tuple-element.111), channel_id=1, source_target_pairs={{0,1},{1,0},{2,3},{3,2},{4,5},{5,4},{6,7},{7,6},{8,9},{9,8},{10,11... | collective-permute-start | bytes 786440 | tf_op jit(solution)/shard_map/ppermute | solution.py:379

commit v9 on v6

--- a/solution.py
+++ b/solution.py
@@ -19,7 +19,9 @@
 ROWS = HALF * W
 TILE = 512
 WORK = 10**10
-UP, DOWN, ACROSS = (0, 3, 2, 1), (0, 3, 2, 1), (0, 1, 2, 3)
+UP = ((0, 3, 2, 1), (0, 3, 2, 1))
+DOWN = ((0, 1, 2, 3), (0, 3, 2, 1))
+ACROSS = (0, 1, 2, 3)
 VMEM = pl.BlockSpec(memory_space=pltpu.VMEM)
 SMEM = pl.BlockSpec(memory_space=pltpu.SMEM)
 
@@ -92,10 +94,10 @@
         out[ROWS:, :] = decay_tile(lasts)
 
 
-def pair_kernel(keep, got, *outs):
+def pair_kernel(group, keep, got, *outs):
     pos = position()
     first = pos[0] & 1 == 0
-    for k, m in enumerate(UP):
+    for k, m in enumerate(UP[group]):
         j = (pos[0] >> 1) ^ m
         state, log = rows_of(j), pl.ds(ROWS + j, 1)
         earlier = jnp.where(first, keep[state, :], got[state, :])
@@ -105,10 +107,10 @@
         outs[k][W:, :] = decay_tile([keep[log, :] + got[log, :]])
 
 
-def row_total_kernel(*refs):
+def row_total_kernel(group, *refs):
     pos = position()
     parts, out = refs[:PAIRS], refs[PAIRS]
-    places = [(pos[0] >> 1) ^ m for m in UP]
+    places = [(pos[0] >> 1) ^ m for m in UP[group]]
     logs = [part[W : W + 1, :] for part in parts]
     total = jnp.zeros((W, W), F32)
     for k in range(PAIRS):
@@ -149,13 +151,13 @@
     before[W:, :] = decay_tile([to_row])
 
 
-def entering_kernel(*refs):
+def entering_kernel(group, *refs):
     pos = position()
     planes, before = refs[: NX - 1], refs[NX - 1]
     parts = refs[NX : NX + PAIRS]
     outs = refs[NX + PAIRS : NX + 2 * PAIRS]
     ordered, entering = refs[NX + 2 * PAIRS :]
-    for k, m in enumerate(UP):
+    for k, m in enumerate(UP[group]):
         ordered[(pos[0] >> 1) ^ m] = parts[k][...]
     carry = jnp.zeros((W, W), F32)
     logs = [plane[W : W + 1, :] for plane in planes]
@@ -173,15 +175,15 @@
         entering[place] = carry
         if place < PAIRS - 1:
             carry = jnp.exp(ordered[place, W : W + 1, :]) * carry + ordered[place, :W, :]
-    for k, m in enumerate(DOWN):
+    for k, m in enumerate(DOWN[group]):
         outs[k][...] = entering[(pos[0] >> 1) ^ m]
 
 
-def spread_kernel(keep, got, *refs):
+def spread_kernel(group, keep, got, *refs):
     pos = position()
     carries, mine, send = refs[:PAIRS], refs[PAIRS], refs[PAIRS + 1]
     first = pos[0] & 1 == 0
-    for k, m in enumerate(DOWN):
+    for k, m in enumerate(DOWN[group]):
         j = (pos[0] >> 1) ^ m
         state, log = rows_of(j), pl.ds(ROWS + j, 1)
         carry = carries[k][...]
@@ -311,13 +313,13 @@
         (keep[0], fixed, slope, read, gain)
     )
     for g in range(GROUPS):
-        pair = call(pair_kernel, [single] * PAIRS, [VMEM] * 2, name=f"pair_{g}")(
+        pair = call(functools.partial(pair_kernel, g), [single] * PAIRS, [VMEM] * 2, name=f"pair_{g}")(
             keep[g], got[g]
         )
-        parts[g] = exchange(pair, 2, UP)
+        parts[g] = exchange(pair, 2, UP[g])
     for g in range(GROUPS):
         total = call(
-            row_total_kernel, single, [VMEM] * PAIRS, name=f"row_total_{g}"
+            functools.partial(row_total_kernel, g), single, [VMEM] * PAIRS, name=f"row_total_{g}"
         )(*parts[g])
         totals[g] = exchange([total] * NY, NZ, ACROSS)
     for g in range(GROUPS):
@@ -327,14 +329,14 @@
         planes[g] = exchange([plane] * NX, NY * NZ, ACROSS)[1:] + [before]
     for g in range(GROUPS):
         back = call(
-            entering_kernel, [shaped(W, W)] * PAIRS, [VMEM] * (NX + PAIRS),
+            functools.partial(entering_kernel, g), [shaped(W, W)] * PAIRS, [VMEM] * (NX + PAIRS),
             [pltpu.VMEM((PAIRS, W + 8, W), F32), pltpu.VMEM((PAIRS, W, W), F32)],
             name=f"entering_{g}", work=WORK,
         )(*planes[g], *parts[g])
-        states[g] = exchange(back, 2, DOWN)
+        states[g] = exchange(back, 2, DOWN[g])
     for g in range(GROUPS):
         mine[g], send = call(
-            spread_kernel, [shaped(ROWS, W)] * 2, [VMEM] * (2 + PAIRS), name=f"spread_{g}"
+            functools.partial(spread_kernel, g), [shaped(ROWS, W)] * 2, [VMEM] * (2 + PAIRS), name=f"spread_{g}"
         )(keep[g], got[g], *states[g])
         states[g] = lax.ppermute(send, "ctx", partners(1, 1))
 

time: 77.8 us -> 77.8 us (level)
  no operation moved by 1% of the time
where the time goes in v9:
time: 77.8 us; the launch traced here: 77.7 us
  starting transfers between devices  51.6 us (66%)
  waiting for transfers between devices  17 us (22%)
  Pallas kernels  6.82 us (9%)
  local copies, waits for them, and re-layouts  1.38 us (2%)
    ppermute x24, starting transfers between devices, exchange(): lax.ppermute(value, 'ctx', partners(stride, m))  40.8 us
    ppermute x24, waiting for transfers between devices, exchange(): lax.ppermute(value, 'ctx', partners(stride, m))  7.1 us
    ppermute x2, waiting for transfers between devices, per_device(): states[g] = lax.ppermute(send, 'ctx', partners(1, 1))  5.99 us
    ppermute x1, starting transfers between devices, per_device(): return (near + lax.ppermute(far, 'tp', [(0, 1), (1, 0)])).astype(BF16)  4.41 us
    ppermute x2, starting transfers between devices, per_device(): states[g] = lax.ppermute(send, 'ctx', partners(1, 1))  3.66 us
    pallas_call x3, Pallas kernels, finish(): call(functools.partial(finish_kernel, group, sides, stage), outs, [VMEM]...  2.9 us
    ppermute x2, starting transfers between devices, per_device(): got[g] = lax.ppermute(send, 'ctx', partners(1, 1))  2.66 us
    ppermute x2, waiting for transfers between devices, per_device(): got[g] = lax.ppermute(send, 'ctx', partners(1, 1))  2.34 us
  transfers between devices with their start and end apart: 29, of which 9 were waited for; matrix products, arithmetic and copies ran while one was open for 0% of the time, Pallas kernels for 7%

profile of v9, /device:TPU:1, one launch (start us, length us, event | category | flops | bytes accessed | tf_op | source)
XLA Modules:
  0.0 77.7 jit_solution(13366792174244199874)
XLA Ops:
  0.1 1.1 %copy-done.5 = bf16[128,16,128]{2,1,0:T(8,128)(2,1)S(1)} copy-done((bf16[128,16,128]{2,1,0:T(8,128)(2,1)S(1)}, bf16[128,16,128]{2,1,0:T(8,128)(2,1)}, u32[]{:S(2)}) %copy-start.5) | copy-done | bytes 524312
  1.1 0.1 copy.14
  1.3 0.8 %local_state_0.1 = (f32[520,128]{1,0:T(8,128)S(1)}, f32[520,128]{1,0:T(8,128)S(1)}) custom-call(f32[128,128]{1,0:T(8,128)S(1)} %lower.1.ones, bf16[128,2048]{1,0:T(8,128)(2,1)S(1)} %bitcast.10, bf16[128,128]{1,0:T(8,128)(2,1)S(1)} %copy-done, f32[16,128]{1,0:T(8,128)S(1)} %copy-done.1), custom_call_target="tpu_custom_call" | custom-call | tf_op jit(solution)/shard_map/local_state_0/pallas_call | solution.py:301
  2.1 2.6 %collective-permute-start.14 = (f32[520,128]{1,0:T(8,128)S(1)}, f32[520,128]{1,0:T(8,128)S(1)}, u32[]{:S(2)}, u32[]{:S(2)}) collective-permute-start(f32[520,128]{1,0:T(8,128)S(1)} %get-tuple-element.89), channel_id=1, source_target_pairs={{0,2},{2,0},{4,6},{6,4},{8,10},{10,8},{12,14},{14,12},{16,18},{18,... | collective-permute-start | bytes 798728 | tf_op jit(solution)/shard_map/ppermute | solution.py:305
  4.6 0.8 %local_state_1.1 = (f32[520,128]{1,0:T(8,128)S(1)}, f32[520,128]{1,0:T(8,128)S(1)}) custom-call(f32[128,128]{1,0:T(8,128)S(1)} %lower.1.ones, bf16[128,2048]{1,0:T(8,128)(2,1)S(1)} %bitcast.11, bf16[128,128]{1,0:T(8,128)(2,1)S(1)} %copy-done, f32[16,128]{1,0:T(8,128)S(1)} %copy-done.1), custom_call_target="tpu_custom_call" | custom-call | tf_op jit(solution)/shard_map/local_state_1/pallas_call | solution.py:301
  5.4 0.1 collective-permute-start
  5.5 0.1 copy.13
  5.7 1.6 %inside.1 = (f32[128,2048]{1,0:T(8,128)S(1)}, f32[128,2048]{1,0:T(8,128)S(1)}, bf16[128,128]{1,0:T(8,128)(2,1)S(1)}, f32[16,128]{1,0:T(8,128)S(1)}) custom-call(f32[16]{0:T(128)S(1)} %copy-done.4, f32[128,128]{1,0:T(8,128)S(1)} %lower.1.ones, bf16[128,2048]{1,0:T(8,128)(2,1)S(1)} %bitcast.12, bf16[128,2048]{1,0:T(8,128)(2,1)S(1)} %bitcast.13, ...), custom_call_target="tpu_custom_call" | custom-call | tf_op jit(solution)/shard_map/inside/pallas_call | solution.py:307
  7.4 2.3 %collective-permute-done.14.got = f32[520,128]{1,0:T(8,128)S(1)} collective-permute-done((f32[520,128]{1,0:T(8,128)S(1)}, f32[520,128]{1,0:T(8,128)S(1)}, u32[]{:S(2)}, u32[]{:S(2)}) %collective-permute-start.14) | collective-permute-done | bytes 266272 | tf_op jit(solution)/shard_map/ppermute | solution.py:305
  9.7 0.1 pair_0.1
  9.8 6.7 %collective-permute-start.15 = (f32[136,128]{1,0:T(8,128)S(1)}, f32[136,128]{1,0:T(8,128)S(1)}, u32[]{:S(2)}, u32[]{:S(2)}) collective-permute-start(f32[136,128]{1,0:T(8,128)S(1)} %get-tuple-element.91), channel_id=1, source_target_pairs={{0,12},{2,14},{4,8},{6,10},{8,4},{10,6},{12,0},{14,2},{16,28},{18,... | collective-permute-start | bytes 208904 | tf_op jit(solution)/shard_map/ppermute | solution.py:287
  16.4 1.0 %collective-permute-start.16 = (f32[136,128]{1,0:T(8,128)S(1)}, f32[136,128]{1,0:T(8,128)S(1)}, u32[]{:S(2)}, u32[]{:S(2)}) collective-permute-start(f32[136,128]{1,0:T(8,128)S(1)} %get-tuple-element.92), channel_id=1, source_target_pairs={{0,8},{2,10},{4,12},{6,14},{8,0},{10,2},{12,4},{14,6},{16,24},{18,... | collective-permute-start | bytes 208904 | tf_op jit(solution)/shard_map/ppermute | solution.py:287
  17.4 1.2 %collective-permute-start.17 = (f32[136,128]{1,0:T(8,128)S(1)}, f32[136,128]{1,0:T(8,128)S(1)}, u32[]{:S(2)}, u32[]{:S(2)}) collective-permute-start(f32[136,128]{1,0:T(8,128)S(1)} %get-tuple-element.93), channel_id=1, source_target_pairs={{0,4},{2,6},{4,0},{6,2},{8,12},{10,14},{12,8},{14,10},{16,20},{18,... | collective-permute-start | bytes 208904 | tf_op jit(solution)/shard_map/ppermute | solution.py:287
  18.6 0.0 collective-permute-done.got
  18.6 0.1 pair_1.1
  18.7 4.0 %collective-permute-start.1 = (f32[136,128]{1,0:T(8,128)S(1)}, f32[136,128]{1,0:T(8,128)S(1)}, u32[]{:S(2)}, u32[]{:S(2)}) collective-permute-start(f32[136,128]{1,0:T(8,128)S(1)} %get-tuple-element.65), channel_id=1, source_target_pairs={{0,12},{2,14},{4,8},{6,10},{8,4},{10,6},{12,0},{14,2},{16,28},{18,... | collective-permute-start | bytes 208904 | tf_op jit(solution)/shard_map/ppermute | solution.py:287
  22.7 0.8 %collective-permute-start.2 = (f32[136,128]{1,0:T(8,128)S(1)}, f32[136,128]{1,0:T(8,128)S(1)}, u32[]{:S(2)}, u32[]{:S(2)}) collective-permute-start(f32[136,128]{1,0:T(8,128)S(1)} %get-tuple-element.66), channel_id=1, source_target_pairs={{0,8},{2,10},{4,12},{6,14},{8,0},{10,2},{12,4},{14,6},{16,24},{18,... | collective-permute-start | bytes 208904 | tf_op jit(solution)/shard_map/ppermute | solution.py:287
  23.5 0.0 collective-permute-done.15.refs_1_.refs_5_
  23.5 1.3 %collective-permute-start.3 = (f32[136,128]{1,0:T(8,128)S(1)}, f32[136,128]{1,0:T(8,128)S(1)}, u32[]{:S(2)}, u32[]{:S(2)}) collective-permute-start(f32[136,128]{1,0:T(8,128)S(1)} %get-tuple-element.67), channel_id=1, source_target_pairs={{0,4},{2,6},{4,0},{6,2},{8,12},{10,14},{12,8},{14,10},{16,20},{18,... | collective-permute-start | bytes 208904 | tf_op jit(solution)/shard_map/ppermute | solution.py:287
  24.9 0.4 collective-permute-done.16.refs_2_.refs_6_
  25.3 2.8 %collective-permute-start.20 = (f32[136,128]{1,0:T(8,128)S(1)}, f32[136,128]{1,0:T(8,128)S(1)}, u32[]{:S(2)}, u32[]{:S(2)}) collective-permute-start(f32[136,128]{1,0:T(8,128)S(1)} %row_total_0.1.refs_0_), channel_id=1, source_target_pairs={{0,48},{2,50},{4,52},{6,54},{8,56},{10,58},{12,60},{14,62},{16,32}... | collective-permute-start | bytes 208904 | tf_op jit(solution)/shard_map/ppermute | solution.py:287
  28.2 0.3 collective-permute-start.19
  28.5 0.0 collective-permute-done.1.refs_1_.refs_5_
  28.5 0.8 collective-permute-start.18
  29.3 1.5 %collective-permute-done.2.refs_2_.refs_6_ = f32[136,128]{1,0:T(8,128)S(1)} collective-permute-done((f32[136,128]{1,0:T(8,128)S(1)}, f32[136,128]{1,0:T(8,128)S(1)}, u32[]{:S(2)}, u32[]{:S(2)}) %collective-permute-start.2) | collective-permute-done | bytes 69664 | tf_op jit(solution)/shard_map/ppermute | solution.py:287
  30.7 0.0 collective-permute-done.3.refs_3_.refs_7_
  30.8 2.8 %collective-permute-start.6 = (f32[136,128]{1,0:T(8,128)S(1)}, f32[136,128]{1,0:T(8,128)S(1)}, u32[]{:S(2)}, u32[]{:S(2)}) collective-permute-start(f32[136,128]{1,0:T(8,128)S(1)} %row_total_1.1.refs_0_), channel_id=1, source_target_pairs={{0,48},{2,50},{4,52},{6,54},{8,56},{10,58},{12,60},{14,62},{16,32}... | collective-permute-start | bytes 208904 | tf_op jit(solution)/shard_map/ppermute | solution.py:287
  33.6 0.3 collective-permute-start.5
  34.0 0.3 collective-permute-start.4
  34.3 0.0 collective-permute-done.19.refs_2_
  34.3 0.0 collective-permute-done.18.refs_1_
  34.3 0.1 plane_0.1
  34.4 2.6 %collective-permute-start.23 = (f32[136,128]{1,0:T(8,128)S(1)}, f32[136,128]{1,0:T(8,128)S(1)}, u32[]{:S(2)}, u32[]{:S(2)}) collective-permute-start(f32[136,128]{1,0:T(8,128)S(1)} %get-tuple-element.94), channel_id=1, source_target_pairs={{0,192},{2,194},{4,196},{6,198},{8,200},{10,202},{12,204},{14,206}... | collective-permute-start | bytes 208904 | tf_op jit(solution)/shard_map/ppermute | solution.py:287
  36.9 0.5 collective-permute-start.22
  37.5 0.0 collective-permute-done.6.refs_3_
  37.5 0.3 collective-permute-start.21
  37.7 1.2 %collective-permute-done.5.refs_2_ = f32[136,128]{1,0:T(8,128)S(1)} collective-permute-done((f32[136,128]{1,0:T(8,128)S(1)}, f32[136,128]{1,0:T(8,128)S(1)}, u32[]{:S(2)}, u32[]{:S(2)}) %collective-permute-start.5) | collective-permute-done | bytes 69664 | tf_op jit(solution)/shard_map/ppermute | solution.py:287
  39.0 0.1 plane_1.1
  39.0 2.7 %collective-permute-start.9 = (f32[136,128]{1,0:T(8,128)S(1)}, f32[136,128]{1,0:T(8,128)S(1)}, u32[]{:S(2)}, u32[]{:S(2)}) collective-permute-start(f32[136,128]{1,0:T(8,128)S(1)} %get-tuple-element.68), channel_id=1, source_target_pairs={{0,192},{2,194},{4,196},{6,198},{8,200},{10,202},{12,204},{14,206}... | collective-permute-start | bytes 208904 | tf_op jit(solution)/shard_map/ppermute | solution.py:287
  41.8 0.5 collective-permute-start.8
  42.3 0.3 collective-permute-start.7
  42.5 0.0 collective-permute-done.22.refs_1_
  42.6 0.1 entering_0.1
  42.7 1.7 %collective-permute-start.24 = (f32[128,128]{1,0:T(8,128)S(1)}, f32[128,128]{1,0:T(8,128)S(1)}, u32[]{:S(2)}, u32[]{:S(2)}) collective-permute-start(f32[128,128]{1,0:T(8,128)S(1)} %get-tuple-element.97), channel_id=1, source_target_pairs={{0,4},{2,6},{4,0},{6,2},{8,12},{10,14},{12,8},{14,10},{16,20},{18,... | collective-permute-start | bytes 196616 | tf_op jit(solution)/shard_map/ppermute | solution.py:287
  44.3 2.5 %collective-permute-start.25 = (f32[128,128]{1,0:T(8,128)S(1)}, f32[128,128]{1,0:T(8,128)S(1)}, u32[]{:S(2)}, u32[]{:S(2)}) collective-permute-start(f32[128,128]{1,0:T(8,128)S(1)} %get-tuple-element.98), channel_id=1, source_target_pairs={{0,8},{2,10},{4,12},{6,14},{8,0},{10,2},{12,4},{14,6},{16,24},{18,... | collective-permute-start | bytes 196616 | tf_op jit(solution)/shard_map/ppermute | solution.py:287
  46.8 1.6 %collective-permute-start.26 = (f32[128,128]{1,0:T(8,128)S(1)}, f32[128,128]{1,0:T(8,128)S(1)}, u32[]{:S(2)}, u32[]{:S(2)}) collective-permute-start(f32[128,128]{1,0:T(8,128)S(1)} %get-tuple-element.99), channel_id=1, source_target_pairs={{0,12},{2,14},{4,8},{6,10},{8,4},{10,6},{12,0},{14,2},{16,28},{18,... | collective-permute-start | bytes 196616 | tf_op jit(solution)/shard_map/ppermute | solution.py:287
  48.4 0.1 entering_1.1
  48.5 2.0 %collective-permute-start.10 = (f32[128,128]{1,0:T(8,128)S(1)}, f32[128,128]{1,0:T(8,128)S(1)}, u32[]{:S(2)}, u32[]{:S(2)}) collective-permute-start(f32[128,128]{1,0:T(8,128)S(1)} %get-tuple-element.71), channel_id=1, source_target_pairs={{0,12},{2,14},{4,8},{6,10},{8,4},{10,6},{12,0},{14,2},{16,28},{18,... | collective-permute-start | bytes 196616 | tf_op jit(solution)/shard_map/ppermute | solution.py:287
  50.5 2.9 %collective-permute-start.11 = (f32[128,128]{1,0:T(8,128)S(1)}, f32[128,128]{1,0:T(8,128)S(1)}, u32[]{:S(2)}, u32[]{:S(2)}) collective-permute-start(f32[128,128]{1,0:T(8,128)S(1)} %get-tuple-element.72), channel_id=1, source_target_pairs={{0,8},{2,10},{4,12},{6,14},{8,0},{10,2},{12,4},{14,6},{16,24},{18,... | collective-permute-start | bytes 196616 | tf_op jit(solution)/shard_map/ppermute | solution.py:287
  53.5 0.8 %collective-permute-start.12 = (f32[128,128]{1,0:T(8,128)S(1)}, f32[128,128]{1,0:T(8,128)S(1)}, u32[]{:S(2)}, u32[]{:S(2)}) collective-permute-start(f32[128,128]{1,0:T(8,128)S(1)} %get-tuple-element.73), channel_id=1, source_target_pairs={{0,4},{2,6},{4,0},{6,2},{8,12},{10,14},{12,8},{14,10},{16,20},{18,... | collective-permute-start | bytes 196616 | tf_op jit(solution)/shard_map/ppermute | solution.py:287
  54.3 0.1 spread_0.1
  54.4 1.0 %collective-permute-start.27 = (f32[512,128]{1,0:T(8,128)S(1)}, f32[512,128]{1,0:T(8,128)S(1)}, u32[]{:S(2)}, u32[]{:S(2)}) collective-permute-start(f32[512,128]{1,0:T(8,128)S(1)} %get-tuple-element.101), channel_id=1, source_target_pairs={{0,2},{2,0},{4,6},{6,4},{8,10},{10,8},{12,14},{14,12},{16,18},{18,... | collective-permute-start | bytes 786440 | tf_op jit(solution)/shard_map/ppermute | solution.py:341
  55.4 2.7 %collective-permute-done.11.refs_2_ = f32[128,128]{1,0:T(8,128)S(1)} collective-permute-done((f32[128,128]{1,0:T(8,128)S(1)}, f32[128,128]{1,0:T(8,128)S(1)}, u32[]{:S(2)}, u32[]{:S(2)}) %collective-permute-start.11) | collective-permute-done | bytes 65568 | tf_op jit(solution)/shard_map/ppermute | solution.py:287
  58.1 1.2 %collective-permute-done.12.refs_3_ = f32[128,128]{1,0:T(8,128)S(1)} collective-permute-done((f32[128,128]{1,0:T(8,128)S(1)}, f32[128,128]{1,0:T(8,128)S(1)}, u32[]{:S(2)}, u32[]{:S(2)}) %collective-permute-start.12) | collective-permute-done | bytes 65568 | tf_op jit(solution)/shard_map/ppermute | solution.py:287
  59.3 0.1 spread_1.1
  59.4 2.7 %collective-permute-start.13 = (f32[512,128]{1,0:T(8,128)S(1)}, f32[512,128]{1,0:T(8,128)S(1)}, u32[]{:S(2)}, u32[]{:S(2)}) collective-permute-start(f32[512,128]{1,0:T(8,128)S(1)} %get-tuple-element.74), channel_id=1, source_target_pairs={{0,2},{2,0},{4,6},{6,4},{8,10},{10,8},{12,14},{14,12},{16,18},{18,... | collective-permute-start | bytes 786440 | tf_op jit(solution)/shard_map/ppermute | solution.py:341
  62.1 1.0 %collective-permute-done.27.refs_1_ = f32[512,128]{1,0:T(8,128)S(1)} collective-permute-done((f32[512,128]{1,0:T(8,128)S(1)}, f32[512,128]{1,0:T(8,128)S(1)}, u32[]{:S(2)}, u32[]{:S(2)}) %collective-permute-start.27) | collective-permute-done | bytes 262176 | tf_op jit(solution)/shard_map/ppermute | solution.py:341
  63.0 1.4 %finish_0.1 = (f32[128,2048]{1,0:T(8,128)S(1)}, bf16[1024,2048]{1,0:T(8,128)(2,1)S(1)}) custom-call(f32[512,128]{1,0:T(8,128)S(1)} %get-tuple-element.100.refs_0_, f32[512,128]{1,0:T(8,128)S(1)} %collective-permute-done.27.refs_1_, bf16[128,128]{1,0:T(8,128)(2,1)S(1)} %get-tuple-element.84.refs_2_.refs_1_, ...), custom_call_target="tpu_custom_call" | custom-call | tf_op jit(solution)/shard_map/finish_0/pallas_call | solution.py:346
  64.5 0.7 finish_1.1.refs_6_
  65.2 5.0 %collective-permute-done.13.refs_0_ = f32[512,128]{1,0:T(8,128)S(1)} collective-permute-done((f32[512,128]{1,0:T(8,128)S(1)}, f32[512,128]{1,0:T(8,128)S(1)}, u32[]{:S(2)}, u32[]{:S(2)}) %collective-permute-start.13) | collective-permute-done | bytes 262176 | tf_op jit(solution)/shard_map/ppermute | solution.py:341
  70.2 0.8 %finish_2.1 = (f32[64,2048]{1,0:T(8,128)S(1)}, f32[64,2048]{1,0:T(8,128)S(1)}) custom-call(f32[512,128]{1,0:T(8,128)S(1)} %collective-permute-done.13.refs_0_, bf16[128,128]{1,0:T(8,128)(2,1)S(1)} %get-tuple-element.84.refs_2_.refs_1_, f32[128,2048]{1,0:T(8,128)S(1)} %get-tuple-element.85.refs_3_.refs_2_, f32[128,2048]{1,0:T(8,128)S(1)} %get-tuple-element.86.refs_4_.refs_3_, ...), custom_call_target="tpu_custom_call" | custom-call | tf_op jit(solution)/shard_map/finish_2/pallas_call | solution.py:346
  71.0 4.4 %collective-permute-start.28 = (f32[64,2048]{1,0:T(8,128)S(1)}, f32[64,2048]{1,0:T(8,128)S(1)}, u32[]{:S(2)}, u32[]{:S(2)}) collective-permute-start(f32[64,2048]{1,0:T(8,128)S(1)} %get-tuple-element.106), channel_id=1, source_target_pairs={{0,1},{1,0},{2,3},{3,2},{4,5},{5,4},{6,7},{7,6},{8,9},{9,8},{10,11... | collective-permute-start | bytes 1572872 | tf_op jit(solution)/shard_map/ppermute | solution.py:357
  75.4 1.5 %collective-permute-done.28 = f32[64,2048]{1,0:T(8,128)S(1)} collective-permute-done((f32[64,2048]{1,0:T(8,128)S(1)}, f32[64,2048]{1,0:T(8,128)S(1)}, u32[]{:S(2)}, u32[]{:S(2)}) %collective-permute-start.28) | collective-permute-done | bytes 524320 | tf_op jit(solution)/shard_map/ppermute | solution.py:357
  77.0 0.8 add_convert_fusion
  (33 shorter events, 0.2 us)
Async XLA Ops:
  0.0 5.7 %copy-start.3 = (f32[16,128]{1,0:T(8,128)S(1)}, f32[16,128]{1,0:T(8,128)}, u32[]{:S(2)}) copy-start(f32[16,128]{1,0:T(8,128)} %gain) | copy-start | bytes 24580
  0.0 5.7 %copy-start.4 = (f32[16]{0:T(128)S(1)}, f32[16]{0:T(128)}, u32[]{:S(2)}) copy-start(f32[16]{0:T(128)} %skip) | copy-start | bytes 196
  0.0 1.3 %copy-start.1 = (f32[16,128]{1,0:T(8,128)S(1)}, f32[16,128]{1,0:T(8,128)}, u32[]{:S(2)}) copy-start(f32[16,128]{1,0:T(8,128)} %log_decay.2) | copy-start | bytes 24580
  0.0 5.7 %copy-start.2 = (bf16[128,128]{1,0:T(8,128)(2,1)S(1)}, bf16[128,128]{1,0:T(8,128)(2,1)}, u32[]{:S(2)}) copy-start(bf16[128,128]{1,0:T(8,128)(2,1)} %c) | copy-start | bytes 98308
  0.0 1.3 %copy-start = (bf16[128,128]{1,0:T(8,128)(2,1)S(1)}, bf16[128,128]{1,0:T(8,128)(2,1)}, u32[]{:S(2)}) copy-start(bf16[128,128]{1,0:T(8,128)(2,1)} %b.2) | copy-start | bytes 98308
  0.0 5.5 %copy-start.6 = (bf16[128,16,128]{2,1,0:T(8,128)(2,1)S(1)}, bf16[128,16,128]{2,1,0:T(8,128)(2,1)}, u32[]{:S(2)}) copy-start(bf16[128,16,128]{2,1,0:T(8,128)(2,1)} %param.9) | copy-start | bytes 1572868
  0.0 1.1 %copy-start.5 = (bf16[128,16,128]{2,1,0:T(8,128)(2,1)S(1)}, bf16[128,16,128]{2,1,0:T(8,128)(2,1)}, u32[]{:S(2)}) copy-start(bf16[128,16,128]{2,1,0:T(8,128)(2,1)} %param.8) | copy-start | bytes 1572868
  2.1 7.6 %collective-permute-start.14 = (f32[520,128]{1,0:T(8,128)S(1)}, f32[520,128]{1,0:T(8,128)S(1)}, u32[]{:S(2)}, u32[]{:S(2)}) collective-permute-start(f32[520,128]{1,0:T(8,128)S(1)} %get-tuple-element.89), channel_id=1, source_target_pairs={{0,2},{2,0},{4,6},{6,4},{8,10},{10,8},{12,14},{14,12},{16,18},{18,... | collective-permute-start | bytes 798728 | tf_op jit(solution)/shard_map/ppermute | solution.py:305
  5.4 13.2 %collective-permute-start = (f32[520,128]{1,0:T(8,128)S(1)}, f32[520,128]{1,0:T(8,128)S(1)}, u32[]{:S(2)}, u32[]{:S(2)}) collective-permute-start(f32[520,128]{1,0:T(8,128)S(1)} %get-tuple-element.63), channel_id=1, source_target_pairs={{0,2},{2,0},{4,6},{6,4},{8,10},{10,8},{12,14},{14,12},{16,18},{18,... | collective-permute-start | bytes 798728 | tf_op jit(solution)/shard_map/ppermute | solution.py:305
  9.8 13.8 %collective-permute-start.15 = (f32[136,128]{1,0:T(8,128)S(1)}, f32[136,128]{1,0:T(8,128)S(1)}, u32[]{:S(2)}, u32[]{:S(2)}) collective-permute-start(f32[136,128]{1,0:T(8,128)S(1)} %get-tuple-element.91), channel_id=1, source_target_pairs={{0,12},{2,14},{4,8},{6,10},{8,4},{10,6},{12,0},{14,2},{16,28},{18,... | collective-permute-start | bytes 208904 | tf_op jit(solution)/shard_map/ppermute | solution.py:287
  16.4 8.8 %collective-permute-start.16 = (f32[136,128]{1,0:T(8,128)S(1)}, f32[136,128]{1,0:T(8,128)S(1)}, u32[]{:S(2)}, u32[]{:S(2)}) collective-permute-start(f32[136,128]{1,0:T(8,128)S(1)} %get-tuple-element.92), channel_id=1, source_target_pairs={{0,8},{2,10},{4,12},{6,14},{8,0},{10,2},{12,4},{14,6},{16,24},{18,... | collective-permute-start | bytes 208904 | tf_op jit(solution)/shard_map/ppermute | solution.py:287
  17.4 7.9 %collective-permute-start.17 = (f32[136,128]{1,0:T(8,128)S(1)}, f32[136,128]{1,0:T(8,128)S(1)}, u32[]{:S(2)}, u32[]{:S(2)}) collective-permute-start(f32[136,128]{1,0:T(8,128)S(1)} %get-tuple-element.93), channel_id=1, source_target_pairs={{0,4},{2,6},{4,0},{6,2},{8,12},{10,14},{12,8},{14,10},{16,20},{18,... | collective-permute-start | bytes 208904 | tf_op jit(solution)/shard_map/ppermute | solution.py:287
  18.7 9.8 %collective-permute-start.1 = (f32[136,128]{1,0:T(8,128)S(1)}, f32[136,128]{1,0:T(8,128)S(1)}, u32[]{:S(2)}, u32[]{:S(2)}) collective-permute-start(f32[136,128]{1,0:T(8,128)S(1)} %get-tuple-element.65), channel_id=1, source_target_pairs={{0,12},{2,14},{4,8},{6,10},{8,4},{10,6},{12,0},{14,2},{16,28},{18,... | collective-permute-start | bytes 208904 | tf_op jit(solution)/shard_map/ppermute | solution.py:287
  22.7 8.0 %collective-permute-start.2 = (f32[136,128]{1,0:T(8,128)S(1)}, f32[136,128]{1,0:T(8,128)S(1)}, u32[]{:S(2)}, u32[]{:S(2)}) collective-permute-start(f32[136,128]{1,0:T(8,128)S(1)} %get-tuple-element.66), channel_id=1, source_target_pairs={{0,8},{2,10},{4,12},{6,14},{8,0},{10,2},{12,4},{14,6},{16,24},{18,... | collective-permute-start | bytes 208904 | tf_op jit(solution)/shard_map/ppermute | solution.py:287
  23.5 7.2 %collective-permute-start.3 = (f32[136,128]{1,0:T(8,128)S(1)}, f32[136,128]{1,0:T(8,128)S(1)}, u32[]{:S(2)}, u32[]{:S(2)}) collective-permute-start(f32[136,128]{1,0:T(8,128)S(1)} %get-tuple-element.67), channel_id=1, source_target_pairs={{0,4},{2,6},{4,0},{6,2},{8,12},{10,14},{12,8},{14,10},{16,20},{18,... | collective-permute-start | bytes 208904 | tf_op jit(solution)/shard_map/ppermute | solution.py:287
  25.3 8.6 %collective-permute-start.20 = (f32[136,128]{1,0:T(8,128)S(1)}, f32[136,128]{1,0:T(8,128)S(1)}, u32[]{:S(2)}, u32[]{:S(2)}) collective-permute-start(f32[136,128]{1,0:T(8,128)S(1)} %row_total_0.1.refs_0_), channel_id=1, source_target_pairs={{0,48},{2,50},{4,52},{6,54},{8,56},{10,58},{12,60},{14,62},{16,32}... | collective-permute-start | bytes 208904 | tf_op jit(solution)/shard_map/ppermute | solution.py:287
  28.2 6.2 %collective-permute-start.19 = (f32[136,128]{1,0:T(8,128)S(1)}, f32[136,128]{1,0:T(8,128)S(1)}, u32[]{:S(2)}, u32[]{:S(2)}) collective-permute-start(f32[136,128]{1,0:T(8,128)S(1)} %row_total_0.1.refs_0_), channel_id=1, source_target_pairs={{0,32},{2,34},{4,36},{6,38},{8,40},{10,42},{12,44},{14,46},{16,48}... | collective-permute-start | bytes 208904 | tf_op jit(solution)/shard_map/ppermute | solution.py:287
  28.5 5.8 %collective-permute-start.18 = (f32[136,128]{1,0:T(8,128)S(1)}, f32[136,128]{1,0:T(8,128)S(1)}, u32[]{:S(2)}, u32[]{:S(2)}) collective-permute-start(f32[136,128]{1,0:T(8,128)S(1)} %row_total_0.1.refs_0_), channel_id=1, source_target_pairs={{0,16},{2,18},{4,20},{6,22},{8,24},{10,26},{12,28},{14,30},{16,0},... | collective-permute-start | bytes 208904 | tf_op jit(solution)/shard_map/ppermute | solution.py:287
  30.8 6.7 %collective-permute-start.6 = (f32[136,128]{1,0:T(8,128)S(1)}, f32[136,128]{1,0:T(8,128)S(1)}, u32[]{:S(2)}, u32[]{:S(2)}) collective-permute-start(f32[136,128]{1,0:T(8,128)S(1)} %row_total_1.1.refs_0_), channel_id=1, source_target_pairs={{0,48},{2,50},{4,52},{6,54},{8,56},{10,58},{12,60},{14,62},{16,32}... | collective-permute-start | bytes 208904 | tf_op jit(solution)/shard_map/ppermute | solution.py:287
  33.6 5.3 %collective-permute-start.5 = (f32[136,128]{1,0:T(8,128)S(1)}, f32[136,128]{1,0:T(8,128)S(1)}, u32[]{:S(2)}, u32[]{:S(2)}) collective-permute-start(f32[136,128]{1,0:T(8,128)S(1)} %row_total_1.1.refs_0_), channel_id=1, source_target_pairs={{0,32},{2,34},{4,36},{6,38},{8,40},{10,42},{12,44},{14,46},{16,48}... | collective-permute-start | bytes 208904 | tf_op jit(solution)/shard_map/ppermute | solution.py:287
  34.0 5.0 %collective-permute-start.4 = (f32[136,128]{1,0:T(8,128)S(1)}, f32[136,128]{1,0:T(8,128)S(1)}, u32[]{:S(2)}, u32[]{:S(2)}) collective-permute-start(f32[136,128]{1,0:T(8,128)S(1)} %row_total_1.1.refs_0_), channel_id=1, source_target_pairs={{0,16},{2,18},{4,20},{6,22},{8,24},{10,26},{12,28},{14,30},{16,0},... | collective-permute-start | bytes 208904 | tf_op jit(solution)/shard_map/ppermute | solution.py:287
  34.4 7.9 %collective-permute-start.23 = (f32[136,128]{1,0:T(8,128)S(1)}, f32[136,128]{1,0:T(8,128)S(1)}, u32[]{:S(2)}, u32[]{:S(2)}) collective-permute-start(f32[136,128]{1,0:T(8,128)S(1)} %get-tuple-element.94), channel_id=1, source_target_pairs={{0,192},{2,194},{4,196},{6,198},{8,200},{10,202},{12,204},{14,206}... | collective-permute-start | bytes 208904 | tf_op jit(solution)/shard_map/ppermute | solution.py:287
  36.9 5.6 %collective-permute-start.22 = (f32[136,128]{1,0:T(8,128)S(1)}, f32[136,128]{1,0:T(8,128)S(1)}, u32[]{:S(2)}, u32[]{:S(2)}) collective-permute-start(f32[136,128]{1,0:T(8,128)S(1)} %get-tuple-element.94), channel_id=1, source_target_pairs={{0,128},{2,130},{4,132},{6,134},{8,136},{10,138},{12,140},{14,142}... | collective-permute-start | bytes 208904 | tf_op jit(solution)/shard_map/ppermute | solution.py:287
  37.5 5.1 %collective-permute-start.21 = (f32[136,128]{1,0:T(8,128)S(1)}, f32[136,128]{1,0:T(8,128)S(1)}, u32[]{:S(2)}, u32[]{:S(2)}) collective-permute-start(f32[136,128]{1,0:T(8,128)S(1)} %get-tuple-element.94), channel_id=1, source_target_pairs={{0,64},{2,66},{4,68},{6,70},{8,72},{10,74},{12,76},{14,78},{16,80}... | collective-permute-start | bytes 208904 | tf_op jit(solution)/shard_map/ppermute | solution.py:287
  39.0 7.8 %collective-permute-start.9 = (f32[136,128]{1,0:T(8,128)S(1)}, f32[136,128]{1,0:T(8,128)S(1)}, u32[]{:S(2)}, u32[]{:S(2)}) collective-permute-start(f32[136,128]{1,0:T(8,128)S(1)} %get-tuple-element.68), channel_id=1, source_target_pairs={{0,192},{2,194},{4,196},{6,198},{8,200},{10,202},{12,204},{14,206}... | collective-permute-start | bytes 208904 | tf_op jit(solution)/shard_map/ppermute | solution.py:287
  41.8 6.6 %collective-permute-start.8 = (f32[136,128]{1,0:T(8,128)S(1)}, f32[136,128]{1,0:T(8,128)S(1)}, u32[]{:S(2)}, u32[]{:S(2)}) collective-permute-start(f32[136,128]{1,0:T(8,128)S(1)} %get-tuple-element.68), channel_id=1, source_target_pairs={{0,128},{2,130},{4,132},{6,134},{8,136},{10,138},{12,140},{14,142}... | collective-permute-start | bytes 208904 | tf_op jit(solution)/shard_map/ppermute | solution.py:287
  42.3 6.1 %collective-permute-start.7 = (f32[136,128]{1,0:T(8,128)S(1)}, f32[136,128]{1,0:T(8,128)S(1)}, u32[]{:S(2)}, u32[]{:S(2)}) collective-permute-start(f32[136,128]{1,0:T(8,128)S(1)} %get-tuple-element.68), channel_id=1, source_target_pairs={{0,64},{2,66},{4,68},{6,70},{8,72},{10,74},{12,76},{14,78},{16,80}... | collective-permute-start | bytes 208904 | tf_op jit(solution)/shard_map/ppermute | solution.py:287
  42.6 20.5 %slice-start = ((s8[8388608]{0:T(1024)(128)(4,1)}), s8[4194304]{0:T(1024)(128)(4,1)S(1)}, s32[]{:S(2)}) async-start(s8[8388608]{0:T(1024)(128)(4,1)} %bitcast.8), calls=%async_computation | async-start | bytes 8388608
  42.7 10.8 %collective-permute-start.24 = (f32[128,128]{1,0:T(8,128)S(1)}, f32[128,128]{1,0:T(8,128)S(1)}, u32[]{:S(2)}, u32[]{:S(2)}) collective-permute-start(f32[128,128]{1,0:T(8,128)S(1)} %get-tuple-element.97), channel_id=1, source_target_pairs={{0,4},{2,6},{4,0},{6,2},{8,12},{10,14},{12,8},{14,10},{16,20},{18,... | collective-permute-start | bytes 196616 | tf_op jit(solution)/shard_map/ppermute | solution.py:287
  44.3 9.9 %collective-permute-start.25 = (f32[128,128]{1,0:T(8,128)S(1)}, f32[128,128]{1,0:T(8,128)S(1)}, u32[]{:S(2)}, u32[]{:S(2)}) collective-permute-start(f32[128,128]{1,0:T(8,128)S(1)} %get-tuple-element.98), channel_id=1, source_target_pairs={{0,8},{2,10},{4,12},{6,14},{8,0},{10,2},{12,4},{14,6},{16,24},{18,... | collective-permute-start | bytes 196616 | tf_op jit(solution)/shard_map/ppermute | solution.py:287
  46.8 7.5 %collective-permute-start.26 = (f32[128,128]{1,0:T(8,128)S(1)}, f32[128,128]{1,0:T(8,128)S(1)}, u32[]{:S(2)}, u32[]{:S(2)}) collective-permute-start(f32[128,128]{1,0:T(8,128)S(1)} %get-tuple-element.99), channel_id=1, source_target_pairs={{0,12},{2,14},{4,8},{6,10},{8,4},{10,6},{12,0},{14,2},{16,28},{18,... | collective-permute-start | bytes 196616 | tf_op jit(solution)/shard_map/ppermute | solution.py:287
  48.4 14.6 %slice-start.1 = ((s8[8388608]{0:T(1024)(128)(4,1)}), s8[4194304]{0:T(1024)(128)(4,1)S(1)}, s32[]{:S(2)}) async-start(s8[8388608]{0:T(1024)(128)(4,1)} %bitcast.8), calls=%async_computation.1 | async-start | bytes 8388608
  48.5 6.8 %collective-permute-start.10 = (f32[128,128]{1,0:T(8,128)S(1)}, f32[128,128]{1,0:T(8,128)S(1)}, u32[]{:S(2)}, u32[]{:S(2)}) collective-permute-start(f32[128,128]{1,0:T(8,128)S(1)} %get-tuple-element.71), channel_id=1, source_target_pairs={{0,12},{2,14},{4,8},{6,10},{8,4},{10,6},{12,0},{14,2},{16,28},{18,... | collective-permute-start | bytes 196616 | tf_op jit(solution)/shard_map/ppermute | solution.py:287
  50.5 7.5 %collective-permute-start.11 = (f32[128,128]{1,0:T(8,128)S(1)}, f32[128,128]{1,0:T(8,128)S(1)}, u32[]{:S(2)}, u32[]{:S(2)}) collective-permute-start(f32[128,128]{1,0:T(8,128)S(1)} %get-tuple-element.72), channel_id=1, source_target_pairs={{0,8},{2,10},{4,12},{6,14},{8,0},{10,2},{12,4},{14,6},{16,24},{18,... | collective-permute-start | bytes 196616 | tf_op jit(solution)/shard_map/ppermute | solution.py:287
  53.5 5.8 %collective-permute-start.12 = (f32[128,128]{1,0:T(8,128)S(1)}, f32[128,128]{1,0:T(8,128)S(1)}, u32[]{:S(2)}, u32[]{:S(2)}) collective-permute-start(f32[128,128]{1,0:T(8,128)S(1)} %get-tuple-element.73), channel_id=1, source_target_pairs={{0,4},{2,6},{4,0},{6,2},{8,12},{10,14},{12,8},{14,10},{16,20},{18,... | collective-permute-start | bytes 196616 | tf_op jit(solution)/shard_map/ppermute | solution.py:287
  54.4 8.7 %collective-permute-start.27 = (f32[512,128]{1,0:T(8,128)S(1)}, f32[512,128]{1,0:T(8,128)S(1)}, u32[]{:S(2)}, u32[]{:S(2)}) collective-permute-start(f32[512,128]{1,0:T(8,128)S(1)} %get-tuple-element.101), channel_id=1, source_target_pairs={{0,2},{2,0},{4,6},{6,4},{8,10},{10,8},{12,14},{14,12},{16,18},{18,... | collective-permute-start | bytes 786440 | tf_op jit(solution)/shard_map/ppermute | solution.py:341
  59.4 10.8 %collective-permute-start.13 = (f32[512,128]{1,0:T(8,128)S(1)}, f32[512,128]{1,0:T(8,128)S(1)}, u32[]{:S(2)}, u32[]{:S(2)}) collective-permute-start(f32[512,128]{1,0:T(8,128)S(1)} %get-tuple-element.74), channel_id=1, source_target_pairs={{0,2},{2,0},{4,6},{6,4},{8,10},{10,8},{12,14},{14,12},{16,18},{18,... | collective-permute-start | bytes 786440 | tf_op jit(solution)/shard_map/ppermute | solution.py:341
  71.0 5.9 %collective-permute-start.28 = (f32[64,2048]{1,0:T(8,128)S(1)}, f32[64,2048]{1,0:T(8,128)S(1)}, u32[]{:S(2)}, u32[]{:S(2)}) collective-permute-start(f32[64,2048]{1,0:T(8,128)S(1)} %get-tuple-element.106), channel_id=1, source_target_pairs={{0,1},{1,0},{2,3},{3,2},{4,5},{5,4},{6,7},{7,6},{8,9},{9,8},{10,11... | collective-permute-start | bytes 1572872 | tf_op jit(solution)/shard_map/ppermute | solution.py:357
